TPU v7x, 32 devices: a whole 2x2x4 slice. The times are simulated.
32 devices in a mesh: dp: 32 (over z, y, x, core).
Axes of the slice: x: 2, y: 2, z: 4, core: 2. Of those that a mesh axis runs over, the one named last changes fastest.
Arguments:
- tokens: bfloat16 [4096, 3072], P('dp'), may hold values from -6 to 6
- slot_token: int32 [512], P('dp'), may hold values from 0 to 127, as said below
- slot_count: int32 [32], replicated, may hold values from 4 to 16, as said below
- slot_gate: float32 [512], P('dp'), may hold values from 0.2 to 1
- grad_out: bfloat16 [512, 3072], P('dp'), may hold values from -6 to 6
- w_gate: bfloat16 [8192, 3072], P('dp'), may hold values from -0.109375 to 0.109375
- w_up: bfloat16 [8192, 3072], P('dp'), may hold values from -0.109375 to 0.109375
- w_down: bfloat16 [8192, 3072], P('dp'), may hold values from -0.125 to 0.125
Outputs:
- expert_out: bfloat16 [512, 3072], P('dp')
- grad_rows: bfloat16 [512, 3072], P('dp')
- grad_gate_w: bfloat16 [8192, 3072], P('dp')
- grad_up_w: bfloat16 [8192, 3072], P('dp')
- grad_down_w: bfloat16 [8192, 3072], P('dp')
Inputs may be any that keep to these rules, and one draw needn't show every extreme that they name: `slot_token`: the 16 slots of one device name distinct tokens of that device. `slot_count`: some device has all 16 of its slots live.
All inputs are finite; a program needn't handle non-finite values.
Results may differ from a plain program's by a relative error of at most 0.009.
Values may be sent and summed in bfloat16 or wider, within the bound.
No kernel may reach another device: no remote copies, remote signals or barrier semaphores. Data moves between devices by JAX's collectives and lax.ppermute only.
A program may use at most 128 MiB of HBM per device.

v0:
```python
import math

import jax
import jax.numpy as jnp
from jax import lax
from jax.sharding import PartitionSpec as P


def swapped(block, axis, distance):
    count = lax.axis_size(axis)
    route = []
    for low in range(count):
        high = low | 1 << distance
        if high != low and high < count:
            route += [(low, high), (high, low)]
    return lax.ppermute(block, axis, route)


def row_product(left, right):
    return lax.dot_general(
        left, right, (((1,), (1,)), ((), ())), preferred_element_type=jnp.float32
    )


def col_product(left, right):
    return lax.dot_general(
        left, right, (((0,), (0,)), ((), ())), preferred_element_type=jnp.float32
    )


def expert_pass(picked, scaled, w_gate, w_up, w_down):
    gate_pre = row_product(picked, w_gate)
    up_pre = row_product(picked, w_up)
    gate_sig = jax.nn.sigmoid(gate_pre)
    activated = gate_pre * gate_sig
    hidden = (activated * up_pre).astype(jnp.bfloat16)
    out_part = jnp.dot(hidden, w_down, preferred_element_type=jnp.float32)
    hidden_grad = row_product(scaled, w_down)
    gate_grad = (hidden_grad * up_pre * (gate_sig * (1.0 + gate_pre * (1.0 - gate_sig)))).astype(
        jnp.bfloat16
    )
    up_grad = (hidden_grad * activated).astype(jnp.bfloat16)
    row_grad = jnp.dot(gate_grad, w_gate, preferred_element_type=jnp.float32) + jnp.dot(
        up_grad, w_up, preferred_element_type=jnp.float32
    )
    grads = jnp.stack(
        [col_product(gate_grad, picked), col_product(up_grad, picked), col_product(hidden, scaled)]
    )
    return (out_part, row_grad, grads)


def double_up(buffer, bit_list, axis_dim, partner):
    device = lax.axis_index("dp")
    for bit in bit_list:
        other = partner(buffer, bit)
        upper_side = device >> bit & 1 == 1
        buffer = jnp.where(
            upper_side,
            jnp.concatenate([other, buffer], axis_dim),
            jnp.concatenate([buffer, other], axis_dim),
        )
    return buffer


def halve_down(buffer, bit_list, axis_dim, partner):
    device = lax.axis_index("dp")
    for bit in bit_list:
        half_len = buffer.shape[axis_dim] // 2
        lower = lax.slice_in_dim(buffer, 0, half_len, axis=axis_dim)
        upper = lax.slice_in_dim(buffer, half_len, 2 * half_len, axis=axis_dim)
        upper_side = device >> bit & 1 == 1
        keeping = jnp.where(upper_side, upper, lower)
        sending = jnp.where(upper_side, lower, upper)
        buffer = keeping + partner(sending, bit)
    return buffer


def shards(tokens, slot_token, slot_count, slot_gate, grad_out, w_gate, w_up, w_down):
    capacity = slot_gate.shape[0]
    devices = lax.axis_size("dp")
    all_bits = devices.bit_length() - 1
    row_bits = 4
    device = lax.axis_index("dp")
    own_count = lax.dynamic_index_in_dim(slot_count, device, 0, keepdims=False)
    live_mask = jnp.arange(capacity, dtype=jnp.int32) < own_count
    weight = jnp.where(live_mask, slot_gate, 0.0)
    token_rows = jnp.take(tokens, slot_token, axis=0)
    scaled = (weight[:, None] * grad_out.astype(jnp.float32)).astype(jnp.bfloat16)
    row_list = list(range(row_bits))
    panel_list = list(range(row_bits, all_bits))
    panels = double_up(
        jnp.stack([w_gate, w_up, w_down]),
        panel_list,
        1,
        lambda piece, bit: swapped(piece, "dp", bit),
    )
    pooled_x = double_up(token_rows, row_list, 0, lambda piece, bit: swapped(piece, "dp", bit))
    pooled_e = double_up(scaled, row_list, 0, lambda piece, bit: swapped(piece, "dp", bit))
    out_part, row_grad, grads = expert_pass(pooled_x, pooled_e, panels[0], panels[1], panels[2])
    out_own = halve_down(out_part, row_list[::-1], 0, lambda piece, bit: swapped(piece, "dp", bit))
    row_own = halve_down(row_grad, row_list[::-1], 0, lambda piece, bit: swapped(piece, "dp", bit))
    owned = halve_down(
        grads,
        panel_list[::-1],
        1,
        lambda piece, bit: swapped(piece.astype(jnp.bfloat16), "dp", bit).astype(piece.dtype),
    )
    factor = 1.0 / math.sqrt(devices * capacity)
    expert_out = (weight[:, None] * out_own).astype(jnp.bfloat16)
    return (
        expert_out,
        row_own.astype(jnp.bfloat16),
        (owned[0] * factor).astype(jnp.bfloat16),
        (owned[1] * factor).astype(jnp.bfloat16),
        (owned[2] * factor).astype(jnp.bfloat16),
    )


def solution(mesh):
    return jax.shard_map(
        shards,
        mesh=mesh,
        in_specs=(
            P("dp", None),
            P("dp"),
            P(),
            P("dp"),
            P("dp", None),
            P("dp", None),
            P("dp", None),
            P("dp", None),
        ),
        out_specs=(P("dp", None), P("dp", None), P("dp", None), P("dp", None), P("dp", None)),
        check_vma=False,
    )
```

profile of v0, /device:TPU:0, one launch (start us, length us, event | category | flops | bytes accessed | tf_op | source)
XLA Modules:
  0.0 462.5 jit_solution(10754947572003293925)
XLA Ops:
  0.7 5.1 %pad_maximum_fusion.1 = bf16[3,256,3072]{2,1,0:T(8,128)(2,1)} fusion(bf16[1,256,3072]{2,1,0:T(8,128)(2,1)} %bitcast.36, bf16[1,256,3072]{2,1,0:T(8,128)(2,1)} %bitcast.38, bf16[1,256,3072]{2,1,0:T(8,128)(2,1)} %bitcast.40), kind=kLoop, calls=%fused_computation.8 | loop fusion | flops 4718592 | bytes 9437184 | tf_op jit(solution)/shard_map/stack | solution.py:92
  5.8 4.0 collective-permute-start.4
  11.2 0.6 compare_select_fusion.1
  12.6 1.6 collective-permute-start.1
  14.2 0.9 collective-permute-start.10
  15.1 5.3 %collective-permute-done.1 = bf16[32,3072]{1,0:T(8,128)(2,1)S(1)} collective-permute-done((bf16[32,3072]{1,0:T(8,128)(2,1)S(1)}, bf16[32,3072]{1,0:T(8,128)(2,1)S(1)}, u32[]{:S(2)}, u32[]{:S(2)}) %collective-permute-start.1) | collective-permute-done | bytes 196640 | tf_op jit(solution)/shard_map/ppermute | solution.py:16
  20.5 1.6 collective-permute-start.2
  22.1 1.6 collective-permute-done.10
  23.8 1.6 collective-permute-start.11
  25.4 7.2 %collective-permute-done.2 = bf16[64,3072]{1,0:T(8,128)(2,1)S(1)} collective-permute-done((bf16[64,3072]{1,0:T(8,128)(2,1)S(1)}, bf16[64,3072]{1,0:T(8,128)(2,1)S(1)}, u32[]{:S(2)}, u32[]{:S(2)}) %collective-permute-start.2) | collective-permute-done | bytes 393248 | tf_op jit(solution)/shard_map/ppermute | solution.py:16
  32.8 1.6 collective-permute-start.3
  34.4 4.1 collective-permute-done.11
  38.5 1.3 maximum_select_fusion.4
  39.8 1.6 collective-permute-start.12
  41.5 171.6 %collective-permute-done.4 = bf16[3,256,3072]{2,1,0:T(8,128)(2,1)} collective-permute-done((bf16[3,256,3072]{2,1,0:T(8,128)(2,1)}, bf16[3,256,3072]{2,1,0:T(8,128)(2,1)}, u32[]{:S(2)}, u32[]{:S(2)}) %collective-permute-start.4) | collective-permute-done | bytes 4718624 | tf_op jit(solution)/shard_map/ppermute | solution.py:16
  213.1 8.1 %maximum_select_fusion = bf16[3,512,3072]{2,1,0:T(8,128)(2,1)S(1)} fusion(bf16[1,256,3072]{2,1,0:T(8,128)(2,1)S(1)} %bitcast.37, bf16[1,256,3072]{2,1,0:T(8,128)(2,1)} %bitcast.39, bf16[1,256,3072]{2,1,0:T(8,128)(2,1)} %bitcast.41, bf16[3,256,3072]{2,1,0:T(8,128)(2,1)} %collective-permute-done.4, pred[]{:T(512)S(6)} %eq.14), kind=kLoop, calls=%fused_computation.2 | loop fusion | flops 80216064 | bytes 18874368 | tf_op jit(solution)/shard_map/jit(_where)/select_n | solution.py:57
  221.2 1.0 fusion.6
  222.2 1.0 fusion.5
  223.3 1.3 multiply_convert_fusion.1
  224.5 1.0 fusion.7
  225.5 1.5 slice_select_fusion.1
  227.0 0.7 collective-permute-start.5
  227.7 1.0 fusion.4
  228.7 1.0 convolution_add_fusion
  229.8 1.5 slice_select_fusion
  231.2 1.3 collective-permute-start.13
  232.5 1.0 convolution_bitcast_fusion
  233.6 1.1 convolution_bitcast_fusion.2
  234.7 1.1 convolution_bitcast_fusion.1
  235.8 6.7 %pad_maximum_fusion = f32[3,512,3072]{2,1,0:T(8,128)} fusion(f32[1,512,3072]{2,1,0:T(8,128)S(1)} %convolution_bitcast_fusion, f32[1,512,3072]{2,1,0:T(8,128)S(1)} %convolution_bitcast_fusion.1, f32[1,512,3072]{2,1,0:T(8,128)S(1)} %convolution_bitcast_fusion.2), kind=kLoop, calls=%fused_computation.1 | loop fusion | flops 9437184 | bytes 37748736 | tf_op jit(solution)/shard_map/stack | solution.py:46
  242.5 9.4 %select_convert_fusion = bf16[3,256,3072]{2,1,0:T(8,128)(2,1)} fusion(f32[3,512,3072]{2,1,0:T(8,128)} %pad_maximum_fusion, pred[]{:T(512)S(6)} %eq.14), kind=kLoop, calls=%fused_computation.4 | loop fusion | flops 2359296 | bytes 14155777 | tf_op jit(solution)/shard_map/convert_element_type | solution.py:106
  251.9 2.1 collective-permute-start.17
  253.9 87.0 %collective-permute-done.13 = f32[128,3072]{1,0:T(8,128)} collective-permute-done((f32[128,3072]{1,0:T(8,128)}, f32[128,3072]{1,0:T(8,128)}, u32[]{:S(2)}, u32[]{:S(2)}) %collective-permute-start.13) | collective-permute-done | bytes 1572896 | tf_op jit(solution)/shard_map/ppermute | solution.py:16
  340.9 2.6 select_add_fusion
  343.6 1.3 collective-permute-start.14
  345.0 1.8 select_add_fusion.1
  346.9 0.8 collective-permute-start.6
  347.7 16.5 %collective-permute-done.14 = f32[64,3072]{1,0:T(8,128)S(1)} collective-permute-done((f32[64,3072]{1,0:T(8,128)S(1)}, f32[64,3072]{1,0:T(8,128)S(1)}, u32[]{:S(2)}, u32[]{:S(2)}) %collective-permute-start.14) | collective-permute-done | bytes 786464 | tf_op jit(solution)/shard_map/ppermute | solution.py:16
  364.3 1.3 collective-permute-start.15
  365.7 12.7 %collective-permute-done.6 = f32[64,3072]{1,0:T(8,128)S(1)} collective-permute-done((f32[64,3072]{1,0:T(8,128)S(1)}, f32[64,3072]{1,0:T(8,128)S(1)}, u32[]{:S(2)}, u32[]{:S(2)}) %collective-permute-start.6) | collective-permute-done | bytes 786464 | tf_op jit(solution)/shard_map/ppermute | solution.py:16
  378.5 1.0 collective-permute-start.7
  379.7 7.3 %collective-permute-done.7 = f32[32,3072]{1,0:T(8,128)S(1)} collective-permute-done((f32[32,3072]{1,0:T(8,128)S(1)}, f32[32,3072]{1,0:T(8,128)S(1)}, u32[]{:S(2)}, u32[]{:S(2)}) %collective-permute-start.7) | collective-permute-done | bytes 393248 | tf_op jit(solution)/shard_map/ppermute | solution.py:16
  387.2 0.7 add_convert_fusion
  387.9 0.7 collective-permute-done.8
  388.7 0.7 multiply_convert_fusion.4
  389.4 67.6 %collective-permute-done.17 = bf16[3,256,3072]{2,1,0:T(8,128)(2,1)S(1)} collective-permute-done((bf16[3,256,3072]{2,1,0:T(8,128)(2,1)}, bf16[3,256,3072]{2,1,0:T(8,128)(2,1)S(1)}, u32[]{:S(2)}, u32[]{:S(2)}) %collective-permute-start.17) | collective-permute-done | bytes 4718624 | tf_op jit(solution)/shard_map/ppermute | solution.py:16
  457.0 2.8 convert_add_fusion
  459.8 2.7 fusion.10
  (55 shorter events, 3.3 us)
Async XLA Ops:
  0.6 9.2 %copy-start = (bf16[128,3072]{1,0:T(8,128)(2,1)S(1)}, bf16[128,3072]{1,0:T(8,128)(2,1)}, u32[]{:S(2)}) copy-start(bf16[128,3072]{1,0:T(8,128)(2,1)} %param.8) | copy-start | bytes 2359300
  0.6 9.2 %copy-start.8 = (s32[16]{0:T(128)S(1)}, s32[16]{0:T(128)}, u32[]{:S(2)}) copy-start(s32[16]{0:T(128)} %param.9) | copy-start | bytes 196
  0.7 10.0 %copy-start.9 = (s32[32]{0:T(128)S(1)}, s32[32]{0:T(128)}, u32[]{:S(2)}) copy-start(s32[32]{0:T(128)} %param.10) | copy-start | bytes 388
  0.7 10.6 %copy-start.10 = (f32[16]{0:T(128)S(1)}, f32[16]{0:T(128)}, u32[]{:S(2)}) copy-start(f32[16]{0:T(128)} %param.11) | copy-start | bytes 196
  0.7 11.2 %copy-start.7 = (bf16[16,3072]{1,0:T(8,128)(2,1)S(1)}, bf16[16,3072]{1,0:T(8,128)(2,1)}, u32[]{:S(2)}) copy-start(bf16[16,3072]{1,0:T(8,128)(2,1)} %param.12) | copy-start | bytes 294916
  5.8 207.3 %collective-permute-start.4 = (bf16[3,256,3072]{2,1,0:T(8,128)(2,1)}, bf16[3,256,3072]{2,1,0:T(8,128)(2,1)}, u32[]{:S(2)}, u32[]{:S(2)}) collective-permute-start(bf16[3,256,3072]{2,1,0:T(8,128)(2,1)} %pad_maximum_fusion.1), channel_id=1, source_target_pairs={{0,16},{16,0},{1,17},{17,1},{2,18},{18,2},{3,19},{19,3},{4,20},{20... | collective-permute-start | bytes 14155784 | tf_op jit(solution)/shard_map/ppermute | solution.py:16
  10.5 202.6 %copy-start.6 = (bf16[256,3072]{1,0:T(8,128)(2,1)S(1)}, bf16[256,3072]{1,0:T(8,128)(2,1)}, u32[]{:S(2)}) copy-start(bf16[256,3072]{1,0:T(8,128)(2,1)} %param.15) | copy-start | bytes 4718596
  10.6 2.0 collective-permute-start
  12.0 2.1 collective-permute-start.9
  12.6 7.8 %collective-permute-start.1 = (bf16[32,3072]{1,0:T(8,128)(2,1)S(1)}, bf16[32,3072]{1,0:T(8,128)(2,1)S(1)}, u32[]{:S(2)}, u32[]{:S(2)}) collective-permute-start(bf16[32,3072]{1,0:T(8,128)(2,1)S(1)} %maximum_select_fusion.9), channel_id=1, source_target_pairs={{0,2},{2,0},{1,3},{3,1},{4,6},{6,4},{5,7},{7,5},{8,10},{10,8},{9,1... | collective-permute-start | bytes 589832 | tf_op jit(solution)/shard_map/ppermute | solution.py:16
  14.2 9.5 %collective-permute-start.10 = (bf16[32,3072]{1,0:T(8,128)(2,1)S(1)}, bf16[32,3072]{1,0:T(8,128)(2,1)S(1)}, u32[]{:S(2)}, u32[]{:S(2)}) collective-permute-start(bf16[32,3072]{1,0:T(8,128)(2,1)S(1)} %maximum_select_fusion.10), channel_id=1, source_target_pairs={{0,2},{2,0},{1,3},{3,1},{4,6},{6,4},{5,7},{7,5},{8,10},{10,8},{9,1... | collective-permute-start | bytes 589832 | tf_op jit(solution)/shard_map/ppermute | solution.py:16
  20.5 12.1 %collective-permute-start.2 = (bf16[64,3072]{1,0:T(8,128)(2,1)S(1)}, bf16[64,3072]{1,0:T(8,128)(2,1)S(1)}, u32[]{:S(2)}, u32[]{:S(2)}) collective-permute-start(bf16[64,3072]{1,0:T(8,128)(2,1)S(1)} %maximum_select_fusion.5), channel_id=1, source_target_pairs={{0,4},{4,0},{1,5},{5,1},{2,6},{6,2},{3,7},{7,3},{8,12},{12,8},{9,1... | collective-permute-start | bytes 1179656 | tf_op jit(solution)/shard_map/ppermute | solution.py:16
  23.8 14.7 %collective-permute-start.11 = (bf16[64,3072]{1,0:T(8,128)(2,1)S(1)}, bf16[64,3072]{1,0:T(8,128)(2,1)}, u32[]{:S(2)}, u32[]{:S(2)}) collective-permute-start(bf16[64,3072]{1,0:T(8,128)(2,1)S(1)} %maximum_select_fusion.6), channel_id=1, source_target_pairs={{0,4},{4,0},{1,5},{5,1},{2,6},{6,2},{3,7},{7,3},{8,12},{12,8},{9,1... | collective-permute-start | bytes 1179656 | tf_op jit(solution)/shard_map/ppermute | solution.py:16
  32.8 189.5 %collective-permute-start.3 = (bf16[128,3072]{1,0:T(8,128)(2,1)S(1)}, bf16[128,3072]{1,0:T(8,128)(2,1)S(1)}, u32[]{:S(2)}, u32[]{:S(2)}) collective-permute-start(bf16[128,3072]{1,0:T(8,128)(2,1)S(1)} %maximum_select_fusion.3), channel_id=1, source_target_pairs={{0,8},{8,0},{1,9},{9,1},{2,10},{10,2},{3,11},{11,3},{4,12},{12,4},... | collective-permute-start | bytes 2359304 | tf_op jit(solution)/shard_map/ppermute | solution.py:16
  39.8 181.4 %collective-permute-start.12 = (bf16[128,3072]{1,0:T(8,128)(2,1)S(1)}, bf16[128,3072]{1,0:T(8,128)(2,1)S(1)}, u32[]{:S(2)}, u32[]{:S(2)}) collective-permute-start(bf16[128,3072]{1,0:T(8,128)(2,1)S(1)} %maximum_select_fusion.4), channel_id=1, source_target_pairs={{0,8},{8,0},{1,9},{9,1},{2,10},{10,2},{3,11},{11,3},{4,12},{12,4},... | collective-permute-start | bytes 2359304 | tf_op jit(solution)/shard_map/ppermute | solution.py:16
  225.5 3.2 copy-start.3
  227.0 118.0 %collective-permute-start.5 = (f32[128,3072]{1,0:T(8,128)}, f32[128,3072]{1,0:T(8,128)}, u32[]{:S(2)}, u32[]{:S(2)}) collective-permute-start(f32[128,3072]{1,0:T(8,128)} %slice_select_fusion.1), channel_id=1, source_target_pairs={{0,8},{8,0},{1,9},{9,1},{2,10},{10,2},{3,11},{11,3},{4,12},{12,4},... | collective-permute-start | bytes 4718600 | tf_op jit(solution)/shard_map/ppermute | solution.py:16
  229.7 3.9 copy-start.5
  231.2 109.7 %collective-permute-start.13 = (f32[128,3072]{1,0:T(8,128)}, f32[128,3072]{1,0:T(8,128)}, u32[]{:S(2)}, u32[]{:S(2)}) collective-permute-start(f32[128,3072]{1,0:T(8,128)} %slice_select_fusion), channel_id=1, source_target_pairs={{0,8},{8,0},{1,9},{9,1},{2,10},{10,2},{3,11},{11,3},{4,12},{12,4},... | collective-permute-start | bytes 4718600 | tf_op jit(solution)/shard_map/ppermute | solution.py:16
  251.9 93.1 %copy-start.4 = (f32[256,3072]{1,0:T(8,128)S(1)}, f32[256,3072]{1,0:T(8,128)}, u32[]{:S(2)}) copy-start(f32[256,3072]{1,0:T(8,128)} %copy-done.3) | copy-start | bytes 9437188
  251.9 205.2 %collective-permute-start.17 = (bf16[3,256,3072]{2,1,0:T(8,128)(2,1)}, bf16[3,256,3072]{2,1,0:T(8,128)(2,1)S(1)}, u32[]{:S(2)}, u32[]{:S(2)}) collective-permute-start(bf16[3,256,3072]{2,1,0:T(8,128)(2,1)} %select_convert_fusion), channel_id=1, source_target_pairs={{0,16},{16,0},{1,17},{17,1},{2,18},{18,2},{3,19},{19,3},{4,20},{20... | collective-permute-start | bytes 14155784 | tf_op jit(solution)/shard_map/ppermute | solution.py:16
  343.6 20.5 %collective-permute-start.14 = (f32[64,3072]{1,0:T(8,128)S(1)}, f32[64,3072]{1,0:T(8,128)S(1)}, u32[]{:S(2)}, u32[]{:S(2)}) collective-permute-start(f32[64,3072]{1,0:T(8,128)S(1)} %slice_select_fusion.2), channel_id=1, source_target_pairs={{0,4},{4,0},{1,5},{5,1},{2,6},{6,2},{3,7},{7,3},{8,12},{12,8},{9,1... | collective-permute-start | bytes 2359304 | tf_op jit(solution)/shard_map/ppermute | solution.py:16
  345.0 112.0 %copy-start.2 = (f32[3,512,3072]{2,1,0:T(8,128)S(1)}, f32[3,512,3072]{2,1,0:T(8,128)}, u32[]{:S(2)}) copy-start(f32[3,512,3072]{2,1,0:T(8,128)} %pad_maximum_fusion) | copy-start | bytes 56623108
  346.9 31.5 %collective-permute-start.6 = (f32[64,3072]{1,0:T(8,128)S(1)}, f32[64,3072]{1,0:T(8,128)S(1)}, u32[]{:S(2)}, u32[]{:S(2)}) collective-permute-start(f32[64,3072]{1,0:T(8,128)S(1)} %slice_select_fusion.3), channel_id=1, source_target_pairs={{0,4},{4,0},{1,5},{5,1},{2,6},{6,2},{3,7},{7,3},{8,12},{12,8},{9,1... | collective-permute-start | bytes 2359304 | tf_op jit(solution)/shard_map/ppermute | solution.py:16
  364.3 15.2 %collective-permute-start.15 = (f32[32,3072]{1,0:T(8,128)S(1)}, f32[32,3072]{1,0:T(8,128)S(1)}, u32[]{:S(2)}, u32[]{:S(2)}) collective-permute-start(f32[32,3072]{1,0:T(8,128)S(1)} %slice_select_fusion.4), channel_id=1, source_target_pairs={{0,2},{2,0},{1,3},{3,1},{4,6},{6,4},{5,7},{7,5},{8,10},{10,8},{9,1... | collective-permute-start | bytes 1179656 | tf_op jit(solution)/shard_map/ppermute | solution.py:16
  378.5 8.5 %collective-permute-start.7 = (f32[32,3072]{1,0:T(8,128)S(1)}, f32[32,3072]{1,0:T(8,128)S(1)}, u32[]{:S(2)}, u32[]{:S(2)}) collective-permute-start(f32[32,3072]{1,0:T(8,128)S(1)} %slice_select_fusion.5), channel_id=1, source_target_pairs={{0,2},{2,0},{1,3},{3,1},{4,6},{6,4},{5,7},{7,5},{8,10},{10,8},{9,1... | collective-permute-start | bytes 1179656 | tf_op jit(solution)/shard_map/ppermute | solution.py:16
  379.7 7.6 %collective-permute-start.16 = (f32[16,3072]{1,0:T(8,128)S(1)}, f32[16,3072]{1,0:T(8,128)S(1)}, u32[]{:S(2)}, u32[]{:S(2)}) collective-permute-start(f32[16,3072]{1,0:T(8,128)S(1)} %slice_select_fusion.6), channel_id=1, source_target_pairs={{0,1},{1,0},{2,3},{3,2},{4,5},{5,4},{6,7},{7,6},{8,9},{9,8},{10,11... | collective-permute-start | bytes 589832 | tf_op jit(solution)/shard_map/ppermute | solution.py:16
  387.2 1.5 collective-permute-start.8
  459.8 2.7 copy-start.1
where the time goes:
time: 463 us
  waiting for transfers between devices  382 us (83%)
  other arithmetic  46.7 us (10%)
  starting transfers between devices  22.3 us (5%)
  matrix products  9.51 us (2%)
    ppermute x18, waiting for transfers between devices, swapped(): return lax.ppermute(block, axis, route)  382 us
    ppermute x18, starting transfers between devices, swapped(): return lax.ppermute(block, axis, route)  22.3 us
    select_n x7, other arithmetic, double_up(): jnp.where(upper_side, jnp.concatenate([other, buffer], axis_dim), jnp.con...  9.81 us
    convert_element_type x1, other arithmetic, shards(): piece.astype(jnp.bfloat16)  9.37 us
  transfers between devices with their start and end apart: 18, of which 11 were waited for; matrix products, arithmetic and copies ran while one was open for 9% of the time, Pallas kernels for 0%

commit v1 on v0

v1 whole, which is shorter than its diff:
```python
import math

import jax
import jax.numpy as jnp
from jax import lax
from jax.sharding import PartitionSpec as P

CORE, LINK_X, LINK_Y, LINK_Z = 0, 1, 2, 3
ROW_BITS = 4


def swapped(block, mask):
    count = lax.axis_size("dp")
    return lax.ppermute(block, "dp", [(low, low ^ mask) for low in range(count)])


def row_product(left, right):
    return lax.dot_general(
        left, right, (((1,), (1,)), ((), ())), preferred_element_type=jnp.float32
    )


def col_product(left, right):
    return lax.dot_general(
        left, right, (((0,), (0,)), ((), ())), preferred_element_type=jnp.float32
    )


def product(left, right):
    return jnp.dot(left, right, preferred_element_type=jnp.float32)


def half(value):
    return value.astype(jnp.bfloat16)


def plane_gather(near, first, second):
    one = swapped(near, first)
    two = swapped(near, second)
    return near, one, two, swapped(one, second)


def plane_scatter(parts, first, second):
    own, near, far, both = parts
    moved = swapped(half(jnp.concatenate([far, both], 0)), first)
    rows = own.shape[0]
    kept = near + moved[rows:]
    return own + moved[:rows] + swapped(half(kept), second)


def forward(x, panels):
    hidden, saved = [], []
    for w_gate, w_up, _ in panels:
        gate_pre = row_product(x, w_gate)
        up_pre = row_product(x, w_up)
        gate_sig = jax.nn.sigmoid(gate_pre)
        activated = gate_pre * gate_sig
        hidden.append(half(activated * up_pre))
        slope = up_pre * (gate_sig * (1.0 + gate_pre * (1.0 - gate_sig)))
        saved.append((slope, activated))
    return hidden, saved


def backward(e, panels, saved):
    gate_grad, up_grad = [], []
    for (_, _, w_down), (slope, activated) in zip(panels, saved):
        hidden_grad = row_product(e, w_down)
        gate_grad.append(half(hidden_grad * slope))
        up_grad.append(half(hidden_grad * activated))
    return gate_grad, up_grad


def summed(terms):
    total = terms[0]
    for term in terms[1:]:
        total = total + term
    return total


def shards(tokens, slot_token, slot_count, slot_gate, grad_out, w_gate, w_up, w_down):
    capacity = slot_gate.shape[0]
    devices = lax.axis_size("dp")
    all_bits = devices.bit_length() - 1
    device = lax.axis_index("dp")
    own_count = lax.dynamic_index_in_dim(slot_count, device, 0, keepdims=False)
    live_mask = jnp.arange(capacity, dtype=jnp.int32) < own_count
    weight = jnp.where(live_mask, slot_gate, 0.0)
    x_own = jnp.take(tokens, slot_token, axis=0)
    e_own = half(weight[:, None] * grad_out.astype(jnp.float32))

    core, along_x, along_y = 1 << CORE, 1 << LINK_X, 1 << LINK_Y
    levels = range(1 << (ROW_BITS + 1 - LINK_Z))
    far_bits = range(ROW_BITS + 1, all_bits)

    x_level = [x_own] + [swapped(x_own, k << LINK_Z) for k in levels[1:]]
    e_level = [e_own] + [swapped(e_own, k << LINK_Z) for k in levels[1:]]
    groups = [levels[:2], levels[2:]]

    near = [w_gate, w_up, w_down]
    for bit in far_bits:
        near = [jnp.concatenate([w, swapped(w, 1 << bit)], 0) for w in near]
    panels = [near, [swapped(w, core) for w in near]]

    x_rows, e_rows, hiddens, gate_grads, up_grads = [], [], [], [], []
    sums = {}
    for group in groups:
        x_near = jnp.concatenate([x_level[k] for k in group], 0)
        e_near = jnp.concatenate([e_level[k] for k in group], 0)
        x_plane = plane_gather(x_near, along_x, along_y)
        e_plane = plane_gather(e_near, along_y, along_x)
        x = jnp.concatenate(x_plane, 0)
        e = jnp.concatenate([e_plane[0], e_plane[2], e_plane[1], e_plane[3]], 0)
        hidden, saved = forward(x, panels)
        gate_grad, up_grad = backward(e, panels, saved)
        out_part = summed([product(h, p[2]) for h, p in zip(hidden, panels)])
        row_part = summed(
            [product(g, p[0]) + product(u, p[1]) for g, u, p in zip(gate_grad, up_grad, panels)]
        )
        rows = x_near.shape[0]
        out_parts = [out_part[i * rows : (i + 1) * rows] for i in range(4)]
        row_parts = [row_part[i * rows : (i + 1) * rows] for i in (0, 2, 1, 3)]
        out_sum = plane_scatter(out_parts, along_y, along_x)
        row_sum = plane_scatter(row_parts, along_x, along_y)
        for i, k in enumerate(group):
            sums[k] = (
                out_sum[i * capacity : (i + 1) * capacity],
                row_sum[i * capacity : (i + 1) * capacity],
            )
        x_rows.append(x)
        e_rows.append(e)
        hiddens.append(hidden)
        gate_grads.append(gate_grad)
        up_grads.append(up_grad)

    out_own, row_own = sums[0]
    for k in levels[1:]:
        out_own = out_own + swapped(half(sums[k][0]), k << LINK_Z)
        row_own = row_own + swapped(half(sums[k][1]), k << LINK_Z)

    x_all = jnp.concatenate(x_rows, 0)
    e_all = jnp.concatenate(e_rows, 0)
    owned = []
    for left, right in ((gate_grads, x_all), (up_grads, x_all), (hiddens, e_all)):
        mine, other = (
            col_product(jnp.concatenate([part[i] for part in left], 0), right) for i in (0, 1)
        )
        total = mine + swapped(half(other), core)
        for bit in reversed(far_bits):
            middle = total.shape[0] // 2
            total = total[:middle] + swapped(half(total[middle:]), 1 << bit)
        owned.append(total)
    factor = 1.0 / math.sqrt(devices * capacity)
    return (
        half(weight[:, None] * out_own),
        half(row_own),
        half(owned[0] * factor),
        half(owned[1] * factor),
        half(owned[2] * factor),
    )


def solution(mesh):
    return jax.shard_map(
        shards,
        mesh=mesh,
        in_specs=(
            P("dp", None),
            P("dp"),
            P(),
            P("dp"),
            P("dp", None),
            P("dp", None),
            P("dp", None),
            P("dp", None),
        ),
        out_specs=(P("dp", None), P("dp", None), P("dp", None), P("dp", None), P("dp", None)),
        check_vma=False,
    )
```

time: 463 us -> 149 us (0.32)
  waiting for transfers between devices: 382 us -> 76.3 us
  other arithmetic: 46.7 us -> 5.63 us
  starting transfers between devices: 22.3 us -> 42.9 us
  matrix products: 9.51 us -> 19.9 us
    ppermute x18 -> x38, waiting for transfers between devices: 382 us -> 76.3 us  [swapped(): lax.ppermute(block, 'dp', [(low, low ^ mask) for low in range(count)])]
    ppermute x18 -> x38, starting transfers between devices: 22.3 us -> 42.9 us  [swapped(): lax.ppermute(block, 'dp', [(low, low ^ mask) for low in range(count)])]
    select_n x17 -> x1, other arithmetic: 13.1 us -> 0.73 us  [shards(): x_own = jnp.take(tokens, slot_token, axis=0)]
    convert_element_type x5 -> x6, other arithmetic: 13.6 us -> 1.55 us  [half(): return value.astype(jnp.bfloat16)]
    another operation x2, other arithmetic: 11.8 us -> 0.12 us  [the longest x1 6.7 us: expert_pass(): jnp.stack([col_product(gate_grad, picked), col_product(up_grad, picked),...]
    add x7 -> x2, other arithmetic: 7.56 us -> 0.11 us  [plane_scatter(): return own + moved[:rows] + swapped(half(kept), second)]
  transfers between devices with their start and end apart: 18 -> 38, of which waited for: 11 -> 24; matrix products, arithmetic and copies ran while one was open for 9% -> 16% of each run, Pallas kernels for 0% -> 0%
where the time goes in v1:
time: 149 us; the launch traced here: 148 us
  waiting for transfers between devices  76.3 us (51%)
  starting transfers between devices  42.9 us (29%)
  matrix products  19.9 us (13%)
  other arithmetic  5.63 us (4%)
  local copies, waits for them, and re-layouts  2.52 us (2%)
    ppermute x38, waiting for transfers between devices, swapped(): lax.ppermute(block, 'dp', [(low, low ^ mask) for low in range(count)])  76.3 us
    ppermute x38, starting transfers between devices, swapped(): lax.ppermute(block, 'dp', [(low, low ^ mask) for low in range(count)])  42.9 us
    dot_general x12, matrix products, row_product(): lax.dot_general(left, right, (((1,), (1,)), ((), ())), preferred_element_...  7.87 us
    dot_general x6, matrix products, col_product(): lax.dot_general(left, right, (((0,), (0,)), ((), ())), preferred_element_...  7.34 us
    dot_general x12, matrix products, product(): return jnp.dot(left, right, preferred_element_type=jnp.float32)  4.64 us
  transfers between devices with their start and end apart: 38, of which 24 were waited for; matrix products, arithmetic and copies ran while one was open for 16% of the time, Pallas kernels for 0%

profile of v1, /device:TPU:0, one launch (start us, length us, event | category | flops | bytes accessed | tf_op | source)
XLA Modules:
  0.0 148.4 jit_solution(14757622196206276309)
XLA Ops:
  2.8 3.1 %collective-permute-start = (bf16[16,3072]{1,0:T(8,128)(2,1)S(1)}, bf16[16,3072]{1,0:T(8,128)(2,1)S(1)}, u32[]{:S(2)}, u32[]{:S(2)}) collective-permute-start(bf16[16,3072]{1,0:T(8,128)(2,1)S(1)} %get-tuple-element.8), channel_id=1, source_target_pairs={{0,8},{1,9},{2,10},{3,11},{4,12},{5,13},{6,14},{7,15},{8,0},{9,1},... | collective-permute-start | bytes 294920 | tf_op jit(solution)/shard_map/ppermute | solution.py:14
  5.8 2.6 %collective-permute-start.10 = (bf16[16,3072]{1,0:T(8,128)(2,1)S(1)}, bf16[16,3072]{1,0:T(8,128)(2,1)S(1)}, u32[]{:S(2)}, u32[]{:S(2)}) collective-permute-start(bf16[16,3072]{1,0:T(8,128)(2,1)S(1)} %get-tuple-element.8), channel_id=1, source_target_pairs={{0,16},{1,17},{2,18},{3,19},{4,20},{5,21},{6,22},{7,23},{8,24},{9,... | collective-permute-start | bytes 294920 | tf_op jit(solution)/shard_map/ppermute | solution.py:14
  8.4 1.2 dynamic_slice.4
  9.7 1.3 compare_select_fusion.1
  13.5 4.3 %collective-permute-done.19 = bf16[16,3072]{1,0:T(8,128)(2,1)S(1)} collective-permute-done((bf16[16,3072]{1,0:T(8,128)(2,1)S(1)}, bf16[16,3072]{1,0:T(8,128)(2,1)S(1)}, u32[]{:S(2)}, u32[]{:S(2)}) %collective-permute-start.19) | collective-permute-done | bytes 98336 | tf_op jit(solution)/shard_map/ppermute | solution.py:14
  17.8 1.5 %collective-permute-start.1 = (bf16[32,3072]{1,0:T(8,128)(2,1)S(1)}, bf16[32,3072]{1,0:T(8,128)(2,1)S(1)}, u32[]{:S(2)}, u32[]{:S(2)}) collective-permute-start(bf16[32,3072]{1,0:T(8,128)(2,1)S(1)} %pad_maximum_fusion.2), channel_id=1, source_target_pairs={{0,2},{1,3},{2,0},{3,1},{4,6},{5,7},{6,4},{7,5},{8,10},{9,11},{10,... | collective-permute-start | bytes 589832 | tf_op jit(solution)/shard_map/ppermute | solution.py:14
  19.4 5.1 %collective-permute-done.1 = bf16[32,3072]{1,0:T(8,128)(2,1)S(1)} collective-permute-done((bf16[32,3072]{1,0:T(8,128)(2,1)S(1)}, bf16[32,3072]{1,0:T(8,128)(2,1)S(1)}, u32[]{:S(2)}, u32[]{:S(2)}) %collective-permute-start.1) | collective-permute-done | bytes 196640 | tf_op jit(solution)/shard_map/ppermute | solution.py:14
  24.5 1.3 collective-permute-start.2
  25.8 4.4 %collective-permute-done.2 = bf16[32,3072]{1,0:T(8,128)(2,1)S(1)} collective-permute-done((bf16[32,3072]{1,0:T(8,128)(2,1)S(1)}, bf16[32,3072]{1,0:T(8,128)(2,1)S(1)}, u32[]{:S(2)}, u32[]{:S(2)}) %collective-permute-start.2) | collective-permute-done | bytes 196640 | tf_op jit(solution)/shard_map/ppermute | solution.py:14
  30.2 1.2 collective-permute-start.20
  31.5 4.4 %collective-permute-done.20 = bf16[32,3072]{1,0:T(8,128)(2,1)S(1)} collective-permute-done((bf16[32,3072]{1,0:T(8,128)(2,1)S(1)}, bf16[32,3072]{1,0:T(8,128)(2,1)S(1)}, u32[]{:S(2)}, u32[]{:S(2)}) %collective-permute-start.20) | collective-permute-done | bytes 196640 | tf_op jit(solution)/shard_map/ppermute | solution.py:14
  35.9 1.2 collective-permute-start.21
  37.2 6.1 %collective-permute-done.21 = bf16[32,3072]{1,0:T(8,128)(2,1)S(1)} collective-permute-done((bf16[32,3072]{1,0:T(8,128)(2,1)S(1)}, bf16[32,3072]{1,0:T(8,128)(2,1)S(1)}, u32[]{:S(2)}, u32[]{:S(2)}) %collective-permute-start.21) | collective-permute-done | bytes 196640 | tf_op jit(solution)/shard_map/ppermute | solution.py:14
  43.3 1.6 %collective-permute-start.3 = (bf16[32,3072]{1,0:T(8,128)(2,1)S(1)}, bf16[32,3072]{1,0:T(8,128)(2,1)S(1)}, u32[]{:S(2)}, u32[]{:S(2)}) collective-permute-start(bf16[32,3072]{1,0:T(8,128)(2,1)S(1)} %collective-permute-done.1), channel_id=1, source_target_pairs={{0,4},{1,5},{2,6},{3,7},{4,0},{5,1},{6,2},{7,3},{8,12},{9,13},{10,... | collective-permute-start | bytes 589832 | tf_op jit(solution)/shard_map/ppermute | solution.py:14
  44.9 4.0 %collective-permute-done.3 = bf16[32,3072]{1,0:T(8,128)(2,1)S(1)} collective-permute-done((bf16[32,3072]{1,0:T(8,128)(2,1)S(1)}, bf16[32,3072]{1,0:T(8,128)(2,1)S(1)}, u32[]{:S(2)}, u32[]{:S(2)}) %collective-permute-start.3) | collective-permute-done | bytes 196640 | tf_op jit(solution)/shard_map/ppermute | solution.py:14
  49.0 1.6 %collective-permute-start.22 = (bf16[32,3072]{1,0:T(8,128)(2,1)S(1)}, bf16[32,3072]{1,0:T(8,128)(2,1)S(1)}, u32[]{:S(2)}, u32[]{:S(2)}) collective-permute-start(bf16[32,3072]{1,0:T(8,128)(2,1)S(1)} %collective-permute-done.21), channel_id=1, source_target_pairs={{0,2},{1,3},{2,0},{3,1},{4,6},{5,7},{6,4},{7,5},{8,10},{9,11},{10,... | collective-permute-start | bytes 589832 | tf_op jit(solution)/shard_map/ppermute | solution.py:14
  51.9 2.7 %collective-permute-done.22 = bf16[32,3072]{1,0:T(8,128)(2,1)S(1)} collective-permute-done((bf16[32,3072]{1,0:T(8,128)(2,1)S(1)}, bf16[32,3072]{1,0:T(8,128)(2,1)S(1)}, u32[]{:S(2)}, u32[]{:S(2)}) %collective-permute-start.22) | collective-permute-done | bytes 196640 | tf_op jit(solution)/shard_map/ppermute | solution.py:14
  56.3 2.2 %collective-permute-start.27 = (bf16[16,3072]{1,0:T(8,128)(2,1)S(1)}, bf16[16,3072]{1,0:T(8,128)(2,1)S(1)}, u32[]{:S(2)}, u32[]{:S(2)}) collective-permute-start(bf16[16,3072]{1,0:T(8,128)(2,1)S(1)} %get-tuple-element.6), channel_id=1, source_target_pairs={{0,24},{1,25},{2,26},{3,27},{4,28},{5,29},{6,30},{7,31},{8,16},{9,... | collective-permute-start | bytes 294920 | tf_op jit(solution)/shard_map/ppermute | solution.py:14
  58.5 7.3 %collective-permute-done.26 = bf16[16,3072]{1,0:T(8,128)(2,1)S(1)} collective-permute-done((bf16[16,3072]{1,0:T(8,128)(2,1)S(1)}, bf16[16,3072]{1,0:T(8,128)(2,1)S(1)}, u32[]{:S(2)}, u32[]{:S(2)}) %collective-permute-start.26) | collective-permute-done | bytes 98336 | tf_op jit(solution)/shard_map/ppermute | solution.py:14
  65.8 1.2 collective-permute-start.12
  67.0 1.6 %collective-permute-start.13 = (bf16[32,3072]{1,0:T(8,128)(2,1)S(1)}, bf16[32,3072]{1,0:T(8,128)(2,1)S(1)}, u32[]{:S(2)}, u32[]{:S(2)}) collective-permute-start(bf16[32,3072]{1,0:T(8,128)(2,1)S(1)} %get-tuple-element.63), channel_id=1, source_target_pairs={{0,4},{1,5},{2,6},{3,7},{4,0},{5,1},{6,2},{7,3},{8,12},{9,13},{10,... | collective-permute-start | bytes 589832 | tf_op jit(solution)/shard_map/ppermute | solution.py:14
  69.0 3.7 %collective-permute-done.12 = bf16[32,3072]{1,0:T(8,128)(2,1)S(1)} collective-permute-done((bf16[32,3072]{1,0:T(8,128)(2,1)S(1)}, bf16[32,3072]{1,0:T(8,128)(2,1)S(1)}, u32[]{:S(2)}, u32[]{:S(2)}) %collective-permute-start.12) | collective-permute-done | bytes 196640 | tf_op jit(solution)/shard_map/ppermute | solution.py:14
  72.6 1.2 collective-permute-start.28
  73.8 4.8 %collective-permute-done.28 = bf16[32,3072]{1,0:T(8,128)(2,1)S(1)} collective-permute-done((bf16[32,3072]{1,0:T(8,128)(2,1)S(1)}, bf16[32,3072]{1,0:T(8,128)(2,1)S(1)}, u32[]{:S(2)}, u32[]{:S(2)}) %collective-permute-start.28) | collective-permute-done | bytes 196640 | tf_op jit(solution)/shard_map/ppermute | solution.py:14
  78.6 1.2 collective-permute-start.29
  79.9 4.7 %collective-permute-done.29 = bf16[32,3072]{1,0:T(8,128)(2,1)S(1)} collective-permute-done((bf16[32,3072]{1,0:T(8,128)(2,1)S(1)}, bf16[32,3072]{1,0:T(8,128)(2,1)S(1)}, u32[]{:S(2)}, u32[]{:S(2)}) %collective-permute-start.29) | collective-permute-done | bytes 196640 | tf_op jit(solution)/shard_map/ppermute | solution.py:14
  84.5 1.2 collective-permute-start.14
  85.8 1.6 %collective-permute-start.30 = (bf16[32,3072]{1,0:T(8,128)(2,1)S(1)}, bf16[32,3072]{1,0:T(8,128)(2,1)S(1)}, u32[]{:S(2)}, u32[]{:S(2)}) collective-permute-start(bf16[32,3072]{1,0:T(8,128)(2,1)S(1)} %collective-permute-done.29), channel_id=1, source_target_pairs={{0,2},{1,3},{2,0},{3,1},{4,6},{5,7},{6,4},{7,5},{8,10},{9,11},{10,... | collective-permute-start | bytes 589832 | tf_op jit(solution)/shard_map/ppermute | solution.py:14
  87.3 2.9 %collective-permute-done.14 = bf16[32,3072]{1,0:T(8,128)(2,1)S(1)} collective-permute-done((bf16[32,3072]{1,0:T(8,128)(2,1)S(1)}, bf16[32,3072]{1,0:T(8,128)(2,1)S(1)}, u32[]{:S(2)}, u32[]{:S(2)}) %collective-permute-start.14) | collective-permute-done | bytes 196640 | tf_op jit(solution)/shard_map/ppermute | solution.py:14
  90.2 1.3 collective-permute-done.30
  100.5 1.3 collective-permute-start.15
  102.6 1.6 %collective-permute-start.23 = (bf16[64,3072]{1,0:T(8,128)(2,1)S(1)}, bf16[64,3072]{1,0:T(8,128)(2,1)S(1)}, u32[]{:S(2)}, u32[]{:S(2)}) collective-permute-start(bf16[64,3072]{1,0:T(8,128)(2,1)S(1)} %pad_maximum_fusion), channel_id=1, source_target_pairs={{0,2},{1,3},{2,0},{3,1},{4,6},{5,7},{6,4},{7,5},{8,10},{9,11},{10,... | collective-permute-start | bytes 1179656 | tf_op jit(solution)/shard_map/ppermute | solution.py:14
  107.9 1.6 %collective-permute-start.8 = (bf16[32,3072]{1,0:T(8,128)(2,1)S(1)}, bf16[32,3072]{1,0:T(8,128)(2,1)S(1)}, u32[]{:S(2)}, u32[]{:S(2)}) collective-permute-start(bf16[32,3072]{1,0:T(8,128)(2,1)S(1)} %fusion.16), channel_id=1, source_target_pairs={{0,2},{1,3},{2,0},{3,1},{4,6},{5,7},{6,4},{7,5},{8,10},{9,11},{10,... | collective-permute-start | bytes 589832 | tf_op jit(solution)/shard_map/ppermute | solution.py:14
  109.5 2.6 %collective-permute-done.15 = bf16[64,3072]{1,0:T(8,128)(2,1)S(1)} collective-permute-done((bf16[64,3072]{1,0:T(8,128)(2,1)S(1)}, bf16[64,3072]{1,0:T(8,128)(2,1)S(1)}, u32[]{:S(2)}, u32[]{:S(2)}) %collective-permute-start.15) | collective-permute-done | bytes 393248 | tf_op jit(solution)/shard_map/ppermute | solution.py:14
  112.1 1.6 %collective-permute-start.16 = (bf16[32,3072]{1,0:T(8,128)(2,1)S(1)}, bf16[32,3072]{1,0:T(8,128)(2,1)S(1)}, u32[]{:S(2)}, u32[]{:S(2)}) collective-permute-start(bf16[32,3072]{1,0:T(8,128)(2,1)S(1)} %fusion.13), channel_id=1, source_target_pairs={{0,2},{1,3},{2,0},{3,1},{4,6},{5,7},{6,4},{7,5},{8,10},{9,11},{10,... | collective-permute-start | bytes 589832 | tf_op jit(solution)/shard_map/ppermute | solution.py:14
  113.7 1.0 collective-permute-done.23
  115.6 5.6 %collective-permute-done.31 = bf16[64,3072]{1,0:T(8,128)(2,1)S(1)} collective-permute-done((bf16[64,3072]{1,0:T(8,128)(2,1)S(1)}, bf16[64,3072]{1,0:T(8,128)(2,1)S(1)}, u32[]{:S(2)}, u32[]{:S(2)}) %collective-permute-start.31) | collective-permute-done | bytes 393248 | tf_op jit(solution)/shard_map/ppermute | solution.py:14
  122.2 3.3 %collective-permute-done.16 = bf16[32,3072]{1,0:T(8,128)(2,1)S(1)} collective-permute-done((bf16[32,3072]{1,0:T(8,128)(2,1)S(1)}, bf16[32,3072]{1,0:T(8,128)(2,1)S(1)}, u32[]{:S(2)}, u32[]{:S(2)}) %collective-permute-start.16) | collective-permute-done | bytes 196640 | tf_op jit(solution)/shard_map/ppermute | solution.py:14
  126.0 1.0 collective-permute-done.32
  127.1 2.5 %collective-permute-start.34 = (bf16[16,3072]{1,0:T(8,128)(2,1)S(1)}, bf16[16,3072]{1,0:T(8,128)(2,1)S(1)}, u32[]{:S(2)}, u32[]{:S(2)}) collective-permute-start(bf16[16,3072]{1,0:T(8,128)(2,1)S(1)} %get-tuple-element.50), channel_id=1, source_target_pairs={{0,24},{1,25},{2,26},{3,27},{4,28},{5,29},{6,30},{7,31},{8,16},{9,... | collective-permute-start | bytes 294920 | tf_op jit(solution)/shard_map/ppermute | solution.py:14
  129.7 2.0 %collective-permute-start.25 = (bf16[16,3072]{1,0:T(8,128)(2,1)S(1)}, bf16[16,3072]{1,0:T(8,128)(2,1)S(1)}, u32[]{:S(2)}, u32[]{:S(2)}) collective-permute-start(bf16[16,3072]{1,0:T(8,128)(2,1)S(1)} %slice.214), channel_id=1, source_target_pairs={{0,8},{1,9},{2,10},{3,11},{4,12},{5,13},{6,14},{7,15},{8,0},{9,1},... | collective-permute-start | bytes 294920 | tf_op jit(solution)/shard_map/ppermute | solution.py:14
  132.1 1.5 %collective-permute-done.34 = bf16[16,3072]{1,0:T(8,128)(2,1)S(1)} collective-permute-done((bf16[16,3072]{1,0:T(8,128)(2,1)S(1)}, bf16[16,3072]{1,0:T(8,128)(2,1)S(1)}, u32[]{:S(2)}, u32[]{:S(2)}) %collective-permute-start.34) | collective-permute-done | bytes 98336 | tf_op jit(solution)/shard_map/ppermute | solution.py:14
  133.6 2.1 %collective-permute-done.33 = bf16[16,3072]{1,0:T(8,128)(2,1)S(1)} collective-permute-done((bf16[16,3072]{1,0:T(8,128)(2,1)S(1)}, bf16[16,3072]{1,0:T(8,128)(2,1)S(1)}, u32[]{:S(2)}, u32[]{:S(2)}) %collective-permute-start.33) | collective-permute-done | bytes 98336 | tf_op jit(solution)/shard_map/ppermute | solution.py:14
  136.2 2.4 %collective-permute-start.9 = (bf16[16,3072]{1,0:T(8,128)(2,1)S(1)}, bf16[16,3072]{1,0:T(8,128)(2,1)S(1)}, u32[]{:S(2)}, u32[]{:S(2)}) collective-permute-start(bf16[16,3072]{1,0:T(8,128)(2,1)S(1)} %slice.215), channel_id=1, source_target_pairs={{0,8},{1,9},{2,10},{3,11},{4,12},{5,13},{6,14},{7,15},{8,0},{9,1},... | collective-permute-start | bytes 294920 | tf_op jit(solution)/shard_map/ppermute | solution.py:14
  139.3 2.8 %collective-permute-done.17 = bf16[16,3072]{1,0:T(8,128)(2,1)S(1)} collective-permute-done((bf16[16,3072]{1,0:T(8,128)(2,1)S(1)}, bf16[16,3072]{1,0:T(8,128)(2,1)S(1)}, u32[]{:S(2)}, u32[]{:S(2)}) %collective-permute-start.17) | collective-permute-done | bytes 98336 | tf_op jit(solution)/shard_map/ppermute | solution.py:14
  143.0 1.8 %fusion.3 = bf16[256,3072]{1,0:T(8,128)(2,1)} fusion(bf16[256,3072]{1,0:T(8,128)(2,1)S(1)} %get-tuple-element.37, bf16[256,3072]{1,0:T(8,128)(2,1)S(1)} %collective-permute-done.35, bf16[128,256]{1,0:T(8,128)(2,1)S(1)} %get-tuple-element.17, bf16[128,256]{1,0:T(8,128)(2,1)S(1)} %get-tuple-element.23), kind=kOutput, calls=%fused_computation.7 | convolution fusion | flops 406061056 | bytes 4849664 | tf_op jit(solution)/shard_map/dot_general | solution.py:24
  144.8 1.8 %fusion.4 = bf16[256,3072]{1,0:T(8,128)(2,1)} fusion(bf16[256,3072]{1,0:T(8,128)(2,1)S(1)} %get-tuple-element.37, bf16[256,3072]{1,0:T(8,128)(2,1)S(1)} %collective-permute-done.36, bf16[128,256]{1,0:T(8,128)(2,1)S(1)} %get-tuple-element.16, bf16[128,256]{1,0:T(8,128)(2,1)S(1)} %get-tuple-element.22), kind=kOutput, calls=%fused_computation.8 | convolution fusion | flops 406061056 | bytes 4849664 | tf_op jit(solution)/shard_map/dot_general | solution.py:24
  146.6 1.8 %fusion.5 = bf16[256,3072]{1,0:T(8,128)(2,1)} fusion(bf16[256,3072]{1,0:T(8,128)(2,1)S(1)} %get-tuple-element.25, bf16[256,3072]{1,0:T(8,128)(2,1)S(1)} %collective-permute-done.37, bf16[128,256]{1,0:T(8,128)(2,1)S(1)} %get-tuple-element.18, bf16[128,256]{1,0:T(8,128)(2,1)S(1)} %get-tuple-element.24), kind=kOutput, calls=%fused_computation.9 | convolution fusion | flops 406061056 | bytes 4849664 | tf_op jit(solution)/shard_map/dot_general | solution.py:24
  (116 shorter events, 26.8 us)
Async XLA Ops:
  0.6 1.4 copy-start
  2.8 10.2 %collective-permute-start = (bf16[16,3072]{1,0:T(8,128)(2,1)S(1)}, bf16[16,3072]{1,0:T(8,128)(2,1)S(1)}, u32[]{:S(2)}, u32[]{:S(2)}) collective-permute-start(bf16[16,3072]{1,0:T(8,128)(2,1)S(1)} %get-tuple-element.8), channel_id=1, source_target_pairs={{0,8},{1,9},{2,10},{3,11},{4,12},{5,13},{6,14},{7,15},{8,0},{9,1},... | collective-permute-start | bytes 294920 | tf_op jit(solution)/shard_map/ppermute | solution.py:14
  5.8 50.3 %collective-permute-start.10 = (bf16[16,3072]{1,0:T(8,128)(2,1)S(1)}, bf16[16,3072]{1,0:T(8,128)(2,1)S(1)}, u32[]{:S(2)}, u32[]{:S(2)}) collective-permute-start(bf16[16,3072]{1,0:T(8,128)(2,1)S(1)} %get-tuple-element.8), channel_id=1, source_target_pairs={{0,16},{1,17},{2,18},{3,19},{4,20},{5,21},{6,22},{7,23},{8,24},{9,... | collective-permute-start | bytes 294920 | tf_op jit(solution)/shard_map/ppermute | solution.py:14
  8.4 47.8 %collective-permute-start.11 = (bf16[16,3072]{1,0:T(8,128)(2,1)S(1)}, bf16[16,3072]{1,0:T(8,128)(2,1)S(1)}, u32[]{:S(2)}, u32[]{:S(2)}) collective-permute-start(bf16[16,3072]{1,0:T(8,128)(2,1)S(1)} %get-tuple-element.8), channel_id=1, source_target_pairs={{0,24},{1,25},{2,26},{3,27},{4,28},{5,29},{6,30},{7,31},{8,16},{9,... | collective-permute-start | bytes 294920 | tf_op jit(solution)/shard_map/ppermute | solution.py:14
  12.0 5.9 %collective-permute-start.19 = (bf16[16,3072]{1,0:T(8,128)(2,1)S(1)}, bf16[16,3072]{1,0:T(8,128)(2,1)S(1)}, u32[]{:S(2)}, u32[]{:S(2)}) collective-permute-start(bf16[16,3072]{1,0:T(8,128)(2,1)S(1)} %get-tuple-element.6), channel_id=1, source_target_pairs={{0,8},{1,9},{2,10},{3,11},{4,12},{5,13},{6,14},{7,15},{8,0},{9,1},... | collective-permute-start | bytes 294920 | tf_op jit(solution)/shard_map/ppermute | solution.py:14
  12.9 81.7 %collective-permute-start.5 = (bf16[256,3072]{1,0:T(8,128)(2,1)}, bf16[256,3072]{1,0:T(8,128)(2,1)S(1)}, u32[]{:S(2)}, u32[]{:S(2)}) collective-permute-start(bf16[256,3072]{1,0:T(8,128)(2,1)} %param.14), channel_id=1, source_target_pairs={{0,1},{1,0},{2,3},{3,2},{4,5},{5,4},{6,7},{7,6},{8,9},{9,8},{10,11... | collective-permute-start | bytes 4718600 | tf_op jit(solution)/shard_map/ppermute | solution.py:14
  13.0 82.4 %collective-permute-start.4 = (bf16[256,3072]{1,0:T(8,128)(2,1)}, bf16[256,3072]{1,0:T(8,128)(2,1)S(1)}, u32[]{:S(2)}, u32[]{:S(2)}) collective-permute-start(bf16[256,3072]{1,0:T(8,128)(2,1)} %param.13), channel_id=1, source_target_pairs={{0,1},{1,0},{2,3},{3,2},{4,5},{5,4},{6,7},{7,6},{8,9},{9,8},{10,11... | collective-permute-start | bytes 4718600 | tf_op jit(solution)/shard_map/ppermute | solution.py:14
  17.8 6.6 %collective-permute-start.1 = (bf16[32,3072]{1,0:T(8,128)(2,1)S(1)}, bf16[32,3072]{1,0:T(8,128)(2,1)S(1)}, u32[]{:S(2)}, u32[]{:S(2)}) collective-permute-start(bf16[32,3072]{1,0:T(8,128)(2,1)S(1)} %pad_maximum_fusion.2), channel_id=1, source_target_pairs={{0,2},{1,3},{2,0},{3,1},{4,6},{5,7},{6,4},{7,5},{8,10},{9,11},{10,... | collective-permute-start | bytes 589832 | tf_op jit(solution)/shard_map/ppermute | solution.py:14
  19.3 31.2 %copy-start.1 = (bf16[256,3072]{1,0:T(8,128)(2,1)S(1)}, bf16[256,3072]{1,0:T(8,128)(2,1)}, u32[]{:S(2)}) copy-start(bf16[256,3072]{1,0:T(8,128)(2,1)} %param.13) | copy-start | bytes 4718596
  24.5 5.8 %collective-permute-start.2 = (bf16[32,3072]{1,0:T(8,128)(2,1)S(1)}, bf16[32,3072]{1,0:T(8,128)(2,1)S(1)}, u32[]{:S(2)}, u32[]{:S(2)}) collective-permute-start(bf16[32,3072]{1,0:T(8,128)(2,1)S(1)} %pad_maximum_fusion.2), channel_id=1, source_target_pairs={{0,4},{1,5},{2,6},{3,7},{4,0},{5,1},{6,2},{7,3},{8,12},{9,13},{10,... | collective-permute-start | bytes 589832 | tf_op jit(solution)/shard_map/ppermute | solution.py:14
  30.2 5.7 %collective-permute-start.20 = (bf16[32,3072]{1,0:T(8,128)(2,1)S(1)}, bf16[32,3072]{1,0:T(8,128)(2,1)S(1)}, u32[]{:S(2)}, u32[]{:S(2)}) collective-permute-start(bf16[32,3072]{1,0:T(8,128)(2,1)S(1)} %pad_maximum_fusion.3), channel_id=1, source_target_pairs={{0,2},{1,3},{2,0},{3,1},{4,6},{5,7},{6,4},{7,5},{8,10},{9,11},{10,... | collective-permute-start | bytes 589832 | tf_op jit(solution)/shard_map/ppermute | solution.py:14
  35.9 7.4 %collective-permute-start.21 = (bf16[32,3072]{1,0:T(8,128)(2,1)S(1)}, bf16[32,3072]{1,0:T(8,128)(2,1)S(1)}, u32[]{:S(2)}, u32[]{:S(2)}) collective-permute-start(bf16[32,3072]{1,0:T(8,128)(2,1)S(1)} %pad_maximum_fusion.3), channel_id=1, source_target_pairs={{0,4},{1,5},{2,6},{3,7},{4,0},{5,1},{6,2},{7,3},{8,12},{9,13},{10,... | collective-permute-start | bytes 589832 | tf_op jit(solution)/shard_map/ppermute | solution.py:14
  43.3 5.7 %collective-permute-start.3 = (bf16[32,3072]{1,0:T(8,128)(2,1)S(1)}, bf16[32,3072]{1,0:T(8,128)(2,1)S(1)}, u32[]{:S(2)}, u32[]{:S(2)}) collective-permute-start(bf16[32,3072]{1,0:T(8,128)(2,1)S(1)} %collective-permute-done.1), channel_id=1, source_target_pairs={{0,4},{1,5},{2,6},{3,7},{4,0},{5,1},{6,2},{7,3},{8,12},{9,13},{10,... | collective-permute-start | bytes 589832 | tf_op jit(solution)/shard_map/ppermute | solution.py:14
  44.9 6.3 %copy-start.2 = (bf16[256,3072]{1,0:T(8,128)(2,1)S(1)}, bf16[256,3072]{1,0:T(8,128)(2,1)}, u32[]{:S(2)}) copy-start(bf16[256,3072]{1,0:T(8,128)(2,1)} %param.14) | copy-start | bytes 4718596
  49.0 5.7 %collective-permute-start.22 = (bf16[32,3072]{1,0:T(8,128)(2,1)S(1)}, bf16[32,3072]{1,0:T(8,128)(2,1)S(1)}, u32[]{:S(2)}, u32[]{:S(2)}) collective-permute-start(bf16[32,3072]{1,0:T(8,128)(2,1)S(1)} %collective-permute-done.21), channel_id=1, source_target_pairs={{0,2},{1,3},{2,0},{3,1},{4,6},{5,7},{6,4},{7,5},{8,10},{9,11},{10,... | collective-permute-start | bytes 589832 | tf_op jit(solution)/shard_map/ppermute | solution.py:14
  51.3 3.4 %copy-start.3 = (bf16[256,3072]{1,0:T(8,128)(2,1)S(1)}, bf16[256,3072]{1,0:T(8,128)(2,1)}, u32[]{:S(2)}) copy-start(bf16[256,3072]{1,0:T(8,128)(2,1)} %param.15) | copy-start | bytes 4718596
  54.7 41.4 %collective-permute-start.6 = (bf16[256,3072]{1,0:T(8,128)(2,1)S(1)}, bf16[256,3072]{1,0:T(8,128)(2,1)S(1)}, u32[]{:S(2)}, u32[]{:S(2)}) collective-permute-start(bf16[256,3072]{1,0:T(8,128)(2,1)S(1)} %copy-done.3), channel_id=1, source_target_pairs={{0,1},{1,0},{2,3},{3,2},{4,5},{5,4},{6,7},{7,6},{8,9},{9,8},{10,11... | collective-permute-start | bytes 4718600 | tf_op jit(solution)/shard_map/ppermute | solution.py:14
  56.1 9.6 %collective-permute-start.26 = (bf16[16,3072]{1,0:T(8,128)(2,1)S(1)}, bf16[16,3072]{1,0:T(8,128)(2,1)S(1)}, u32[]{:S(2)}, u32[]{:S(2)}) collective-permute-start(bf16[16,3072]{1,0:T(8,128)(2,1)S(1)} %get-tuple-element.6), channel_id=1, source_target_pairs={{0,16},{1,17},{2,18},{3,19},{4,20},{5,21},{6,22},{7,23},{8,24},{9,... | collective-permute-start | bytes 294920 | tf_op jit(solution)/shard_map/ppermute | solution.py:14
  56.3 10.7 %collective-permute-start.27 = (bf16[16,3072]{1,0:T(8,128)(2,1)S(1)}, bf16[16,3072]{1,0:T(8,128)(2,1)S(1)}, u32[]{:S(2)}, u32[]{:S(2)}) collective-permute-start(bf16[16,3072]{1,0:T(8,128)(2,1)S(1)} %get-tuple-element.6), channel_id=1, source_target_pairs={{0,24},{1,25},{2,26},{3,27},{4,28},{5,29},{6,30},{7,31},{8,16},{9,... | collective-permute-start | bytes 294920 | tf_op jit(solution)/shard_map/ppermute | solution.py:14
  65.8 6.8 %collective-permute-start.12 = (bf16[32,3072]{1,0:T(8,128)(2,1)S(1)}, bf16[32,3072]{1,0:T(8,128)(2,1)S(1)}, u32[]{:S(2)}, u32[]{:S(2)}) collective-permute-start(bf16[32,3072]{1,0:T(8,128)(2,1)S(1)} %get-tuple-element.63), channel_id=1, source_target_pairs={{0,2},{1,3},{2,0},{3,1},{4,6},{5,7},{6,4},{7,5},{8,10},{9,11},{10,... | collective-permute-start | bytes 589832 | tf_op jit(solution)/shard_map/ppermute | solution.py:14
  67.0 18.8 %collective-permute-start.13 = (bf16[32,3072]{1,0:T(8,128)(2,1)S(1)}, bf16[32,3072]{1,0:T(8,128)(2,1)S(1)}, u32[]{:S(2)}, u32[]{:S(2)}) collective-permute-start(bf16[32,3072]{1,0:T(8,128)(2,1)S(1)} %get-tuple-element.63), channel_id=1, source_target_pairs={{0,4},{1,5},{2,6},{3,7},{4,0},{5,1},{6,2},{7,3},{8,12},{9,13},{10,... | collective-permute-start | bytes 589832 | tf_op jit(solution)/shard_map/ppermute | solution.py:14
  72.6 6.0 %collective-permute-start.28 = (bf16[32,3072]{1,0:T(8,128)(2,1)S(1)}, bf16[32,3072]{1,0:T(8,128)(2,1)S(1)}, u32[]{:S(2)}, u32[]{:S(2)}) collective-permute-start(bf16[32,3072]{1,0:T(8,128)(2,1)S(1)} %get-tuple-element.55), channel_id=1, source_target_pairs={{0,2},{1,3},{2,0},{3,1},{4,6},{5,7},{6,4},{7,5},{8,10},{9,11},{10,... | collective-permute-start | bytes 589832 | tf_op jit(solution)/shard_map/ppermute | solution.py:14
  78.6 5.9 %collective-permute-start.29 = (bf16[32,3072]{1,0:T(8,128)(2,1)S(1)}, bf16[32,3072]{1,0:T(8,128)(2,1)S(1)}, u32[]{:S(2)}, u32[]{:S(2)}) collective-permute-start(bf16[32,3072]{1,0:T(8,128)(2,1)S(1)} %get-tuple-element.55), channel_id=1, source_target_pairs={{0,4},{1,5},{2,6},{3,7},{4,0},{5,1},{6,2},{7,3},{8,12},{9,13},{10,... | collective-permute-start | bytes 589832 | tf_op jit(solution)/shard_map/ppermute | solution.py:14
  84.5 5.7 %collective-permute-start.14 = (bf16[32,3072]{1,0:T(8,128)(2,1)S(1)}, bf16[32,3072]{1,0:T(8,128)(2,1)S(1)}, u32[]{:S(2)}, u32[]{:S(2)}) collective-permute-start(bf16[32,3072]{1,0:T(8,128)(2,1)S(1)} %collective-permute-done.12), channel_id=1, source_target_pairs={{0,4},{1,5},{2,6},{3,7},{4,0},{5,1},{6,2},{7,3},{8,12},{9,13},{10,... | collective-permute-start | bytes 589832 | tf_op jit(solution)/shard_map/ppermute | solution.py:14
  85.8 5.7 %collective-permute-start.30 = (bf16[32,3072]{1,0:T(8,128)(2,1)S(1)}, bf16[32,3072]{1,0:T(8,128)(2,1)S(1)}, u32[]{:S(2)}, u32[]{:S(2)}) collective-permute-start(bf16[32,3072]{1,0:T(8,128)(2,1)S(1)} %collective-permute-done.29), channel_id=1, source_target_pairs={{0,2},{1,3},{2,0},{3,1},{4,6},{5,7},{6,4},{7,5},{8,10},{9,11},{10,... | collective-permute-start | bytes 589832 | tf_op jit(solution)/shard_map/ppermute | solution.py:14
  97.1 10.8 %collective-permute-start.7 = (bf16[64,3072]{1,0:T(8,128)(2,1)S(1)}, bf16[64,3072]{1,0:T(8,128)(2,1)S(1)}, u32[]{:S(2)}, u32[]{:S(2)}) collective-permute-start(bf16[64,3072]{1,0:T(8,128)(2,1)S(1)} %concatenate.93), channel_id=1, source_target_pairs={{0,4},{1,5},{2,6},{3,7},{4,0},{5,1},{6,2},{7,3},{8,12},{9,13},{10,... | collective-permute-start | bytes 1179656 | tf_op jit(solution)/shard_map/ppermute | solution.py:14
  100.5 11.7 %collective-permute-start.15 = (bf16[64,3072]{1,0:T(8,128)(2,1)S(1)}, bf16[64,3072]{1,0:T(8,128)(2,1)S(1)}, u32[]{:S(2)}, u32[]{:S(2)}) collective-permute-start(bf16[64,3072]{1,0:T(8,128)(2,1)S(1)} %concatenate.92), channel_id=1, source_target_pairs={{0,4},{1,5},{2,6},{3,7},{4,0},{5,1},{6,2},{7,3},{8,12},{9,13},{10,... | collective-permute-start | bytes 1179656 | tf_op jit(solution)/shard_map/ppermute | solution.py:14
  102.6 12.1 %collective-permute-start.23 = (bf16[64,3072]{1,0:T(8,128)(2,1)S(1)}, bf16[64,3072]{1,0:T(8,128)(2,1)S(1)}, u32[]{:S(2)}, u32[]{:S(2)}) collective-permute-start(bf16[64,3072]{1,0:T(8,128)(2,1)S(1)} %pad_maximum_fusion), channel_id=1, source_target_pairs={{0,2},{1,3},{2,0},{3,1},{4,6},{5,7},{6,4},{7,5},{8,10},{9,11},{10,... | collective-permute-start | bytes 1179656 | tf_op jit(solution)/shard_map/ppermute | solution.py:14
  106.4 14.8 %collective-permute-start.31 = (bf16[64,3072]{1,0:T(8,128)(2,1)S(1)}, bf16[64,3072]{1,0:T(8,128)(2,1)S(1)}, u32[]{:S(2)}, u32[]{:S(2)}) collective-permute-start(bf16[64,3072]{1,0:T(8,128)(2,1)S(1)} %pad_maximum_fusion.1), channel_id=1, source_target_pairs={{0,2},{1,3},{2,0},{3,1},{4,6},{5,7},{6,4},{7,5},{8,10},{9,11},{10,... | collective-permute-start | bytes 1179656 | tf_op jit(solution)/shard_map/ppermute | solution.py:14
  107.0 36.0 %collective-permute-start.35 = (bf16[256,3072]{1,0:T(8,128)(2,1)S(1)}, bf16[256,3072]{1,0:T(8,128)(2,1)S(1)}, u32[]{:S(2)}, u32[]{:S(2)}) collective-permute-start(bf16[256,3072]{1,0:T(8,128)(2,1)S(1)} %convolution_convert_fusion.2), channel_id=1, source_target_pairs={{0,1},{1,0},{2,3},{3,2},{4,5},{5,4},{6,7},{7,6},{8,9},{9,8},{10,11... | collective-permute-start | bytes 4718600 | tf_op jit(solution)/shard_map/ppermute | solution.py:14
  107.9 21.7 %collective-permute-start.8 = (bf16[32,3072]{1,0:T(8,128)(2,1)S(1)}, bf16[32,3072]{1,0:T(8,128)(2,1)S(1)}, u32[]{:S(2)}, u32[]{:S(2)}) collective-permute-start(bf16[32,3072]{1,0:T(8,128)(2,1)S(1)} %fusion.16), channel_id=1, source_target_pairs={{0,2},{1,3},{2,0},{3,1},{4,6},{5,7},{6,4},{7,5},{8,10},{9,11},{10,... | collective-permute-start | bytes 589832 | tf_op jit(solution)/shard_map/ppermute | solution.py:14
  112.1 13.3 %collective-permute-start.16 = (bf16[32,3072]{1,0:T(8,128)(2,1)S(1)}, bf16[32,3072]{1,0:T(8,128)(2,1)S(1)}, u32[]{:S(2)}, u32[]{:S(2)}) collective-permute-start(bf16[32,3072]{1,0:T(8,128)(2,1)S(1)} %fusion.13), channel_id=1, source_target_pairs={{0,2},{1,3},{2,0},{3,1},{4,6},{5,7},{6,4},{7,5},{8,10},{9,11},{10,... | collective-permute-start | bytes 589832 | tf_op jit(solution)/shard_map/ppermute | solution.py:14
  114.7 14.8 %collective-permute-start.24 = (bf16[32,3072]{1,0:T(8,128)(2,1)S(1)}, bf16[32,3072]{1,0:T(8,128)(2,1)S(1)}, u32[]{:S(2)}, u32[]{:S(2)}) collective-permute-start(bf16[32,3072]{1,0:T(8,128)(2,1)S(1)} %fusion.11), channel_id=1, source_target_pairs={{0,4},{1,5},{2,6},{3,7},{4,0},{5,1},{6,2},{7,3},{8,12},{9,13},{10,... | collective-permute-start | bytes 589832 | tf_op jit(solution)/shard_map/ppermute | solution.py:14
  121.2 5.7 %collective-permute-start.32 = (bf16[32,3072]{1,0:T(8,128)(2,1)S(1)}, bf16[32,3072]{1,0:T(8,128)(2,1)S(1)}, u32[]{:S(2)}, u32[]{:S(2)}) collective-permute-start(bf16[32,3072]{1,0:T(8,128)(2,1)S(1)} %fusion.8), channel_id=1, source_target_pairs={{0,4},{1,5},{2,6},{3,7},{4,0},{5,1},{6,2},{7,3},{8,12},{9,13},{10,... | collective-permute-start | bytes 589832 | tf_op jit(solution)/shard_map/ppermute | solution.py:14
  125.5 6.6 %collective-permute-start.18 = (bf16[16,3072]{1,0:T(8,128)(2,1)S(1)}, bf16[16,3072]{1,0:T(8,128)(2,1)S(1)}, u32[]{:S(2)}, u32[]{:S(2)}) collective-permute-start(bf16[16,3072]{1,0:T(8,128)(2,1)S(1)} %get-tuple-element.52), channel_id=1, source_target_pairs={{0,24},{1,25},{2,26},{3,27},{4,28},{5,29},{6,30},{7,31},{8,16},{9,... | collective-permute-start | bytes 294920 | tf_op jit(solution)/shard_map/ppermute | solution.py:14
  127.1 6.6 %collective-permute-start.34 = (bf16[16,3072]{1,0:T(8,128)(2,1)S(1)}, bf16[16,3072]{1,0:T(8,128)(2,1)S(1)}, u32[]{:S(2)}, u32[]{:S(2)}) collective-permute-start(bf16[16,3072]{1,0:T(8,128)(2,1)S(1)} %get-tuple-element.50), channel_id=1, source_target_pairs={{0,24},{1,25},{2,26},{3,27},{4,28},{5,29},{6,30},{7,31},{8,16},{9,... | collective-permute-start | bytes 294920 | tf_op jit(solution)/shard_map/ppermute | solution.py:14
  129.6 6.2 %collective-permute-start.33 = (bf16[16,3072]{1,0:T(8,128)(2,1)S(1)}, bf16[16,3072]{1,0:T(8,128)(2,1)S(1)}, u32[]{:S(2)}, u32[]{:S(2)}) collective-permute-start(bf16[16,3072]{1,0:T(8,128)(2,1)S(1)} %get-tuple-element.49), channel_id=1, source_target_pairs={{0,16},{1,17},{2,18},{3,19},{4,20},{5,21},{6,22},{7,23},{8,24},{9,... | collective-permute-start | bytes 294920 | tf_op jit(solution)/shard_map/ppermute | solution.py:14
  129.7 6.6 %collective-permute-start.25 = (bf16[16,3072]{1,0:T(8,128)(2,1)S(1)}, bf16[16,3072]{1,0:T(8,128)(2,1)S(1)}, u32[]{:S(2)}, u32[]{:S(2)}) collective-permute-start(bf16[16,3072]{1,0:T(8,128)(2,1)S(1)} %slice.214), channel_id=1, source_target_pairs={{0,8},{1,9},{2,10},{3,11},{4,12},{5,13},{6,14},{7,15},{8,0},{9,1},... | collective-permute-start | bytes 294920 | tf_op jit(solution)/shard_map/ppermute | solution.py:14
  132.1 12.7 %collective-permute-start.36 = (bf16[256,3072]{1,0:T(8,128)(2,1)S(1)}, bf16[256,3072]{1,0:T(8,128)(2,1)S(1)}, u32[]{:S(2)}, u32[]{:S(2)}) collective-permute-start(bf16[256,3072]{1,0:T(8,128)(2,1)S(1)} %convolution_convert_fusion.1), channel_id=1, source_target_pairs={{0,1},{1,0},{2,3},{3,2},{4,5},{5,4},{6,7},{7,6},{8,9},{9,8},{10,11... | collective-permute-start | bytes 4718600 | tf_op jit(solution)/shard_map/ppermute | solution.py:14
  133.6 13.0 %collective-permute-start.37 = (bf16[256,3072]{1,0:T(8,128)(2,1)S(1)}, bf16[256,3072]{1,0:T(8,128)(2,1)S(1)}, u32[]{:S(2)}, u32[]{:S(2)}) collective-permute-start(bf16[256,3072]{1,0:T(8,128)(2,1)S(1)} %convolution_convert_fusion), channel_id=1, source_target_pairs={{0,1},{1,0},{2,3},{3,2},{4,5},{5,4},{6,7},{7,6},{8,9},{9,8},{10,11... | collective-permute-start | bytes 4718600 | tf_op jit(solution)/shard_map/ppermute | solution.py:14
  135.7 6.4 %collective-permute-start.17 = (bf16[16,3072]{1,0:T(8,128)(2,1)S(1)}, bf16[16,3072]{1,0:T(8,128)(2,1)S(1)}, u32[]{:S(2)}, u32[]{:S(2)}) collective-permute-start(bf16[16,3072]{1,0:T(8,128)(2,1)S(1)} %get-tuple-element.51), channel_id=1, source_target_pairs={{0,16},{1,17},{2,18},{3,19},{4,20},{5,21},{6,22},{7,23},{8,24},{9,... | collective-permute-start | bytes 294920 | tf_op jit(solution)/shard_map/ppermute | solution.py:14
  136.2 6.1 %collective-permute-start.9 = (bf16[16,3072]{1,0:T(8,128)(2,1)S(1)}, bf16[16,3072]{1,0:T(8,128)(2,1)S(1)}, u32[]{:S(2)}, u32[]{:S(2)}) collective-permute-start(bf16[16,3072]{1,0:T(8,128)(2,1)S(1)} %slice.215), channel_id=1, source_target_pairs={{0,8},{1,9},{2,10},{3,11},{4,12},{5,13},{6,14},{7,15},{8,0},{9,1},... | collective-permute-start | bytes 294920 | tf_op jit(solution)/shard_map/ppermute | solution.py:14

commit v2 on v1

v2 whole, which is shorter than its diff:
```python
import functools
import math

import jax
import jax.numpy as jnp
from jax import lax
from jax.experimental import pallas as pl
from jax.experimental.pallas import tpu as pltpu
from jax.sharding import PartitionSpec as P

CORE, LINK_X, LINK_Y, LINK_Z = 0, 1, 2, 3
ROW_BITS = 4
PANEL = 512
TURN = pltpu.VMEM((8, 128), jnp.float32)
VMEM = pl.BlockSpec(memory_space=pltpu.VMEM)
HBM = pl.BlockSpec(memory_space=pltpu.HBM)
SMEM = pl.BlockSpec(memory_space=pltpu.SMEM)


def swapped(block, mask):
    count = lax.axis_size("dp")
    return lax.ppermute(block, "dp", [(low, low ^ mask) for low in range(count)])


def row_product(left, right):
    return lax.dot_general(
        left, right, (((1,), (1,)), ((), ())), preferred_element_type=jnp.float32
    )


def col_product(left, right):
    return lax.dot_general(
        left, right, (((0,), (0,)), ((), ())), preferred_element_type=jnp.float32
    )


def product(left, right):
    return jnp.dot(left, right, preferred_element_type=jnp.float32)


def half(value):
    return value.astype(jnp.bfloat16)


def shape(dims, dtype=jnp.bfloat16):
    return jax.ShapeDtypeStruct(dims, dtype)


def held(dims, dtype=jnp.bfloat16):
    return pltpu.VMEM(dims, dtype)


def fetched(*values):
    return [pltpu.with_memory_space_constraint(value, pltpu.VMEM) for value in values]


def in_hbm(value):
    return pltpu.with_memory_space_constraint(value, pltpu.HBM)


def limit(mib):
    return pltpu.CompilerParams(vmem_limit_bytes=mib << 20)


def cost(flops, moved):
    return pl.CostEstimate(flops=flops, bytes_accessed=moved, transcendentals=0)


def pick_kernel(
    place, token, count, gate, tokens, grad, w_gate, w_up, w_down, rows, weight, panels, turn,
    token_here, count_here, gate_here, tokens_here, grad_here, arrived,
):
    pairs = (
        (token, token_here),
        (count, count_here),
        (gate, gate_here),
        (tokens, tokens_here),
        (grad, grad_here),
    )
    copies = [pltpu.make_async_copy(*pair, arrived.at[i]) for i, pair in enumerate(pairs)]
    loads = [
        pltpu.make_async_copy(w, panels.at[i], arrived.at[len(pairs) + i])
        for i, w in enumerate((w_gate, w_up, w_down))
    ]
    for copy in copies + loads:
        copy.start()
    turn[...] = jnp.zeros_like(turn)
    for copy in copies:
        copy.wait()
    capacity, lanes = weight.shape
    row = lax.broadcasted_iota(jnp.int32, (capacity, lanes), 0)
    live = count_here[place[0]]
    index = jnp.zeros((capacity, lanes), jnp.int32)
    scale = jnp.zeros((capacity, lanes), jnp.float32)
    for slot in range(capacity):
        index = jnp.where(row == slot, token_here[slot], index)
        scale = jnp.where(row == slot, jnp.where(slot < live, gate_here[slot], 0.0), scale)
    weight[...] = scale
    lane = lax.broadcasted_iota(jnp.int32, (capacity, tokens.shape[0]), 1)
    chosen = jnp.where(lane == index[:, :1], 1.0, 0.0).astype(jnp.bfloat16)
    rows[0] = half(product(chosen, tokens_here[...]))
    rows[1] = half(scale[:, :1] * grad_here[...].astype(jnp.float32))
    for copy in loads:
        copy.wait()


def pick(tokens, slot_token, slot_count, slot_gate, grad_out, weights):
    capacity, width = grad_out.shape
    inputs = (slot_token, slot_count, slot_gate, tokens, grad_out)
    return pl.pallas_call(
        pick_kernel,
        out_shape=(
            held((2, capacity, width)),
            held((capacity, 128), jnp.float32),
            held((3, *weights[0].shape)),
            TURN,
        ),
        in_specs=[SMEM] + [HBM] * 8,
        out_specs=(VMEM,) * 4,
        scratch_shapes=[pltpu.SMEM(v.shape, v.dtype) for v in inputs[:3]]
        + [pltpu.VMEM(v.shape, v.dtype) for v in inputs[3:]]
        + [pltpu.SemaphoreType.DMA((8,))],
        compiler_params=limit(4),
        cost_estimate=cost(0, 0),
        name="pick",
    )(lax.axis_index("dp")[None], *(in_hbm(v) for v in (*inputs, *weights)))


def expert_kernel(
    x_pair, x_far, e_pair, e_far, near, other, _,
    x, e, hidden, gate_grad, up_grad, out_keep, out_send, row_keep, row_send, turn,
):
    turn[...] = jnp.zeros_like(turn)
    units = near.shape[1]
    rows = x.shape[0] // 4
    x[: 2 * rows] = x_pair[...]
    x[2 * rows :] = x_far[...]
    e[:rows] = e_pair[:rows]
    e[rows : 2 * rows] = e_far[:rows]
    e[2 * rows : 3 * rows] = e_pair[rows:]
    e[3 * rows :] = e_far[rows:]
    for i, panels in enumerate((near, other)):
        mine = slice(i * units, (i + 1) * units)
        gate_pre = row_product(x[...], panels[0])
        up_pre = row_product(x[...], panels[1])
        hidden_grad = row_product(e[...], panels[2])
        gate_sig = jax.nn.sigmoid(gate_pre)
        activated = gate_pre * gate_sig
        hidden[:, mine] = half(activated * up_pre)
        gate_grad[:, mine] = half(
            hidden_grad * up_pre * (gate_sig * (1.0 + gate_pre * (1.0 - gate_sig)))
        )
        up_grad[:, mine] = half(hidden_grad * activated)
    for at in range(0, x.shape[1], PANEL):
        part = slice(at, at + PANEL)
        out = product(hidden[:, :units], near[2, :, part]) + product(
            hidden[:, units:], other[2, :, part]
        )
        out_keep[:, part] = out[: 2 * rows]
        out_send[:, part] = half(out[2 * rows :])
        row = (
            product(gate_grad[:, :units], near[0, :, part])
            + product(gate_grad[:, units:], other[0, :, part])
            + product(up_grad[:, :units], near[1, :, part])
            + product(up_grad[:, units:], other[1, :, part])
        )
        row_keep[:rows, part] = row[:rows]
        row_keep[rows:, part] = row[2 * rows : 3 * rows]
        row_send[:rows, part] = half(row[rows : 2 * rows])
        row_send[rows:, part] = half(row[3 * rows :])


def expert(x_pair, x_far, e_pair, e_far, near, other, turn):
    rows, width = 2 * x_pair.shape[0], x_pair.shape[1]
    units = 2 * near.shape[1]
    saved, kept, sent = (
        held((rows, units)),
        held((rows // 2, width), jnp.float32),
        held((rows // 2, width)),
    )
    return pl.pallas_call(
        expert_kernel,
        out_shape=(held((rows, width)),) * 2 + (saved,) * 3 + (kept, sent, kept, sent, TURN),
        in_specs=[VMEM] * 7,
        out_specs=(VMEM,) * 10,
        compiler_params=limit(12),
        cost_estimate=cost(12 * rows * units * width, 6 * units * width),
        name="expert",
    )(*fetched(x_pair, x_far, e_pair, e_far, near, other, turn))


def other_kernel(x, e, hidden, gate_grad, up_grad, _, grads, turn):
    turn[...] = jnp.zeros_like(turn)
    units = hidden.shape[1] // 2
    grads[0] = half(col_product(gate_grad[:, units:], x[...]))
    grads[1] = half(col_product(up_grad[:, units:], x[...]))
    grads[2] = half(col_product(hidden[:, units:], e[...]))


def other_grads(x, e, hidden, gate_grad, up_grad, turn):
    rows, width = x.shape
    units = hidden.shape[1] // 2
    wide = pl.BlockSpec((rows, PANEL), lambda i: (0, i))
    return pl.pallas_call(
        other_kernel,
        grid=(width // PANEL,),
        out_shape=(held((3, units, width)), TURN),
        in_specs=[wide, wide, VMEM, VMEM, VMEM, VMEM],
        out_specs=(pl.BlockSpec((3, units, PANEL), lambda i: (0, 0, i)), VMEM),
        compiler_params=limit(16),
        cost_estimate=cost(6 * rows * units * width, 6 * units * width),
        name="other_grads",
    )(*fetched(x, e, hidden, gate_grad, up_grad, turn))


def own_kernel(factor, x, e, hidden, gate_grad, up_grad, received, _, *grads):
    grads, turn = grads[:3], grads[3]
    turn[...] = jnp.zeros_like(turn)
    units = hidden.shape[1] // 2
    for i, (left, right) in enumerate(((gate_grad, x), (up_grad, x), (hidden, e))):
        total = col_product(left[:, :units], right[...]) + received[i].astype(jnp.float32)
        grads[i][...] = (total * factor).astype(grads[i].dtype)


def own_grads(x, e, hidden, gate_grad, up_grad, received, turn, factor, dtype):
    rows, width = x.shape
    units = hidden.shape[1] // 2
    wide = pl.BlockSpec((rows, PANEL), lambda i: (0, i))
    block = pl.BlockSpec((units, PANEL), lambda i: (0, i))
    return pl.pallas_call(
        functools.partial(own_kernel, factor),
        grid=(width // PANEL,),
        out_shape=(shape((units, width), dtype),) * 3 + (TURN,),
        in_specs=[wide, wide, VMEM, VMEM, VMEM]
        + [pl.BlockSpec((3, units, PANEL), lambda i: (0, 0, i)), VMEM],
        out_specs=(block,) * 3 + (VMEM,),
        compiler_params=limit(16),
        cost_estimate=cost(6 * rows * units * width, 6 * units * width),
        name="own_grads",
    )(*fetched(x, e, hidden, gate_grad, up_grad, received, turn))


def staged(body, name, outs, *values):
    def kernel(*refs):
        refs[-1][...] = jnp.zeros(TURN.shape, TURN.dtype)
        body(*refs[: len(values) - 1], *refs[len(values) : -1])

    return pl.pallas_call(
        kernel,
        out_shape=(*outs, TURN),
        in_specs=[VMEM] * len(values),
        out_specs=(VMEM,) * (len(outs) + 1),
        compiler_params=limit(4),
        cost_estimate=cost(0, 0),
        name=name,
    )(*fetched(*values))


def split_body(first, second, x, e):
    rows = first.shape[1]
    for out, i in ((x, 0), (e, 1)):
        out[:rows] = first[i]
        out[rows:] = second[i]


def pair_body(x, x_side, e, e_side, x_pair, e_pair):
    rows = x.shape[0]
    for out, near, side in ((x_pair, x, x_side), (e_pair, e, e_side)):
        out[:rows] = near[...]
        out[rows:] = side[...]


def plane_body(out_keep, out_far, row_keep, row_far, out_mid, out_side, row_mid, row_side):
    rows = out_mid.shape[0]
    for keep, far, mid, side in (
        (out_keep, out_far, out_mid, out_side),
        (row_keep, row_far, row_mid, row_side),
    ):
        mid[...] = keep[:rows] + far[:rows].astype(jnp.float32)
        side[...] = half(keep[rows:] + far[rows:].astype(jnp.float32))


def line_body(out_mid, out_side, row_mid, row_side, first, second):
    rows = first.shape[1]
    for i, (mid, side) in enumerate(((out_mid, out_side), (row_mid, row_side))):
        total = mid[...] + side[...].astype(jnp.float32)
        first[i] = total[:rows].astype(first.dtype)
        second[i] = total[rows:].astype(second.dtype)


def final_body(own, one, two, three, weight, expert_out, grad_rows):
    out, row = (
        own[i] + one[i].astype(jnp.float32) + two[i].astype(jnp.float32) + three[i].astype(jnp.float32)
        for i in (0, 1)
    )
    expert_out[...] = half(weight[:, :1] * out)
    grad_rows[...] = half(row)


def shards(tokens, slot_token, slot_count, slot_gate, grad_out, w_gate, w_up, w_down):
    capacity = slot_gate.shape[0]
    devices = lax.axis_size("dp")
    all_bits = devices.bit_length() - 1
    core, along_x, along_y = 1 << CORE, 1 << LINK_X, 1 << LINK_Y
    levels = range(1 << (ROW_BITS + 1 - LINK_Z))
    far_bits = range(ROW_BITS + 1, all_bits)

    weights = [w_gate, w_up, w_down]
    for bit in far_bits:
        weights = [jnp.concatenate([w, swapped(w, 1 << bit)], 0) for w in weights]
    own, weight, near, turn = pick(tokens, slot_token, slot_count, slot_gate, grad_out, weights)
    other = swapped(near, core)

    level = [own] + [None] * (len(levels) - 1)
    groups = [(1, 3), (0, 2)]
    for k in (1, 3, 2):
        level[k] = swapped(own, k << LINK_Z)

    width = own.shape[2]
    rows = 2 * capacity
    near_rows, pairs, works, sides = [], [], [], []
    for first, second in groups:
        x, e, turn = staged(
            split_body, "split", [held((rows, width))] * 2, level[first], level[second], turn
        )
        near_rows.append((x, swapped(x, along_x), e, swapped(e, along_y)))
    for group in near_rows:
        x, e, turn = staged(pair_body, "pair", [held((2 * rows, width))] * 2, *group, turn)
        pairs.append((x, swapped(x, along_y), e, swapped(e, along_x)))
    for group in pairs:
        *work, out_keep, out_send, row_keep, row_send, _ = expert(*group, near, other, turn)
        works.append(work)
        sides.append((out_keep, swapped(out_send, along_y), row_keep, swapped(row_send, along_x)))
    kept = [jnp.concatenate(pieces, 0) for pieces in zip(*works)]
    sent, turn = other_grads(*kept, turn)
    received = swapped(sent, core)

    whole, piece = held((rows, width), jnp.float32), held((rows, width))

    def plane_sum(side, turn):
        out_mid, out_side, row_mid, row_side, turn = staged(
            plane_body, "plane_sum", [whole, piece, whole, piece], *side, turn
        )
        return (out_mid, swapped(out_side, along_x), row_mid, swapped(row_side, along_y)), turn

    def line_sum(middle, turn, first):
        level_dims = (2, capacity, width)
        return staged(
            line_body, "line_sum", [held(level_dims, first), held(level_dims)], *middle, turn
        )

    middles = []
    for side in sides:
        middle, turn = plane_sum(side, turn)
        middles.append(middle)
    sum_1, sum_3, turn = line_sum(middles[0], turn, jnp.bfloat16)
    one, three = swapped(sum_1, 1 << LINK_Z), swapped(sum_3, 3 << LINK_Z)
    factor = 1.0 / math.sqrt(devices * capacity)
    if far_bits:
        *owned, turn = own_grads(*kept, received, turn, 1.0, jnp.float32)
        for bit in reversed(far_bits):
            cut = owned[0].shape[0] // 2
            owned = [t[:cut] + swapped(half(t[cut:]), 1 << bit) for t in owned]
        owned = [half(total * factor) for total in owned]
    else:
        *owned, turn = own_grads(*kept, received, turn, factor, jnp.bfloat16)
    sum_0, sum_2, turn = line_sum(middles[1], turn, jnp.float32)
    two = swapped(sum_2, 2 << LINK_Z)
    expert_out, grad_rows, turn = staged(
        final_body, "final", [shape((capacity, width))] * 2, sum_0, one, two, three, weight, turn
    )
    return (expert_out, grad_rows, *owned)


def solution(mesh):
    return jax.shard_map(
        shards,
        mesh=mesh,
        in_specs=(
            P("dp", None),
            P("dp"),
            P(),
            P("dp"),
            P("dp", None),
            P("dp", None),
            P("dp", None),
            P("dp", None),
        ),
        out_specs=(P("dp", None), P("dp", None), P("dp", None), P("dp", None), P("dp", None)),
        check_vma=False,
    )
```

time: 149 us -> 107 us (0.72)
  Pallas kernels: 0 us -> 21.8 us
  matrix products: 19.9 us -> 0 us
  starting transfers between devices: 42.9 us -> 25 us
  waiting for transfers between devices: 76.3 us -> 58.8 us
  other arithmetic: 5.63 us -> 0 us
  local copies, waits for them, and re-layouts: 2.52 us -> 0.27 us
    pallas_call x0 -> x14, Pallas kernels: none -> 21.8 us  [the longest x2 10.2 us: expert(): pl.pallas_call(expert_kernel, out_shape=(held((rows, width)),) * 2 + (sav...]
    dot_general x30 -> x0, matrix products: 19.9 us -> none  [the longest x12 7.87 us: row_product(): lax.dot_general(left, right, (((1,), (1,)), ((), ())), preferred_element_...]
    ppermute x38 -> x24, starting transfers between devices: 42.9 us -> 25 us  [swapped(): lax.ppermute(block, 'dp', [(low, low ^ mask) for low in range(count)])]
    ppermute x38 -> x24, waiting for transfers between devices: 76.3 us -> 58.8 us  [swapped(): lax.ppermute(block, 'dp', [(low, low ^ mask) for low in range(count)])]
    select_n x2 -> x0, other arithmetic: 2.04 us -> none  [the longest x1 1.3 us: shards(): weight = jnp.where(live_mask, slot_gate, 0.0)]
    convert_element_type x6 -> x0, other arithmetic: 1.55 us -> none  [half(): return value.astype(jnp.bfloat16)]
  transfers between devices with their start and end apart: 38 -> 24, of which waited for: 24 -> 15; matrix products, arithmetic and copies ran while one was open for 16% -> 0% of each run, Pallas kernels for 0% -> 10%
where the time goes in v2:
time: 107 us
  waiting for transfers between devices  58.8 us (55%)
  starting transfers between devices  25 us (23%)
  Pallas kernels  21.8 us (20%)
    ppermute x24, waiting for transfers between devices, swapped(): lax.ppermute(block, 'dp', [(low, low ^ mask) for low in range(count)])  58.8 us
    ppermute x24, starting transfers between devices, swapped(): lax.ppermute(block, 'dp', [(low, low ^ mask) for low in range(count)])  25 us
    pallas_call x2, Pallas kernels, expert(): pl.pallas_call(expert_kernel, out_shape=(held((rows, width)),) * 2 + (sav...  10.2 us
    pallas_call x1, Pallas kernels, own_grads(): pl.pallas_call(functools.partial(own_kernel, factor), grid=(width // PANE...  4.44 us
    pallas_call x1, Pallas kernels, other_grads(): pl.pallas_call(other_kernel, grid=(width // PANEL,), out_shape=(held((3,...  2.99 us
    pallas_call x1, Pallas kernels, pick(): pl.pallas_call(pick_kernel, out_shape=(held((2, capacity, width)), held((...  2.71 us
  transfers between devices with their start and end apart: 24, of which 15 were waited for; matrix products, arithmetic and copies ran while one was open for 0% of the time, Pallas kernels for 10%

profile of v2, /device:TPU:0, one launch (start us, length us, event | category | flops | bytes accessed | tf_op | source)
XLA Modules:
  0.0 106.7 jit_solution(3838275865783553018)
XLA Ops:
  0.6 2.7 %pick.1 = (bf16[2,16,3072]{2,1,0:T(8,128)(2,1)S(1)}, f32[16,128]{1,0:T(8,128)S(1)}, bf16[3,256,3072]{2,1,0:T(8,128)(2,1)S(1)}, f32[8,128]{1,0:T(8,128)S(1)}) custom-call(s32[1]{0:T(128)} %bitcast.place, s32[16]{0:T(128)} %token_.1, s32[32]{0:T(128)} %count.1, f32[16]{0:T(128)} %gate.1, bf16[128,3072]{1,0:T(8,128)(2,1)} %tokens.1, bf16[16,3072]{1,0:T(8,128)(2,1)} %grad.1, ...), custom_call_target="tpu_custom_call" | custom-call | tf_op jit(solution)/shard_map/pick/pallas_call | solution.py:110
  3.4 0.5 collective-permute-start.9
  3.9 4.7 %collective-permute-start.2 = (bf16[2,16,3072]{2,1,0:T(8,128)(2,1)S(1)}, bf16[2,16,3072]{2,1,0:T(8,128)(2,1)S(1)}, u32[]{:S(2)}, u32[]{:S(2)}) collective-permute-start(bf16[2,16,3072]{2,1,0:T(8,128)(2,1)S(1)} %get-tuple-element.63.refs_0_), channel_id=1, source_target_pairs={{0,24},{1,25},{2,26},{3,27},{4,28},{5,29},{6,30},{7,31},{8,16},{9,... | collective-permute-start | bytes 589832 | tf_op jit(solution)/shard_map/ppermute | solution.py:22
  8.5 0.6 collective-permute-start
  9.2 5.2 %collective-permute-done.2.refs_1_ = bf16[2,16,3072]{2,1,0:T(8,128)(2,1)S(1)} collective-permute-done((bf16[2,16,3072]{2,1,0:T(8,128)(2,1)S(1)}, bf16[2,16,3072]{2,1,0:T(8,128)(2,1)S(1)}, u32[]{:S(2)}, u32[]{:S(2)}) %collective-permute-start.2) | collective-permute-done | bytes 196640 | tf_op jit(solution)/shard_map/ppermute | solution.py:22
  14.4 5.0 %collective-permute-done.1.refs_0_ = bf16[2,16,3072]{2,1,0:T(8,128)(2,1)S(1)} collective-permute-done((bf16[2,16,3072]{2,1,0:T(8,128)(2,1)S(1)}, bf16[2,16,3072]{2,1,0:T(8,128)(2,1)S(1)}, u32[]{:S(2)}, u32[]{:S(2)}) %collective-permute-start.1) | collective-permute-done | bytes 196640 | tf_op jit(solution)/shard_map/ppermute | solution.py:22
  19.4 1.5 %collective-permute-start.5 = (bf16[32,3072]{1,0:T(8,128)(2,1)S(1)}, bf16[32,3072]{1,0:T(8,128)(2,1)S(1)}, u32[]{:S(2)}, u32[]{:S(2)}) collective-permute-start(bf16[32,3072]{1,0:T(8,128)(2,1)S(1)} %get-tuple-element.68.refs_0_), channel_id=1, source_target_pairs={{0,2},{1,3},{2,0},{3,1},{4,6},{5,7},{6,4},{7,5},{8,10},{9,11},{10,... | collective-permute-start | bytes 589832 | tf_op jit(solution)/shard_map/ppermute | solution.py:22
  20.9 1.5 %collective-permute-start.6 = (bf16[32,3072]{1,0:T(8,128)(2,1)S(1)}, bf16[32,3072]{1,0:T(8,128)(2,1)S(1)}, u32[]{:S(2)}, u32[]{:S(2)}) collective-permute-start(bf16[32,3072]{1,0:T(8,128)(2,1)S(1)} %get-tuple-element.69.refs_2_), channel_id=1, source_target_pairs={{0,4},{1,5},{2,6},{3,7},{4,0},{5,1},{6,2},{7,3},{8,12},{9,13},{10,... | collective-permute-start | bytes 589832 | tf_op jit(solution)/shard_map/ppermute | solution.py:22
  22.4 3.4 %collective-permute-done.refs_1_ = bf16[2,16,3072]{2,1,0:T(8,128)(2,1)S(1)} collective-permute-done((bf16[2,16,3072]{2,1,0:T(8,128)(2,1)S(1)}, bf16[2,16,3072]{2,1,0:T(8,128)(2,1)S(1)}, u32[]{:S(2)}, u32[]{:S(2)}) %collective-permute-start) | collective-permute-done | bytes 196640 | tf_op jit(solution)/shard_map/ppermute | solution.py:22
  25.9 0.4 collective-permute-done.5.refs_1_
  26.3 1.2 %collective-permute-done.6.refs_3_ = bf16[32,3072]{1,0:T(8,128)(2,1)S(1)} collective-permute-done((bf16[32,3072]{1,0:T(8,128)(2,1)S(1)}, bf16[32,3072]{1,0:T(8,128)(2,1)S(1)}, u32[]{:S(2)}, u32[]{:S(2)}) %collective-permute-start.6) | collective-permute-done | bytes 196640 | tf_op jit(solution)/shard_map/ppermute | solution.py:22
  27.5 1.6 %collective-permute-start.12 = (bf16[64,3072]{1,0:T(8,128)(2,1)S(1)}, bf16[64,3072]{1,0:T(8,128)(2,1)S(1)}, u32[]{:S(2)}, u32[]{:S(2)}) collective-permute-start(bf16[64,3072]{1,0:T(8,128)(2,1)S(1)} %get-tuple-element.80.x_pair), channel_id=1, source_target_pairs={{0,4},{1,5},{2,6},{3,7},{4,0},{5,1},{6,2},{7,3},{8,12},{9,13},{10,... | collective-permute-start | bytes 1179656 | tf_op jit(solution)/shard_map/ppermute | solution.py:22
  29.1 0.5 collective-permute-start.13
  29.7 1.5 %collective-permute-start.3 = (bf16[32,3072]{1,0:T(8,128)(2,1)S(1)}, bf16[32,3072]{1,0:T(8,128)(2,1)S(1)}, u32[]{:S(2)}, u32[]{:S(2)}) collective-permute-start(bf16[32,3072]{1,0:T(8,128)(2,1)S(1)} %get-tuple-element.66.refs_0_), channel_id=1, source_target_pairs={{0,2},{1,3},{2,0},{3,1},{4,6},{5,7},{6,4},{7,5},{8,10},{9,11},{10,... | collective-permute-start | bytes 589832 | tf_op jit(solution)/shard_map/ppermute | solution.py:22
  31.2 0.5 collective-permute-start.4
  31.7 11.3 %collective-permute-done.3.refs_1_ = bf16[32,3072]{1,0:T(8,128)(2,1)S(1)} collective-permute-done((bf16[32,3072]{1,0:T(8,128)(2,1)S(1)}, bf16[32,3072]{1,0:T(8,128)(2,1)S(1)}, u32[]{:S(2)}, u32[]{:S(2)}) %collective-permute-start.3) | collective-permute-done | bytes 196640 | tf_op jit(solution)/shard_map/ppermute | solution.py:22
  43.0 0.6 collective-permute-start.7
  43.6 0.7 collective-permute-start.8
  44.3 5.1 %expert.3 = (bf16[128,3072]{1,0:T(8,128)(2,1)S(1)}, bf16[128,3072]{1,0:T(8,128)(2,1)S(1)}, bf16[128,512]{1,0:T(8,128)(2,1)S(1)}, bf16[128,512]{1,0:T(8,128)(2,1)...) custom-call(bf16[64,3072]{1,0:T(8,128)(2,1)S(1)} %get-tuple-element., ...), custom_call_target="tpu_custom_call" | custom-call | flops 2415919104 | bytes 9437184 | tf_op jit(solution)/shard_map/expert/pallas_call | solution.py:181
  49.6 2.2 %collective-permute-done.7.x_far = bf16[64,3072]{1,0:T(8,128)(2,1)S(1)} collective-permute-done((bf16[64,3072]{1,0:T(8,128)(2,1)S(1)}, bf16[64,3072]{1,0:T(8,128)(2,1)S(1)}, u32[]{:S(2)}, u32[]{:S(2)}) %collective-permute-start.7) | collective-permute-done | bytes 393248 | tf_op jit(solution)/shard_map/ppermute | solution.py:22
  51.8 0.3 collective-permute-done.8.e_far
  52.1 5.1 %expert.2 = (bf16[128,3072]{1,0:T(8,128)(2,1)S(1)}, bf16[128,3072]{1,0:T(8,128)(2,1)S(1)}, bf16[128,512]{1,0:T(8,128)(2,1)S(1)}, bf16[128,512]{1,0:T(8,128)(2,1)...) custom-call(bf16[64,3072]{1,0:T(8,128)(2,1)S(1)} %get-tuple-element., ...), custom_call_target="tpu_custom_call" | custom-call | flops 2415919104 | bytes 9437184 | tf_op jit(solution)/shard_map/expert/pallas_call | solution.py:181
  57.2 0.1 constant_dynamic-update-slice_fusion
  57.3 3.0 %other_grads.1 = (bf16[3,256,3072]{2,1,0:T(8,128)(2,1)S(1)}, f32[8,128]{1,0:T(8,128)S(1)}) custom-call(bf16[256,3072]{1,0:T(8,128)(2,1)S(1)} %get-tuple-element.121.x, bf16[256,3072]{1,0:T(8,128)(2,1)S(1)} %get-tuple-element.122.e, bf16[256,512]{1,0:T(8,128)(2,1)S(1)} %get-tuple-element.123.hidden, bf16[256,512]{1,0:T(8,128)(2,1)S(1)} %get-tuple-element.124.gate_grad, ...), custom_call_target="tpu_custom_call" | custom-call | flops 1207959552 | bytes 4718592 | tf_op jit(solution)/shard_map/other_grads/pallas_call | solution.py:204
  60.3 0.1 collective-permute-start.18
  60.4 1.5 %collective-permute-start.14 = (bf16[64,3072]{1,0:T(8,128)(2,1)S(1)}, bf16[64,3072]{1,0:T(8,128)(2,1)S(1)}, u32[]{:S(2)}, u32[]{:S(2)}) collective-permute-start(bf16[64,3072]{1,0:T(8,128)(2,1)S(1)} %get-tuple-element.83), channel_id=1, source_target_pairs={{0,4},{1,5},{2,6},{3,7},{4,0},{5,1},{6,2},{7,3},{8,12},{9,13},{10,... | collective-permute-start | bytes 1179656 | tf_op jit(solution)/shard_map/ppermute | solution.py:22
  61.9 0.9 collective-permute-start.15
  62.8 0.6 collective-permute-start.10
  63.4 1.2 %collective-permute-start.11 = (bf16[64,3072]{1,0:T(8,128)(2,1)S(1)}, bf16[64,3072]{1,0:T(8,128)(2,1)S(1)}, u32[]{:S(2)}, u32[]{:S(2)}) collective-permute-start(bf16[64,3072]{1,0:T(8,128)(2,1)S(1)} %get-tuple-element.79), channel_id=1, source_target_pairs={{0,2},{1,3},{2,0},{3,1},{4,6},{5,7},{6,4},{7,5},{8,10},{9,11},{10,... | collective-permute-start | bytes 1179656 | tf_op jit(solution)/shard_map/ppermute | solution.py:22
  64.5 7.9 %collective-permute-done.14.refs_1_ = bf16[64,3072]{1,0:T(8,128)(2,1)S(1)} collective-permute-done((bf16[64,3072]{1,0:T(8,128)(2,1)S(1)}, bf16[64,3072]{1,0:T(8,128)(2,1)S(1)}, u32[]{:S(2)}, u32[]{:S(2)}) %collective-permute-start.14) | collective-permute-done | bytes 393248 | tf_op jit(solution)/shard_map/ppermute | solution.py:22
  72.4 1.5 %collective-permute-done.15.refs_3_ = bf16[64,3072]{1,0:T(8,128)(2,1)S(1)} collective-permute-done((bf16[64,3072]{1,0:T(8,128)(2,1)S(1)}, bf16[64,3072]{1,0:T(8,128)(2,1)S(1)}, u32[]{:S(2)}, u32[]{:S(2)}) %collective-permute-start.15) | collective-permute-done | bytes 393248 | tf_op jit(solution)/shard_map/ppermute | solution.py:22
  73.9 0.2 plane_sum.2
  74.1 0.9 collective-permute-start.19
  75.0 0.6 collective-permute-start.20
  75.6 5.3 %collective-permute-done.10.refs_1_ = bf16[64,3072]{1,0:T(8,128)(2,1)S(1)} collective-permute-done((bf16[64,3072]{1,0:T(8,128)(2,1)S(1)}, bf16[64,3072]{1,0:T(8,128)(2,1)S(1)}, u32[]{:S(2)}, u32[]{:S(2)}) %collective-permute-start.10) | collective-permute-done | bytes 393248 | tf_op jit(solution)/shard_map/ppermute | solution.py:22
  80.8 1.5 %collective-permute-done.11.refs_3_ = bf16[64,3072]{1,0:T(8,128)(2,1)S(1)} collective-permute-done((bf16[64,3072]{1,0:T(8,128)(2,1)S(1)}, bf16[64,3072]{1,0:T(8,128)(2,1)S(1)}, u32[]{:S(2)}, u32[]{:S(2)}) %collective-permute-start.11) | collective-permute-done | bytes 393248 | tf_op jit(solution)/shard_map/ppermute | solution.py:22
  82.3 0.2 plane_sum.3
  82.5 0.9 collective-permute-start.16
  83.4 0.6 collective-permute-start.17
  84.0 2.5 %collective-permute-done.19.refs_1_ = bf16[32,3072]{1,0:T(8,128)(2,1)S(1)} collective-permute-done((bf16[32,3072]{1,0:T(8,128)(2,1)S(1)}, bf16[32,3072]{1,0:T(8,128)(2,1)S(1)}, u32[]{:S(2)}, u32[]{:S(2)}) %collective-permute-start.19) | collective-permute-done | bytes 196640 | tf_op jit(solution)/shard_map/ppermute | solution.py:22
  86.6 0.1 collective-permute-start.21
  86.7 2.6 %collective-permute-start.23 = (bf16[2,16,3072]{2,1,0:T(8,128)(2,1)S(1)}, bf16[2,16,3072]{2,1,0:T(8,128)(2,1)S(1)}, u32[]{:S(2)}, u32[]{:S(2)}) collective-permute-start(bf16[2,16,3072]{2,1,0:T(8,128)(2,1)S(1)} %get-tuple-element.113), channel_id=1, source_target_pairs={{0,24},{1,25},{2,26},{3,27},{4,28},{5,29},{6,30},{7,31},{8,16},{9,... | collective-permute-start | bytes 589832 | tf_op jit(solution)/shard_map/ppermute | solution.py:22
  89.3 4.4 %own_grads.1 = (bf16[256,3072]{1,0:T(8,128)(2,1)}, bf16[256,3072]{1,0:T(8,128)(2,1)}, bf16[256,3072]{1,0:T(8,128)(2,1)}, f32[8,128]{1,0:T(8,128)S(1)}) custom-call(bf16[256,3072]{1,0:T(8,128)(2,1)S(1)} %get-tuple-element.121.x, bf16[256,3072]{1,0:T(8,128)(2,1)S(1)} %get-tuple-element.122.e, bf16[256,512]{1,0:T(8,128)(2,1)S(1)} %get-tuple-element.123.hidden, ...), custom_call_target="tpu_custom_call" | custom-call | flops 1207959552 | bytes 4718592 | tf_op jit(solution)/shard_map/own_grads/pallas_call | solution.py:230
  93.7 0.1 line_sum.3
  93.8 0.9 collective-permute-start.22
  94.7 3.5 %collective-permute-done.23.refs_3_ = bf16[2,16,3072]{2,1,0:T(8,128)(2,1)S(1)} collective-permute-done((bf16[2,16,3072]{2,1,0:T(8,128)(2,1)S(1)}, bf16[2,16,3072]{2,1,0:T(8,128)(2,1)S(1)}, u32[]{:S(2)}, u32[]{:S(2)}) %collective-permute-start.23) | collective-permute-done | bytes 196640 | tf_op jit(solution)/shard_map/ppermute | solution.py:22
  98.2 7.7 %collective-permute-done.22.refs_2_ = bf16[2,16,3072]{2,1,0:T(8,128)(2,1)S(1)} collective-permute-done((bf16[2,16,3072]{2,1,0:T(8,128)(2,1)S(1)}, bf16[2,16,3072]{2,1,0:T(8,128)(2,1)S(1)}, u32[]{:S(2)}, u32[]{:S(2)}) %collective-permute-start.22) | collective-permute-done | bytes 196640 | tf_op jit(solution)/shard_map/ppermute | solution.py:22
  105.9 0.8 final.1
  (22 shorter events, 0.4 us)
Async XLA Ops:
  3.4 40.9 %collective-permute-start.9 = (bf16[3,256,3072]{2,1,0:T(8,128)(2,1)S(1)}, bf16[3,256,3072]{2,1,0:T(8,128)(2,1)S(1)}, u32[]{:S(2)}, u32[]{:S(2)}) collective-permute-start(bf16[3,256,3072]{2,1,0:T(8,128)(2,1)S(1)} %get-tuple-element.74.near), channel_id=1, source_target_pairs={{0,1},{1,0},{2,3},{3,2},{4,5},{5,4},{6,7},{7,6},{8,9},{9,8},{10,11... | collective-permute-start | bytes 14155784 | tf_op jit(solution)/shard_map/ppermute | solution.py:22
  3.9 10.5 %collective-permute-start.2 = (bf16[2,16,3072]{2,1,0:T(8,128)(2,1)S(1)}, bf16[2,16,3072]{2,1,0:T(8,128)(2,1)S(1)}, u32[]{:S(2)}, u32[]{:S(2)}) collective-permute-start(bf16[2,16,3072]{2,1,0:T(8,128)(2,1)S(1)} %get-tuple-element.63.refs_0_), channel_id=1, source_target_pairs={{0,24},{1,25},{2,26},{3,27},{4,28},{5,29},{6,30},{7,31},{8,16},{9,... | collective-permute-start | bytes 589832 | tf_op jit(solution)/shard_map/ppermute | solution.py:22
  8.5 10.8 %collective-permute-start.1 = (bf16[2,16,3072]{2,1,0:T(8,128)(2,1)S(1)}, bf16[2,16,3072]{2,1,0:T(8,128)(2,1)S(1)}, u32[]{:S(2)}, u32[]{:S(2)}) collective-permute-start(bf16[2,16,3072]{2,1,0:T(8,128)(2,1)S(1)} %get-tuple-element.63.refs_0_), channel_id=1, source_target_pairs={{0,8},{1,9},{2,10},{3,11},{4,12},{5,13},{6,14},{7,15},{8,0},{9,1},... | collective-permute-start | bytes 589832 | tf_op jit(solution)/shard_map/ppermute | solution.py:22
  8.5 17.3 %collective-permute-start = (bf16[2,16,3072]{2,1,0:T(8,128)(2,1)S(1)}, bf16[2,16,3072]{2,1,0:T(8,128)(2,1)S(1)}, u32[]{:S(2)}, u32[]{:S(2)}) collective-permute-start(bf16[2,16,3072]{2,1,0:T(8,128)(2,1)S(1)} %get-tuple-element.63.refs_0_), channel_id=1, source_target_pairs={{0,16},{1,17},{2,18},{3,19},{4,20},{5,21},{6,22},{7,23},{8,24},{9,... | collective-permute-start | bytes 589832 | tf_op jit(solution)/shard_map/ppermute | solution.py:22
  19.4 6.9 %collective-permute-start.5 = (bf16[32,3072]{1,0:T(8,128)(2,1)S(1)}, bf16[32,3072]{1,0:T(8,128)(2,1)S(1)}, u32[]{:S(2)}, u32[]{:S(2)}) collective-permute-start(bf16[32,3072]{1,0:T(8,128)(2,1)S(1)} %get-tuple-element.68.refs_0_), channel_id=1, source_target_pairs={{0,2},{1,3},{2,0},{3,1},{4,6},{5,7},{6,4},{7,5},{8,10},{9,11},{10,... | collective-permute-start | bytes 589832 | tf_op jit(solution)/shard_map/ppermute | solution.py:22
  20.9 6.6 %collective-permute-start.6 = (bf16[32,3072]{1,0:T(8,128)(2,1)S(1)}, bf16[32,3072]{1,0:T(8,128)(2,1)S(1)}, u32[]{:S(2)}, u32[]{:S(2)}) collective-permute-start(bf16[32,3072]{1,0:T(8,128)(2,1)S(1)} %get-tuple-element.69.refs_2_), channel_id=1, source_target_pairs={{0,4},{1,5},{2,6},{3,7},{4,0},{5,1},{6,2},{7,3},{8,12},{9,13},{10,... | collective-permute-start | bytes 589832 | tf_op jit(solution)/shard_map/ppermute | solution.py:22
  27.5 16.7 %collective-permute-start.12 = (bf16[64,3072]{1,0:T(8,128)(2,1)S(1)}, bf16[64,3072]{1,0:T(8,128)(2,1)S(1)}, u32[]{:S(2)}, u32[]{:S(2)}) collective-permute-start(bf16[64,3072]{1,0:T(8,128)(2,1)S(1)} %get-tuple-element.80.x_pair), channel_id=1, source_target_pairs={{0,4},{1,5},{2,6},{3,7},{4,0},{5,1},{6,2},{7,3},{8,12},{9,13},{10,... | collective-permute-start | bytes 1179656 | tf_op jit(solution)/shard_map/ppermute | solution.py:22
  29.1 15.2 %collective-permute-start.13 = (bf16[64,3072]{1,0:T(8,128)(2,1)S(1)}, bf16[64,3072]{1,0:T(8,128)(2,1)S(1)}, u32[]{:S(2)}, u32[]{:S(2)}) collective-permute-start(bf16[64,3072]{1,0:T(8,128)(2,1)S(1)} %get-tuple-element.81.e_pair), channel_id=1, source_target_pairs={{0,2},{1,3},{2,0},{3,1},{4,6},{5,7},{6,4},{7,5},{8,10},{9,11},{10,... | collective-permute-start | bytes 1179656 | tf_op jit(solution)/shard_map/ppermute | solution.py:22
  29.7 13.3 %collective-permute-start.3 = (bf16[32,3072]{1,0:T(8,128)(2,1)S(1)}, bf16[32,3072]{1,0:T(8,128)(2,1)S(1)}, u32[]{:S(2)}, u32[]{:S(2)}) collective-permute-start(bf16[32,3072]{1,0:T(8,128)(2,1)S(1)} %get-tuple-element.66.refs_0_), channel_id=1, source_target_pairs={{0,2},{1,3},{2,0},{3,1},{4,6},{5,7},{6,4},{7,5},{8,10},{9,11},{10,... | collective-permute-start | bytes 589832 | tf_op jit(solution)/shard_map/ppermute | solution.py:22
  31.2 11.8 %collective-permute-start.4 = (bf16[32,3072]{1,0:T(8,128)(2,1)S(1)}, bf16[32,3072]{1,0:T(8,128)(2,1)S(1)}, u32[]{:S(2)}, u32[]{:S(2)}) collective-permute-start(bf16[32,3072]{1,0:T(8,128)(2,1)S(1)} %get-tuple-element.67.refs_2_), channel_id=1, source_target_pairs={{0,4},{1,5},{2,6},{3,7},{4,0},{5,1},{6,2},{7,3},{8,12},{9,13},{10,... | collective-permute-start | bytes 589832 | tf_op jit(solution)/shard_map/ppermute | solution.py:22
  43.0 8.8 %collective-permute-start.7 = (bf16[64,3072]{1,0:T(8,128)(2,1)S(1)}, bf16[64,3072]{1,0:T(8,128)(2,1)S(1)}, u32[]{:S(2)}, u32[]{:S(2)}) collective-permute-start(bf16[64,3072]{1,0:T(8,128)(2,1)S(1)} %get-tuple-element.72.x_pair), channel_id=1, source_target_pairs={{0,4},{1,5},{2,6},{3,7},{4,0},{5,1},{6,2},{7,3},{8,12},{9,13},{10,... | collective-permute-start | bytes 1179656 | tf_op jit(solution)/shard_map/ppermute | solution.py:22
  43.6 8.5 %collective-permute-start.8 = (bf16[64,3072]{1,0:T(8,128)(2,1)S(1)}, bf16[64,3072]{1,0:T(8,128)(2,1)S(1)}, u32[]{:S(2)}, u32[]{:S(2)}) collective-permute-start(bf16[64,3072]{1,0:T(8,128)(2,1)S(1)} %get-tuple-element.73.e_pair), channel_id=1, source_target_pairs={{0,2},{1,3},{2,0},{3,1},{4,6},{5,7},{6,4},{7,5},{8,10},{9,11},{10,... | collective-permute-start | bytes 1179656 | tf_op jit(solution)/shard_map/ppermute | solution.py:22
  60.3 29.0 %collective-permute-start.18 = (bf16[3,256,3072]{2,1,0:T(8,128)(2,1)S(1)}, bf16[3,256,3072]{2,1,0:T(8,128)(2,1)S(1)}, u32[]{:S(2)}, u32[]{:S(2)}) collective-permute-start(bf16[3,256,3072]{2,1,0:T(8,128)(2,1)S(1)} %get-tuple-element.102), channel_id=1, source_target_pairs={{0,1},{1,0},{2,3},{3,2},{4,5},{5,4},{6,7},{7,6},{8,9},{9,8},{10,11... | collective-permute-start | bytes 14155784 | tf_op jit(solution)/shard_map/ppermute | solution.py:22
  60.4 12.0 %collective-permute-start.14 = (bf16[64,3072]{1,0:T(8,128)(2,1)S(1)}, bf16[64,3072]{1,0:T(8,128)(2,1)S(1)}, u32[]{:S(2)}, u32[]{:S(2)}) collective-permute-start(bf16[64,3072]{1,0:T(8,128)(2,1)S(1)} %get-tuple-element.83), channel_id=1, source_target_pairs={{0,4},{1,5},{2,6},{3,7},{4,0},{5,1},{6,2},{7,3},{8,12},{9,13},{10,... | collective-permute-start | bytes 1179656 | tf_op jit(solution)/shard_map/ppermute | solution.py:22
  61.9 12.0 %collective-permute-start.15 = (bf16[64,3072]{1,0:T(8,128)(2,1)S(1)}, bf16[64,3072]{1,0:T(8,128)(2,1)S(1)}, u32[]{:S(2)}, u32[]{:S(2)}) collective-permute-start(bf16[64,3072]{1,0:T(8,128)(2,1)S(1)} %get-tuple-element.85), channel_id=1, source_target_pairs={{0,2},{1,3},{2,0},{3,1},{4,6},{5,7},{6,4},{7,5},{8,10},{9,11},{10,... | collective-permute-start | bytes 1179656 | tf_op jit(solution)/shard_map/ppermute | solution.py:22
  62.8 18.0 %collective-permute-start.10 = (bf16[64,3072]{1,0:T(8,128)(2,1)S(1)}, bf16[64,3072]{1,0:T(8,128)(2,1)S(1)}, u32[]{:S(2)}, u32[]{:S(2)}) collective-permute-start(bf16[64,3072]{1,0:T(8,128)(2,1)S(1)} %get-tuple-element.77), channel_id=1, source_target_pairs={{0,4},{1,5},{2,6},{3,7},{4,0},{5,1},{6,2},{7,3},{8,12},{9,13},{10,... | collective-permute-start | bytes 1179656 | tf_op jit(solution)/shard_map/ppermute | solution.py:22
  63.4 19.0 %collective-permute-start.11 = (bf16[64,3072]{1,0:T(8,128)(2,1)S(1)}, bf16[64,3072]{1,0:T(8,128)(2,1)S(1)}, u32[]{:S(2)}, u32[]{:S(2)}) collective-permute-start(bf16[64,3072]{1,0:T(8,128)(2,1)S(1)} %get-tuple-element.79), channel_id=1, source_target_pairs={{0,2},{1,3},{2,0},{3,1},{4,6},{5,7},{6,4},{7,5},{8,10},{9,11},{10,... | collective-permute-start | bytes 1179656 | tf_op jit(solution)/shard_map/ppermute | solution.py:22
  74.1 12.5 %collective-permute-start.19 = (bf16[32,3072]{1,0:T(8,128)(2,1)S(1)}, bf16[32,3072]{1,0:T(8,128)(2,1)S(1)}, u32[]{:S(2)}, u32[]{:S(2)}) collective-permute-start(bf16[32,3072]{1,0:T(8,128)(2,1)S(1)} %get-tuple-element.104), channel_id=1, source_target_pairs={{0,2},{1,3},{2,0},{3,1},{4,6},{5,7},{6,4},{7,5},{8,10},{9,11},{10,... | collective-permute-start | bytes 589832 | tf_op jit(solution)/shard_map/ppermute | solution.py:22
  75.0 11.5 %collective-permute-start.20 = (bf16[32,3072]{1,0:T(8,128)(2,1)S(1)}, bf16[32,3072]{1,0:T(8,128)(2,1)S(1)}, u32[]{:S(2)}, u32[]{:S(2)}) collective-permute-start(bf16[32,3072]{1,0:T(8,128)(2,1)S(1)} %get-tuple-element.106), channel_id=1, source_target_pairs={{0,4},{1,5},{2,6},{3,7},{4,0},{5,1},{6,2},{7,3},{8,12},{9,13},{10,... | collective-permute-start | bytes 589832 | tf_op jit(solution)/shard_map/ppermute | solution.py:22
  82.5 11.2 %collective-permute-start.16 = (bf16[32,3072]{1,0:T(8,128)(2,1)S(1)}, bf16[32,3072]{1,0:T(8,128)(2,1)S(1)}, u32[]{:S(2)}, u32[]{:S(2)}) collective-permute-start(bf16[32,3072]{1,0:T(8,128)(2,1)S(1)} %get-tuple-element.99), channel_id=1, source_target_pairs={{0,2},{1,3},{2,0},{3,1},{4,6},{5,7},{6,4},{7,5},{8,10},{9,11},{10,... | collective-permute-start | bytes 589832 | tf_op jit(solution)/shard_map/ppermute | solution.py:22
  83.4 10.3 %collective-permute-start.17 = (bf16[32,3072]{1,0:T(8,128)(2,1)S(1)}, bf16[32,3072]{1,0:T(8,128)(2,1)S(1)}, u32[]{:S(2)}, u32[]{:S(2)}) collective-permute-start(bf16[32,3072]{1,0:T(8,128)(2,1)S(1)} %get-tuple-element.101), channel_id=1, source_target_pairs={{0,4},{1,5},{2,6},{3,7},{4,0},{5,1},{6,2},{7,3},{8,12},{9,13},{10,... | collective-permute-start | bytes 589832 | tf_op jit(solution)/shard_map/ppermute | solution.py:22
  86.6 8.1 %collective-permute-start.21 = (bf16[2,16,3072]{2,1,0:T(8,128)(2,1)S(1)}, bf16[2,16,3072]{2,1,0:T(8,128)(2,1)S(1)}, u32[]{:S(2)}, u32[]{:S(2)}) collective-permute-start(bf16[2,16,3072]{2,1,0:T(8,128)(2,1)S(1)} %get-tuple-element.111), channel_id=1, source_target_pairs={{0,8},{1,9},{2,10},{3,11},{4,12},{5,13},{6,14},{7,15},{8,0},{9,1},... | collective-permute-start | bytes 589832 | tf_op jit(solution)/shard_map/ppermute | solution.py:22
  86.7 11.5 %collective-permute-start.23 = (bf16[2,16,3072]{2,1,0:T(8,128)(2,1)S(1)}, bf16[2,16,3072]{2,1,0:T(8,128)(2,1)S(1)}, u32[]{:S(2)}, u32[]{:S(2)}) collective-permute-start(bf16[2,16,3072]{2,1,0:T(8,128)(2,1)S(1)} %get-tuple-element.113), channel_id=1, source_target_pairs={{0,24},{1,25},{2,26},{3,27},{4,28},{5,29},{6,30},{7,31},{8,16},{9,... | collective-permute-start | bytes 589832 | tf_op jit(solution)/shard_map/ppermute | solution.py:22
  93.8 12.1 %collective-permute-start.22 = (bf16[2,16,3072]{2,1,0:T(8,128)(2,1)S(1)}, bf16[2,16,3072]{2,1,0:T(8,128)(2,1)S(1)}, u32[]{:S(2)}, u32[]{:S(2)}) collective-permute-start(bf16[2,16,3072]{2,1,0:T(8,128)(2,1)S(1)} %get-tuple-element.112), channel_id=1, source_target_pairs={{0,16},{1,17},{2,18},{3,19},{4,20},{5,21},{6,22},{7,23},{8,24},{9,... | collective-permute-start | bytes 589832 | tf_op jit(solution)/shard_map/ppermute | solution.py:22

commit v3 on v2

v3 whole, which is shorter than its diff:
```python
import functools
import math

import jax
import jax.numpy as jnp
from jax import lax
from jax.experimental import pallas as pl
from jax.experimental.pallas import tpu as pltpu
from jax.sharding import PartitionSpec as P

CORE, LINK_X, LINK_Y, LINK_Z = 0, 1, 2, 3
ROW_BITS = 4
LONG = 10**11
PANEL = 512
TURN = pltpu.VMEM((8, 128), jnp.float32)
VMEM = pl.BlockSpec(memory_space=pltpu.VMEM)
HBM = pl.BlockSpec(memory_space=pltpu.HBM)
SMEM = pl.BlockSpec(memory_space=pltpu.SMEM)


def swapped(block, mask):
    count = lax.axis_size("dp")
    return lax.ppermute(block, "dp", [(low, low ^ mask) for low in range(count)])


def row_product(left, right):
    return lax.dot_general(
        left, right, (((1,), (1,)), ((), ())), preferred_element_type=jnp.float32
    )


def col_product(left, right):
    return lax.dot_general(
        left, right, (((0,), (0,)), ((), ())), preferred_element_type=jnp.float32
    )


def product(left, right):
    return jnp.dot(left, right, preferred_element_type=jnp.float32)


def half(value):
    return value.astype(jnp.bfloat16)


def shape(dims, dtype=jnp.bfloat16):
    return jax.ShapeDtypeStruct(dims, dtype)


def held(dims, dtype=jnp.bfloat16):
    return pltpu.VMEM(dims, dtype)


def fetched(*values):
    return [pltpu.with_memory_space_constraint(value, pltpu.VMEM) for value in values]


def in_hbm(value):
    return pltpu.with_memory_space_constraint(value, pltpu.HBM)


def limit(mib):
    return pltpu.CompilerParams(vmem_limit_bytes=mib << 20)


def cost(flops, moved):
    return pl.CostEstimate(flops=flops, bytes_accessed=moved, transcendentals=0)


def pick_kernel(
    place, token, count, gate, tokens, grad, rows, x, e, weight, turn,
    token_here, count_here, gate_here, tokens_here, grad_here, arrived,
):
    pairs = (
        (token, token_here),
        (count, count_here),
        (gate, gate_here),
        (tokens, tokens_here),
        (grad, grad_here),
    )
    copies = [pltpu.make_async_copy(*pair, arrived.at[i]) for i, pair in enumerate(pairs)]
    for copy in copies:
        copy.start()
    turn[...] = jnp.zeros_like(turn)
    for copy in copies:
        copy.wait()
    capacity, lanes = weight.shape
    row = lax.broadcasted_iota(jnp.int32, (capacity, lanes), 0)
    live = count_here[place[0]]
    index = jnp.zeros((capacity, lanes), jnp.int32)
    scale = jnp.zeros((capacity, lanes), jnp.float32)
    for slot in range(capacity):
        index = jnp.where(row == slot, token_here[slot], index)
        scale = jnp.where(row == slot, jnp.where(slot < live, gate_here[slot], 0.0), scale)
    weight[...] = scale
    lane = lax.broadcasted_iota(jnp.int32, (capacity, tokens.shape[0]), 1)
    chosen = jnp.where(lane == index[:, :1], 1.0, 0.0).astype(jnp.bfloat16)
    x[...] = half(product(chosen, tokens_here[...]))
    e[...] = half(scale[:, :1] * grad_here[...].astype(jnp.float32))
    rows[0] = x[...]
    rows[1] = e[...]


def pick(tokens, slot_token, slot_count, slot_gate, grad_out):
    capacity, width = grad_out.shape
    inputs = (slot_token, slot_count, slot_gate, tokens, grad_out)
    return pl.pallas_call(
        pick_kernel,
        out_shape=(
            held((2, capacity, width)),
            held((capacity, width)),
            held((capacity, width)),
            held((capacity, 128), jnp.float32),
            TURN,
        ),
        in_specs=[SMEM] + [HBM] * 5,
        out_specs=(VMEM,) * 5,
        scratch_shapes=[pltpu.SMEM(v.shape, v.dtype) for v in inputs[:3]]
        + [pltpu.VMEM(v.shape, v.dtype) for v in inputs[3:]]
        + [pltpu.SemaphoreType.DMA((5,))],
        compiler_params=limit(4),
        cost_estimate=cost(0, 0),
        name="pick",
    )(lax.axis_index("dp")[None], *(in_hbm(v) for v in inputs))


def last_split_kernel(level, x_far, e_far, w_gate, w_up, w_down, _, x, e, panels, turn, arrived):
    loads = [
        pltpu.make_async_copy(w, panels.at[i], arrived.at[i])
        for i, w in enumerate((w_gate, w_up, w_down))
    ]
    for copy in loads:
        copy.start()
    split_body(level, x, e)
    turn[...] = jnp.zeros_like(turn)
    for copy in loads:
        copy.wait()


def last_split(level, fars, weights, turn):
    rows = held(level.shape[1:])
    return pl.pallas_call(
        last_split_kernel,
        out_shape=(rows, rows, held((3, *weights[0].shape)), TURN),
        in_specs=[VMEM] * 3 + [HBM] * 3 + [VMEM],
        out_specs=(VMEM,) * 4,
        scratch_shapes=[pltpu.SemaphoreType.DMA((3,))],
        compiler_params=limit(4),
        cost_estimate=cost(0, 0),
        name="split_2",
    )(*fetched(level, *fars), *(in_hbm(w) for w in weights), *fetched(turn))


def expert_kernel(count, *refs):
    parts, refs = refs[: 4 * count], refs[4 * count :]
    near, other, _, x, e, hidden, gate_grad, up_grad, out_keep, out_send, row_keep, row_send, turn = refs
    turn[...] = jnp.zeros_like(turn)
    units = near.shape[1]
    rows = x.shape[0] // 4
    size = rows // count
    for i in range(count):
        x_pair, x_far, e_pair, e_far = parts[4 * i : 4 * i + 4]
        for plane, (x_from, e_from, x_half, e_half) in enumerate(
            ((x_pair, e_pair, 0, 0), (x_pair, e_far, 1, 0), (x_far, e_pair, 0, 1), (x_far, e_far, 1, 1))
        ):
            into = slice(plane * rows + i * size, plane * rows + (i + 1) * size)
            x[into] = x_from[x_half * size : (x_half + 1) * size]
            e[into] = e_from[e_half * size : (e_half + 1) * size]
    for i, panels in enumerate((near, other)):
        mine = slice(i * units, (i + 1) * units)
        gate_pre = row_product(x[...], panels[0])
        up_pre = row_product(x[...], panels[1])
        hidden_grad = row_product(e[...], panels[2])
        gate_sig = jax.nn.sigmoid(gate_pre)
        activated = gate_pre * gate_sig
        hidden[:, mine] = half(activated * up_pre)
        gate_grad[:, mine] = half(
            hidden_grad * up_pre * (gate_sig * (1.0 + gate_pre * (1.0 - gate_sig)))
        )
        up_grad[:, mine] = half(hidden_grad * activated)
    for at in range(0, x.shape[1], PANEL):
        part = slice(at, at + PANEL)
        out = product(hidden[:, :units], near[2, :, part]) + product(
            hidden[:, units:], other[2, :, part]
        )
        out_keep[:, part] = out[: 2 * rows]
        out_send[:, part] = half(out[2 * rows :])
        row = (
            product(gate_grad[:, :units], near[0, :, part])
            + product(gate_grad[:, units:], other[0, :, part])
            + product(up_grad[:, :units], near[1, :, part])
            + product(up_grad[:, units:], other[1, :, part])
        )
        row_keep[:rows, part] = row[:rows]
        row_keep[rows:, part] = row[2 * rows : 3 * rows]
        row_send[:rows, part] = half(row[rows : 2 * rows])
        row_send[rows:, part] = half(row[3 * rows :])


def expert(parts, near, other, turn):
    rows, width = 2 * sum(part[0].shape[0] for part in parts), parts[0][0].shape[1]
    units = 2 * near.shape[1]
    saved, kept, sent = (
        held((rows, units)),
        held((rows // 2, width), jnp.float32),
        held((rows // 2, width)),
    )
    return pl.pallas_call(
        functools.partial(expert_kernel, len(parts)),
        out_shape=(held((rows, width)),) * 2 + (saved,) * 3 + (kept, sent, kept, sent, TURN),
        in_specs=[VMEM] * (4 * len(parts) + 3),
        out_specs=(VMEM,) * 10,
        compiler_params=limit(12),
        cost_estimate=cost(12 * rows * units * width, 6 * units * width),
        name="expert",
    )(*fetched(*(ref for part in parts for ref in part), near, other, turn))


def slot_sums(works, units, columns):
    x, e, hidden, gate_grad, up_grad = (
        [refs[i][:, units if i > 1 else columns] for refs in works] for i in range(5)
    )
    for left, right in ((gate_grad, x), (up_grad, x), (hidden, e)):
        yield col_product(jnp.concatenate(left, 0), jnp.concatenate(right, 0))


def other_kernel(*refs):
    works, (_, grads, turn) = (refs[:5], refs[5:10]), refs[10:]
    turn[...] = jnp.zeros_like(turn)
    units = grads.shape[1]
    for at in range(0, grads.shape[2], PANEL):
        columns = slice(at, at + PANEL)
        for i, total in enumerate(slot_sums(works, slice(units, 2 * units), columns)):
            grads[i, :, columns] = half(total)


def other_grads(works, turn):
    width = works[0][0].shape[1]
    units = works[0][2].shape[1] // 2
    return pl.pallas_call(
        other_kernel,
        out_shape=(held((3, units, width)), TURN),
        in_specs=[VMEM] * 11,
        out_specs=(VMEM, VMEM),
        compiler_params=limit(8),
        cost_estimate=cost(LONG, 0),
        name="other_grads",
    )(*fetched(*works[0], *works[1], turn))


def own_kernel(factor, *refs):
    works, (received, _, *grads, turn) = (refs[:5], refs[5:10]), refs[10:]
    turn[...] = jnp.zeros_like(turn)
    units = received.shape[1]
    columns = pl.ds(pl.multiple_of(pl.program_id(0) * PANEL, PANEL), PANEL)
    for i, total in enumerate(slot_sums(works, slice(0, units), columns)):
        total = total + received[i, :, columns].astype(jnp.float32)
        grads[i][...] = (total * factor).astype(grads[i].dtype)


def own_grads(works, received, turn, factor, dtype):
    _, units, width = received.shape
    block = pl.BlockSpec((units, PANEL), lambda i: (0, i))
    return pl.pallas_call(
        functools.partial(own_kernel, factor),
        grid=(width // PANEL,),
        out_shape=(shape((units, width), dtype),) * 3 + (TURN,),
        in_specs=[VMEM] * 12,
        out_specs=(block,) * 3 + (VMEM,),
        compiler_params=limit(12),
        cost_estimate=cost(0, 0),
        name="own_grads",
    )(*fetched(*works[0], *works[1], received, turn))


def staged(body, name, outs, *values, flops=0):
    def kernel(*refs):
        refs[-1][...] = jnp.zeros(TURN.shape, TURN.dtype)
        body(*refs[: len(values) - 1], *refs[len(values) : -1])

    return pl.pallas_call(
        kernel,
        out_shape=(*outs, TURN),
        in_specs=[VMEM] * len(values),
        out_specs=(VMEM,) * (len(outs) + 1),
        compiler_params=limit(4),
        cost_estimate=cost(flops, 0),
        name=name,
    )(*fetched(*values))


def split_body(*refs):
    levels, (x, e) = refs[:-2], refs[-2:]
    rows = levels[0].shape[1]
    for i, level in enumerate(levels):
        x[i * rows : (i + 1) * rows] = level[0]
        e[i * rows : (i + 1) * rows] = level[1]


def pair_body(x, x_side, e, e_side, x_pair, e_pair):
    rows = x.shape[0]
    for out, near, side in ((x_pair, x, x_side), (e_pair, e, e_side)):
        out[:rows] = near[...]
        out[rows:] = side[...]


def plane_body(out_keep, out_far, row_keep, row_far, out_mid, out_side, row_mid, row_side):
    rows = out_mid.shape[0]
    for keep, far, mid, side in (
        (out_keep, out_far, out_mid, out_side),
        (row_keep, row_far, row_mid, row_side),
    ):
        mid[...] = keep[:rows] + far[:rows].astype(jnp.float32)
        side[...] = half(keep[rows:] + far[rows:].astype(jnp.float32))


def line_body(out_mid, out_side, row_mid, row_side, first, second):
    rows = first.shape[1]
    for i, (mid, side) in enumerate(((out_mid, out_side), (row_mid, row_side))):
        total = mid[...] + side[...].astype(jnp.float32)
        first[i] = total[:rows].astype(first.dtype)
        second[i] = total[rows:].astype(second.dtype)


def far_body(own, one, three, total):
    total[...] = own[...] + one[...].astype(jnp.float32) + three[...].astype(jnp.float32)


def final_body(total, two, weight, expert_out, grad_rows):
    expert_out[...] = half(weight[:, :1] * (total[0] + two[0].astype(jnp.float32)))
    grad_rows[...] = half(total[1] + two[1].astype(jnp.float32))


def shards(tokens, slot_token, slot_count, slot_gate, grad_out, w_gate, w_up, w_down):
    capacity = slot_gate.shape[0]
    devices = lax.axis_size("dp")
    all_bits = devices.bit_length() - 1
    core, along_x, along_y = 1 << CORE, 1 << LINK_X, 1 << LINK_Y
    far_bits = range(ROW_BITS + 1, all_bits)

    weights = [w_gate, w_up, w_down]
    for bit in far_bits:
        weights = [jnp.concatenate([w, swapped(w, 1 << bit)], 0) for w in weights]
    own, x, e, weight, turn = pick(tokens, slot_token, slot_count, slot_gate, grad_out)

    width = own.shape[2]
    rows = 2 * capacity

    def sides_of(x, e):
        return x, swapped(x, along_x), e, swapped(e, along_y)

    def fars_of(x, e):
        return x, swapped(x, along_y), e, swapped(e, along_x)

    one, three, two = (swapped(own, k << LINK_Z) for k in (1, 3, 2))
    x, e, turn = staged(pair_body, "pair_0", [held((rows, width))] * 2, *sides_of(x, e), turn)
    part_0 = fars_of(x, e)
    x, e, turn = staged(split_body, "split_13", [held((rows, width))] * 2, one, three, turn)
    sides_13 = sides_of(x, e)
    x, e, near, turn = last_split(two, part_0[1::2], weights, turn)
    sides_2 = sides_of(x, e)
    other = swapped(near, core)
    x, e, turn = staged(pair_body, "pair_13", [held((2 * rows, width))] * 2, *sides_13, turn)
    part_13 = fars_of(x, e)
    x, e, turn = staged(pair_body, "pair_2", [held((rows, width))] * 2, *sides_2, turn, flops=LONG)
    part_2 = fars_of(x, e)

    works, sides = [], []
    for parts in ((part_13,), (part_0, part_2)):
        *work, out_keep, out_send, row_keep, row_send, turn = expert(parts, near, other, turn)
        works.append(work)
        sides.append((out_keep, swapped(out_send, along_y), row_keep, swapped(row_send, along_x)))

    whole, piece = held((rows, width), jnp.float32), held((rows, width))

    def plane_sum(side, turn):
        out_mid, out_side, row_mid, row_side, turn = staged(
            plane_body, "plane_sum", [whole, piece, whole, piece], *side, turn
        )
        return (out_mid, swapped(out_side, along_x), row_mid, swapped(row_side, along_y)), turn

    def line_sum(middle, turn, first, flops=0):
        level_dims = (2, capacity, width)
        return staged(
            line_body, "line_sum", [held(level_dims, first), held(level_dims)], *middle, turn,
            flops=flops,
        )

    middle_13, turn = plane_sum(sides[0], turn)
    sent, turn = other_grads(works, turn)
    received = swapped(sent, core)
    middle_02, turn = plane_sum(sides[1], turn)
    sum_1, sum_3, turn = line_sum(middle_13, turn, jnp.bfloat16)
    one, three = swapped(sum_1, 1 << LINK_Z), swapped(sum_3, 3 << LINK_Z)
    sum_0, sum_2, turn = line_sum(middle_02, turn, jnp.float32, flops=LONG)
    two = swapped(sum_2, 2 << LINK_Z)
    factor = 1.0 / math.sqrt(devices * capacity)
    if far_bits:
        *owned, turn = own_grads(works, received, turn, 1.0, jnp.float32)
        for bit in reversed(far_bits):
            cut = owned[0].shape[0] // 2
            owned = [t[:cut] + swapped(half(t[cut:]), 1 << bit) for t in owned]
        owned = [half(total * factor) for total in owned]
    else:
        *owned, turn = own_grads(works, received, turn, factor, jnp.bfloat16)
    total, turn = staged(
        far_body, "far_sum", [held(own.shape, jnp.float32)], sum_0, one, three, turn, flops=LONG // 10
    )
    expert_out, grad_rows, turn = staged(
        final_body, "final", [shape((capacity, width))] * 2, total, two, weight, turn
    )
    return (expert_out, grad_rows, *owned)


def solution(mesh):
    return jax.shard_map(
        shards,
        mesh=mesh,
        in_specs=(
            P("dp", None),
            P("dp"),
            P(),
            P("dp"),
            P("dp", None),
            P("dp", None),
            P("dp", None),
            P("dp", None),
        ),
        out_specs=(P("dp", None), P("dp", None), P("dp", None), P("dp", None), P("dp", None)),
        check_vma=False,
    )
```

time: 107 us -> 94.5 us (0.88)
  waiting for transfers between devices: 58.8 us -> 42.6 us
  starting transfers between devices: 25 us -> 31.1 us
  Pallas kernels: 21.8 us -> 19.8 us
    ppermute x24 -> x28, waiting for transfers between devices: 58.8 us -> 42.6 us  [swapped(): lax.ppermute(block, 'dp', [(low, low ^ mask) for low in range(count)])]
    ppermute x24 -> x28, starting transfers between devices: 25 us -> 31.1 us  [swapped(): lax.ppermute(block, 'dp', [(low, low ^ mask) for low in range(count)])]
    pallas_call x1, Pallas kernels: 2.71 us -> 1.42 us  [pick(): pl.pallas_call(pick_kernel, out_shape=(held((2, capacity, width)), held((...]
    pallas_call x3 -> x4, Pallas kernels: 13.2 us -> 13 us  [the longest x2 9.14 us: expert(): pl.pallas_call(functools.partial(expert_kernel, len(parts)), out_shape=(h...]
  transfers between devices with their start and end apart: 24 -> 28, of which waited for: 15 -> 14; matrix products, arithmetic and copies ran while one was open for 0% -> 0% of each run, Pallas kernels for 10% -> 19%
where the time goes in v3:
time: 94.5 us; the launch traced here: 94.3 us
  waiting for transfers between devices  42.6 us (45%)
  starting transfers between devices  31.1 us (33%)
  Pallas kernels  19.8 us (21%)
    ppermute x28, waiting for transfers between devices, swapped(): lax.ppermute(block, 'dp', [(low, low ^ mask) for low in range(count)])  42.6 us
    ppermute x28, starting transfers between devices, swapped(): lax.ppermute(block, 'dp', [(low, low ^ mask) for low in range(count)])  31.1 us
    pallas_call x2, Pallas kernels, expert(): pl.pallas_call(functools.partial(expert_kernel, len(parts)), out_shape=(h...  9.14 us
    pallas_call x1, Pallas kernels, own_grads(): pl.pallas_call(functools.partial(own_kernel, factor), grid=(width // PANE...  4.08 us
    pallas_call x1, Pallas kernels, last_split(): pl.pallas_call(last_split_kernel, out_shape=(rows, rows, held((3, *weight...  2.38 us
  transfers between devices with their start and end apart: 28, of which 14 were waited for; matrix products, arithmetic and copies ran while one was open for 0% of the time, Pallas kernels for 19%

profile of v3, /device:TPU:0, one launch (start us, length us, event | category | flops | bytes accessed | tf_op | source)
XLA Modules:
  0.0 94.3 jit_solution(13489378230463233969)
XLA Ops:
  0.6 1.4 %pick.1 = (bf16[2,16,3072]{2,1,0:T(8,128)(2,1)S(1)}, bf16[16,3072]{1,0:T(8,128)(2,1)S(1)}, bf16[16,3072]{1,0:T(8,128)(2,1)S(1)}, f32[16,128]{1,0:T(8,128)S(1)}, f32[8,128]{1,0:T(8,128)S(1)}) custom-call(s32[1]{0:T(128)} %bitcast.place, s32[16]{0:T(128)} %token_.1, s32[32]{0:T(128)} %count.1, f32[16]{0:T(128)} %gate.1, bf16[128,3072]{1,0:T(8,128)(2,1)} %tokens.1, ...), custom_call_target="tpu_custom_call" | custom-call | tf_op jit(solution)/shard_map/pick/pallas_call | solution.py:107
  2.1 3.0 %collective-permute-start = (bf16[16,3072]{1,0:T(8,128)(2,1)S(1)}, bf16[16,3072]{1,0:T(8,128)(2,1)S(1)}, u32[]{:S(2)}, u32[]{:S(2)}) collective-permute-start(bf16[16,3072]{1,0:T(8,128)(2,1)S(1)} %get-tuple-element.72.refs_0_), channel_id=1, source_target_pairs={{0,2},{1,3},{2,0},{3,1},{4,6},{5,7},{6,4},{7,5},{8,10},{9,11},{10,... | collective-permute-start | bytes 294920 | tf_op jit(solution)/shard_map/ppermute | solution.py:23
  5.1 1.5 %collective-permute-start.1 = (bf16[16,3072]{1,0:T(8,128)(2,1)S(1)}, bf16[16,3072]{1,0:T(8,128)(2,1)S(1)}, u32[]{:S(2)}, u32[]{:S(2)}) collective-permute-start(bf16[16,3072]{1,0:T(8,128)(2,1)S(1)} %get-tuple-element.73.refs_2_), channel_id=1, source_target_pairs={{0,4},{1,5},{2,6},{3,7},{4,0},{5,1},{6,2},{7,3},{8,12},{9,13},{10,... | collective-permute-start | bytes 294920 | tf_op jit(solution)/shard_map/ppermute | solution.py:23
  6.6 3.6 %collective-permute-start.6 = (bf16[2,16,3072]{2,1,0:T(8,128)(2,1)S(1)}, bf16[2,16,3072]{2,1,0:T(8,128)(2,1)S(1)}, u32[]{:S(2)}, u32[]{:S(2)}) collective-permute-start(bf16[2,16,3072]{2,1,0:T(8,128)(2,1)S(1)} %get-tuple-element.77), channel_id=1, source_target_pairs={{0,24},{1,25},{2,26},{3,27},{4,28},{5,29},{6,30},{7,31},{8,16},{9,... | collective-permute-start | bytes 589832 | tf_op jit(solution)/shard_map/ppermute | solution.py:23
  10.2 0.8 collective-permute-start.4
  11.0 0.6 collective-permute-start.2
  11.6 0.3 collective-permute-start.3
  11.9 4.3 %collective-permute-done.6.refs_1_ = bf16[2,16,3072]{2,1,0:T(8,128)(2,1)S(1)} collective-permute-done((bf16[2,16,3072]{2,1,0:T(8,128)(2,1)S(1)}, bf16[2,16,3072]{2,1,0:T(8,128)(2,1)S(1)}, u32[]{:S(2)}, u32[]{:S(2)}) %collective-permute-start.6) | collective-permute-done | bytes 196640 | tf_op jit(solution)/shard_map/ppermute | solution.py:23
  16.2 3.5 %collective-permute-done.5.refs_0_ = bf16[2,16,3072]{2,1,0:T(8,128)(2,1)S(1)} collective-permute-done((bf16[2,16,3072]{2,1,0:T(8,128)(2,1)S(1)}, bf16[2,16,3072]{2,1,0:T(8,128)(2,1)S(1)}, u32[]{:S(2)}, u32[]{:S(2)}) %collective-permute-start.5) | collective-permute-done | bytes 196640 | tf_op jit(solution)/shard_map/ppermute | solution.py:23
  19.8 0.6 collective-permute-start.9
  20.4 0.5 collective-permute-start.10
  20.9 5.4 %collective-permute-done.4.level = bf16[2,16,3072]{2,1,0:T(8,128)(2,1)S(1)} collective-permute-done((bf16[2,16,3072]{2,1,0:T(8,128)(2,1)S(1)}, bf16[2,16,3072]{2,1,0:T(8,128)(2,1)S(1)}, u32[]{:S(2)}, u32[]{:S(2)}) %collective-permute-start.4) | collective-permute-done | bytes 196640 | tf_op jit(solution)/shard_map/ppermute | solution.py:23
  26.3 2.4 %split_2.1 = (bf16[16,3072]{1,0:T(8,128)(2,1)S(1)}, bf16[16,3072]{1,0:T(8,128)(2,1)S(1)}, bf16[3,256,3072]{2,1,0:T(8,128)(2,1)S(1)}, f32[8,128]{1,0:T(8,128)S(1)}) custom-call(bf16[2,16,3072]{2,1,0:T(8,128)(2,1)S(1)} %collective-permute-done.4.level, bf16[32,3072]{1,0:T(8,128)(2,1)S(1)} %collective-permute-done.2.x_far.refs_1_, ...), custom_call_target="tpu_custom_call" | custom-call | tf_op jit(solution)/shard_map/split_2/pallas_call | solution.py:142
  28.7 0.6 collective-permute-start.7
  29.3 0.5 collective-permute-start.8
  29.9 1.6 %collective-permute-start.14 = (bf16[64,3072]{1,0:T(8,128)(2,1)S(1)}, bf16[64,3072]{1,0:T(8,128)(2,1)S(1)}, u32[]{:S(2)}, u32[]{:S(2)}) collective-permute-start(bf16[64,3072]{1,0:T(8,128)(2,1)S(1)} %get-tuple-element.89.refs_0_), channel_id=1, source_target_pairs={{0,4},{1,5},{2,6},{3,7},{4,0},{5,1},{6,2},{7,3},{8,12},{9,13},{10,... | collective-permute-start | bytes 1179656 | tf_op jit(solution)/shard_map/ppermute | solution.py:23
  31.5 1.5 %collective-permute-start.15 = (bf16[64,3072]{1,0:T(8,128)(2,1)S(1)}, bf16[64,3072]{1,0:T(8,128)(2,1)S(1)}, u32[]{:S(2)}, u32[]{:S(2)}) collective-permute-start(bf16[64,3072]{1,0:T(8,128)(2,1)S(1)} %get-tuple-element.90.refs_2_), channel_id=1, source_target_pairs={{0,2},{1,3},{2,0},{3,1},{4,6},{5,7},{6,4},{7,5},{8,10},{9,11},{10,... | collective-permute-start | bytes 1179656 | tf_op jit(solution)/shard_map/ppermute | solution.py:23
  33.0 0.4 collective-permute-done.7.refs_1_
  33.4 1.4 %collective-permute-done.8.refs_3_ = bf16[16,3072]{1,0:T(8,128)(2,1)S(1)} collective-permute-done((bf16[16,3072]{1,0:T(8,128)(2,1)S(1)}, bf16[16,3072]{1,0:T(8,128)(2,1)S(1)}, u32[]{:S(2)}, u32[]{:S(2)}) %collective-permute-start.8) | collective-permute-done | bytes 98336 | tf_op jit(solution)/shard_map/ppermute | solution.py:23
  34.9 1.6 %collective-permute-start.12 = (bf16[32,3072]{1,0:T(8,128)(2,1)S(1)}, bf16[32,3072]{1,0:T(8,128)(2,1)S(1)}, u32[]{:S(2)}, u32[]{:S(2)}) collective-permute-start(bf16[32,3072]{1,0:T(8,128)(2,1)S(1)} %get-tuple-element.87.refs_6_), channel_id=1, source_target_pairs={{0,2},{1,3},{2,0},{3,1},{4,6},{5,7},{6,4},{7,5},{8,10},{9,11},{10,... | collective-permute-start | bytes 589832 | tf_op jit(solution)/shard_map/ppermute | solution.py:23
  36.5 6.8 %collective-permute-done.14.refs_1_ = bf16[64,3072]{1,0:T(8,128)(2,1)S(1)} collective-permute-done((bf16[64,3072]{1,0:T(8,128)(2,1)S(1)}, bf16[64,3072]{1,0:T(8,128)(2,1)S(1)}, u32[]{:S(2)}, u32[]{:S(2)}) %collective-permute-start.14) | collective-permute-done | bytes 393248 | tf_op jit(solution)/shard_map/ppermute | solution.py:23
  43.2 0.2 collective-permute-done.15.refs_3_
  43.4 4.6 %expert.2 = (bf16[128,3072]{1,0:T(8,128)(2,1)S(1)}, bf16[128,3072]{1,0:T(8,128)(2,1)S(1)}, bf16[128,512]{1,0:T(8,128)(2,1)S(1)}, bf16[128,512]{1,0:T(8,128)(2,1)...) custom-call(bf16[64,3072]{1,0:T(8,128)(2,1)S(1)} %get-tuple-element., ...), custom_call_target="tpu_custom_call" | custom-call | flops 2415919104 | bytes 9437184 | tf_op jit(solution)/shard_map/expert/pallas_call | solution.py:208
  48.0 0.6 collective-permute-start.18
  48.6 1.5 %collective-permute-start.19 = (bf16[64,3072]{1,0:T(8,128)(2,1)S(1)}, bf16[64,3072]{1,0:T(8,128)(2,1)S(1)}, u32[]{:S(2)}, u32[]{:S(2)}) collective-permute-start(bf16[64,3072]{1,0:T(8,128)(2,1)S(1)} %get-tuple-element.110), channel_id=1, source_target_pairs={{0,2},{1,3},{2,0},{3,1},{4,6},{5,7},{6,4},{7,5},{8,10},{9,11},{10,... | collective-permute-start | bytes 1179656 | tf_op jit(solution)/shard_map/ppermute | solution.py:23
  50.1 4.6 %expert.3 = (bf16[128,3072]{1,0:T(8,128)(2,1)S(1)}, bf16[128,3072]{1,0:T(8,128)(2,1)S(1)}, bf16[128,512]{1,0:T(8,128)(2,1)S(1)}, bf16[128,512]{1,0:T(8,128)(2,1)...) custom-call(bf16[32,3072]{1,0:T(8,128)(2,1)S(1)} %get-tuple-element., ...), custom_call_target="tpu_custom_call" | custom-call | flops 2415919104 | bytes 9437184 | tf_op jit(solution)/shard_map/expert/pallas_call | solution.py:208
  54.7 1.6 %collective-permute-start.16 = (bf16[64,3072]{1,0:T(8,128)(2,1)S(1)}, bf16[64,3072]{1,0:T(8,128)(2,1)S(1)}, u32[]{:S(2)}, u32[]{:S(2)}) collective-permute-start(bf16[64,3072]{1,0:T(8,128)(2,1)S(1)} %get-tuple-element.94), channel_id=1, source_target_pairs={{0,4},{1,5},{2,6},{3,7},{4,0},{5,1},{6,2},{7,3},{8,12},{9,13},{10,... | collective-permute-start | bytes 1179656 | tf_op jit(solution)/shard_map/ppermute | solution.py:23
  56.3 0.5 collective-permute-start.17
  56.8 3.2 %collective-permute-done.18.refs_1_ = bf16[64,3072]{1,0:T(8,128)(2,1)S(1)} collective-permute-done((bf16[64,3072]{1,0:T(8,128)(2,1)S(1)}, bf16[64,3072]{1,0:T(8,128)(2,1)S(1)}, u32[]{:S(2)}, u32[]{:S(2)}) %collective-permute-start.18) | collective-permute-done | bytes 393248 | tf_op jit(solution)/shard_map/ppermute | solution.py:23
  60.0 0.2 plane_sum.2
  60.1 2.0 %collective-permute-start.22 = (bf16[32,3072]{1,0:T(8,128)(2,1)S(1)}, bf16[32,3072]{1,0:T(8,128)(2,1)S(1)}, u32[]{:S(2)}, u32[]{:S(2)}) collective-permute-start(bf16[32,3072]{1,0:T(8,128)(2,1)S(1)} %get-tuple-element.119), channel_id=1, source_target_pairs={{0,2},{1,3},{2,0},{3,1},{4,6},{5,7},{6,4},{7,5},{8,10},{9,11},{10,... | collective-permute-start | bytes 589832 | tf_op jit(solution)/shard_map/ppermute | solution.py:23
  62.1 1.7 %collective-permute-start.23 = (bf16[32,3072]{1,0:T(8,128)(2,1)S(1)}, bf16[32,3072]{1,0:T(8,128)(2,1)S(1)}, u32[]{:S(2)}, u32[]{:S(2)}) collective-permute-start(bf16[32,3072]{1,0:T(8,128)(2,1)S(1)} %get-tuple-element.121), channel_id=1, source_target_pairs={{0,4},{1,5},{2,6},{3,7},{4,0},{5,1},{6,2},{7,3},{8,12},{9,13},{10,... | collective-permute-start | bytes 589832 | tf_op jit(solution)/shard_map/ppermute | solution.py:23
  63.9 1.4 %other_grads.1 = (bf16[3,256,3072]{2,1,0:T(8,128)(2,1)S(1)}, f32[8,128]{1,0:T(8,128)S(1)}) custom-call(bf16[128,3072]{1,0:T(8,128)(2,1)S(1)} %get-tuple-element.97.refs_0_, bf16[128,3072]{1,0:T(8,128)(2,1)S(1)} %get-tuple-element.98.refs_1_, bf16[128,512]{1,0:T(8,128)(2,1)S(1)} %get-tuple-element.99.refs_2_, ...), custom_call_target="tpu_custom_call" | custom-call | flops 99999997952 | tf_op jit(solution)/shard_map/other_grads/pallas_call | solution.py:240
  65.3 3.0 %collective-permute-done.16.refs_1_ = bf16[64,3072]{1,0:T(8,128)(2,1)S(1)} collective-permute-done((bf16[64,3072]{1,0:T(8,128)(2,1)S(1)}, bf16[64,3072]{1,0:T(8,128)(2,1)S(1)}, u32[]{:S(2)}, u32[]{:S(2)}) %collective-permute-start.16) | collective-permute-done | bytes 393248 | tf_op jit(solution)/shard_map/ppermute | solution.py:23
  68.3 0.2 plane_sum.3
  68.5 2.1 %collective-permute-start.20 = (bf16[32,3072]{1,0:T(8,128)(2,1)S(1)}, bf16[32,3072]{1,0:T(8,128)(2,1)S(1)}, u32[]{:S(2)}, u32[]{:S(2)}) collective-permute-start(bf16[32,3072]{1,0:T(8,128)(2,1)S(1)} %get-tuple-element.115), channel_id=1, source_target_pairs={{0,2},{1,3},{2,0},{3,1},{4,6},{5,7},{6,4},{7,5},{8,10},{9,11},{10,... | collective-permute-start | bytes 589832 | tf_op jit(solution)/shard_map/ppermute | solution.py:23
  70.6 1.7 %collective-permute-start.21 = (bf16[32,3072]{1,0:T(8,128)(2,1)S(1)}, bf16[32,3072]{1,0:T(8,128)(2,1)S(1)}, u32[]{:S(2)}, u32[]{:S(2)}) collective-permute-start(bf16[32,3072]{1,0:T(8,128)(2,1)S(1)} %get-tuple-element.117), channel_id=1, source_target_pairs={{0,4},{1,5},{2,6},{3,7},{4,0},{5,1},{6,2},{7,3},{8,12},{9,13},{10,... | collective-permute-start | bytes 589832 | tf_op jit(solution)/shard_map/ppermute | solution.py:23
  72.3 0.2 collective-permute-done.22.refs_1_
  72.5 0.1 line_sum.2
  72.6 0.6 collective-permute-start.24
  73.2 2.0 %collective-permute-start.25 = (bf16[2,16,3072]{2,1,0:T(8,128)(2,1)S(1)}, bf16[2,16,3072]{2,1,0:T(8,128)(2,1)S(1)}, u32[]{:S(2)}, u32[]{:S(2)}) collective-permute-start(bf16[2,16,3072]{2,1,0:T(8,128)(2,1)S(1)} %get-tuple-element.126), channel_id=1, source_target_pairs={{0,24},{1,25},{2,26},{3,27},{4,28},{5,29},{6,30},{7,31},{8,16},{9,... | collective-permute-start | bytes 589832 | tf_op jit(solution)/shard_map/ppermute | solution.py:23
  75.2 1.0 %collective-permute-done.21.refs_3_ = bf16[32,3072]{1,0:T(8,128)(2,1)S(1)} collective-permute-done((bf16[32,3072]{1,0:T(8,128)(2,1)S(1)}, bf16[32,3072]{1,0:T(8,128)(2,1)S(1)}, u32[]{:S(2)}, u32[]{:S(2)}) %collective-permute-start.21) | collective-permute-done | bytes 196640 | tf_op jit(solution)/shard_map/ppermute | solution.py:23
  76.2 0.1 line_sum.3
  76.4 3.8 %collective-permute-done.26.refs_10_ = bf16[3,256,3072]{2,1,0:T(8,128)(2,1)S(1)} collective-permute-done((bf16[3,256,3072]{2,1,0:T(8,128)(2,1)S(1)}, bf16[3,256,3072]{2,1,0:T(8,128)(2,1)S(1)}, u32[]{:S(2)}, u32[]{:S(2)}) %collective-permute-start.26) | collective-permute-done | bytes 4718624 | tf_op jit(solution)/shard_map/ppermute | solution.py:23
  80.2 4.1 %own_grads.1 = (bf16[256,3072]{1,0:T(8,128)(2,1)}, bf16[256,3072]{1,0:T(8,128)(2,1)}, bf16[256,3072]{1,0:T(8,128)(2,1)}, f32[8,128]{1,0:T(8,128)S(1)}) custom-call(bf16[128,3072]{1,0:T(8,128)(2,1)S(1)} %get-tuple-element.97.refs_0_, bf16[128,3072]{1,0:T(8,128)(2,1)S(1)} %get-tuple-element.98.refs_1_, bf16[128,512]{1,0:T(8,128)(2,1)S(1)} %get-tuple-element.99.refs_2_, ...), custom_call_target="tpu_custom_call" | custom-call | tf_op jit(solution)/shard_map/own_grads/pallas_call | solution.py:264
  84.3 0.8 collective-permute-done.25.refs_2_
  85.2 8.4 %collective-permute-done.27.refs_1_ = bf16[2,16,3072]{2,1,0:T(8,128)(2,1)S(1)} collective-permute-done((bf16[2,16,3072]{2,1,0:T(8,128)(2,1)S(1)}, bf16[2,16,3072]{2,1,0:T(8,128)(2,1)S(1)}, u32[]{:S(2)}, u32[]{:S(2)}) %collective-permute-start.27) | collective-permute-done | bytes 196640 | tf_op jit(solution)/shard_map/ppermute | solution.py:23
  93.6 0.7 final.1
  (24 shorter events, 0.4 us)
Async XLA Ops:
  2.1 8.9 %collective-permute-start = (bf16[16,3072]{1,0:T(8,128)(2,1)S(1)}, bf16[16,3072]{1,0:T(8,128)(2,1)S(1)}, u32[]{:S(2)}, u32[]{:S(2)}) collective-permute-start(bf16[16,3072]{1,0:T(8,128)(2,1)S(1)} %get-tuple-element.72.refs_0_), channel_id=1, source_target_pairs={{0,2},{1,3},{2,0},{3,1},{4,6},{5,7},{6,4},{7,5},{8,10},{9,11},{10,... | collective-permute-start | bytes 294920 | tf_op jit(solution)/shard_map/ppermute | solution.py:23
  5.1 5.9 %collective-permute-start.1 = (bf16[16,3072]{1,0:T(8,128)(2,1)S(1)}, bf16[16,3072]{1,0:T(8,128)(2,1)S(1)}, u32[]{:S(2)}, u32[]{:S(2)}) collective-permute-start(bf16[16,3072]{1,0:T(8,128)(2,1)S(1)} %get-tuple-element.73.refs_2_), channel_id=1, source_target_pairs={{0,4},{1,5},{2,6},{3,7},{4,0},{5,1},{6,2},{7,3},{8,12},{9,13},{10,... | collective-permute-start | bytes 294920 | tf_op jit(solution)/shard_map/ppermute | solution.py:23
  6.6 9.6 %collective-permute-start.6 = (bf16[2,16,3072]{2,1,0:T(8,128)(2,1)S(1)}, bf16[2,16,3072]{2,1,0:T(8,128)(2,1)S(1)}, u32[]{:S(2)}, u32[]{:S(2)}) collective-permute-start(bf16[2,16,3072]{2,1,0:T(8,128)(2,1)S(1)} %get-tuple-element.77), channel_id=1, source_target_pairs={{0,24},{1,25},{2,26},{3,27},{4,28},{5,29},{6,30},{7,31},{8,16},{9,... | collective-permute-start | bytes 589832 | tf_op jit(solution)/shard_map/ppermute | solution.py:23
  10.2 9.6 %collective-permute-start.5 = (bf16[2,16,3072]{2,1,0:T(8,128)(2,1)S(1)}, bf16[2,16,3072]{2,1,0:T(8,128)(2,1)S(1)}, u32[]{:S(2)}, u32[]{:S(2)}) collective-permute-start(bf16[2,16,3072]{2,1,0:T(8,128)(2,1)S(1)} %get-tuple-element.77), channel_id=1, source_target_pairs={{0,8},{1,9},{2,10},{3,11},{4,12},{5,13},{6,14},{7,15},{8,0},{9,1},... | collective-permute-start | bytes 589832 | tf_op jit(solution)/shard_map/ppermute | solution.py:23
  10.2 16.1 %collective-permute-start.4 = (bf16[2,16,3072]{2,1,0:T(8,128)(2,1)S(1)}, bf16[2,16,3072]{2,1,0:T(8,128)(2,1)S(1)}, u32[]{:S(2)}, u32[]{:S(2)}) collective-permute-start(bf16[2,16,3072]{2,1,0:T(8,128)(2,1)S(1)} %get-tuple-element.77), channel_id=1, source_target_pairs={{0,16},{1,17},{2,18},{3,19},{4,20},{5,21},{6,22},{7,23},{8,24},{9,... | collective-permute-start | bytes 589832 | tf_op jit(solution)/shard_map/ppermute | solution.py:23
  11.0 15.3 %collective-permute-start.2 = (bf16[32,3072]{1,0:T(8,128)(2,1)S(1)}, bf16[32,3072]{1,0:T(8,128)(2,1)S(1)}, u32[]{:S(2)}, u32[]{:S(2)}) collective-permute-start(bf16[32,3072]{1,0:T(8,128)(2,1)S(1)} %get-tuple-element.75.refs_0_), channel_id=1, source_target_pairs={{0,4},{1,5},{2,6},{3,7},{4,0},{5,1},{6,2},{7,3},{8,12},{9,13},{10,... | collective-permute-start | bytes 589832 | tf_op jit(solution)/shard_map/ppermute | solution.py:23
  11.6 14.7 %collective-permute-start.3 = (bf16[32,3072]{1,0:T(8,128)(2,1)S(1)}, bf16[32,3072]{1,0:T(8,128)(2,1)S(1)}, u32[]{:S(2)}, u32[]{:S(2)}) collective-permute-start(bf16[32,3072]{1,0:T(8,128)(2,1)S(1)} %get-tuple-element.76.refs_2_), channel_id=1, source_target_pairs={{0,2},{1,3},{2,0},{3,1},{4,6},{5,7},{6,4},{7,5},{8,10},{9,11},{10,... | collective-permute-start | bytes 589832 | tf_op jit(solution)/shard_map/ppermute | solution.py:23
  19.8 10.0 %collective-permute-start.9 = (bf16[32,3072]{1,0:T(8,128)(2,1)S(1)}, bf16[32,3072]{1,0:T(8,128)(2,1)S(1)}, u32[]{:S(2)}, u32[]{:S(2)}) collective-permute-start(bf16[32,3072]{1,0:T(8,128)(2,1)S(1)} %get-tuple-element.82.refs_0_), channel_id=1, source_target_pairs={{0,2},{1,3},{2,0},{3,1},{4,6},{5,7},{6,4},{7,5},{8,10},{9,11},{10,... | collective-permute-start | bytes 589832 | tf_op jit(solution)/shard_map/ppermute | solution.py:23
  20.4 9.4 %collective-permute-start.10 = (bf16[32,3072]{1,0:T(8,128)(2,1)S(1)}, bf16[32,3072]{1,0:T(8,128)(2,1)S(1)}, u32[]{:S(2)}, u32[]{:S(2)}) collective-permute-start(bf16[32,3072]{1,0:T(8,128)(2,1)S(1)} %get-tuple-element.83.refs_2_), channel_id=1, source_target_pairs={{0,4},{1,5},{2,6},{3,7},{4,0},{5,1},{6,2},{7,3},{8,12},{9,13},{10,... | collective-permute-start | bytes 589832 | tf_op jit(solution)/shard_map/ppermute | solution.py:23
  28.7 4.7 %collective-permute-start.7 = (bf16[16,3072]{1,0:T(8,128)(2,1)S(1)}, bf16[16,3072]{1,0:T(8,128)(2,1)S(1)}, u32[]{:S(2)}, u32[]{:S(2)}) collective-permute-start(bf16[16,3072]{1,0:T(8,128)(2,1)S(1)} %get-tuple-element.80.refs_0_), channel_id=1, source_target_pairs={{0,2},{1,3},{2,0},{3,1},{4,6},{5,7},{6,4},{7,5},{8,10},{9,11},{10,... | collective-permute-start | bytes 294920 | tf_op jit(solution)/shard_map/ppermute | solution.py:23
  29.3 5.5 %collective-permute-start.8 = (bf16[16,3072]{1,0:T(8,128)(2,1)S(1)}, bf16[16,3072]{1,0:T(8,128)(2,1)S(1)}, u32[]{:S(2)}, u32[]{:S(2)}) collective-permute-start(bf16[16,3072]{1,0:T(8,128)(2,1)S(1)} %get-tuple-element.81.refs_2_), channel_id=1, source_target_pairs={{0,4},{1,5},{2,6},{3,7},{4,0},{5,1},{6,2},{7,3},{8,12},{9,13},{10,... | collective-permute-start | bytes 294920 | tf_op jit(solution)/shard_map/ppermute | solution.py:23
  29.8 13.6 %collective-permute-start.13 = (bf16[3,256,3072]{2,1,0:T(8,128)(2,1)S(1)}, bf16[3,256,3072]{2,1,0:T(8,128)(2,1)S(1)}, u32[]{:S(2)}, u32[]{:S(2)}) collective-permute-start(bf16[3,256,3072]{2,1,0:T(8,128)(2,1)S(1)} %get-tuple-element.88.refs_4_.refs_8_), channel_id=1, source_target_pairs={{0,1},{1,0},{2,3},{3,2},{4,5},{5,4},{6,7},{7,6},{8,9},{9,8},{10,11... | collective-permute-start | bytes 14155784 | tf_op jit(solution)/shard_map/ppermute | solution.py:23
  29.9 13.3 %collective-permute-start.14 = (bf16[64,3072]{1,0:T(8,128)(2,1)S(1)}, bf16[64,3072]{1,0:T(8,128)(2,1)S(1)}, u32[]{:S(2)}, u32[]{:S(2)}) collective-permute-start(bf16[64,3072]{1,0:T(8,128)(2,1)S(1)} %get-tuple-element.89.refs_0_), channel_id=1, source_target_pairs={{0,4},{1,5},{2,6},{3,7},{4,0},{5,1},{6,2},{7,3},{8,12},{9,13},{10,... | collective-permute-start | bytes 1179656 | tf_op jit(solution)/shard_map/ppermute | solution.py:23
  31.5 11.9 %collective-permute-start.15 = (bf16[64,3072]{1,0:T(8,128)(2,1)S(1)}, bf16[64,3072]{1,0:T(8,128)(2,1)S(1)}, u32[]{:S(2)}, u32[]{:S(2)}) collective-permute-start(bf16[64,3072]{1,0:T(8,128)(2,1)S(1)} %get-tuple-element.90.refs_2_), channel_id=1, source_target_pairs={{0,2},{1,3},{2,0},{3,1},{4,6},{5,7},{6,4},{7,5},{8,10},{9,11},{10,... | collective-permute-start | bytes 1179656 | tf_op jit(solution)/shard_map/ppermute | solution.py:23
  34.8 15.2 %collective-permute-start.11 = (bf16[32,3072]{1,0:T(8,128)(2,1)S(1)}, bf16[32,3072]{1,0:T(8,128)(2,1)S(1)}, u32[]{:S(2)}, u32[]{:S(2)}) collective-permute-start(bf16[32,3072]{1,0:T(8,128)(2,1)S(1)} %get-tuple-element.86.refs_4_), channel_id=1, source_target_pairs={{0,4},{1,5},{2,6},{3,7},{4,0},{5,1},{6,2},{7,3},{8,12},{9,13},{10,... | collective-permute-start | bytes 589832 | tf_op jit(solution)/shard_map/ppermute | solution.py:23
  34.9 15.2 %collective-permute-start.12 = (bf16[32,3072]{1,0:T(8,128)(2,1)S(1)}, bf16[32,3072]{1,0:T(8,128)(2,1)S(1)}, u32[]{:S(2)}, u32[]{:S(2)}) collective-permute-start(bf16[32,3072]{1,0:T(8,128)(2,1)S(1)} %get-tuple-element.87.refs_6_), channel_id=1, source_target_pairs={{0,2},{1,3},{2,0},{3,1},{4,6},{5,7},{6,4},{7,5},{8,10},{9,11},{10,... | collective-permute-start | bytes 589832 | tf_op jit(solution)/shard_map/ppermute | solution.py:23
  48.0 12.0 %collective-permute-start.18 = (bf16[64,3072]{1,0:T(8,128)(2,1)S(1)}, bf16[64,3072]{1,0:T(8,128)(2,1)S(1)}, u32[]{:S(2)}, u32[]{:S(2)}) collective-permute-start(bf16[64,3072]{1,0:T(8,128)(2,1)S(1)} %get-tuple-element.108), channel_id=1, source_target_pairs={{0,4},{1,5},{2,6},{3,7},{4,0},{5,1},{6,2},{7,3},{8,12},{9,13},{10,... | collective-permute-start | bytes 1179656 | tf_op jit(solution)/shard_map/ppermute | solution.py:23
  48.6 11.4 %collective-permute-start.19 = (bf16[64,3072]{1,0:T(8,128)(2,1)S(1)}, bf16[64,3072]{1,0:T(8,128)(2,1)S(1)}, u32[]{:S(2)}, u32[]{:S(2)}) collective-permute-start(bf16[64,3072]{1,0:T(8,128)(2,1)S(1)} %get-tuple-element.110), channel_id=1, source_target_pairs={{0,2},{1,3},{2,0},{3,1},{4,6},{5,7},{6,4},{7,5},{8,10},{9,11},{10,... | collective-permute-start | bytes 1179656 | tf_op jit(solution)/shard_map/ppermute | solution.py:23
  54.7 13.7 %collective-permute-start.16 = (bf16[64,3072]{1,0:T(8,128)(2,1)S(1)}, bf16[64,3072]{1,0:T(8,128)(2,1)S(1)}, u32[]{:S(2)}, u32[]{:S(2)}) collective-permute-start(bf16[64,3072]{1,0:T(8,128)(2,1)S(1)} %get-tuple-element.94), channel_id=1, source_target_pairs={{0,4},{1,5},{2,6},{3,7},{4,0},{5,1},{6,2},{7,3},{8,12},{9,13},{10,... | collective-permute-start | bytes 1179656 | tf_op jit(solution)/shard_map/ppermute | solution.py:23
  56.3 12.1 %collective-permute-start.17 = (bf16[64,3072]{1,0:T(8,128)(2,1)S(1)}, bf16[64,3072]{1,0:T(8,128)(2,1)S(1)}, u32[]{:S(2)}, u32[]{:S(2)}) collective-permute-start(bf16[64,3072]{1,0:T(8,128)(2,1)S(1)} %get-tuple-element.96), channel_id=1, source_target_pairs={{0,2},{1,3},{2,0},{3,1},{4,6},{5,7},{6,4},{7,5},{8,10},{9,11},{10,... | collective-permute-start | bytes 1179656 | tf_op jit(solution)/shard_map/ppermute | solution.py:23
  60.1 12.4 %collective-permute-start.22 = (bf16[32,3072]{1,0:T(8,128)(2,1)S(1)}, bf16[32,3072]{1,0:T(8,128)(2,1)S(1)}, u32[]{:S(2)}, u32[]{:S(2)}) collective-permute-start(bf16[32,3072]{1,0:T(8,128)(2,1)S(1)} %get-tuple-element.119), channel_id=1, source_target_pairs={{0,2},{1,3},{2,0},{3,1},{4,6},{5,7},{6,4},{7,5},{8,10},{9,11},{10,... | collective-permute-start | bytes 589832 | tf_op jit(solution)/shard_map/ppermute | solution.py:23
  62.1 10.4 %collective-permute-start.23 = (bf16[32,3072]{1,0:T(8,128)(2,1)S(1)}, bf16[32,3072]{1,0:T(8,128)(2,1)S(1)}, u32[]{:S(2)}, u32[]{:S(2)}) collective-permute-start(bf16[32,3072]{1,0:T(8,128)(2,1)S(1)} %get-tuple-element.121), channel_id=1, source_target_pairs={{0,4},{1,5},{2,6},{3,7},{4,0},{5,1},{6,2},{7,3},{8,12},{9,13},{10,... | collective-permute-start | bytes 589832 | tf_op jit(solution)/shard_map/ppermute | solution.py:23
  68.5 6.7 %collective-permute-start.20 = (bf16[32,3072]{1,0:T(8,128)(2,1)S(1)}, bf16[32,3072]{1,0:T(8,128)(2,1)S(1)}, u32[]{:S(2)}, u32[]{:S(2)}) collective-permute-start(bf16[32,3072]{1,0:T(8,128)(2,1)S(1)} %get-tuple-element.115), channel_id=1, source_target_pairs={{0,2},{1,3},{2,0},{3,1},{4,6},{5,7},{6,4},{7,5},{8,10},{9,11},{10,... | collective-permute-start | bytes 589832 | tf_op jit(solution)/shard_map/ppermute | solution.py:23
  70.6 5.7 %collective-permute-start.21 = (bf16[32,3072]{1,0:T(8,128)(2,1)S(1)}, bf16[32,3072]{1,0:T(8,128)(2,1)S(1)}, u32[]{:S(2)}, u32[]{:S(2)}) collective-permute-start(bf16[32,3072]{1,0:T(8,128)(2,1)S(1)} %get-tuple-element.117), channel_id=1, source_target_pairs={{0,4},{1,5},{2,6},{3,7},{4,0},{5,1},{6,2},{7,3},{8,12},{9,13},{10,... | collective-permute-start | bytes 589832 | tf_op jit(solution)/shard_map/ppermute | solution.py:23
  72.3 7.9 %collective-permute-start.26 = (bf16[3,256,3072]{2,1,0:T(8,128)(2,1)S(1)}, bf16[3,256,3072]{2,1,0:T(8,128)(2,1)S(1)}, u32[]{:S(2)}, u32[]{:S(2)}) collective-permute-start(bf16[3,256,3072]{2,1,0:T(8,128)(2,1)S(1)} %get-tuple-element.127), channel_id=1, source_target_pairs={{0,1},{1,0},{2,3},{3,2},{4,5},{5,4},{6,7},{7,6},{8,9},{9,8},{10,11... | collective-permute-start | bytes 14155784 | tf_op jit(solution)/shard_map/ppermute | solution.py:23
  72.6 11.7 %collective-permute-start.24 = (bf16[2,16,3072]{2,1,0:T(8,128)(2,1)S(1)}, bf16[2,16,3072]{2,1,0:T(8,128)(2,1)S(1)}, u32[]{:S(2)}, u32[]{:S(2)}) collective-permute-start(bf16[2,16,3072]{2,1,0:T(8,128)(2,1)S(1)} %get-tuple-element.125), channel_id=1, source_target_pairs={{0,8},{1,9},{2,10},{3,11},{4,12},{5,13},{6,14},{7,15},{8,0},{9,1},... | collective-permute-start | bytes 589832 | tf_op jit(solution)/shard_map/ppermute | solution.py:23
  73.2 11.9 %collective-permute-start.25 = (bf16[2,16,3072]{2,1,0:T(8,128)(2,1)S(1)}, bf16[2,16,3072]{2,1,0:T(8,128)(2,1)S(1)}, u32[]{:S(2)}, u32[]{:S(2)}) collective-permute-start(bf16[2,16,3072]{2,1,0:T(8,128)(2,1)S(1)} %get-tuple-element.126), channel_id=1, source_target_pairs={{0,24},{1,25},{2,26},{3,27},{4,28},{5,29},{6,30},{7,31},{8,16},{9,... | collective-permute-start | bytes 589832 | tf_op jit(solution)/shard_map/ppermute | solution.py:23
  76.3 17.3 %collective-permute-start.27 = (bf16[2,16,3072]{2,1,0:T(8,128)(2,1)S(1)}, bf16[2,16,3072]{2,1,0:T(8,128)(2,1)S(1)}, u32[]{:S(2)}, u32[]{:S(2)}) collective-permute-start(bf16[2,16,3072]{2,1,0:T(8,128)(2,1)S(1)} %get-tuple-element.131), channel_id=1, source_target_pairs={{0,16},{1,17},{2,18},{3,19},{4,20},{5,21},{6,22},{7,23},{8,24},{9,... | collective-permute-start | bytes 589832 | tf_op jit(solution)/shard_map/ppermute | solution.py:23

commit v4 on v3

--- a/solution.py
+++ b/solution.py
@@ -11,6 +11,12 @@
 CORE, LINK_X, LINK_Y, LINK_Z = 0, 1, 2, 3
 ROW_BITS = 4
 LONG = 10**11
+C_PACK = 0
+C_PAIR3 = 0
+C_SPLIT3 = LONG * 4 // 100
+C_SPLIT2 = LONG * 3 // 100
+C_PAIR2 = LONG // 100
+C_COPY = 0
 PANEL = 512
 TURN = pltpu.VMEM((8, 128), jnp.float32)
 VMEM = pl.BlockSpec(memory_space=pltpu.VMEM)
@@ -68,7 +74,7 @@
 
 
 def pick_kernel(
-    place, token, count, gate, tokens, grad, rows, x, e, weight, turn,
+    place, token, count, gate, tokens, grad, w_gate, w_up, w_down, rows, weight, panels, turn,
     token_here, count_here, gate_here, tokens_here, grad_here, arrived,
 ):
     pairs = (
@@ -79,7 +85,11 @@
         (grad, grad_here),
     )
     copies = [pltpu.make_async_copy(*pair, arrived.at[i]) for i, pair in enumerate(pairs)]
-    for copy in copies:
+    loads = [
+        pltpu.make_async_copy(w, panels.at[i], arrived.at[len(pairs) + i])
+        for i, w in enumerate((w_gate, w_up, w_down))
+    ]
+    for copy in copies + loads:
         copy.start()
     turn[...] = jnp.zeros_like(turn)
     for copy in copies:
@@ -95,71 +105,48 @@
     weight[...] = scale
     lane = lax.broadcasted_iota(jnp.int32, (capacity, tokens.shape[0]), 1)
     chosen = jnp.where(lane == index[:, :1], 1.0, 0.0).astype(jnp.bfloat16)
-    x[...] = half(product(chosen, tokens_here[...]))
-    e[...] = half(scale[:, :1] * grad_here[...].astype(jnp.float32))
-    rows[0] = x[...]
-    rows[1] = e[...]
-
-
-def pick(tokens, slot_token, slot_count, slot_gate, grad_out):
+    rows[0] = half(product(chosen, tokens_here[...]))
+    rows[1] = half(scale[:, :1] * grad_here[...].astype(jnp.float32))
+    for copy in loads:
+        copy.wait()
+
+
+def pick(tokens, slot_token, slot_count, slot_gate, grad_out, weights):
     capacity, width = grad_out.shape
     inputs = (slot_token, slot_count, slot_gate, tokens, grad_out)
     return pl.pallas_call(
         pick_kernel,
         out_shape=(
             held((2, capacity, width)),
-            held((capacity, width)),
-            held((capacity, width)),
             held((capacity, 128), jnp.float32),
+            held((3, *weights[0].shape)),
             TURN,
         ),
-        in_specs=[SMEM] + [HBM] * 5,
-        out_specs=(VMEM,) * 5,
+        in_specs=[SMEM] + [HBM] * 8,
+        out_specs=(VMEM,) * 4,
         scratch_shapes=[pltpu.SMEM(v.shape, v.dtype) for v in inputs[:3]]
         + [pltpu.VMEM(v.shape, v.dtype) for v in inputs[3:]]
-        + [pltpu.SemaphoreType.DMA((5,))],
+        + [pltpu.SemaphoreType.DMA((8,))],
         compiler_params=limit(4),
         cost_estimate=cost(0, 0),
         name="pick",
-    )(lax.axis_index("dp")[None], *(in_hbm(v) for v in inputs))
-
-
-def last_split_kernel(level, x_far, e_far, w_gate, w_up, w_down, _, x, e, panels, turn, arrived):
-    loads = [
-        pltpu.make_async_copy(w, panels.at[i], arrived.at[i])
-        for i, w in enumerate((w_gate, w_up, w_down))
-    ]
-    for copy in loads:
-        copy.start()
-    split_body(level, x, e)
-    turn[...] = jnp.zeros_like(turn)
-    for copy in loads:
-        copy.wait()
-
-
-def last_split(level, fars, weights, turn):
-    rows = held(level.shape[1:])
-    return pl.pallas_call(
-        last_split_kernel,
-        out_shape=(rows, rows, held((3, *weights[0].shape)), TURN),
-        in_specs=[VMEM] * 3 + [HBM] * 3 + [VMEM],
-        out_specs=(VMEM,) * 4,
-        scratch_shapes=[pltpu.SemaphoreType.DMA((3,))],
-        compiler_params=limit(4),
-        cost_estimate=cost(0, 0),
-        name="split_2",
-    )(*fetched(level, *fars), *(in_hbm(w) for w in weights), *fetched(turn))
-
-
-def expert_kernel(count, *refs):
-    parts, refs = refs[: 4 * count], refs[4 * count :]
+    )(lax.axis_index("dp")[None], *(in_hbm(v) for v in (*inputs, *weights)))
+
+
+def expert_kernel(sizes, *refs):
+    parts = []
+    for size in sizes:
+        part, refs = refs[:size], refs[size:]
+        if size == 1:
+            cut = part[0].shape[0] // 4
+            part = [part[0].at[i * cut : (i + 1) * cut] for i in range(4)]
+        parts.append(part)
     near, other, _, x, e, hidden, gate_grad, up_grad, out_keep, out_send, row_keep, row_send, turn = refs
     turn[...] = jnp.zeros_like(turn)
     units = near.shape[1]
     rows = x.shape[0] // 4
-    size = rows // count
-    for i in range(count):
-        x_pair, x_far, e_pair, e_far = parts[4 * i : 4 * i + 4]
+    size = rows // len(parts)
+    for i, (x_pair, x_far, e_pair, e_far) in enumerate(parts):
         for plane, (x_from, e_from, x_half, e_half) in enumerate(
             ((x_pair, e_pair, 0, 0), (x_pair, e_far, 1, 0), (x_far, e_pair, 0, 1), (x_far, e_far, 1, 1))
         ):
@@ -168,28 +155,28 @@
             e[into] = e_from[e_half * size : (e_half + 1) * size]
     for i, panels in enumerate((near, other)):
         mine = slice(i * units, (i + 1) * units)
-        gate_pre = row_product(x[...], panels[0])
-        up_pre = row_product(x[...], panels[1])
-        hidden_grad = row_product(e[...], panels[2])
+        gate_pre = row_product(panels[0], x[...])
+        up_pre = row_product(panels[1], x[...])
+        hidden_grad = row_product(panels[2], e[...])
         gate_sig = jax.nn.sigmoid(gate_pre)
         activated = gate_pre * gate_sig
-        hidden[:, mine] = half(activated * up_pre)
-        gate_grad[:, mine] = half(
+        hidden[mine] = half(activated * up_pre)
+        gate_grad[mine] = half(
             hidden_grad * up_pre * (gate_sig * (1.0 + gate_pre * (1.0 - gate_sig)))
         )
-        up_grad[:, mine] = half(hidden_grad * activated)
+        up_grad[mine] = half(hidden_grad * activated)
     for at in range(0, x.shape[1], PANEL):
         part = slice(at, at + PANEL)
-        out = product(hidden[:, :units], near[2, :, part]) + product(
-            hidden[:, units:], other[2, :, part]
+        out = col_product(hidden[:units], near[2, :, part]) + col_product(
+            hidden[units:], other[2, :, part]
         )
         out_keep[:, part] = out[: 2 * rows]
         out_send[:, part] = half(out[2 * rows :])
         row = (
-            product(gate_grad[:, :units], near[0, :, part])
-            + product(gate_grad[:, units:], other[0, :, part])
-            + product(up_grad[:, :units], near[1, :, part])
-            + product(up_grad[:, units:], other[1, :, part])
+            col_product(gate_grad[:units], near[0, :, part])
+            + col_product(gate_grad[units:], other[0, :, part])
+            + col_product(up_grad[:units], near[1, :, part])
+            + col_product(up_grad[units:], other[1, :, part])
         )
         row_keep[:rows, part] = row[:rows]
         row_keep[rows:, part] = row[2 * rows : 3 * rows]
@@ -198,17 +185,18 @@
 
 
 def expert(parts, near, other, turn):
-    rows, width = 2 * sum(part[0].shape[0] for part in parts), parts[0][0].shape[1]
+    rows = sum(ref.shape[0] for part in parts for ref in part) // 2
+    width = parts[0][0].shape[1]
     units = 2 * near.shape[1]
     saved, kept, sent = (
-        held((rows, units)),
+        held((units, rows)),
         held((rows // 2, width), jnp.float32),
         held((rows // 2, width)),
     )
     return pl.pallas_call(
-        functools.partial(expert_kernel, len(parts)),
+        functools.partial(expert_kernel, [len(part) for part in parts]),
         out_shape=(held((rows, width)),) * 2 + (saved,) * 3 + (kept, sent, kept, sent, TURN),
-        in_specs=[VMEM] * (4 * len(parts) + 3),
+        in_specs=[VMEM] * (sum(len(part) for part in parts) + 3),
         out_specs=(VMEM,) * 10,
         compiler_params=limit(12),
         cost_estimate=cost(12 * rows * units * width, 6 * units * width),
@@ -217,11 +205,9 @@
 
 
 def slot_sums(works, units, columns):
-    x, e, hidden, gate_grad, up_grad = (
-        [refs[i][:, units if i > 1 else columns] for refs in works] for i in range(5)
-    )
-    for left, right in ((gate_grad, x), (up_grad, x), (hidden, e)):
-        yield col_product(jnp.concatenate(left, 0), jnp.concatenate(right, 0))
+    x, e = (jnp.concatenate([refs[i][:, columns] for refs in works], 0) for i in (0, 1))
+    for i, right in ((3, x), (4, x), (2, e)):
+        yield product(jnp.concatenate([refs[i][units] for refs in works], 1), right)
 
 
 def other_kernel(*refs):
@@ -236,14 +222,14 @@
 
 def other_grads(works, turn):
     width = works[0][0].shape[1]
-    units = works[0][2].shape[1] // 2
+    units = works[0][2].shape[0] // 2
     return pl.pallas_call(
         other_kernel,
         out_shape=(held((3, units, width)), TURN),
         in_specs=[VMEM] * 11,
         out_specs=(VMEM, VMEM),
         compiler_params=limit(8),
-        cost_estimate=cost(LONG, 0),
+        cost_estimate=cost(LONG // 50, 0),
         name="other_grads",
     )(*fetched(*works[0], *works[1], turn))
 
@@ -304,6 +290,22 @@
         out[rows:] = side[...]
 
 
+def first_pair_body(x, x_side, e, e_side, _, x_pair, e_pair):
+    pair_body(x, x_side, e, e_side, x_pair, e_pair)
+
+
+def pack_body(x_pair, x_far, e_pair, e_far, plane):
+    rows = x_pair.shape[0]
+    for i, part in enumerate((x_pair, x_far, e_pair, e_far)):
+        plane[i * rows : (i + 1) * rows] = part[...]
+
+
+def copy_body(rows, again, x, e):
+    again[...] = rows[...]
+    x[...] = rows[0]
+    e[...] = rows[1]
+
+
 def plane_body(out_keep, out_far, row_keep, row_far, out_mid, out_side, row_mid, row_side):
     rows = out_mid.shape[0]
     for keep, far, mid, side in (
@@ -322,13 +324,16 @@
         second[i] = total[rows:].astype(second.dtype)
 
 
-def far_body(own, one, three, total):
-    total[...] = own[...] + one[...].astype(jnp.float32) + three[...].astype(jnp.float32)
-
-
-def final_body(total, two, weight, expert_out, grad_rows):
-    expert_out[...] = half(weight[:, :1] * (total[0] + two[0].astype(jnp.float32)))
-    grad_rows[...] = half(total[1] + two[1].astype(jnp.float32))
+def far_body(own, three, total):
+    total[...] = own[...] + three[...].astype(jnp.float32)
+
+
+def final_body(total, one, two, weight, expert_out, grad_rows):
+    out, row = (
+        total[i] + one[i].astype(jnp.float32) + two[i].astype(jnp.float32) for i in (0, 1)
+    )
+    expert_out[...] = half(weight[:, :1] * out)
+    grad_rows[...] = half(row)
 
 
 def shards(tokens, slot_token, slot_count, slot_gate, grad_out, w_gate, w_up, w_down):
@@ -341,7 +346,10 @@
     weights = [w_gate, w_up, w_down]
     for bit in far_bits:
         weights = [jnp.concatenate([w, swapped(w, 1 << bit)], 0) for w in weights]
-    own, x, e, weight, turn = pick(tokens, slot_token, slot_count, slot_gate, grad_out)
+    own, weight, near, turn = pick(
+        tokens, slot_token, slot_count, slot_gate, grad_out, weights
+    )
+    other = swapped(near, core)
 
     width = own.shape[2]
     rows = 2 * capacity
@@ -352,21 +360,27 @@
     def fars_of(x, e):
         return x, swapped(x, along_y), e, swapped(e, along_x)
 
-    one, three, two = (swapped(own, k << LINK_Z) for k in (1, 3, 2))
-    x, e, turn = staged(pair_body, "pair_0", [held((rows, width))] * 2, *sides_of(x, e), turn)
+    three = swapped(own, 3 << LINK_Z)
+    one_level, two_levels = [held((capacity, width))] * 2, [held((rows, width))] * 2
+    own, x, e, turn = staged(
+        copy_body, "copy", [held(own.shape), *one_level], own, turn, flops=C_COPY
+    )
+    two = swapped(own, 2 << LINK_Z)
+    x, e, turn = staged(first_pair_body, "pair_0", two_levels, *sides_of(x, e), other, turn)
     part_0 = fars_of(x, e)
-    x, e, turn = staged(split_body, "split_13", [held((rows, width))] * 2, one, three, turn)
-    sides_13 = sides_of(x, e)
-    x, e, near, turn = last_split(two, part_0[1::2], weights, turn)
+    x, e, turn = staged(split_body, "split_3", one_level, three, turn, flops=C_SPLIT3)
+    sides_3 = sides_of(x, e)
+    plane, turn = staged(pack_body, "pack", [held((4 * rows, width))], *part_0, turn, flops=C_PACK)
+    part_1 = (swapped(plane, 1 << LINK_Z),)
+    x, e, turn = staged(pair_body, "pair_3", two_levels, *sides_3, turn, flops=C_PAIR3)
+    part_3 = fars_of(x, e)
+    x, e, turn = staged(split_body, "split_2", one_level, two, turn, flops=C_SPLIT2)
     sides_2 = sides_of(x, e)
-    other = swapped(near, core)
-    x, e, turn = staged(pair_body, "pair_13", [held((2 * rows, width))] * 2, *sides_13, turn)
-    part_13 = fars_of(x, e)
-    x, e, turn = staged(pair_body, "pair_2", [held((rows, width))] * 2, *sides_2, turn, flops=LONG)
+    x, e, turn = staged(pair_body, "pair_2", two_levels, *sides_2, turn, flops=C_PAIR2)
     part_2 = fars_of(x, e)
 
     works, sides = [], []
-    for parts in ((part_13,), (part_0, part_2)):
+    for parts in ((part_0, part_3), (part_1, part_2)):
         *work, out_keep, out_send, row_keep, row_send, turn = expert(parts, near, other, turn)
         works.append(work)
         sides.append((out_keep, swapped(out_send, along_y), row_keep, swapped(row_send, along_x)))
@@ -386,14 +400,14 @@
             flops=flops,
         )
 
-    middle_13, turn = plane_sum(sides[0], turn)
+    middle_03, turn = plane_sum(sides[0], turn)
     sent, turn = other_grads(works, turn)
     received = swapped(sent, core)
-    middle_02, turn = plane_sum(sides[1], turn)
-    sum_1, sum_3, turn = line_sum(middle_13, turn, jnp.bfloat16)
-    one, three = swapped(sum_1, 1 << LINK_Z), swapped(sum_3, 3 << LINK_Z)
-    sum_0, sum_2, turn = line_sum(middle_02, turn, jnp.float32, flops=LONG)
-    two = swapped(sum_2, 2 << LINK_Z)
+    middle_12, turn = plane_sum(sides[1], turn)
+    sum_0, sum_3, turn = line_sum(middle_03, turn, jnp.float32)
+    three = swapped(sum_3, 3 << LINK_Z)
+    sum_1, sum_2, turn = line_sum(middle_12, turn, jnp.bfloat16, flops=LONG)
+    two, one = swapped(sum_2, 2 << LINK_Z), swapped(sum_1, 1 << LINK_Z)
     factor = 1.0 / math.sqrt(devices * capacity)
     if far_bits:
         *owned, turn = own_grads(works, received, turn, 1.0, jnp.float32)
@@ -404,10 +418,10 @@
     else:
         *owned, turn = own_grads(works, received, turn, factor, jnp.bfloat16)
     total, turn = staged(
-        far_body, "far_sum", [held(own.shape, jnp.float32)], sum_0, one, three, turn, flops=LONG // 10
+        far_body, "far_sum", [held(own.shape, jnp.float32)], sum_0, three, turn, flops=LONG // 10
     )
     expert_out, grad_rows, turn = staged(
-        final_body, "final", [shape((capacity, width))] * 2, total, two, weight, turn
+        final_body, "final", [shape((capacity, width))] * 2, total, one, two, weight, turn
     )
     return (expert_out, grad_rows, *owned)
 

time: 94.5 us -> 85.4 us (0.904)
  waiting for transfers between devices: 42.6 us -> 30.6 us
  starting transfers between devices: 31.1 us -> 36.3 us
  Pallas kernels: 19.8 us -> 17.7 us
    ppermute x28, waiting for transfers between devices: 42.6 us -> 30.6 us  [swapped(): lax.ppermute(block, 'dp', [(low, low ^ mask) for low in range(count)])]
    ppermute x28, starting transfers between devices: 31.1 us -> 36.3 us  [swapped(): lax.ppermute(block, 'dp', [(low, low ^ mask) for low in range(count)])]
    pallas_call x3 -> x2, Pallas kernels: 11.5 us -> 8.22 us  [expert(): pl.pallas_call(functools.partial(expert_kernel, [len(part) for part in pa...]
    pallas_call x1, Pallas kernels: 1.42 us -> 2.71 us  [pick(): pl.pallas_call(pick_kernel, out_shape=(held((2, capacity, width)), held((...]
  transfers between devices with their start and end apart: 28 -> 28, of which waited for: 14 -> 14; matrix products, arithmetic and copies ran while one was open for 0% -> 0% of each run, Pallas kernels for 19% -> 17%
where the time goes in v4:
time: 85.4 us; the launch traced here: 85.2 us
  starting transfers between devices  36.3 us (43%)
  waiting for transfers between devices  30.6 us (36%)
  Pallas kernels  17.7 us (21%)
    ppermute x28, starting transfers between devices, swapped(): lax.ppermute(block, 'dp', [(low, low ^ mask) for low in range(count)])  36.3 us
    ppermute x28, waiting for transfers between devices, swapped(): lax.ppermute(block, 'dp', [(low, low ^ mask) for low in range(count)])  30.6 us
    pallas_call x2, Pallas kernels, expert(): pl.pallas_call(functools.partial(expert_kernel, [len(part) for part in pa...  8.22 us
    pallas_call x1, Pallas kernels, own_grads(): pl.pallas_call(functools.partial(own_kernel, factor), grid=(width // PANE...  3.94 us
    pallas_call x1, Pallas kernels, pick(): pl.pallas_call(pick_kernel, out_shape=(held((2, capacity, width)), held((...  2.71 us
  transfers between devices with their start and end apart: 28, of which 14 were waited for; matrix products, arithmetic and copies ran while one was open for 0% of the time, Pallas kernels for 17%

profile of v4, /device:TPU:0, one launch (start us, length us, event | category | flops | bytes accessed | tf_op | source)
XLA Modules:
  0.0 85.2 jit_solution(2435684265271413410)
XLA Ops:
  0.6 2.7 %pick.1 = (bf16[2,16,3072]{2,1,0:T(8,128)(2,1)S(1)}, f32[16,128]{1,0:T(8,128)S(1)}, bf16[3,256,3072]{2,1,0:T(8,128)(2,1)S(1)}, f32[8,128]{1,0:T(8,128)S(1)}) custom-call(s32[1]{0:T(128)} %bitcast.place, s32[16]{0:T(128)} %token_.1, s32[32]{0:T(128)} %count.1, f32[16]{0:T(128)} %gate.1, bf16[128,3072]{1,0:T(8,128)(2,1)} %tokens.1, bf16[16,3072]{1,0:T(8,128)(2,1)} %grad.1, ...), custom_call_target="tpu_custom_call" | custom-call | tf_op jit(solution)/shard_map/pick/pallas_call | solution.py:117
  3.4 0.5 collective-permute-start.2
  3.9 4.7 %collective-permute-start.5 = (bf16[2,16,3072]{2,1,0:T(8,128)(2,1)S(1)}, bf16[2,16,3072]{2,1,0:T(8,128)(2,1)S(1)}, u32[]{:S(2)}, u32[]{:S(2)}) collective-permute-start(bf16[2,16,3072]{2,1,0:T(8,128)(2,1)S(1)} %get-tuple-element.76.refs_0_), channel_id=1, source_target_pairs={{0,24},{1,25},{2,26},{3,27},{4,28},{5,29},{6,30},{7,31},{8,16},{9,... | collective-permute-start | bytes 589832 | tf_op jit(solution)/shard_map/ppermute | solution.py:29
  8.6 1.6 %collective-permute-start = (bf16[16,3072]{1,0:T(8,128)(2,1)S(1)}, bf16[16,3072]{1,0:T(8,128)(2,1)S(1)}, u32[]{:S(2)}, u32[]{:S(2)}) collective-permute-start(bf16[16,3072]{1,0:T(8,128)(2,1)S(1)} %get-tuple-element.78.refs_0_), channel_id=1, source_target_pairs={{0,2},{1,3},{2,0},{3,1},{4,6},{5,7},{6,4},{7,5},{8,10},{9,11},{10,... | collective-permute-start | bytes 294920 | tf_op jit(solution)/shard_map/ppermute | solution.py:29
  10.1 1.5 %collective-permute-start.1 = (bf16[16,3072]{1,0:T(8,128)(2,1)S(1)}, bf16[16,3072]{1,0:T(8,128)(2,1)S(1)}, u32[]{:S(2)}, u32[]{:S(2)}) collective-permute-start(bf16[16,3072]{1,0:T(8,128)(2,1)S(1)} %get-tuple-element.79.refs_2_), channel_id=1, source_target_pairs={{0,4},{1,5},{2,6},{3,7},{4,0},{5,1},{6,2},{7,3},{8,12},{9,13},{10,... | collective-permute-start | bytes 294920 | tf_op jit(solution)/shard_map/ppermute | solution.py:29
  11.7 1.9 %collective-permute-done.refs_1_ = bf16[16,3072]{1,0:T(8,128)(2,1)S(1)} collective-permute-done((bf16[16,3072]{1,0:T(8,128)(2,1)S(1)}, bf16[16,3072]{1,0:T(8,128)(2,1)S(1)}, u32[]{:S(2)}, u32[]{:S(2)}) %collective-permute-start) | collective-permute-done | bytes 98336 | tf_op jit(solution)/shard_map/ppermute | solution.py:29
  13.5 1.2 %collective-permute-done.1.refs_3_ = bf16[16,3072]{1,0:T(8,128)(2,1)S(1)} collective-permute-done((bf16[16,3072]{1,0:T(8,128)(2,1)S(1)}, bf16[16,3072]{1,0:T(8,128)(2,1)S(1)}, u32[]{:S(2)}, u32[]{:S(2)}) %collective-permute-start.1) | collective-permute-done | bytes 98336 | tf_op jit(solution)/shard_map/ppermute | solution.py:29
  14.8 1.6 %collective-permute-start.3 = (bf16[32,3072]{1,0:T(8,128)(2,1)S(1)}, bf16[32,3072]{1,0:T(8,128)(2,1)S(1)}, u32[]{:S(2)}, u32[]{:S(2)}) collective-permute-start(bf16[32,3072]{1,0:T(8,128)(2,1)S(1)} %get-tuple-element.82.refs_0_), channel_id=1, source_target_pairs={{0,4},{1,5},{2,6},{3,7},{4,0},{5,1},{6,2},{7,3},{8,12},{9,13},{10,... | collective-permute-start | bytes 589832 | tf_op jit(solution)/shard_map/ppermute | solution.py:29
  16.4 0.5 collective-permute-start.4
  16.9 1.6 %collective-permute-start.6 = (bf16[16,3072]{1,0:T(8,128)(2,1)S(1)}, bf16[16,3072]{1,0:T(8,128)(2,1)S(1)}, u32[]{:S(2)}, u32[]{:S(2)}) collective-permute-start(bf16[16,3072]{1,0:T(8,128)(2,1)S(1)} %get-tuple-element.85.refs_0_), channel_id=1, source_target_pairs={{0,2},{1,3},{2,0},{3,1},{4,6},{5,7},{6,4},{7,5},{8,10},{9,11},{10,... | collective-permute-start | bytes 294920 | tf_op jit(solution)/shard_map/ppermute | solution.py:29
  18.5 0.5 collective-permute-start.7
  19.0 2.8 %collective-permute-done.3.refs_1_ = bf16[32,3072]{1,0:T(8,128)(2,1)S(1)} collective-permute-done((bf16[32,3072]{1,0:T(8,128)(2,1)S(1)}, bf16[32,3072]{1,0:T(8,128)(2,1)S(1)}, u32[]{:S(2)}, u32[]{:S(2)}) %collective-permute-start.3) | collective-permute-done | bytes 196640 | tf_op jit(solution)/shard_map/ppermute | solution.py:29
  21.7 1.2 %collective-permute-done.4.refs_3_ = bf16[32,3072]{1,0:T(8,128)(2,1)S(1)} collective-permute-done((bf16[32,3072]{1,0:T(8,128)(2,1)S(1)}, bf16[32,3072]{1,0:T(8,128)(2,1)S(1)}, u32[]{:S(2)}, u32[]{:S(2)}) %collective-permute-start.4) | collective-permute-done | bytes 196640 | tf_op jit(solution)/shard_map/ppermute | solution.py:29
  23.0 2.8 %collective-permute-start.15 = (bf16[128,3072]{1,0:T(8,128)(2,1)S(1)}, bf16[128,3072]{1,0:T(8,128)(2,1)S(1)}, u32[]{:S(2)}, u32[]{:S(2)}) collective-permute-start(bf16[128,3072]{1,0:T(8,128)(2,1)S(1)} %get-tuple-element.101), channel_id=1, source_target_pairs={{0,8},{1,9},{2,10},{3,11},{4,12},{5,13},{6,14},{7,15},{8,0},{9,1},... | collective-permute-start | bytes 2359304 | tf_op jit(solution)/shard_map/ppermute | solution.py:29
  25.9 0.6 collective-permute-start.8
  26.5 0.5 collective-permute-start.9
  27.0 1.6 %collective-permute-start.11 = (bf16[16,3072]{1,0:T(8,128)(2,1)S(1)}, bf16[16,3072]{1,0:T(8,128)(2,1)S(1)}, u32[]{:S(2)}, u32[]{:S(2)}) collective-permute-start(bf16[16,3072]{1,0:T(8,128)(2,1)S(1)} %get-tuple-element.93.refs_0_), channel_id=1, source_target_pairs={{0,2},{1,3},{2,0},{3,1},{4,6},{5,7},{6,4},{7,5},{8,10},{9,11},{10,... | collective-permute-start | bytes 294920 | tf_op jit(solution)/shard_map/ppermute | solution.py:29
  28.6 1.5 %collective-permute-start.12 = (bf16[16,3072]{1,0:T(8,128)(2,1)S(1)}, bf16[16,3072]{1,0:T(8,128)(2,1)S(1)}, u32[]{:S(2)}, u32[]{:S(2)}) collective-permute-start(bf16[16,3072]{1,0:T(8,128)(2,1)S(1)} %get-tuple-element.94.refs_2_), channel_id=1, source_target_pairs={{0,4},{1,5},{2,6},{3,7},{4,0},{5,1},{6,2},{7,3},{8,12},{9,13},{10,... | collective-permute-start | bytes 294920 | tf_op jit(solution)/shard_map/ppermute | solution.py:29
  30.1 3.4 %collective-permute-done.11.refs_1_ = bf16[16,3072]{1,0:T(8,128)(2,1)S(1)} collective-permute-done((bf16[16,3072]{1,0:T(8,128)(2,1)S(1)}, bf16[16,3072]{1,0:T(8,128)(2,1)S(1)}, u32[]{:S(2)}, u32[]{:S(2)}) %collective-permute-start.11) | collective-permute-done | bytes 98336 | tf_op jit(solution)/shard_map/ppermute | solution.py:29
  33.5 0.1 collective-permute-done.12.refs_3_
  33.6 1.5 %collective-permute-start.16 = (bf16[32,3072]{1,0:T(8,128)(2,1)S(1)}, bf16[32,3072]{1,0:T(8,128)(2,1)S(1)}, u32[]{:S(2)}, u32[]{:S(2)}) collective-permute-start(bf16[32,3072]{1,0:T(8,128)(2,1)S(1)} %get-tuple-element.102.refs_1_), channel_id=1, source_target_pairs={{0,4},{1,5},{2,6},{3,7},{4,0},{5,1},{6,2},{7,3},{8,12},{9,13},{10,... | collective-permute-start | bytes 589832 | tf_op jit(solution)/shard_map/ppermute | solution.py:29
  35.1 0.5 collective-permute-start.17
  35.7 4.1 %expert.2 = (bf16[128,3072]{1,0:T(8,128)(2,1)S(1)}, bf16[128,3072]{1,0:T(8,128)(2,1)S(1)}, bf16[512,128]{1,0:T(8,128)(2,1)S(1)}, bf16[512,128]{1,0:T(8,128)(2,1)...) custom-call(bf16[32,3072]{1,0:T(8,128)(2,1)S(1)} %get-tuple-element., ...), custom_call_target="tpu_custom_call" | custom-call | flops 2415919104 | bytes 9437184 | tf_op jit(solution)/shard_map/expert/pallas_call | solution.py:196
  39.8 0.7 collective-permute-start.13
  40.5 1.5 %collective-permute-start.14 = (bf16[64,3072]{1,0:T(8,128)(2,1)S(1)}, bf16[64,3072]{1,0:T(8,128)(2,1)S(1)}, u32[]{:S(2)}, u32[]{:S(2)}) collective-permute-start(bf16[64,3072]{1,0:T(8,128)(2,1)S(1)} %get-tuple-element.100), channel_id=1, source_target_pairs={{0,2},{1,3},{2,0},{3,1},{4,6},{5,7},{6,4},{7,5},{8,10},{9,11},{10,... | collective-permute-start | bytes 1179656 | tf_op jit(solution)/shard_map/ppermute | solution.py:29
  42.0 0.7 collective-permute-done.15.refs_0_
  42.7 4.1 %expert.3 = (bf16[128,3072]{1,0:T(8,128)(2,1)S(1)}, bf16[128,3072]{1,0:T(8,128)(2,1)S(1)}, bf16[512,128]{1,0:T(8,128)(2,1)S(1)}, bf16[512,128]{1,0:T(8,128)(2,1)...) custom-call(bf16[128,3072]{1,0:T(8,128)(2,1)S(1)} %collective-permut, ...), custom_call_target="tpu_custom_call" | custom-call | flops 2415919104 | bytes 9437184 | tf_op jit(solution)/shard_map/expert/pallas_call | solution.py:196
  46.8 1.6 %collective-permute-start.20 = (bf16[64,3072]{1,0:T(8,128)(2,1)S(1)}, bf16[64,3072]{1,0:T(8,128)(2,1)S(1)}, u32[]{:S(2)}, u32[]{:S(2)}) collective-permute-start(bf16[64,3072]{1,0:T(8,128)(2,1)S(1)} %get-tuple-element.111), channel_id=1, source_target_pairs={{0,4},{1,5},{2,6},{3,7},{4,0},{5,1},{6,2},{7,3},{8,12},{9,13},{10,... | collective-permute-start | bytes 1179656 | tf_op jit(solution)/shard_map/ppermute | solution.py:29
  48.4 1.5 %collective-permute-start.21 = (bf16[64,3072]{1,0:T(8,128)(2,1)S(1)}, bf16[64,3072]{1,0:T(8,128)(2,1)S(1)}, u32[]{:S(2)}, u32[]{:S(2)}) collective-permute-start(bf16[64,3072]{1,0:T(8,128)(2,1)S(1)} %get-tuple-element.113), channel_id=1, source_target_pairs={{0,2},{1,3},{2,0},{3,1},{4,6},{5,7},{6,4},{7,5},{8,10},{9,11},{10,... | collective-permute-start | bytes 1179656 | tf_op jit(solution)/shard_map/ppermute | solution.py:29
  49.9 0.2 plane_sum.2
  50.1 0.6 collective-permute-start.18
  50.7 1.3 %collective-permute-start.19 = (bf16[32,3072]{1,0:T(8,128)(2,1)S(1)}, bf16[32,3072]{1,0:T(8,128)(2,1)S(1)}, u32[]{:S(2)}, u32[]{:S(2)}) collective-permute-start(bf16[32,3072]{1,0:T(8,128)(2,1)S(1)} %get-tuple-element.109), channel_id=1, source_target_pairs={{0,4},{1,5},{2,6},{3,7},{4,0},{5,1},{6,2},{7,3},{8,12},{9,13},{10,... | collective-permute-start | bytes 589832 | tf_op jit(solution)/shard_map/ppermute | solution.py:29
  51.9 1.4 %other_grads.1 = (bf16[3,256,3072]{2,1,0:T(8,128)(2,1)S(1)}, f32[8,128]{1,0:T(8,128)S(1)}) custom-call(bf16[128,3072]{1,0:T(8,128)(2,1)S(1)} %get-tuple-element.114.refs_0_, bf16[128,3072]{1,0:T(8,128)(2,1)S(1)} %get-tuple-element.115.refs_1_, bf16[512,128]{1,0:T(8,128)(2,1)S(1)} %get-tuple-element.116.refs_2_, ...), custom_call_target="tpu_custom_call" | custom-call | flops 2000000000 | tf_op jit(solution)/shard_map/other_grads/pallas_call | solution.py:226
  53.3 5.6 %collective-permute-done.20.refs_1_ = bf16[64,3072]{1,0:T(8,128)(2,1)S(1)} collective-permute-done((bf16[64,3072]{1,0:T(8,128)(2,1)S(1)}, bf16[64,3072]{1,0:T(8,128)(2,1)S(1)}, u32[]{:S(2)}, u32[]{:S(2)}) %collective-permute-start.20) | collective-permute-done | bytes 393248 | tf_op jit(solution)/shard_map/ppermute | solution.py:29
  58.9 1.5 %collective-permute-done.21.refs_3_ = bf16[64,3072]{1,0:T(8,128)(2,1)S(1)} collective-permute-done((bf16[64,3072]{1,0:T(8,128)(2,1)S(1)}, bf16[64,3072]{1,0:T(8,128)(2,1)S(1)}, u32[]{:S(2)}, u32[]{:S(2)}) %collective-permute-start.21) | collective-permute-done | bytes 393248 | tf_op jit(solution)/shard_map/ppermute | solution.py:29
  60.5 0.1 plane_sum.3
  60.6 1.5 %collective-permute-start.24 = (bf16[32,3072]{1,0:T(8,128)(2,1)S(1)}, bf16[32,3072]{1,0:T(8,128)(2,1)S(1)}, u32[]{:S(2)}, u32[]{:S(2)}) collective-permute-start(bf16[32,3072]{1,0:T(8,128)(2,1)S(1)} %get-tuple-element.131), channel_id=1, source_target_pairs={{0,2},{1,3},{2,0},{3,1},{4,6},{5,7},{6,4},{7,5},{8,10},{9,11},{10,... | collective-permute-start | bytes 589832 | tf_op jit(solution)/shard_map/ppermute | solution.py:29
  62.1 0.5 collective-permute-start.25
  62.6 2.0 %collective-permute-done.18.refs_1_ = bf16[32,3072]{1,0:T(8,128)(2,1)S(1)} collective-permute-done((bf16[32,3072]{1,0:T(8,128)(2,1)S(1)}, bf16[32,3072]{1,0:T(8,128)(2,1)S(1)}, u32[]{:S(2)}, u32[]{:S(2)}) %collective-permute-start.18) | collective-permute-done | bytes 196640 | tf_op jit(solution)/shard_map/ppermute | solution.py:29
  64.7 2.5 %collective-permute-start.22 = (bf16[2,16,3072]{2,1,0:T(8,128)(2,1)S(1)}, bf16[2,16,3072]{2,1,0:T(8,128)(2,1)S(1)}, u32[]{:S(2)}, u32[]{:S(2)}) collective-permute-start(bf16[2,16,3072]{2,1,0:T(8,128)(2,1)S(1)} %get-tuple-element.128), channel_id=1, source_target_pairs={{0,24},{1,25},{2,26},{3,27},{4,28},{5,29},{6,30},{7,31},{8,16},{9,... | collective-permute-start | bytes 589832 | tf_op jit(solution)/shard_map/ppermute | solution.py:29
  67.3 0.4 collective-permute-done.25.refs_3_
  67.8 0.1 line_sum.3
  67.9 1.6 %collective-permute-start.26 = (bf16[2,16,3072]{2,1,0:T(8,128)(2,1)S(1)}, bf16[2,16,3072]{2,1,0:T(8,128)(2,1)S(1)}, u32[]{:S(2)}, u32[]{:S(2)}) collective-permute-start(bf16[2,16,3072]{2,1,0:T(8,128)(2,1)S(1)} %get-tuple-element.138), channel_id=1, source_target_pairs={{0,8},{1,9},{2,10},{3,11},{4,12},{5,13},{6,14},{7,15},{8,0},{9,1},... | collective-permute-start | bytes 589832 | tf_op jit(solution)/shard_map/ppermute | solution.py:29
  69.5 1.5 %collective-permute-start.27 = (bf16[2,16,3072]{2,1,0:T(8,128)(2,1)S(1)}, bf16[2,16,3072]{2,1,0:T(8,128)(2,1)S(1)}, u32[]{:S(2)}, u32[]{:S(2)}) collective-permute-start(bf16[2,16,3072]{2,1,0:T(8,128)(2,1)S(1)} %get-tuple-element.139), channel_id=1, source_target_pairs={{0,16},{1,17},{2,18},{3,19},{4,20},{5,21},{6,22},{7,23},{8,24},{9,... | collective-permute-start | bytes 589832 | tf_op jit(solution)/shard_map/ppermute | solution.py:29
  71.0 3.9 %own_grads.1 = (bf16[256,3072]{1,0:T(8,128)(2,1)}, bf16[256,3072]{1,0:T(8,128)(2,1)}, bf16[256,3072]{1,0:T(8,128)(2,1)}, f32[8,128]{1,0:T(8,128)S(1)}) custom-call(bf16[128,3072]{1,0:T(8,128)(2,1)S(1)} %get-tuple-element.114.refs_0_, bf16[128,3072]{1,0:T(8,128)(2,1)S(1)} %get-tuple-element.115.refs_1_, bf16[512,128]{1,0:T(8,128)(2,1)S(1)} %get-tuple-element.116.refs_2_, ...), custom_call_target="tpu_custom_call" | custom-call | tf_op jit(solution)/shard_map/own_grads/pallas_call | solution.py:250
  75.0 1.5 %collective-permute-done.26.refs_1_ = bf16[2,16,3072]{2,1,0:T(8,128)(2,1)S(1)} collective-permute-done((bf16[2,16,3072]{2,1,0:T(8,128)(2,1)S(1)}, bf16[2,16,3072]{2,1,0:T(8,128)(2,1)S(1)}, u32[]{:S(2)}, u32[]{:S(2)}) %collective-permute-start.26) | collective-permute-done | bytes 196640 | tf_op jit(solution)/shard_map/ppermute | solution.py:29
  76.5 8.1 %collective-permute-done.27.refs_2_ = bf16[2,16,3072]{2,1,0:T(8,128)(2,1)S(1)} collective-permute-done((bf16[2,16,3072]{2,1,0:T(8,128)(2,1)S(1)}, bf16[2,16,3072]{2,1,0:T(8,128)(2,1)S(1)}, u32[]{:S(2)}, u32[]{:S(2)}) %collective-permute-start.27) | collective-permute-done | bytes 196640 | tf_op jit(solution)/shard_map/ppermute | solution.py:29
  84.5 0.7 final.1
  (26 shorter events, 0.4 us)
Async XLA Ops:
  3.4 11.4 %collective-permute-start.2 = (bf16[3,256,3072]{2,1,0:T(8,128)(2,1)S(1)}, bf16[3,256,3072]{2,1,0:T(8,128)(2,1)S(1)}, u32[]{:S(2)}, u32[]{:S(2)}) collective-permute-start(bf16[3,256,3072]{2,1,0:T(8,128)(2,1)S(1)} %get-tuple-element.80.refs_8_.refs_5_), channel_id=1, source_target_pairs={{0,1},{1,0},{2,3},{3,2},{4,5},{5,4},{6,7},{7,6},{8,9},{9,8},{10,11... | collective-permute-start | bytes 14155784 | tf_op jit(solution)/shard_map/ppermute | solution.py:29
  3.9 13.0 %collective-permute-start.5 = (bf16[2,16,3072]{2,1,0:T(8,128)(2,1)S(1)}, bf16[2,16,3072]{2,1,0:T(8,128)(2,1)S(1)}, u32[]{:S(2)}, u32[]{:S(2)}) collective-permute-start(bf16[2,16,3072]{2,1,0:T(8,128)(2,1)S(1)} %get-tuple-element.76.refs_0_), channel_id=1, source_target_pairs={{0,24},{1,25},{2,26},{3,27},{4,28},{5,29},{6,30},{7,31},{8,16},{9,... | collective-permute-start | bytes 589832 | tf_op jit(solution)/shard_map/ppermute | solution.py:29
  8.6 4.9 %collective-permute-start = (bf16[16,3072]{1,0:T(8,128)(2,1)S(1)}, bf16[16,3072]{1,0:T(8,128)(2,1)S(1)}, u32[]{:S(2)}, u32[]{:S(2)}) collective-permute-start(bf16[16,3072]{1,0:T(8,128)(2,1)S(1)} %get-tuple-element.78.refs_0_), channel_id=1, source_target_pairs={{0,2},{1,3},{2,0},{3,1},{4,6},{5,7},{6,4},{7,5},{8,10},{9,11},{10,... | collective-permute-start | bytes 294920 | tf_op jit(solution)/shard_map/ppermute | solution.py:29
  10.1 4.6 %collective-permute-start.1 = (bf16[16,3072]{1,0:T(8,128)(2,1)S(1)}, bf16[16,3072]{1,0:T(8,128)(2,1)S(1)}, u32[]{:S(2)}, u32[]{:S(2)}) collective-permute-start(bf16[16,3072]{1,0:T(8,128)(2,1)S(1)} %get-tuple-element.79.refs_2_), channel_id=1, source_target_pairs={{0,4},{1,5},{2,6},{3,7},{4,0},{5,1},{6,2},{7,3},{8,12},{9,13},{10,... | collective-permute-start | bytes 294920 | tf_op jit(solution)/shard_map/ppermute | solution.py:29
  11.7 15.4 %collective-permute-start.10 = (bf16[2,16,3072]{2,1,0:T(8,128)(2,1)S(1)}, bf16[2,16,3072]{2,1,0:T(8,128)(2,1)S(1)}, u32[]{:S(2)}, u32[]{:S(2)}) collective-permute-start(bf16[2,16,3072]{2,1,0:T(8,128)(2,1)S(1)} %get-tuple-element.91), channel_id=1, source_target_pairs={{0,16},{1,17},{2,18},{3,19},{4,20},{5,21},{6,22},{7,23},{8,24},{9,... | collective-permute-start | bytes 589832 | tf_op jit(solution)/shard_map/ppermute | solution.py:29
  14.8 7.0 %collective-permute-start.3 = (bf16[32,3072]{1,0:T(8,128)(2,1)S(1)}, bf16[32,3072]{1,0:T(8,128)(2,1)S(1)}, u32[]{:S(2)}, u32[]{:S(2)}) collective-permute-start(bf16[32,3072]{1,0:T(8,128)(2,1)S(1)} %get-tuple-element.82.refs_0_), channel_id=1, source_target_pairs={{0,4},{1,5},{2,6},{3,7},{4,0},{5,1},{6,2},{7,3},{8,12},{9,13},{10,... | collective-permute-start | bytes 589832 | tf_op jit(solution)/shard_map/ppermute | solution.py:29
  16.4 6.6 %collective-permute-start.4 = (bf16[32,3072]{1,0:T(8,128)(2,1)S(1)}, bf16[32,3072]{1,0:T(8,128)(2,1)S(1)}, u32[]{:S(2)}, u32[]{:S(2)}) collective-permute-start(bf16[32,3072]{1,0:T(8,128)(2,1)S(1)} %get-tuple-element.83.refs_2_), channel_id=1, source_target_pairs={{0,2},{1,3},{2,0},{3,1},{4,6},{5,7},{6,4},{7,5},{8,10},{9,11},{10,... | collective-permute-start | bytes 589832 | tf_op jit(solution)/shard_map/ppermute | solution.py:29
  16.9 8.9 %collective-permute-start.6 = (bf16[16,3072]{1,0:T(8,128)(2,1)S(1)}, bf16[16,3072]{1,0:T(8,128)(2,1)S(1)}, u32[]{:S(2)}, u32[]{:S(2)}) collective-permute-start(bf16[16,3072]{1,0:T(8,128)(2,1)S(1)} %get-tuple-element.85.refs_0_), channel_id=1, source_target_pairs={{0,2},{1,3},{2,0},{3,1},{4,6},{5,7},{6,4},{7,5},{8,10},{9,11},{10,... | collective-permute-start | bytes 294920 | tf_op jit(solution)/shard_map/ppermute | solution.py:29
  18.5 7.4 %collective-permute-start.7 = (bf16[16,3072]{1,0:T(8,128)(2,1)S(1)}, bf16[16,3072]{1,0:T(8,128)(2,1)S(1)}, u32[]{:S(2)}, u32[]{:S(2)}) collective-permute-start(bf16[16,3072]{1,0:T(8,128)(2,1)S(1)} %get-tuple-element.86.refs_2_), channel_id=1, source_target_pairs={{0,4},{1,5},{2,6},{3,7},{4,0},{5,1},{6,2},{7,3},{8,12},{9,13},{10,... | collective-permute-start | bytes 294920 | tf_op jit(solution)/shard_map/ppermute | solution.py:29
  23.0 19.7 %collective-permute-start.15 = (bf16[128,3072]{1,0:T(8,128)(2,1)S(1)}, bf16[128,3072]{1,0:T(8,128)(2,1)S(1)}, u32[]{:S(2)}, u32[]{:S(2)}) collective-permute-start(bf16[128,3072]{1,0:T(8,128)(2,1)S(1)} %get-tuple-element.101), channel_id=1, source_target_pairs={{0,8},{1,9},{2,10},{3,11},{4,12},{5,13},{6,14},{7,15},{8,0},{9,1},... | collective-permute-start | bytes 2359304 | tf_op jit(solution)/shard_map/ppermute | solution.py:29
  25.9 9.7 %collective-permute-start.8 = (bf16[32,3072]{1,0:T(8,128)(2,1)S(1)}, bf16[32,3072]{1,0:T(8,128)(2,1)S(1)}, u32[]{:S(2)}, u32[]{:S(2)}) collective-permute-start(bf16[32,3072]{1,0:T(8,128)(2,1)S(1)} %get-tuple-element.89.refs_4_), channel_id=1, source_target_pairs={{0,4},{1,5},{2,6},{3,7},{4,0},{5,1},{6,2},{7,3},{8,12},{9,13},{10,... | collective-permute-start | bytes 589832 | tf_op jit(solution)/shard_map/ppermute | solution.py:29
  26.5 9.2 %collective-permute-start.9 = (bf16[32,3072]{1,0:T(8,128)(2,1)S(1)}, bf16[32,3072]{1,0:T(8,128)(2,1)S(1)}, u32[]{:S(2)}, u32[]{:S(2)}) collective-permute-start(bf16[32,3072]{1,0:T(8,128)(2,1)S(1)} %get-tuple-element.90.refs_6_), channel_id=1, source_target_pairs={{0,2},{1,3},{2,0},{3,1},{4,6},{5,7},{6,4},{7,5},{8,10},{9,11},{10,... | collective-permute-start | bytes 589832 | tf_op jit(solution)/shard_map/ppermute | solution.py:29
  27.0 6.4 %collective-permute-start.11 = (bf16[16,3072]{1,0:T(8,128)(2,1)S(1)}, bf16[16,3072]{1,0:T(8,128)(2,1)S(1)}, u32[]{:S(2)}, u32[]{:S(2)}) collective-permute-start(bf16[16,3072]{1,0:T(8,128)(2,1)S(1)} %get-tuple-element.93.refs_0_), channel_id=1, source_target_pairs={{0,2},{1,3},{2,0},{3,1},{4,6},{5,7},{6,4},{7,5},{8,10},{9,11},{10,... | collective-permute-start | bytes 294920 | tf_op jit(solution)/shard_map/ppermute | solution.py:29
  28.6 5.0 %collective-permute-start.12 = (bf16[16,3072]{1,0:T(8,128)(2,1)S(1)}, bf16[16,3072]{1,0:T(8,128)(2,1)S(1)}, u32[]{:S(2)}, u32[]{:S(2)}) collective-permute-start(bf16[16,3072]{1,0:T(8,128)(2,1)S(1)} %get-tuple-element.94.refs_2_), channel_id=1, source_target_pairs={{0,4},{1,5},{2,6},{3,7},{4,0},{5,1},{6,2},{7,3},{8,12},{9,13},{10,... | collective-permute-start | bytes 294920 | tf_op jit(solution)/shard_map/ppermute | solution.py:29
  33.6 8.3 %collective-permute-start.16 = (bf16[32,3072]{1,0:T(8,128)(2,1)S(1)}, bf16[32,3072]{1,0:T(8,128)(2,1)S(1)}, u32[]{:S(2)}, u32[]{:S(2)}) collective-permute-start(bf16[32,3072]{1,0:T(8,128)(2,1)S(1)} %get-tuple-element.102.refs_1_), channel_id=1, source_target_pairs={{0,4},{1,5},{2,6},{3,7},{4,0},{5,1},{6,2},{7,3},{8,12},{9,13},{10,... | collective-permute-start | bytes 589832 | tf_op jit(solution)/shard_map/ppermute | solution.py:29
  35.1 6.8 %collective-permute-start.17 = (bf16[32,3072]{1,0:T(8,128)(2,1)S(1)}, bf16[32,3072]{1,0:T(8,128)(2,1)S(1)}, u32[]{:S(2)}, u32[]{:S(2)}) collective-permute-start(bf16[32,3072]{1,0:T(8,128)(2,1)S(1)} %get-tuple-element.103.refs_3_), channel_id=1, source_target_pairs={{0,2},{1,3},{2,0},{3,1},{4,6},{5,7},{6,4},{7,5},{8,10},{9,11},{10,... | collective-permute-start | bytes 589832 | tf_op jit(solution)/shard_map/ppermute | solution.py:29
  39.8 10.1 %collective-permute-start.13 = (bf16[64,3072]{1,0:T(8,128)(2,1)S(1)}, bf16[64,3072]{1,0:T(8,128)(2,1)S(1)}, u32[]{:S(2)}, u32[]{:S(2)}) collective-permute-start(bf16[64,3072]{1,0:T(8,128)(2,1)S(1)} %get-tuple-element.98), channel_id=1, source_target_pairs={{0,4},{1,5},{2,6},{3,7},{4,0},{5,1},{6,2},{7,3},{8,12},{9,13},{10,... | collective-permute-start | bytes 1179656 | tf_op jit(solution)/shard_map/ppermute | solution.py:29
  40.5 9.4 %collective-permute-start.14 = (bf16[64,3072]{1,0:T(8,128)(2,1)S(1)}, bf16[64,3072]{1,0:T(8,128)(2,1)S(1)}, u32[]{:S(2)}, u32[]{:S(2)}) collective-permute-start(bf16[64,3072]{1,0:T(8,128)(2,1)S(1)} %get-tuple-element.100), channel_id=1, source_target_pairs={{0,2},{1,3},{2,0},{3,1},{4,6},{5,7},{6,4},{7,5},{8,10},{9,11},{10,... | collective-permute-start | bytes 1179656 | tf_op jit(solution)/shard_map/ppermute | solution.py:29
  46.8 12.1 %collective-permute-start.20 = (bf16[64,3072]{1,0:T(8,128)(2,1)S(1)}, bf16[64,3072]{1,0:T(8,128)(2,1)S(1)}, u32[]{:S(2)}, u32[]{:S(2)}) collective-permute-start(bf16[64,3072]{1,0:T(8,128)(2,1)S(1)} %get-tuple-element.111), channel_id=1, source_target_pairs={{0,4},{1,5},{2,6},{3,7},{4,0},{5,1},{6,2},{7,3},{8,12},{9,13},{10,... | collective-permute-start | bytes 1179656 | tf_op jit(solution)/shard_map/ppermute | solution.py:29
  48.4 12.1 %collective-permute-start.21 = (bf16[64,3072]{1,0:T(8,128)(2,1)S(1)}, bf16[64,3072]{1,0:T(8,128)(2,1)S(1)}, u32[]{:S(2)}, u32[]{:S(2)}) collective-permute-start(bf16[64,3072]{1,0:T(8,128)(2,1)S(1)} %get-tuple-element.113), channel_id=1, source_target_pairs={{0,2},{1,3},{2,0},{3,1},{4,6},{5,7},{6,4},{7,5},{8,10},{9,11},{10,... | collective-permute-start | bytes 1179656 | tf_op jit(solution)/shard_map/ppermute | solution.py:29
  50.1 14.6 %collective-permute-start.18 = (bf16[32,3072]{1,0:T(8,128)(2,1)S(1)}, bf16[32,3072]{1,0:T(8,128)(2,1)S(1)}, u32[]{:S(2)}, u32[]{:S(2)}) collective-permute-start(bf16[32,3072]{1,0:T(8,128)(2,1)S(1)} %get-tuple-element.107), channel_id=1, source_target_pairs={{0,2},{1,3},{2,0},{3,1},{4,6},{5,7},{6,4},{7,5},{8,10},{9,11},{10,... | collective-permute-start | bytes 589832 | tf_op jit(solution)/shard_map/ppermute | solution.py:29
  50.7 14.0 %collective-permute-start.19 = (bf16[32,3072]{1,0:T(8,128)(2,1)S(1)}, bf16[32,3072]{1,0:T(8,128)(2,1)S(1)}, u32[]{:S(2)}, u32[]{:S(2)}) collective-permute-start(bf16[32,3072]{1,0:T(8,128)(2,1)S(1)} %get-tuple-element.109), channel_id=1, source_target_pairs={{0,4},{1,5},{2,6},{3,7},{4,0},{5,1},{6,2},{7,3},{8,12},{9,13},{10,... | collective-permute-start | bytes 589832 | tf_op jit(solution)/shard_map/ppermute | solution.py:29
  60.6 6.8 %collective-permute-start.24 = (bf16[32,3072]{1,0:T(8,128)(2,1)S(1)}, bf16[32,3072]{1,0:T(8,128)(2,1)S(1)}, u32[]{:S(2)}, u32[]{:S(2)}) collective-permute-start(bf16[32,3072]{1,0:T(8,128)(2,1)S(1)} %get-tuple-element.131), channel_id=1, source_target_pairs={{0,2},{1,3},{2,0},{3,1},{4,6},{5,7},{6,4},{7,5},{8,10},{9,11},{10,... | collective-permute-start | bytes 589832 | tf_op jit(solution)/shard_map/ppermute | solution.py:29
  62.1 5.7 %collective-permute-start.25 = (bf16[32,3072]{1,0:T(8,128)(2,1)S(1)}, bf16[32,3072]{1,0:T(8,128)(2,1)S(1)}, u32[]{:S(2)}, u32[]{:S(2)}) collective-permute-start(bf16[32,3072]{1,0:T(8,128)(2,1)S(1)} %get-tuple-element.133), channel_id=1, source_target_pairs={{0,4},{1,5},{2,6},{3,7},{4,0},{5,1},{6,2},{7,3},{8,12},{9,13},{10,... | collective-permute-start | bytes 589832 | tf_op jit(solution)/shard_map/ppermute | solution.py:29
  62.6 8.3 %collective-permute-start.23 = (bf16[3,256,3072]{2,1,0:T(8,128)(2,1)S(1)}, bf16[3,256,3072]{2,1,0:T(8,128)(2,1)S(1)}, u32[]{:S(2)}, u32[]{:S(2)}) collective-permute-start(bf16[3,256,3072]{2,1,0:T(8,128)(2,1)S(1)} %get-tuple-element.129), channel_id=1, source_target_pairs={{0,1},{1,0},{2,3},{3,2},{4,5},{5,4},{6,7},{7,6},{8,9},{9,8},{10,11... | collective-permute-start | bytes 14155784 | tf_op jit(solution)/shard_map/ppermute | solution.py:29
  64.7 10.2 %collective-permute-start.22 = (bf16[2,16,3072]{2,1,0:T(8,128)(2,1)S(1)}, bf16[2,16,3072]{2,1,0:T(8,128)(2,1)S(1)}, u32[]{:S(2)}, u32[]{:S(2)}) collective-permute-start(bf16[2,16,3072]{2,1,0:T(8,128)(2,1)S(1)} %get-tuple-element.128), channel_id=1, source_target_pairs={{0,24},{1,25},{2,26},{3,27},{4,28},{5,29},{6,30},{7,31},{8,16},{9,... | collective-permute-start | bytes 589832 | tf_op jit(solution)/shard_map/ppermute | solution.py:29
  67.9 8.6 %collective-permute-start.26 = (bf16[2,16,3072]{2,1,0:T(8,128)(2,1)S(1)}, bf16[2,16,3072]{2,1,0:T(8,128)(2,1)S(1)}, u32[]{:S(2)}, u32[]{:S(2)}) collective-permute-start(bf16[2,16,3072]{2,1,0:T(8,128)(2,1)S(1)} %get-tuple-element.138), channel_id=1, source_target_pairs={{0,8},{1,9},{2,10},{3,11},{4,12},{5,13},{6,14},{7,15},{8,0},{9,1},... | collective-permute-start | bytes 589832 | tf_op jit(solution)/shard_map/ppermute | solution.py:29
  69.5 15.1 %collective-permute-start.27 = (bf16[2,16,3072]{2,1,0:T(8,128)(2,1)S(1)}, bf16[2,16,3072]{2,1,0:T(8,128)(2,1)S(1)}, u32[]{:S(2)}, u32[]{:S(2)}) collective-permute-start(bf16[2,16,3072]{2,1,0:T(8,128)(2,1)S(1)} %get-tuple-element.139), channel_id=1, source_target_pairs={{0,16},{1,17},{2,18},{3,19},{4,20},{5,21},{6,22},{7,23},{8,24},{9,... | collective-permute-start | bytes 589832 | tf_op jit(solution)/shard_map/ppermute | solution.py:29

commit v5 on v4

--- a/solution.py
+++ b/solution.py
@@ -12,11 +12,12 @@
 ROW_BITS = 4
 LONG = 10**11
 C_PACK = 0
-C_PAIR3 = 0
-C_SPLIT3 = LONG * 4 // 100
-C_SPLIT2 = LONG * 3 // 100
-C_PAIR2 = LONG // 100
+C_PAIR_FIRST = 0
+C_FIRST = LONG * 4 // 100
+C_LAST = LONG * 3 // 100
+C_PAIR_LAST = LONG // 100
 C_COPY = 0
+C_TURN = 0
 PANEL = 512
 TURN = pltpu.VMEM((8, 128), jnp.float32)
 VMEM = pl.BlockSpec(memory_space=pltpu.VMEM)
@@ -27,6 +28,14 @@
 def swapped(block, mask):
     count = lax.axis_size("dp")
     return lax.ppermute(block, "dp", [(low, low ^ mask) for low in range(count)])
+
+
+def shifted(block, steps):
+    count = lax.axis_size("dp")
+    span = 1 << (ROW_BITS + 1)
+    rise = (steps << LINK_Z) % span
+    route = [(low, low // span * span + (low + rise) % span) for low in range(count)]
+    return lax.ppermute(block, "dp", route)
 
 
 def row_product(left, right):
@@ -141,7 +150,8 @@
             cut = part[0].shape[0] // 4
             part = [part[0].at[i * cut : (i + 1) * cut] for i in range(4)]
         parts.append(part)
-    near, other, _, x, e, hidden, gate_grad, up_grad, out_keep, out_send, row_keep, row_send, turn = refs
+    near, other, near_turned, other_turned, _, *refs = refs
+    x, e, hidden, gate_grad, up_grad, out_keep, out_send, row_keep, row_send, turn = refs
     turn[...] = jnp.zeros_like(turn)
     units = near.shape[1]
     rows = x.shape[0] // 4
@@ -153,30 +163,30 @@
             into = slice(plane * rows + i * size, plane * rows + (i + 1) * size)
             x[into] = x_from[x_half * size : (x_half + 1) * size]
             e[into] = e_from[e_half * size : (e_half + 1) * size]
-    for i, panels in enumerate((near, other)):
+    for i, panels in enumerate((near_turned, other_turned)):
         mine = slice(i * units, (i + 1) * units)
-        gate_pre = row_product(panels[0], x[...])
-        up_pre = row_product(panels[1], x[...])
-        hidden_grad = row_product(panels[2], e[...])
+        gate_pre = product(x[...], panels[0])
+        up_pre = product(x[...], panels[1])
+        hidden_grad = product(e[...], panels[2])
         gate_sig = jax.nn.sigmoid(gate_pre)
         activated = gate_pre * gate_sig
-        hidden[mine] = half(activated * up_pre)
-        gate_grad[mine] = half(
+        hidden[:, mine] = half(activated * up_pre)
+        gate_grad[:, mine] = half(
             hidden_grad * up_pre * (gate_sig * (1.0 + gate_pre * (1.0 - gate_sig)))
         )
-        up_grad[mine] = half(hidden_grad * activated)
+        up_grad[:, mine] = half(hidden_grad * activated)
     for at in range(0, x.shape[1], PANEL):
         part = slice(at, at + PANEL)
-        out = col_product(hidden[:units], near[2, :, part]) + col_product(
-            hidden[units:], other[2, :, part]
+        out = product(hidden[:, :units], near[2, :, part]) + product(
+            hidden[:, units:], other[2, :, part]
         )
         out_keep[:, part] = out[: 2 * rows]
         out_send[:, part] = half(out[2 * rows :])
         row = (
-            col_product(gate_grad[:units], near[0, :, part])
-            + col_product(gate_grad[units:], other[0, :, part])
-            + col_product(up_grad[:units], near[1, :, part])
-            + col_product(up_grad[units:], other[1, :, part])
+            product(gate_grad[:, :units], near[0, :, part])
+            + product(gate_grad[:, units:], other[0, :, part])
+            + product(up_grad[:, :units], near[1, :, part])
+            + product(up_grad[:, units:], other[1, :, part])
         )
         row_keep[:rows, part] = row[:rows]
         row_keep[rows:, part] = row[2 * rows : 3 * rows]
@@ -184,30 +194,33 @@
         row_send[rows:, part] = half(row[3 * rows :])
 
 
-def expert(parts, near, other, turn):
+def expert(parts, panels, turn):
     rows = sum(ref.shape[0] for part in parts for ref in part) // 2
     width = parts[0][0].shape[1]
-    units = 2 * near.shape[1]
+    units = 2 * panels[0].shape[1]
     saved, kept, sent = (
-        held((units, rows)),
+        held((rows, units)),
         held((rows // 2, width), jnp.float32),
         held((rows // 2, width)),
     )
     return pl.pallas_call(
         functools.partial(expert_kernel, [len(part) for part in parts]),
         out_shape=(held((rows, width)),) * 2 + (saved,) * 3 + (kept, sent, kept, sent, TURN),
-        in_specs=[VMEM] * (sum(len(part) for part in parts) + 3),
+        in_specs=[VMEM] * (sum(len(part) for part in parts) + 5),
         out_specs=(VMEM,) * 10,
         compiler_params=limit(12),
         cost_estimate=cost(12 * rows * units * width, 6 * units * width),
         name="expert",
-    )(*fetched(*(ref for part in parts for ref in part), near, other, turn))
+    )(*fetched(*(ref for part in parts for ref in part), *panels, turn))
 
 
 def slot_sums(works, units, columns):
-    x, e = (jnp.concatenate([refs[i][:, columns] for refs in works], 0) for i in (0, 1))
-    for i, right in ((3, x), (4, x), (2, e)):
-        yield product(jnp.concatenate([refs[i][units] for refs in works], 1), right)
+    x, e, hidden, gate_grad, up_grad = (
+        jnp.concatenate([refs[i][:, units if i > 1 else columns] for refs in works], 0)
+        for i in range(5)
+    )
+    for left, right in ((gate_grad, x), (up_grad, x), (hidden, e)):
+        yield col_product(left, right)
 
 
 def other_kernel(*refs):
@@ -222,7 +235,7 @@
 
 def other_grads(works, turn):
     width = works[0][0].shape[1]
-    units = works[0][2].shape[0] // 2
+    units = works[0][2].shape[1] // 2
     return pl.pallas_call(
         other_kernel,
         out_shape=(held((3, units, width)), TURN),
@@ -294,6 +307,12 @@
     pair_body(x, x_side, e, e_side, x_pair, e_pair)
 
 
+def turn_body(panels, turned):
+    for i in range(panels.shape[0]):
+        for at in range(0, panels.shape[2], PANEL):
+            turned[i, at : at + PANEL] = panels[i, :, at : at + PANEL].T
+
+
 def pack_body(x_pair, x_far, e_pair, e_far, plane):
     rows = x_pair.shape[0]
     for i, part in enumerate((x_pair, x_far, e_pair, e_far)):
@@ -324,14 +343,16 @@
         second[i] = total[rows:].astype(second.dtype)
 
 
-def far_body(own, three, total):
+def relay_body(own, passed, total):
+    total[...] = half(own[...] + passed[...].astype(jnp.float32))
+
+
+def near_body(own, three, total):
     total[...] = own[...] + three[...].astype(jnp.float32)
 
 
-def final_body(total, one, two, weight, expert_out, grad_rows):
-    out, row = (
-        total[i] + one[i].astype(jnp.float32) + two[i].astype(jnp.float32) for i in (0, 1)
-    )
+def final_body(total, one, weight, expert_out, grad_rows):
+    out, row = (total[i] + one[i].astype(jnp.float32) for i in (0, 1))
     expert_out[...] = half(weight[:, :1] * out)
     grad_rows[...] = half(row)
 
@@ -360,28 +381,32 @@
     def fars_of(x, e):
         return x, swapped(x, along_y), e, swapped(e, along_x)
 
-    three = swapped(own, 3 << LINK_Z)
+    two = shifted(own, 2)
     one_level, two_levels = [held((capacity, width))] * 2, [held((rows, width))] * 2
     own, x, e, turn = staged(
         copy_body, "copy", [held(own.shape), *one_level], own, turn, flops=C_COPY
     )
-    two = swapped(own, 2 << LINK_Z)
+    one = shifted(own, 1)
+    turned = held((near.shape[0], near.shape[2], near.shape[1]))
+    near_turned, turn = staged(turn_body, "turn_near", [turned], near, turn, flops=C_TURN)
     x, e, turn = staged(first_pair_body, "pair_0", two_levels, *sides_of(x, e), other, turn)
     part_0 = fars_of(x, e)
-    x, e, turn = staged(split_body, "split_3", one_level, three, turn, flops=C_SPLIT3)
-    sides_3 = sides_of(x, e)
+    x, e, turn = staged(split_body, "split_2", one_level, two, turn, flops=C_FIRST)
+    sides_2 = sides_of(x, e)
     plane, turn = staged(pack_body, "pack", [held((4 * rows, width))], *part_0, turn, flops=C_PACK)
-    part_1 = (swapped(plane, 1 << LINK_Z),)
-    x, e, turn = staged(pair_body, "pair_3", two_levels, *sides_3, turn, flops=C_PAIR3)
-    part_3 = fars_of(x, e)
-    x, e, turn = staged(split_body, "split_2", one_level, two, turn, flops=C_SPLIT2)
-    sides_2 = sides_of(x, e)
-    x, e, turn = staged(pair_body, "pair_2", two_levels, *sides_2, turn, flops=C_PAIR2)
+    part_3 = (shifted(plane, -1),)
+    x, e, turn = staged(pair_body, "pair_2", two_levels, *sides_2, turn, flops=C_PAIR_FIRST)
     part_2 = fars_of(x, e)
+    x, e, turn = staged(split_body, "split_1", one_level, one, turn, flops=C_LAST)
+    sides_1 = sides_of(x, e)
+    other_turned, turn = staged(turn_body, "turn_other", [turned], other, turn, flops=C_TURN)
+    panels = (near, other, near_turned, other_turned)
+    x, e, turn = staged(pair_body, "pair_1", two_levels, *sides_1, turn, flops=C_PAIR_LAST)
+    part_1 = fars_of(x, e)
 
     works, sides = [], []
-    for parts in ((part_0, part_3), (part_1, part_2)):
-        *work, out_keep, out_send, row_keep, row_send, turn = expert(parts, near, other, turn)
+    for parts in ((part_0, part_2), (part_1, part_3)):
+        *work, out_keep, out_send, row_keep, row_send, turn = expert(parts, panels, turn)
         works.append(work)
         sides.append((out_keep, swapped(out_send, along_y), row_keep, swapped(row_send, along_x)))
 
@@ -400,14 +425,16 @@
             flops=flops,
         )
 
-    middle_03, turn = plane_sum(sides[0], turn)
+    middle_02, turn = plane_sum(sides[0], turn)
     sent, turn = other_grads(works, turn)
     received = swapped(sent, core)
-    middle_12, turn = plane_sum(sides[1], turn)
-    sum_0, sum_3, turn = line_sum(middle_03, turn, jnp.float32)
-    three = swapped(sum_3, 3 << LINK_Z)
-    sum_1, sum_2, turn = line_sum(middle_12, turn, jnp.bfloat16, flops=LONG)
-    two, one = swapped(sum_2, 2 << LINK_Z), swapped(sum_1, 1 << LINK_Z)
+    middle_31, turn = plane_sum(sides[1], turn)
+    sum_0, sum_2, turn = line_sum(middle_02, turn, jnp.float32)
+    passed = shifted(sum_2, -1)
+    sum_1, sum_3, turn = line_sum(middle_31, turn, jnp.float32)
+    three = shifted(sum_3, 1)
+    sum_1, turn = staged(relay_body, "relay", [held(own.shape)], sum_1, passed, turn, flops=LONG)
+    one = shifted(sum_1, -1)
     factor = 1.0 / math.sqrt(devices * capacity)
     if far_bits:
         *owned, turn = own_grads(works, received, turn, 1.0, jnp.float32)
@@ -418,10 +445,10 @@
     else:
         *owned, turn = own_grads(works, received, turn, factor, jnp.bfloat16)
     total, turn = staged(
-        far_body, "far_sum", [held(own.shape, jnp.float32)], sum_0, three, turn, flops=LONG // 10
+        near_body, "near_sum", [held(own.shape, jnp.float32)], sum_0, three, turn, flops=LONG // 10
     )
     expert_out, grad_rows, turn = staged(
-        final_body, "final", [shape((capacity, width))] * 2, total, one, two, weight, turn
+        final_body, "final", [shape((capacity, width))] * 2, total, one, weight, turn
     )
     return (expert_out, grad_rows, *owned)
 

time: 85.4 us -> 81.1 us (0.950)
  starting transfers between devices: 36.3 us -> 30.5 us
  waiting for transfers between devices: 30.6 us -> 31.6 us
    ppermute x28 -> x22, starting transfers between devices: 36.3 us -> 24 us  [swapped(): lax.ppermute(block, 'dp', [(low, low ^ mask) for low in range(count)])]
    ppermute x0 -> x6, waiting for transfers between devices: none -> 11.4 us  [shifted(): return lax.ppermute(block, 'dp', route)]
    ppermute x28 -> x22, waiting for transfers between devices: 30.6 us -> 20.2 us  [swapped(): lax.ppermute(block, 'dp', [(low, low ^ mask) for low in range(count)])]
    ppermute x0 -> x6, starting transfers between devices: none -> 6.5 us  [shifted(): return lax.ppermute(block, 'dp', route)]
    pallas_call x13 -> x16, Pallas kernels: 1.4 us -> 3.95 us  [staged(): pl.pallas_call(kernel, out_shape=(*outs, TURN), in_specs=[VMEM] * len(val...]
    pallas_call x2, Pallas kernels: 8.22 us -> 5.84 us  [expert(): pl.pallas_call(functools.partial(expert_kernel, [len(part) for part in pa...]
  transfers between devices with their start and end apart: 28 -> 28, of which waited for: 14 -> 16; matrix products, arithmetic and copies ran while one was open for 0% -> 0% of each run, Pallas kernels for 17% -> 18%
where the time goes in v5:
time: 81.1 us; the launch traced here: 80.9 us
  waiting for transfers between devices  31.6 us (39%)
  starting transfers between devices  30.5 us (38%)
  Pallas kernels  18 us (22%)
    ppermute x22, starting transfers between devices, swapped(): lax.ppermute(block, 'dp', [(low, low ^ mask) for low in range(count)])  24 us
    ppermute x22, waiting for transfers between devices, swapped(): lax.ppermute(block, 'dp', [(low, low ^ mask) for low in range(count)])  20.2 us
    ppermute x6, waiting for transfers between devices, shifted(): return lax.ppermute(block, 'dp', route)  11.4 us
    ppermute x6, starting transfers between devices, shifted(): return lax.ppermute(block, 'dp', route)  6.5 us
    pallas_call x2, Pallas kernels, expert(): pl.pallas_call(functools.partial(expert_kernel, [len(part) for part in pa...  5.84 us
    pallas_call x1, Pallas kernels, own_grads(): pl.pallas_call(functools.partial(own_kernel, factor), grid=(width // PANE...  4.11 us
    pallas_call x16, Pallas kernels, staged(): pl.pallas_call(kernel, out_shape=(*outs, TURN), in_specs=[VMEM] * len(val...  3.95 us
    pallas_call x1, Pallas kernels, pick(): pl.pallas_call(pick_kernel, out_shape=(held((2, capacity, width)), held((...  2.71 us
  transfers between devices with their start and end apart: 28, of which 16 were waited for; matrix products, arithmetic and copies ran while one was open for 0% of the time, Pallas kernels for 18%

profile of v5, /device:TPU:0, one launch (start us, length us, event | category | flops | bytes accessed | tf_op | source)
XLA Modules:
  0.0 80.9 jit_solution(15792434067911610459)
XLA Ops:
  0.6 2.7 %pick.1 = (bf16[2,16,3072]{2,1,0:T(8,128)(2,1)S(1)}, f32[16,128]{1,0:T(8,128)S(1)}, bf16[3,256,3072]{2,1,0:T(8,128)(2,1)S(1)}, f32[8,128]{1,0:T(8,128)S(1)}) custom-call(s32[1]{0:T(128)} %bitcast.place, s32[16]{0:T(128)} %token_.1, s32[32]{0:T(128)} %count.1, f32[16]{0:T(128)} %gate.1, bf16[128,3072]{1,0:T(8,128)(2,1)} %tokens.1, bf16[16,3072]{1,0:T(8,128)(2,1)} %grad.1, ...), custom_call_target="tpu_custom_call" | custom-call | tf_op jit(solution)/shard_map/pick/pallas_call | solution.py:126
  3.4 0.5 collective-permute-start.2
  3.9 3.7 %collective-permute-start.5 = (bf16[2,16,3072]{2,1,0:T(8,128)(2,1)S(1)}, bf16[2,16,3072]{2,1,0:T(8,128)(2,1)S(1)}, u32[]{:S(2)}, u32[]{:S(2)}) collective-permute-start(bf16[2,16,3072]{2,1,0:T(8,128)(2,1)S(1)} %get-tuple-element.82.refs_0_), channel_id=1, source_target_pairs={{0,16},{1,17},{2,18},{3,19},{4,20},{5,21},{6,22},{7,23},{8,24},{9,... | collective-permute-start | bytes 589832 | tf_op jit(solution)/shard_map/ppermute | solution.py:38
  7.6 1.6 %collective-permute-start = (bf16[16,3072]{1,0:T(8,128)(2,1)S(1)}, bf16[16,3072]{1,0:T(8,128)(2,1)S(1)}, u32[]{:S(2)}, u32[]{:S(2)}) collective-permute-start(bf16[16,3072]{1,0:T(8,128)(2,1)S(1)} %get-tuple-element.84.refs_0_), channel_id=1, source_target_pairs={{0,2},{1,3},{2,0},{3,1},{4,6},{5,7},{6,4},{7,5},{8,10},{9,11},{10,... | collective-permute-start | bytes 294920 | tf_op jit(solution)/shard_map/ppermute | solution.py:30
  9.1 1.5 %collective-permute-start.1 = (bf16[16,3072]{1,0:T(8,128)(2,1)S(1)}, bf16[16,3072]{1,0:T(8,128)(2,1)S(1)}, u32[]{:S(2)}, u32[]{:S(2)}) collective-permute-start(bf16[16,3072]{1,0:T(8,128)(2,1)S(1)} %get-tuple-element.85.refs_2_), channel_id=1, source_target_pairs={{0,4},{1,5},{2,6},{3,7},{4,0},{5,1},{6,2},{7,3},{8,12},{9,13},{10,... | collective-permute-start | bytes 294920 | tf_op jit(solution)/shard_map/ppermute | solution.py:30
  10.6 1.6 %collective-permute-start.10 = (bf16[2,16,3072]{2,1,0:T(8,128)(2,1)S(1)}, bf16[2,16,3072]{2,1,0:T(8,128)(2,1)S(1)}, u32[]{:S(2)}, u32[]{:S(2)}) collective-permute-start(bf16[2,16,3072]{2,1,0:T(8,128)(2,1)S(1)} %get-tuple-element.99), channel_id=1, source_target_pairs={{0,8},{1,9},{2,10},{3,11},{4,12},{5,13},{6,14},{7,15},{8,16},{9,17... | collective-permute-start | bytes 589832 | tf_op jit(solution)/shard_map/ppermute | solution.py:38
  12.2 1.3 %turn_near.1 = (bf16[3,3072,256]{2,1,0:T(8,128)(2,1)S(1)}, f32[8,128]{1,0:T(8,128)S(1)}) custom-call(bf16[3,256,3072]{2,1,0:T(8,128)(2,1)S(1)} %get-tuple-element.86.refs_0_.refs_8_.refs_5_, f32[8,128]{1,0:T(8,128)S(1)} %get-tuple-element.87.refs_1_), custom_call_target="tpu_custom_call" | custom-call | tf_op jit(solution)/shard_map/turn_near/pallas_call | solution.py:280
  13.5 0.2 collective-permute-done.1.refs_3_
  13.8 1.6 %collective-permute-start.3 = (bf16[32,3072]{1,0:T(8,128)(2,1)S(1)}, bf16[32,3072]{1,0:T(8,128)(2,1)S(1)}, u32[]{:S(2)}, u32[]{:S(2)}) collective-permute-start(bf16[32,3072]{1,0:T(8,128)(2,1)S(1)} %get-tuple-element.89.refs_0_), channel_id=1, source_target_pairs={{0,4},{1,5},{2,6},{3,7},{4,0},{5,1},{6,2},{7,3},{8,12},{9,13},{10,... | collective-permute-start | bytes 589832 | tf_op jit(solution)/shard_map/ppermute | solution.py:30
  15.4 0.5 collective-permute-start.4
  15.9 5.6 %collective-permute-done.5.refs_0_ = bf16[2,16,3072]{2,1,0:T(8,128)(2,1)S(1)} collective-permute-done((bf16[2,16,3072]{2,1,0:T(8,128)(2,1)S(1)}, bf16[2,16,3072]{2,1,0:T(8,128)(2,1)S(1)}, u32[]{:S(2)}, u32[]{:S(2)}) %collective-permute-start.5) | collective-permute-done | bytes 196640 | tf_op jit(solution)/shard_map/ppermute | solution.py:38
  21.5 1.6 %collective-permute-start.6 = (bf16[16,3072]{1,0:T(8,128)(2,1)S(1)}, bf16[16,3072]{1,0:T(8,128)(2,1)S(1)}, u32[]{:S(2)}, u32[]{:S(2)}) collective-permute-start(bf16[16,3072]{1,0:T(8,128)(2,1)S(1)} %get-tuple-element.92.refs_0_), channel_id=1, source_target_pairs={{0,2},{1,3},{2,0},{3,1},{4,6},{5,7},{6,4},{7,5},{8,10},{9,11},{10,... | collective-permute-start | bytes 294920 | tf_op jit(solution)/shard_map/ppermute | solution.py:30
  23.1 1.5 %collective-permute-start.7 = (bf16[16,3072]{1,0:T(8,128)(2,1)S(1)}, bf16[16,3072]{1,0:T(8,128)(2,1)S(1)}, u32[]{:S(2)}, u32[]{:S(2)}) collective-permute-start(bf16[16,3072]{1,0:T(8,128)(2,1)S(1)} %get-tuple-element.93.refs_2_), channel_id=1, source_target_pairs={{0,4},{1,5},{2,6},{3,7},{4,0},{5,1},{6,2},{7,3},{8,12},{9,13},{10,... | collective-permute-start | bytes 294920 | tf_op jit(solution)/shard_map/ppermute | solution.py:30
  24.7 1.1 %collective-permute-start.17 = (bf16[128,3072]{1,0:T(8,128)(2,1)S(1)}, bf16[128,3072]{1,0:T(8,128)(2,1)S(1)}, u32[]{:S(2)}, u32[]{:S(2)}) collective-permute-start(bf16[128,3072]{1,0:T(8,128)(2,1)S(1)} %get-tuple-element.113), channel_id=1, source_target_pairs={{0,24},{1,25},{2,26},{3,27},{4,28},{5,29},{6,30},{7,31},{8,0},{9,1... | collective-permute-start | bytes 2359304 | tf_op jit(solution)/shard_map/ppermute | solution.py:38
  25.8 0.4 collective-permute-done.6.refs_1_
  26.2 1.6 %collective-permute-done.7.refs_3_ = bf16[16,3072]{1,0:T(8,128)(2,1)S(1)} collective-permute-done((bf16[16,3072]{1,0:T(8,128)(2,1)S(1)}, bf16[16,3072]{1,0:T(8,128)(2,1)S(1)}, u32[]{:S(2)}, u32[]{:S(2)}) %collective-permute-start.7) | collective-permute-done | bytes 98336 | tf_op jit(solution)/shard_map/ppermute | solution.py:30
  27.7 1.6 %collective-permute-start.8 = (bf16[32,3072]{1,0:T(8,128)(2,1)S(1)}, bf16[32,3072]{1,0:T(8,128)(2,1)S(1)}, u32[]{:S(2)}, u32[]{:S(2)}) collective-permute-start(bf16[32,3072]{1,0:T(8,128)(2,1)S(1)} %get-tuple-element.96.refs_4_), channel_id=1, source_target_pairs={{0,4},{1,5},{2,6},{3,7},{4,0},{5,1},{6,2},{7,3},{8,12},{9,13},{10,... | collective-permute-start | bytes 589832 | tf_op jit(solution)/shard_map/ppermute | solution.py:30
  29.3 0.5 collective-permute-start.9
  29.9 1.6 %collective-permute-start.11 = (bf16[16,3072]{1,0:T(8,128)(2,1)S(1)}, bf16[16,3072]{1,0:T(8,128)(2,1)S(1)}, u32[]{:S(2)}, u32[]{:S(2)}) collective-permute-start(bf16[16,3072]{1,0:T(8,128)(2,1)S(1)} %get-tuple-element.103.refs_0_), channel_id=1, source_target_pairs={{0,2},{1,3},{2,0},{3,1},{4,6},{5,7},{6,4},{7,5},{8,10},{9,11},{10,... | collective-permute-start | bytes 294920 | tf_op jit(solution)/shard_map/ppermute | solution.py:30
  31.4 0.5 collective-permute-start.12
  32.0 1.3 %turn_other.1 = (bf16[3,3072,256]{2,1,0:T(8,128)(2,1)S(1)}, f32[8,128]{1,0:T(8,128)S(1)}) custom-call(bf16[3,256,3072]{2,1,0:T(8,128)(2,1)S(1)} %collective-permute-done.2.refs_4_.refs_0_.refs_9_.refs_6_, f32[8,128]{1,0:T(8,128)S(1)} %get-tuple-element.101.refs_1_), custom_call_target="tpu_custom_call" | custom-call | tf_op jit(solution)/shard_map/turn_other/pallas_call | solution.py:280
  33.2 3.3 %collective-permute-done.11.refs_1_ = bf16[16,3072]{1,0:T(8,128)(2,1)S(1)} collective-permute-done((bf16[16,3072]{1,0:T(8,128)(2,1)S(1)}, bf16[16,3072]{1,0:T(8,128)(2,1)S(1)}, u32[]{:S(2)}, u32[]{:S(2)}) %collective-permute-start.11) | collective-permute-done | bytes 98336 | tf_op jit(solution)/shard_map/ppermute | solution.py:30
  36.5 0.6 collective-permute-start.15
  37.1 0.7 collective-permute-start.16
  37.8 2.9 %expert.2 = (bf16[128,3072]{1,0:T(8,128)(2,1)S(1)}, bf16[128,3072]{1,0:T(8,128)(2,1)S(1)}, bf16[128,512]{1,0:T(8,128)(2,1)S(1)}, bf16[128,512]{1,0:T(8,128)(2,1)...) custom-call(bf16[32,3072]{1,0:T(8,128)(2,1)S(1)} %get-tuple-element., ...), custom_call_target="tpu_custom_call" | custom-call | flops 2415919104 | bytes 9437184 | tf_op jit(solution)/shard_map/expert/pallas_call | solution.py:206
  40.7 1.2 %collective-permute-start.13 = (bf16[64,3072]{1,0:T(8,128)(2,1)S(1)}, bf16[64,3072]{1,0:T(8,128)(2,1)S(1)}, u32[]{:S(2)}, u32[]{:S(2)}) collective-permute-start(bf16[64,3072]{1,0:T(8,128)(2,1)S(1)} %get-tuple-element.108), channel_id=1, source_target_pairs={{0,4},{1,5},{2,6},{3,7},{4,0},{5,1},{6,2},{7,3},{8,12},{9,13},{10,... | collective-permute-start | bytes 1179656 | tf_op jit(solution)/shard_map/ppermute | solution.py:30
  41.9 1.7 %collective-permute-start.14 = (bf16[64,3072]{1,0:T(8,128)(2,1)S(1)}, bf16[64,3072]{1,0:T(8,128)(2,1)S(1)}, u32[]{:S(2)}, u32[]{:S(2)}) collective-permute-start(bf16[64,3072]{1,0:T(8,128)(2,1)S(1)} %get-tuple-element.110), channel_id=1, source_target_pairs={{0,2},{1,3},{2,0},{3,1},{4,6},{5,7},{6,4},{7,5},{8,10},{9,11},{10,... | collective-permute-start | bytes 1179656 | tf_op jit(solution)/shard_map/ppermute | solution.py:30
  43.6 0.6 collective-permute-done.15.refs_1_
  44.2 0.2 collective-permute-done.16.refs_3_
  44.4 2.9 %expert.3 = (bf16[128,3072]{1,0:T(8,128)(2,1)S(1)}, bf16[128,3072]{1,0:T(8,128)(2,1)S(1)}, bf16[128,512]{1,0:T(8,128)(2,1)S(1)}, bf16[128,512]{1,0:T(8,128)(2,1)...) custom-call(bf16[32,3072]{1,0:T(8,128)(2,1)S(1)} %get-tuple-element., ...), custom_call_target="tpu_custom_call" | custom-call | flops 2415919104 | bytes 9437184 | tf_op jit(solution)/shard_map/expert/pallas_call | solution.py:206
  47.4 2.0 %collective-permute-start.20 = (bf16[64,3072]{1,0:T(8,128)(2,1)S(1)}, bf16[64,3072]{1,0:T(8,128)(2,1)S(1)}, u32[]{:S(2)}, u32[]{:S(2)}) collective-permute-start(bf16[64,3072]{1,0:T(8,128)(2,1)S(1)} %get-tuple-element.121), channel_id=1, source_target_pairs={{0,4},{1,5},{2,6},{3,7},{4,0},{5,1},{6,2},{7,3},{8,12},{9,13},{10,... | collective-permute-start | bytes 1179656 | tf_op jit(solution)/shard_map/ppermute | solution.py:30
  49.4 3.4 %collective-permute-done.13.refs_1_ = bf16[64,3072]{1,0:T(8,128)(2,1)S(1)} collective-permute-done((bf16[64,3072]{1,0:T(8,128)(2,1)S(1)}, bf16[64,3072]{1,0:T(8,128)(2,1)S(1)}, u32[]{:S(2)}, u32[]{:S(2)}) %collective-permute-start.13) | collective-permute-done | bytes 393248 | tf_op jit(solution)/shard_map/ppermute | solution.py:30
  52.8 1.1 %collective-permute-done.14.refs_3_ = bf16[64,3072]{1,0:T(8,128)(2,1)S(1)} collective-permute-done((bf16[64,3072]{1,0:T(8,128)(2,1)S(1)}, bf16[64,3072]{1,0:T(8,128)(2,1)S(1)}, u32[]{:S(2)}, u32[]{:S(2)}) %collective-permute-start.14) | collective-permute-done | bytes 393248 | tf_op jit(solution)/shard_map/ppermute | solution.py:30
  54.1 1.7 %collective-permute-start.18 = (bf16[32,3072]{1,0:T(8,128)(2,1)S(1)}, bf16[32,3072]{1,0:T(8,128)(2,1)S(1)}, u32[]{:S(2)}, u32[]{:S(2)}) collective-permute-start(bf16[32,3072]{1,0:T(8,128)(2,1)S(1)} %get-tuple-element.117), channel_id=1, source_target_pairs={{0,2},{1,3},{2,0},{3,1},{4,6},{5,7},{6,4},{7,5},{8,10},{9,11},{10,... | collective-permute-start | bytes 589832 | tf_op jit(solution)/shard_map/ppermute | solution.py:30
  55.8 0.6 collective-permute-start.19
  56.4 1.4 %other_grads.1 = (bf16[3,256,3072]{2,1,0:T(8,128)(2,1)S(1)}, f32[8,128]{1,0:T(8,128)S(1)}) custom-call(bf16[128,3072]{1,0:T(8,128)(2,1)S(1)} %get-tuple-element.124.refs_0_, bf16[128,3072]{1,0:T(8,128)(2,1)S(1)} %get-tuple-element.125.refs_1_, bf16[128,512]{1,0:T(8,128)(2,1)S(1)} %get-tuple-element.126.refs_2_, ...), custom_call_target="tpu_custom_call" | custom-call | flops 2000000000 | tf_op jit(solution)/shard_map/other_grads/pallas_call | solution.py:239
  57.8 3.4 %collective-permute-done.20.refs_1_ = bf16[64,3072]{1,0:T(8,128)(2,1)S(1)} collective-permute-done((bf16[64,3072]{1,0:T(8,128)(2,1)S(1)}, bf16[64,3072]{1,0:T(8,128)(2,1)S(1)}, u32[]{:S(2)}, u32[]{:S(2)}) %collective-permute-start.20) | collective-permute-done | bytes 393248 | tf_op jit(solution)/shard_map/ppermute | solution.py:30
  61.2 1.1 %collective-permute-done.21.refs_3_ = bf16[64,3072]{1,0:T(8,128)(2,1)S(1)} collective-permute-done((bf16[64,3072]{1,0:T(8,128)(2,1)S(1)}, bf16[64,3072]{1,0:T(8,128)(2,1)S(1)}, u32[]{:S(2)}, u32[]{:S(2)}) %collective-permute-start.21) | collective-permute-done | bytes 393248 | tf_op jit(solution)/shard_map/ppermute | solution.py:30
  62.4 0.1 plane_sum.3
  62.5 1.7 %collective-permute-start.22 = (bf16[32,3072]{1,0:T(8,128)(2,1)S(1)}, bf16[32,3072]{1,0:T(8,128)(2,1)S(1)}, u32[]{:S(2)}, u32[]{:S(2)}) collective-permute-start(bf16[32,3072]{1,0:T(8,128)(2,1)S(1)} %get-tuple-element.139), channel_id=1, source_target_pairs={{0,2},{1,3},{2,0},{3,1},{4,6},{5,7},{6,4},{7,5},{8,10},{9,11},{10,... | collective-permute-start | bytes 589832 | tf_op jit(solution)/shard_map/ppermute | solution.py:30
  64.2 0.6 collective-permute-start.23
  64.9 1.1 %collective-permute-done.18.refs_1_ = bf16[32,3072]{1,0:T(8,128)(2,1)S(1)} collective-permute-done((bf16[32,3072]{1,0:T(8,128)(2,1)S(1)}, bf16[32,3072]{1,0:T(8,128)(2,1)S(1)}, u32[]{:S(2)}, u32[]{:S(2)}) %collective-permute-start.18) | collective-permute-done | bytes 196640 | tf_op jit(solution)/shard_map/ppermute | solution.py:30
  66.2 2.1 %collective-permute-done.22.refs_1_ = bf16[32,3072]{1,0:T(8,128)(2,1)S(1)} collective-permute-done((bf16[32,3072]{1,0:T(8,128)(2,1)S(1)}, bf16[32,3072]{1,0:T(8,128)(2,1)S(1)}, u32[]{:S(2)}, u32[]{:S(2)}) %collective-permute-start.22) | collective-permute-done | bytes 196640 | tf_op jit(solution)/shard_map/ppermute | solution.py:30
  68.3 1.6 %collective-permute-done.23.refs_3_ = bf16[32,3072]{1,0:T(8,128)(2,1)S(1)} collective-permute-done((bf16[32,3072]{1,0:T(8,128)(2,1)S(1)}, bf16[32,3072]{1,0:T(8,128)(2,1)S(1)}, u32[]{:S(2)}, u32[]{:S(2)}) %collective-permute-start.23) | collective-permute-done | bytes 196640 | tf_op jit(solution)/shard_map/ppermute | solution.py:30
  70.1 4.3 %collective-permute-done.26.refs_1_ = bf16[2,16,3072]{2,1,0:T(8,128)(2,1)S(1)} collective-permute-done((bf16[2,16,3072]{2,1,0:T(8,128)(2,1)S(1)}, bf16[2,16,3072]{2,1,0:T(8,128)(2,1)S(1)}, u32[]{:S(2)}, u32[]{:S(2)}) %collective-permute-start.26) | collective-permute-done | bytes 196640 | tf_op jit(solution)/shard_map/ppermute | solution.py:38
  74.5 4.1 %own_grads.1 = (bf16[256,3072]{1,0:T(8,128)(2,1)}, bf16[256,3072]{1,0:T(8,128)(2,1)}, bf16[256,3072]{1,0:T(8,128)(2,1)}, f32[8,128]{1,0:T(8,128)S(1)}) custom-call(bf16[128,3072]{1,0:T(8,128)(2,1)S(1)} %get-tuple-element.124.refs_0_, bf16[128,3072]{1,0:T(8,128)(2,1)S(1)} %get-tuple-element.125.refs_1_, bf16[128,512]{1,0:T(8,128)(2,1)S(1)} %get-tuple-element.126.refs_2_, ...), custom_call_target="tpu_custom_call" | custom-call | tf_op jit(solution)/shard_map/own_grads/pallas_call | solution.py:263
  78.7 1.5 %collective-permute-done.27.refs_1_ = bf16[2,16,3072]{2,1,0:T(8,128)(2,1)S(1)} collective-permute-done((bf16[2,16,3072]{2,1,0:T(8,128)(2,1)S(1)}, bf16[2,16,3072]{2,1,0:T(8,128)(2,1)S(1)}, u32[]{:S(2)}, u32[]{:S(2)}) %collective-permute-start.27) | collective-permute-done | bytes 196640 | tf_op jit(solution)/shard_map/ppermute | solution.py:38
  80.2 0.7 final.1
  (29 shorter events, 0.8 us)
Async XLA Ops:
  3.4 10.4 %collective-permute-start.2 = (bf16[3,256,3072]{2,1,0:T(8,128)(2,1)S(1)}, bf16[3,256,3072]{2,1,0:T(8,128)(2,1)S(1)}, u32[]{:S(2)}, u32[]{:S(2)}) collective-permute-start(bf16[3,256,3072]{2,1,0:T(8,128)(2,1)S(1)} %get-tuple-element.86.refs_0_.refs_8_.refs_5_), channel_id=1, source_target_pairs={{0,1},{1,0},{2,3},{3,2},{4,5},{5,4},{6,7},{7,6},{8,9},{9,8},{10,11... | collective-permute-start | bytes 14155784 | tf_op jit(solution)/shard_map/ppermute | solution.py:30
  3.9 17.6 %collective-permute-start.5 = (bf16[2,16,3072]{2,1,0:T(8,128)(2,1)S(1)}, bf16[2,16,3072]{2,1,0:T(8,128)(2,1)S(1)}, u32[]{:S(2)}, u32[]{:S(2)}) collective-permute-start(bf16[2,16,3072]{2,1,0:T(8,128)(2,1)S(1)} %get-tuple-element.82.refs_0_), channel_id=1, source_target_pairs={{0,16},{1,17},{2,18},{3,19},{4,20},{5,21},{6,22},{7,23},{8,24},{9,... | collective-permute-start | bytes 589832 | tf_op jit(solution)/shard_map/ppermute | solution.py:38
  7.6 5.9 %collective-permute-start = (bf16[16,3072]{1,0:T(8,128)(2,1)S(1)}, bf16[16,3072]{1,0:T(8,128)(2,1)S(1)}, u32[]{:S(2)}, u32[]{:S(2)}) collective-permute-start(bf16[16,3072]{1,0:T(8,128)(2,1)S(1)} %get-tuple-element.84.refs_0_), channel_id=1, source_target_pairs={{0,2},{1,3},{2,0},{3,1},{4,6},{5,7},{6,4},{7,5},{8,10},{9,11},{10,... | collective-permute-start | bytes 294920 | tf_op jit(solution)/shard_map/ppermute | solution.py:30
  9.1 4.6 %collective-permute-start.1 = (bf16[16,3072]{1,0:T(8,128)(2,1)S(1)}, bf16[16,3072]{1,0:T(8,128)(2,1)S(1)}, u32[]{:S(2)}, u32[]{:S(2)}) collective-permute-start(bf16[16,3072]{1,0:T(8,128)(2,1)S(1)} %get-tuple-element.85.refs_2_), channel_id=1, source_target_pairs={{0,4},{1,5},{2,6},{3,7},{4,0},{5,1},{6,2},{7,3},{8,12},{9,13},{10,... | collective-permute-start | bytes 294920 | tf_op jit(solution)/shard_map/ppermute | solution.py:30
  10.6 19.2 %collective-permute-start.10 = (bf16[2,16,3072]{2,1,0:T(8,128)(2,1)S(1)}, bf16[2,16,3072]{2,1,0:T(8,128)(2,1)S(1)}, u32[]{:S(2)}, u32[]{:S(2)}) collective-permute-start(bf16[2,16,3072]{2,1,0:T(8,128)(2,1)S(1)} %get-tuple-element.99), channel_id=1, source_target_pairs={{0,8},{1,9},{2,10},{3,11},{4,12},{5,13},{6,14},{7,15},{8,16},{9,17... | collective-permute-start | bytes 589832 | tf_op jit(solution)/shard_map/ppermute | solution.py:38
  13.8 10.8 %collective-permute-start.3 = (bf16[32,3072]{1,0:T(8,128)(2,1)S(1)}, bf16[32,3072]{1,0:T(8,128)(2,1)S(1)}, u32[]{:S(2)}, u32[]{:S(2)}) collective-permute-start(bf16[32,3072]{1,0:T(8,128)(2,1)S(1)} %get-tuple-element.89.refs_0_), channel_id=1, source_target_pairs={{0,4},{1,5},{2,6},{3,7},{4,0},{5,1},{6,2},{7,3},{8,12},{9,13},{10,... | collective-permute-start | bytes 589832 | tf_op jit(solution)/shard_map/ppermute | solution.py:30
  15.4 9.3 %collective-permute-start.4 = (bf16[32,3072]{1,0:T(8,128)(2,1)S(1)}, bf16[32,3072]{1,0:T(8,128)(2,1)S(1)}, u32[]{:S(2)}, u32[]{:S(2)}) collective-permute-start(bf16[32,3072]{1,0:T(8,128)(2,1)S(1)} %get-tuple-element.90.refs_2_), channel_id=1, source_target_pairs={{0,2},{1,3},{2,0},{3,1},{4,6},{5,7},{6,4},{7,5},{8,10},{9,11},{10,... | collective-permute-start | bytes 589832 | tf_op jit(solution)/shard_map/ppermute | solution.py:30
  21.5 4.7 %collective-permute-start.6 = (bf16[16,3072]{1,0:T(8,128)(2,1)S(1)}, bf16[16,3072]{1,0:T(8,128)(2,1)S(1)}, u32[]{:S(2)}, u32[]{:S(2)}) collective-permute-start(bf16[16,3072]{1,0:T(8,128)(2,1)S(1)} %get-tuple-element.92.refs_0_), channel_id=1, source_target_pairs={{0,2},{1,3},{2,0},{3,1},{4,6},{5,7},{6,4},{7,5},{8,10},{9,11},{10,... | collective-permute-start | bytes 294920 | tf_op jit(solution)/shard_map/ppermute | solution.py:30
  23.1 4.6 %collective-permute-start.7 = (bf16[16,3072]{1,0:T(8,128)(2,1)S(1)}, bf16[16,3072]{1,0:T(8,128)(2,1)S(1)}, u32[]{:S(2)}, u32[]{:S(2)}) collective-permute-start(bf16[16,3072]{1,0:T(8,128)(2,1)S(1)} %get-tuple-element.93.refs_2_), channel_id=1, source_target_pairs={{0,4},{1,5},{2,6},{3,7},{4,0},{5,1},{6,2},{7,3},{8,12},{9,13},{10,... | collective-permute-start | bytes 294920 | tf_op jit(solution)/shard_map/ppermute | solution.py:30
  24.7 19.7 %collective-permute-start.17 = (bf16[128,3072]{1,0:T(8,128)(2,1)S(1)}, bf16[128,3072]{1,0:T(8,128)(2,1)S(1)}, u32[]{:S(2)}, u32[]{:S(2)}) collective-permute-start(bf16[128,3072]{1,0:T(8,128)(2,1)S(1)} %get-tuple-element.113), channel_id=1, source_target_pairs={{0,24},{1,25},{2,26},{3,27},{4,28},{5,29},{6,30},{7,31},{8,0},{9,1... | collective-permute-start | bytes 2359304 | tf_op jit(solution)/shard_map/ppermute | solution.py:38
  27.7 10.0 %collective-permute-start.8 = (bf16[32,3072]{1,0:T(8,128)(2,1)S(1)}, bf16[32,3072]{1,0:T(8,128)(2,1)S(1)}, u32[]{:S(2)}, u32[]{:S(2)}) collective-permute-start(bf16[32,3072]{1,0:T(8,128)(2,1)S(1)} %get-tuple-element.96.refs_4_), channel_id=1, source_target_pairs={{0,4},{1,5},{2,6},{3,7},{4,0},{5,1},{6,2},{7,3},{8,12},{9,13},{10,... | collective-permute-start | bytes 589832 | tf_op jit(solution)/shard_map/ppermute | solution.py:30
  29.3 8.4 %collective-permute-start.9 = (bf16[32,3072]{1,0:T(8,128)(2,1)S(1)}, bf16[32,3072]{1,0:T(8,128)(2,1)S(1)}, u32[]{:S(2)}, u32[]{:S(2)}) collective-permute-start(bf16[32,3072]{1,0:T(8,128)(2,1)S(1)} %get-tuple-element.97.refs_6_), channel_id=1, source_target_pairs={{0,2},{1,3},{2,0},{3,1},{4,6},{5,7},{6,4},{7,5},{8,10},{9,11},{10,... | collective-permute-start | bytes 589832 | tf_op jit(solution)/shard_map/ppermute | solution.py:30
  29.9 6.6 %collective-permute-start.11 = (bf16[16,3072]{1,0:T(8,128)(2,1)S(1)}, bf16[16,3072]{1,0:T(8,128)(2,1)S(1)}, u32[]{:S(2)}, u32[]{:S(2)}) collective-permute-start(bf16[16,3072]{1,0:T(8,128)(2,1)S(1)} %get-tuple-element.103.refs_0_), channel_id=1, source_target_pairs={{0,2},{1,3},{2,0},{3,1},{4,6},{5,7},{6,4},{7,5},{8,10},{9,11},{10,... | collective-permute-start | bytes 294920 | tf_op jit(solution)/shard_map/ppermute | solution.py:30
  31.4 5.0 %collective-permute-start.12 = (bf16[16,3072]{1,0:T(8,128)(2,1)S(1)}, bf16[16,3072]{1,0:T(8,128)(2,1)S(1)}, u32[]{:S(2)}, u32[]{:S(2)}) collective-permute-start(bf16[16,3072]{1,0:T(8,128)(2,1)S(1)} %get-tuple-element.104.refs_2_), channel_id=1, source_target_pairs={{0,4},{1,5},{2,6},{3,7},{4,0},{5,1},{6,2},{7,3},{8,12},{9,13},{10,... | collective-permute-start | bytes 294920 | tf_op jit(solution)/shard_map/ppermute | solution.py:30
  36.5 7.7 %collective-permute-start.15 = (bf16[32,3072]{1,0:T(8,128)(2,1)S(1)}, bf16[32,3072]{1,0:T(8,128)(2,1)S(1)}, u32[]{:S(2)}, u32[]{:S(2)}) collective-permute-start(bf16[32,3072]{1,0:T(8,128)(2,1)S(1)} %get-tuple-element.111.refs_0_), channel_id=1, source_target_pairs={{0,4},{1,5},{2,6},{3,7},{4,0},{5,1},{6,2},{7,3},{8,12},{9,13},{10,... | collective-permute-start | bytes 589832 | tf_op jit(solution)/shard_map/ppermute | solution.py:30
  37.1 7.3 %collective-permute-start.16 = (bf16[32,3072]{1,0:T(8,128)(2,1)S(1)}, bf16[32,3072]{1,0:T(8,128)(2,1)S(1)}, u32[]{:S(2)}, u32[]{:S(2)}) collective-permute-start(bf16[32,3072]{1,0:T(8,128)(2,1)S(1)} %get-tuple-element.112.refs_2_), channel_id=1, source_target_pairs={{0,2},{1,3},{2,0},{3,1},{4,6},{5,7},{6,4},{7,5},{8,10},{9,11},{10,... | collective-permute-start | bytes 589832 | tf_op jit(solution)/shard_map/ppermute | solution.py:30
  40.7 12.1 %collective-permute-start.13 = (bf16[64,3072]{1,0:T(8,128)(2,1)S(1)}, bf16[64,3072]{1,0:T(8,128)(2,1)S(1)}, u32[]{:S(2)}, u32[]{:S(2)}) collective-permute-start(bf16[64,3072]{1,0:T(8,128)(2,1)S(1)} %get-tuple-element.108), channel_id=1, source_target_pairs={{0,4},{1,5},{2,6},{3,7},{4,0},{5,1},{6,2},{7,3},{8,12},{9,13},{10,... | collective-permute-start | bytes 1179656 | tf_op jit(solution)/shard_map/ppermute | solution.py:30
  41.9 12.1 %collective-permute-start.14 = (bf16[64,3072]{1,0:T(8,128)(2,1)S(1)}, bf16[64,3072]{1,0:T(8,128)(2,1)S(1)}, u32[]{:S(2)}, u32[]{:S(2)}) collective-permute-start(bf16[64,3072]{1,0:T(8,128)(2,1)S(1)} %get-tuple-element.110), channel_id=1, source_target_pairs={{0,2},{1,3},{2,0},{3,1},{4,6},{5,7},{6,4},{7,5},{8,10},{9,11},{10,... | collective-permute-start | bytes 1179656 | tf_op jit(solution)/shard_map/ppermute | solution.py:30
  47.4 13.9 %collective-permute-start.20 = (bf16[64,3072]{1,0:T(8,128)(2,1)S(1)}, bf16[64,3072]{1,0:T(8,128)(2,1)S(1)}, u32[]{:S(2)}, u32[]{:S(2)}) collective-permute-start(bf16[64,3072]{1,0:T(8,128)(2,1)S(1)} %get-tuple-element.121), channel_id=1, source_target_pairs={{0,4},{1,5},{2,6},{3,7},{4,0},{5,1},{6,2},{7,3},{8,12},{9,13},{10,... | collective-permute-start | bytes 1179656 | tf_op jit(solution)/shard_map/ppermute | solution.py:30
  49.4 13.0 %collective-permute-start.21 = (bf16[64,3072]{1,0:T(8,128)(2,1)S(1)}, bf16[64,3072]{1,0:T(8,128)(2,1)S(1)}, u32[]{:S(2)}, u32[]{:S(2)}) collective-permute-start(bf16[64,3072]{1,0:T(8,128)(2,1)S(1)} %get-tuple-element.123), channel_id=1, source_target_pairs={{0,2},{1,3},{2,0},{3,1},{4,6},{5,7},{6,4},{7,5},{8,10},{9,11},{10,... | collective-permute-start | bytes 1179656 | tf_op jit(solution)/shard_map/ppermute | solution.py:30
  54.1 11.8 %collective-permute-start.18 = (bf16[32,3072]{1,0:T(8,128)(2,1)S(1)}, bf16[32,3072]{1,0:T(8,128)(2,1)S(1)}, u32[]{:S(2)}, u32[]{:S(2)}) collective-permute-start(bf16[32,3072]{1,0:T(8,128)(2,1)S(1)} %get-tuple-element.117), channel_id=1, source_target_pairs={{0,2},{1,3},{2,0},{3,1},{4,6},{5,7},{6,4},{7,5},{8,10},{9,11},{10,... | collective-permute-start | bytes 589832 | tf_op jit(solution)/shard_map/ppermute | solution.py:30
  55.8 10.1 %collective-permute-start.19 = (bf16[32,3072]{1,0:T(8,128)(2,1)S(1)}, bf16[32,3072]{1,0:T(8,128)(2,1)S(1)}, u32[]{:S(2)}, u32[]{:S(2)}) collective-permute-start(bf16[32,3072]{1,0:T(8,128)(2,1)S(1)} %get-tuple-element.119), channel_id=1, source_target_pairs={{0,4},{1,5},{2,6},{3,7},{4,0},{5,1},{6,2},{7,3},{8,12},{9,13},{10,... | collective-permute-start | bytes 589832 | tf_op jit(solution)/shard_map/ppermute | solution.py:30
  62.5 5.7 %collective-permute-start.22 = (bf16[32,3072]{1,0:T(8,128)(2,1)S(1)}, bf16[32,3072]{1,0:T(8,128)(2,1)S(1)}, u32[]{:S(2)}, u32[]{:S(2)}) collective-permute-start(bf16[32,3072]{1,0:T(8,128)(2,1)S(1)} %get-tuple-element.139), channel_id=1, source_target_pairs={{0,2},{1,3},{2,0},{3,1},{4,6},{5,7},{6,4},{7,5},{8,10},{9,11},{10,... | collective-permute-start | bytes 589832 | tf_op jit(solution)/shard_map/ppermute | solution.py:30
  64.2 5.7 %collective-permute-start.23 = (bf16[32,3072]{1,0:T(8,128)(2,1)S(1)}, bf16[32,3072]{1,0:T(8,128)(2,1)S(1)}, u32[]{:S(2)}, u32[]{:S(2)}) collective-permute-start(bf16[32,3072]{1,0:T(8,128)(2,1)S(1)} %get-tuple-element.141), channel_id=1, source_target_pairs={{0,4},{1,5},{2,6},{3,7},{4,0},{5,1},{6,2},{7,3},{8,12},{9,13},{10,... | collective-permute-start | bytes 589832 | tf_op jit(solution)/shard_map/ppermute | solution.py:30
  66.0 8.3 %collective-permute-start.26 = (bf16[2,16,3072]{2,1,0:T(8,128)(2,1)S(1)}, bf16[2,16,3072]{2,1,0:T(8,128)(2,1)S(1)}, u32[]{:S(2)}, u32[]{:S(2)}) collective-permute-start(bf16[2,16,3072]{2,1,0:T(8,128)(2,1)S(1)} %get-tuple-element.146), channel_id=1, source_target_pairs={{0,24},{1,25},{2,26},{3,27},{4,28},{5,29},{6,30},{7,31},{8,0},{9,1... | collective-permute-start | bytes 589832 | tf_op jit(solution)/shard_map/ppermute | solution.py:38
  66.1 8.4 %collective-permute-start.25 = (bf16[3,256,3072]{2,1,0:T(8,128)(2,1)S(1)}, bf16[3,256,3072]{2,1,0:T(8,128)(2,1)S(1)}, u32[]{:S(2)}, u32[]{:S(2)}) collective-permute-start(bf16[3,256,3072]{2,1,0:T(8,128)(2,1)S(1)} %get-tuple-element.144), channel_id=1, source_target_pairs={{0,1},{1,0},{2,3},{3,2},{4,5},{5,4},{6,7},{7,6},{8,9},{9,8},{10,11... | collective-permute-start | bytes 14155784 | tf_op jit(solution)/shard_map/ppermute | solution.py:30
  70.0 8.6 %collective-permute-start.24 = (bf16[2,16,3072]{2,1,0:T(8,128)(2,1)S(1)}, bf16[2,16,3072]{2,1,0:T(8,128)(2,1)S(1)}, u32[]{:S(2)}, u32[]{:S(2)}) collective-permute-start(bf16[2,16,3072]{2,1,0:T(8,128)(2,1)S(1)} %get-tuple-element.143), channel_id=1, source_target_pairs={{0,8},{1,9},{2,10},{3,11},{4,12},{5,13},{6,14},{7,15},{8,16},{9,17... | collective-permute-start | bytes 589832 | tf_op jit(solution)/shard_map/ppermute | solution.py:38
  74.4 5.8 %collective-permute-start.27 = (bf16[2,16,3072]{2,1,0:T(8,128)(2,1)S(1)}, bf16[2,16,3072]{2,1,0:T(8,128)(2,1)S(1)}, u32[]{:S(2)}, u32[]{:S(2)}) collective-permute-start(bf16[2,16,3072]{2,1,0:T(8,128)(2,1)S(1)} %get-tuple-element.151), channel_id=1, source_target_pairs={{0,24},{1,25},{2,26},{3,27},{4,28},{5,29},{6,30},{7,31},{8,0},{9,1... | collective-permute-start | bytes 589832 | tf_op jit(solution)/shard_map/ppermute | solution.py:38

commit v6 on v5

--- a/solution.py
+++ b/solution.py
@@ -16,8 +16,9 @@
 C_FIRST = LONG * 4 // 100
 C_LAST = LONG * 3 // 100
 C_PAIR_LAST = LONG // 100
-C_COPY = 0
+C_COPY = LONG // 5
 C_TURN = 0
+C_LOAD = LONG // 5
 PANEL = 512
 TURN = pltpu.VMEM((8, 128), jnp.float32)
 VMEM = pl.BlockSpec(memory_space=pltpu.VMEM)
@@ -83,7 +84,7 @@
 
 
 def pick_kernel(
-    place, token, count, gate, tokens, grad, w_gate, w_up, w_down, rows, weight, panels, turn,
+    place, token, count, gate, tokens, grad, rows, weight, turn,
     token_here, count_here, gate_here, tokens_here, grad_here, arrived,
 ):
     pairs = (
@@ -94,11 +95,7 @@
         (grad, grad_here),
     )
     copies = [pltpu.make_async_copy(*pair, arrived.at[i]) for i, pair in enumerate(pairs)]
-    loads = [
-        pltpu.make_async_copy(w, panels.at[i], arrived.at[len(pairs) + i])
-        for i, w in enumerate((w_gate, w_up, w_down))
-    ]
-    for copy in copies + loads:
+    for copy in copies:
         copy.start()
     turn[...] = jnp.zeros_like(turn)
     for copy in copies:
@@ -116,11 +113,9 @@
     chosen = jnp.where(lane == index[:, :1], 1.0, 0.0).astype(jnp.bfloat16)
     rows[0] = half(product(chosen, tokens_here[...]))
     rows[1] = half(scale[:, :1] * grad_here[...].astype(jnp.float32))
-    for copy in loads:
-        copy.wait()
-
-
-def pick(tokens, slot_token, slot_count, slot_gate, grad_out, weights):
+
+
+def pick(tokens, slot_token, slot_count, slot_gate, grad_out):
     capacity, width = grad_out.shape
     inputs = (slot_token, slot_count, slot_gate, tokens, grad_out)
     return pl.pallas_call(
@@ -128,18 +123,17 @@
         out_shape=(
             held((2, capacity, width)),
             held((capacity, 128), jnp.float32),
-            held((3, *weights[0].shape)),
             TURN,
         ),
-        in_specs=[SMEM] + [HBM] * 8,
-        out_specs=(VMEM,) * 4,
+        in_specs=[SMEM] + [HBM] * 5,
+        out_specs=(VMEM,) * 3,
         scratch_shapes=[pltpu.SMEM(v.shape, v.dtype) for v in inputs[:3]]
         + [pltpu.VMEM(v.shape, v.dtype) for v in inputs[3:]]
-        + [pltpu.SemaphoreType.DMA((8,))],
+        + [pltpu.SemaphoreType.DMA((5,))],
         compiler_params=limit(4),
         cost_estimate=cost(0, 0),
         name="pick",
-    )(lax.axis_index("dp")[None], *(in_hbm(v) for v in (*inputs, *weights)))
+    )(lax.axis_index("dp")[None], *(in_hbm(v) for v in inputs))
 
 
 def expert_kernel(sizes, *refs):
@@ -150,10 +144,11 @@
             cut = part[0].shape[0] // 4
             part = [part[0].at[i * cut : (i + 1) * cut] for i in range(4)]
         parts.append(part)
-    near, other, near_turned, other_turned, _, *refs = refs
+    near, other, (near_turned, other_turned, _) = refs[:3], refs[3:6], refs[6:9]
+    refs = refs[9:]
     x, e, hidden, gate_grad, up_grad, out_keep, out_send, row_keep, row_send, turn = refs
     turn[...] = jnp.zeros_like(turn)
-    units = near.shape[1]
+    units = near[0].shape[0]
     rows = x.shape[0] // 4
     size = rows // len(parts)
     for i, (x_pair, x_far, e_pair, e_far) in enumerate(parts):
@@ -177,16 +172,16 @@
         up_grad[:, mine] = half(hidden_grad * activated)
     for at in range(0, x.shape[1], PANEL):
         part = slice(at, at + PANEL)
-        out = product(hidden[:, :units], near[2, :, part]) + product(
-            hidden[:, units:], other[2, :, part]
+        out = product(hidden[:, :units], near[2][:, part]) + product(
+            hidden[:, units:], other[2][:, part]
         )
         out_keep[:, part] = out[: 2 * rows]
         out_send[:, part] = half(out[2 * rows :])
         row = (
-            product(gate_grad[:, :units], near[0, :, part])
-            + product(gate_grad[:, units:], other[0, :, part])
-            + product(up_grad[:, :units], near[1, :, part])
-            + product(up_grad[:, units:], other[1, :, part])
+            product(gate_grad[:, :units], near[0][:, part])
+            + product(gate_grad[:, units:], other[0][:, part])
+            + product(up_grad[:, :units], near[1][:, part])
+            + product(up_grad[:, units:], other[1][:, part])
         )
         row_keep[:rows, part] = row[:rows]
         row_keep[rows:, part] = row[2 * rows : 3 * rows]
@@ -197,7 +192,7 @@
 def expert(parts, panels, turn):
     rows = sum(ref.shape[0] for part in parts for ref in part) // 2
     width = parts[0][0].shape[1]
-    units = 2 * panels[0].shape[1]
+    units = 2 * panels[0].shape[0]
     saved, kept, sent = (
         held((rows, units)),
         held((rows // 2, width), jnp.float32),
@@ -206,7 +201,7 @@
     return pl.pallas_call(
         functools.partial(expert_kernel, [len(part) for part in parts]),
         out_shape=(held((rows, width)),) * 2 + (saved,) * 3 + (kept, sent, kept, sent, TURN),
-        in_specs=[VMEM] * (sum(len(part) for part in parts) + 5),
+        in_specs=[VMEM] * (sum(len(part) for part in parts) + 9),
         out_specs=(VMEM,) * 10,
         compiler_params=limit(12),
         cost_estimate=cost(12 * rows * units * width, 6 * units * width),
@@ -303,14 +298,18 @@
         out[rows:] = side[...]
 
 
-def first_pair_body(x, x_side, e, e_side, _, x_pair, e_pair):
+def first_pair_body(x, x_side, e, e_side, up, down, x_pair, e_pair, rows):
     pair_body(x, x_side, e, e_side, x_pair, e_pair)
-
-
-def turn_body(panels, turned):
-    for i in range(panels.shape[0]):
-        for at in range(0, panels.shape[2], PANEL):
-            turned[i, at : at + PANEL] = panels[i, :, at : at + PANEL].T
+    rows[0] = x[...]
+    rows[1] = e[...]
+
+
+def turn_body(*refs):
+    near, other, turned = refs[:3], refs[3:6], refs[6:]
+    for panels, into in zip((near, other), turned):
+        for i, panel in enumerate(panels):
+            for at in range(0, panel.shape[1], PANEL):
+                into[i, at : at + PANEL] = panel[:, at : at + PANEL].T
 
 
 def pack_body(x_pair, x_far, e_pair, e_far, plane):
@@ -319,8 +318,7 @@
         plane[i * rows : (i + 1) * rows] = part[...]
 
 
-def copy_body(rows, again, x, e):
-    again[...] = rows[...]
+def spread_body(rows, gate, x, e):
     x[...] = rows[0]
     e[...] = rows[1]
 
@@ -367,10 +365,8 @@
     weights = [w_gate, w_up, w_down]
     for bit in far_bits:
         weights = [jnp.concatenate([w, swapped(w, 1 << bit)], 0) for w in weights]
-    own, weight, near, turn = pick(
-        tokens, slot_token, slot_count, slot_gate, grad_out, weights
-    )
-    other = swapped(near, core)
+    own, weight, turn = pick(tokens, slot_token, slot_count, slot_gate, grad_out)
+    other = [swapped(w, core) for w in weights]
 
     width = own.shape[2]
     rows = 2 * capacity
@@ -383,13 +379,11 @@
 
     two = shifted(own, 2)
     one_level, two_levels = [held((capacity, width))] * 2, [held((rows, width))] * 2
-    own, x, e, turn = staged(
-        copy_body, "copy", [held(own.shape), *one_level], own, turn, flops=C_COPY
+    x, e, turn = staged(spread_body, "spread", one_level, own, other[0], turn, flops=C_COPY)
+    x, e, own, turn = staged(
+        first_pair_body, "pair_0", [*two_levels, held(own.shape)], *sides_of(x, e), *other[1:], turn
     )
     one = shifted(own, 1)
-    turned = held((near.shape[0], near.shape[2], near.shape[1]))
-    near_turned, turn = staged(turn_body, "turn_near", [turned], near, turn, flops=C_TURN)
-    x, e, turn = staged(first_pair_body, "pair_0", two_levels, *sides_of(x, e), other, turn)
     part_0 = fars_of(x, e)
     x, e, turn = staged(split_body, "split_2", one_level, two, turn, flops=C_FIRST)
     sides_2 = sides_of(x, e)
@@ -399,8 +393,11 @@
     part_2 = fars_of(x, e)
     x, e, turn = staged(split_body, "split_1", one_level, one, turn, flops=C_LAST)
     sides_1 = sides_of(x, e)
-    other_turned, turn = staged(turn_body, "turn_other", [turned], other, turn, flops=C_TURN)
-    panels = (near, other, near_turned, other_turned)
+    turned = held((3, *weights[0].shape[::-1]))
+    near_turned, other_turned, turn = staged(
+        turn_body, "turn_panels", [turned] * 2, *weights, *other, turn, flops=C_TURN
+    )
+    panels = (*weights, *other, near_turned, other_turned)
     x, e, turn = staged(pair_body, "pair_1", two_levels, *sides_1, turn, flops=C_PAIR_LAST)
     part_1 = fars_of(x, e)
 

time: 81.1 us -> 79.7 us (0.983)
  waiting for transfers between devices: 31.6 us -> 23.7 us
  starting transfers between devices: 30.5 us -> 38.4 us
  Pallas kernels: 18 us -> 16.6 us
    ppermute x6, waiting for transfers between devices: 11.4 us -> 3.19 us  [shifted(): return lax.ppermute(block, 'dp', route)]
    ppermute x6, starting transfers between devices: 6.5 us -> 14.1 us  [shifted(): return lax.ppermute(block, 'dp', route)]
    pallas_call x1, Pallas kernels: 2.71 us -> 1.41 us  [pick(): pl.pallas_call(pick_kernel, out_shape=(held((2, capacity, width)), held((...]
    ppermute x22 -> x24, waiting for transfers between devices: 20.2 us -> 20.5 us  [swapped(): lax.ppermute(block, 'dp', [(low, low ^ mask) for low in range(count)])]
    ppermute x22 -> x24, starting transfers between devices: 24 us -> 24.2 us  [swapped(): lax.ppermute(block, 'dp', [(low, low ^ mask) for low in range(count)])]
    pallas_call x16 -> x15, Pallas kernels: 3.95 us -> 3.88 us  [staged(): pl.pallas_call(kernel, out_shape=(*outs, TURN), in_specs=[VMEM] * len(val...]
  transfers between devices with their start and end apart: 28 -> 30, of which waited for: 16 -> 15; matrix products, arithmetic and copies ran while one was open for 0% -> 0% of each run, Pallas kernels for 18% -> 20%
where the time goes in v6:
time: 79.7 us; the launch traced here: 79.5 us
  starting transfers between devices  38.4 us (48%)
  waiting for transfers between devices  23.7 us (30%)
  Pallas kernels  16.6 us (21%)
    ppermute x24, starting transfers between devices, swapped(): lax.ppermute(block, 'dp', [(low, low ^ mask) for low in range(count)])  24.2 us
    ppermute x24, waiting for transfers between devices, swapped(): lax.ppermute(block, 'dp', [(low, low ^ mask) for low in range(count)])  20.5 us
    ppermute x6, starting transfers between devices, shifted(): return lax.ppermute(block, 'dp', route)  14.1 us
    pallas_call x2, Pallas kernels, expert(): pl.pallas_call(functools.partial(expert_kernel, [len(part) for part in pa...  5.83 us
    pallas_call x1, Pallas kernels, own_grads(): pl.pallas_call(functools.partial(own_kernel, factor), grid=(width // PANE...  4.07 us
    pallas_call x15, Pallas kernels, staged(): pl.pallas_call(kernel, out_shape=(*outs, TURN), in_specs=[VMEM] * len(val...  3.88 us
    ppermute x6, waiting for transfers between devices, shifted(): return lax.ppermute(block, 'dp', route)  3.19 us
  transfers between devices with their start and end apart: 30, of which 15 were waited for; matrix products, arithmetic and copies ran while one was open for 0% of the time, Pallas kernels for 20%

profile of v6, /device:TPU:0, one launch (start us, length us, event | category | flops | bytes accessed | tf_op | source)
XLA Modules:
  0.0 79.5 jit_solution(12760115543786637634)
XLA Ops:
  0.6 0.5 collective-permute-start
  1.2 1.4 %pick.1 = (bf16[2,16,3072]{2,1,0:T(8,128)(2,1)S(1)}, f32[16,128]{1,0:T(8,128)S(1)}, f32[8,128]{1,0:T(8,128)S(1)}) custom-call(s32[1]{0:T(128)} %bitcast.place, s32[16]{0:T(128)} %token_.1, s32[32]{0:T(128)} %count.1, f32[16]{0:T(128)} %gate.1, bf16[128,3072]{1,0:T(8,128)(2,1)} %tokens.1, bf16[16,3072]{1,0:T(8,128)(2,1)} %grad.1), custom_call_target="tpu_custom_call" | custom-call | tf_op jit(solution)/shard_map/pick/pallas_call | solution.py:121
  2.6 3.7 %collective-permute-start.7 = (bf16[2,16,3072]{2,1,0:T(8,128)(2,1)S(1)}, bf16[2,16,3072]{2,1,0:T(8,128)(2,1)S(1)}, u32[]{:S(2)}, u32[]{:S(2)}) collective-permute-start(bf16[2,16,3072]{2,1,0:T(8,128)(2,1)S(1)} %get-tuple-element.80.refs_0_), channel_id=1, source_target_pairs={{0,16},{1,17},{2,18},{3,19},{4,20},{5,21},{6,22},{7,23},{8,24},{9,... | collective-permute-start | bytes 589832 | tf_op jit(solution)/shard_map/ppermute | solution.py:39
  6.2 0.2 collective-permute-start.3
  6.5 0.3 collective-permute-start.4
  6.8 1.6 %collective-permute-start.1 = (bf16[16,3072]{1,0:T(8,128)(2,1)S(1)}, bf16[16,3072]{1,0:T(8,128)(2,1)S(1)}, u32[]{:S(2)}, u32[]{:S(2)}) collective-permute-start(bf16[16,3072]{1,0:T(8,128)(2,1)S(1)} %get-tuple-element.82.refs_0_), channel_id=1, source_target_pairs={{0,2},{1,3},{2,0},{3,1},{4,6},{5,7},{6,4},{7,5},{8,10},{9,11},{10,... | collective-permute-start | bytes 294920 | tf_op jit(solution)/shard_map/ppermute | solution.py:31
  8.3 1.5 %collective-permute-start.2 = (bf16[16,3072]{1,0:T(8,128)(2,1)S(1)}, bf16[16,3072]{1,0:T(8,128)(2,1)S(1)}, u32[]{:S(2)}, u32[]{:S(2)}) collective-permute-start(bf16[16,3072]{1,0:T(8,128)(2,1)S(1)} %get-tuple-element.83.refs_2_), channel_id=1, source_target_pairs={{0,4},{1,5},{2,6},{3,7},{4,0},{5,1},{6,2},{7,3},{8,12},{9,13},{10,... | collective-permute-start | bytes 294920 | tf_op jit(solution)/shard_map/ppermute | solution.py:31
  9.9 2.2 %collective-permute-done.4.refs_5_.refs_13_.refs_10_ = bf16[256,3072]{1,0:T(8,128)(2,1)S(1)} collective-permute-done((bf16[256,3072]{1,0:T(8,128)(2,1)}, bf16[256,3072]{1,0:T(8,128)(2,1)S(1)}, u32[]{:S(2)}, u32[]{:S(2)}) %collective-permute-start.4) | collective-permute-done | bytes 1572896 | tf_op jit(solution)/shard_map/ppermute | solution.py:31
  12.1 0.8 %collective-permute-done.2.refs_3_ = bf16[16,3072]{1,0:T(8,128)(2,1)S(1)} collective-permute-done((bf16[16,3072]{1,0:T(8,128)(2,1)S(1)}, bf16[16,3072]{1,0:T(8,128)(2,1)S(1)}, u32[]{:S(2)}, u32[]{:S(2)}) %collective-permute-start.2) | collective-permute-done | bytes 98336 | tf_op jit(solution)/shard_map/ppermute | solution.py:31
  13.0 1.6 %collective-permute-start.12 = (bf16[2,16,3072]{2,1,0:T(8,128)(2,1)S(1)}, bf16[2,16,3072]{2,1,0:T(8,128)(2,1)S(1)}, u32[]{:S(2)}, u32[]{:S(2)}) collective-permute-start(bf16[2,16,3072]{2,1,0:T(8,128)(2,1)S(1)} %get-tuple-element.94), channel_id=1, source_target_pairs={{0,8},{1,9},{2,10},{3,11},{4,12},{5,13},{6,14},{7,15},{8,16},{9,17... | collective-permute-start | bytes 589832 | tf_op jit(solution)/shard_map/ppermute | solution.py:39
  14.6 1.5 %collective-permute-start.5 = (bf16[32,3072]{1,0:T(8,128)(2,1)S(1)}, bf16[32,3072]{1,0:T(8,128)(2,1)S(1)}, u32[]{:S(2)}, u32[]{:S(2)}) collective-permute-start(bf16[32,3072]{1,0:T(8,128)(2,1)S(1)} %get-tuple-element.85.refs_0_), channel_id=1, source_target_pairs={{0,4},{1,5},{2,6},{3,7},{4,0},{5,1},{6,2},{7,3},{8,12},{9,13},{10,... | collective-permute-start | bytes 589832 | tf_op jit(solution)/shard_map/ppermute | solution.py:31
  16.2 0.7 collective-permute-start.6
  16.8 1.4 %collective-permute-start.8 = (bf16[16,3072]{1,0:T(8,128)(2,1)S(1)}, bf16[16,3072]{1,0:T(8,128)(2,1)S(1)}, u32[]{:S(2)}, u32[]{:S(2)}) collective-permute-start(bf16[16,3072]{1,0:T(8,128)(2,1)S(1)} %get-tuple-element.88.refs_0_), channel_id=1, source_target_pairs={{0,2},{1,3},{2,0},{3,1},{4,6},{5,7},{6,4},{7,5},{8,10},{9,11},{10,... | collective-permute-start | bytes 294920 | tf_op jit(solution)/shard_map/ppermute | solution.py:31
  18.3 0.9 %collective-permute-start.9 = (bf16[16,3072]{1,0:T(8,128)(2,1)S(1)}, bf16[16,3072]{1,0:T(8,128)(2,1)S(1)}, u32[]{:S(2)}, u32[]{:S(2)}) collective-permute-start(bf16[16,3072]{1,0:T(8,128)(2,1)S(1)} %get-tuple-element.89.refs_2_), channel_id=1, source_target_pairs={{0,4},{1,5},{2,6},{3,7},{4,0},{5,1},{6,2},{7,3},{8,12},{9,13},{10,... | collective-permute-start | bytes 294920 | tf_op jit(solution)/shard_map/ppermute | solution.py:31
  19.2 2.2 %collective-permute-done.5.refs_1_ = bf16[32,3072]{1,0:T(8,128)(2,1)S(1)} collective-permute-done((bf16[32,3072]{1,0:T(8,128)(2,1)S(1)}, bf16[32,3072]{1,0:T(8,128)(2,1)S(1)}, u32[]{:S(2)}, u32[]{:S(2)}) %collective-permute-start.5) | collective-permute-done | bytes 196640 | tf_op jit(solution)/shard_map/ppermute | solution.py:31
  21.3 1.5 %collective-permute-done.6.refs_3_ = bf16[32,3072]{1,0:T(8,128)(2,1)S(1)} collective-permute-done((bf16[32,3072]{1,0:T(8,128)(2,1)S(1)}, bf16[32,3072]{1,0:T(8,128)(2,1)S(1)}, u32[]{:S(2)}, u32[]{:S(2)}) %collective-permute-start.6) | collective-permute-done | bytes 196640 | tf_op jit(solution)/shard_map/ppermute | solution.py:31
  22.9 2.4 %collective-permute-start.19 = (bf16[128,3072]{1,0:T(8,128)(2,1)S(1)}, bf16[128,3072]{1,0:T(8,128)(2,1)S(1)}, u32[]{:S(2)}, u32[]{:S(2)}) collective-permute-start(bf16[128,3072]{1,0:T(8,128)(2,1)S(1)} %get-tuple-element.109), channel_id=1, source_target_pairs={{0,24},{1,25},{2,26},{3,27},{4,28},{5,29},{6,30},{7,31},{8,0},{9,1... | collective-permute-start | bytes 2359304 | tf_op jit(solution)/shard_map/ppermute | solution.py:39
  25.3 0.2 collective-permute-start.10
  25.5 1.4 %collective-permute-start.11 = (bf16[32,3072]{1,0:T(8,128)(2,1)S(1)}, bf16[32,3072]{1,0:T(8,128)(2,1)S(1)}, u32[]{:S(2)}, u32[]{:S(2)}) collective-permute-start(bf16[32,3072]{1,0:T(8,128)(2,1)S(1)} %get-tuple-element.93.refs_6_), channel_id=1, source_target_pairs={{0,2},{1,3},{2,0},{3,1},{4,6},{5,7},{6,4},{7,5},{8,10},{9,11},{10,... | collective-permute-start | bytes 589832 | tf_op jit(solution)/shard_map/ppermute | solution.py:31
  26.9 0.7 collective-permute-start.13
  27.6 1.9 %collective-permute-start.14 = (bf16[16,3072]{1,0:T(8,128)(2,1)S(1)}, bf16[16,3072]{1,0:T(8,128)(2,1)S(1)}, u32[]{:S(2)}, u32[]{:S(2)}) collective-permute-start(bf16[16,3072]{1,0:T(8,128)(2,1)S(1)} %get-tuple-element.100.refs_2_), channel_id=1, source_target_pairs={{0,4},{1,5},{2,6},{3,7},{4,0},{5,1},{6,2},{7,3},{8,12},{9,13},{10,... | collective-permute-start | bytes 294920 | tf_op jit(solution)/shard_map/ppermute | solution.py:31
  29.5 2.5 %turn_panels.1 = (bf16[3,3072,256]{2,1,0:T(8,128)(2,1)S(1)}, bf16[3,3072,256]{2,1,0:T(8,128)(2,1)S(1)}, f32[8,128]{1,0:T(8,128)S(1)}) custom-call(bf16[256,3072]{1,0:T(8,128)(2,1)S(1)} %copy-done, bf16[256,3072]{1,0:T(8,128)(2,1)S(1)} %copy-done.1, bf16[256,3072]{1,0:T(8,128)(2,1)S(1)} %copy-done.2, ...), custom_call_target="tpu_custom_call" | custom-call | tf_op jit(solution)/shard_map/turn_panels/pallas_call | solution.py:275
  32.0 0.2 collective-permute-done.13.refs_1_
  32.2 0.4 collective-permute-done.14.refs_3_
  32.7 2.4 %collective-permute-start.17 = (bf16[32,3072]{1,0:T(8,128)(2,1)S(1)}, bf16[32,3072]{1,0:T(8,128)(2,1)S(1)}, u32[]{:S(2)}, u32[]{:S(2)}) collective-permute-start(bf16[32,3072]{1,0:T(8,128)(2,1)S(1)} %get-tuple-element.107.refs_0_), channel_id=1, source_target_pairs={{0,4},{1,5},{2,6},{3,7},{4,0},{5,1},{6,2},{7,3},{8,12},{9,13},{10,... | collective-permute-start | bytes 589832 | tf_op jit(solution)/shard_map/ppermute | solution.py:31
  35.1 1.3 %collective-permute-start.18 = (bf16[32,3072]{1,0:T(8,128)(2,1)S(1)}, bf16[32,3072]{1,0:T(8,128)(2,1)S(1)}, u32[]{:S(2)}, u32[]{:S(2)}) collective-permute-start(bf16[32,3072]{1,0:T(8,128)(2,1)S(1)} %get-tuple-element.108.refs_2_), channel_id=1, source_target_pairs={{0,2},{1,3},{2,0},{3,1},{4,6},{5,7},{6,4},{7,5},{8,10},{9,11},{10,... | collective-permute-start | bytes 589832 | tf_op jit(solution)/shard_map/ppermute | solution.py:31
  36.4 2.9 %expert.2 = (bf16[128,3072]{1,0:T(8,128)(2,1)S(1)}, bf16[128,3072]{1,0:T(8,128)(2,1)S(1)}, bf16[128,512]{1,0:T(8,128)(2,1)S(1)}, bf16[128,512]{1,0:T(8,128)(2,1)...) custom-call(bf16[32,3072]{1,0:T(8,128)(2,1)S(1)} %get-tuple-element., ...), custom_call_target="tpu_custom_call" | custom-call | flops 2415919104 | bytes 9437184 | tf_op jit(solution)/shard_map/expert/pallas_call | solution.py:201
  39.3 0.2 collective-permute-start.15
  39.5 0.7 collective-permute-start.16
  40.2 0.2 collective-permute-done.17.refs_1_
  40.4 2.5 %collective-permute-done.18.refs_3_ = bf16[32,3072]{1,0:T(8,128)(2,1)S(1)} collective-permute-done((bf16[32,3072]{1,0:T(8,128)(2,1)S(1)}, bf16[32,3072]{1,0:T(8,128)(2,1)S(1)}, u32[]{:S(2)}, u32[]{:S(2)}) %collective-permute-start.18) | collective-permute-done | bytes 196640 | tf_op jit(solution)/shard_map/ppermute | solution.py:31
  42.9 2.9 %expert.3 = (bf16[128,3072]{1,0:T(8,128)(2,1)S(1)}, bf16[128,3072]{1,0:T(8,128)(2,1)S(1)}, bf16[128,512]{1,0:T(8,128)(2,1)S(1)}, bf16[128,512]{1,0:T(8,128)(2,1)...) custom-call(bf16[32,3072]{1,0:T(8,128)(2,1)S(1)} %get-tuple-element., ...), custom_call_target="tpu_custom_call" | custom-call | flops 2415919104 | bytes 9437184 | tf_op jit(solution)/shard_map/expert/pallas_call | solution.py:201
  45.9 1.4 %collective-permute-start.23 = (bf16[64,3072]{1,0:T(8,128)(2,1)S(1)}, bf16[64,3072]{1,0:T(8,128)(2,1)S(1)}, u32[]{:S(2)}, u32[]{:S(2)}) collective-permute-start(bf16[64,3072]{1,0:T(8,128)(2,1)S(1)} %get-tuple-element.119), channel_id=1, source_target_pairs={{0,2},{1,3},{2,0},{3,1},{4,6},{5,7},{6,4},{7,5},{8,10},{9,11},{10,... | collective-permute-start | bytes 1179656 | tf_op jit(solution)/shard_map/ppermute | solution.py:31
  47.3 4.1 %collective-permute-done.15.refs_1_ = bf16[64,3072]{1,0:T(8,128)(2,1)S(1)} collective-permute-done((bf16[64,3072]{1,0:T(8,128)(2,1)S(1)}, bf16[64,3072]{1,0:T(8,128)(2,1)S(1)}, u32[]{:S(2)}, u32[]{:S(2)}) %collective-permute-start.15) | collective-permute-done | bytes 393248 | tf_op jit(solution)/shard_map/ppermute | solution.py:31
  51.7 1.0 %collective-permute-start.20 = (bf16[32,3072]{1,0:T(8,128)(2,1)S(1)}, bf16[32,3072]{1,0:T(8,128)(2,1)S(1)}, u32[]{:S(2)}, u32[]{:S(2)}) collective-permute-start(bf16[32,3072]{1,0:T(8,128)(2,1)S(1)} %get-tuple-element.113), channel_id=1, source_target_pairs={{0,2},{1,3},{2,0},{3,1},{4,6},{5,7},{6,4},{7,5},{8,10},{9,11},{10,... | collective-permute-start | bytes 589832 | tf_op jit(solution)/shard_map/ppermute | solution.py:31
  52.7 1.6 %collective-permute-start.21 = (bf16[32,3072]{1,0:T(8,128)(2,1)S(1)}, bf16[32,3072]{1,0:T(8,128)(2,1)S(1)}, u32[]{:S(2)}, u32[]{:S(2)}) collective-permute-start(bf16[32,3072]{1,0:T(8,128)(2,1)S(1)} %get-tuple-element.115), channel_id=1, source_target_pairs={{0,4},{1,5},{2,6},{3,7},{4,0},{5,1},{6,2},{7,3},{8,12},{9,13},{10,... | collective-permute-start | bytes 589832 | tf_op jit(solution)/shard_map/ppermute | solution.py:31
  54.4 1.5 %other_grads.1 = (bf16[3,256,3072]{2,1,0:T(8,128)(2,1)S(1)}, f32[8,128]{1,0:T(8,128)S(1)}) custom-call(bf16[128,3072]{1,0:T(8,128)(2,1)S(1)} %get-tuple-element.120.refs_0_, bf16[128,3072]{1,0:T(8,128)(2,1)S(1)} %get-tuple-element.121.refs_1_, bf16[128,512]{1,0:T(8,128)(2,1)S(1)} %get-tuple-element.122.refs_2_, ...), custom_call_target="tpu_custom_call" | custom-call | flops 2000000000 | tf_op jit(solution)/shard_map/other_grads/pallas_call | solution.py:234
  55.8 3.8 %collective-permute-done.22.refs_1_ = bf16[64,3072]{1,0:T(8,128)(2,1)S(1)} collective-permute-done((bf16[64,3072]{1,0:T(8,128)(2,1)S(1)}, bf16[64,3072]{1,0:T(8,128)(2,1)S(1)}, u32[]{:S(2)}, u32[]{:S(2)}) %collective-permute-start.22) | collective-permute-done | bytes 393248 | tf_op jit(solution)/shard_map/ppermute | solution.py:31
  59.6 0.4 collective-permute-done.23.refs_3_
  60.1 1.0 %collective-permute-start.24 = (bf16[32,3072]{1,0:T(8,128)(2,1)S(1)}, bf16[32,3072]{1,0:T(8,128)(2,1)S(1)}, u32[]{:S(2)}, u32[]{:S(2)}) collective-permute-start(bf16[32,3072]{1,0:T(8,128)(2,1)S(1)} %get-tuple-element.135), channel_id=1, source_target_pairs={{0,2},{1,3},{2,0},{3,1},{4,6},{5,7},{6,4},{7,5},{8,10},{9,11},{10,... | collective-permute-start | bytes 589832 | tf_op jit(solution)/shard_map/ppermute | solution.py:31
  61.1 1.6 %collective-permute-start.25 = (bf16[32,3072]{1,0:T(8,128)(2,1)S(1)}, bf16[32,3072]{1,0:T(8,128)(2,1)S(1)}, u32[]{:S(2)}, u32[]{:S(2)}) collective-permute-start(bf16[32,3072]{1,0:T(8,128)(2,1)S(1)} %get-tuple-element.137), channel_id=1, source_target_pairs={{0,4},{1,5},{2,6},{3,7},{4,0},{5,1},{6,2},{7,3},{8,12},{9,13},{10,... | collective-permute-start | bytes 589832 | tf_op jit(solution)/shard_map/ppermute | solution.py:31
  62.9 2.0 %collective-permute-start.28 = (bf16[2,16,3072]{2,1,0:T(8,128)(2,1)S(1)}, bf16[2,16,3072]{2,1,0:T(8,128)(2,1)S(1)}, u32[]{:S(2)}, u32[]{:S(2)}) collective-permute-start(bf16[2,16,3072]{2,1,0:T(8,128)(2,1)S(1)} %get-tuple-element.142), channel_id=1, source_target_pairs={{0,24},{1,25},{2,26},{3,27},{4,28},{5,29},{6,30},{7,31},{8,0},{9,1... | collective-permute-start | bytes 589832 | tf_op jit(solution)/shard_map/ppermute | solution.py:39
  64.9 1.0 %collective-permute-done.24.refs_1_ = bf16[32,3072]{1,0:T(8,128)(2,1)S(1)} collective-permute-done((bf16[32,3072]{1,0:T(8,128)(2,1)S(1)}, bf16[32,3072]{1,0:T(8,128)(2,1)S(1)}, u32[]{:S(2)}, u32[]{:S(2)}) %collective-permute-start.24) | collective-permute-done | bytes 196640 | tf_op jit(solution)/shard_map/ppermute | solution.py:31
  65.8 1.0 %collective-permute-done.25.refs_3_ = bf16[32,3072]{1,0:T(8,128)(2,1)S(1)} collective-permute-done((bf16[32,3072]{1,0:T(8,128)(2,1)S(1)}, bf16[32,3072]{1,0:T(8,128)(2,1)S(1)}, u32[]{:S(2)}, u32[]{:S(2)}) %collective-permute-start.25) | collective-permute-done | bytes 196640 | tf_op jit(solution)/shard_map/ppermute | solution.py:31
  67.0 3.2 %collective-permute-done.28.refs_1_ = bf16[2,16,3072]{2,1,0:T(8,128)(2,1)S(1)} collective-permute-done((bf16[2,16,3072]{2,1,0:T(8,128)(2,1)S(1)}, bf16[2,16,3072]{2,1,0:T(8,128)(2,1)S(1)}, u32[]{:S(2)}, u32[]{:S(2)}) %collective-permute-start.28) | collective-permute-done | bytes 196640 | tf_op jit(solution)/shard_map/ppermute | solution.py:39
  70.2 4.4 %collective-permute-start.29 = (bf16[2,16,3072]{2,1,0:T(8,128)(2,1)S(1)}, bf16[2,16,3072]{2,1,0:T(8,128)(2,1)S(1)}, u32[]{:S(2)}, u32[]{:S(2)}) collective-permute-start(bf16[2,16,3072]{2,1,0:T(8,128)(2,1)S(1)} %get-tuple-element.147), channel_id=1, source_target_pairs={{0,24},{1,25},{2,26},{3,27},{4,28},{5,29},{6,30},{7,31},{8,0},{9,1... | collective-permute-start | bytes 589832 | tf_op jit(solution)/shard_map/ppermute | solution.py:39
  74.6 4.1 %own_grads.1 = (bf16[256,3072]{1,0:T(8,128)(2,1)}, bf16[256,3072]{1,0:T(8,128)(2,1)}, bf16[256,3072]{1,0:T(8,128)(2,1)}, f32[8,128]{1,0:T(8,128)S(1)}) custom-call(bf16[128,3072]{1,0:T(8,128)(2,1)S(1)} %get-tuple-element.120.refs_0_, bf16[128,3072]{1,0:T(8,128)(2,1)S(1)} %get-tuple-element.121.refs_1_, bf16[128,512]{1,0:T(8,128)(2,1)S(1)} %get-tuple-element.122.refs_2_, ...), custom_call_target="tpu_custom_call" | custom-call | tf_op jit(solution)/shard_map/own_grads/pallas_call | solution.py:258
  78.8 0.7 final.1
  (38 shorter events, 1.0 us)
Async XLA Ops:
  0.6 6.1 %collective-permute-start = (bf16[256,3072]{1,0:T(8,128)(2,1)}, bf16[256,3072]{1,0:T(8,128)(2,1)S(1)}, u32[]{:S(2)}, u32[]{:S(2)}) collective-permute-start(bf16[256,3072]{1,0:T(8,128)(2,1)} %refs_5_.1), channel_id=1, source_target_pairs={{0,1},{1,0},{2,3},{3,2},{4,5},{5,4},{6,7},{7,6},{8,9},{9,8},{10,11... | collective-permute-start | bytes 4718600 | tf_op jit(solution)/shard_map/ppermute | solution.py:31
  2.6 14.2 %collective-permute-start.7 = (bf16[2,16,3072]{2,1,0:T(8,128)(2,1)S(1)}, bf16[2,16,3072]{2,1,0:T(8,128)(2,1)S(1)}, u32[]{:S(2)}, u32[]{:S(2)}) collective-permute-start(bf16[2,16,3072]{2,1,0:T(8,128)(2,1)S(1)} %get-tuple-element.80.refs_0_), channel_id=1, source_target_pairs={{0,16},{1,17},{2,18},{3,19},{4,20},{5,21},{6,22},{7,23},{8,24},{9,... | collective-permute-start | bytes 589832 | tf_op jit(solution)/shard_map/ppermute | solution.py:39
  6.2 3.6 %collective-permute-start.3 = (bf16[256,3072]{1,0:T(8,128)(2,1)}, bf16[256,3072]{1,0:T(8,128)(2,1)S(1)}, u32[]{:S(2)}, u32[]{:S(2)}) collective-permute-start(bf16[256,3072]{1,0:T(8,128)(2,1)} %refs_6_.1), channel_id=1, source_target_pairs={{0,1},{1,0},{2,3},{3,2},{4,5},{5,4},{6,7},{7,6},{8,9},{9,8},{10,11... | collective-permute-start | bytes 4718600 | tf_op jit(solution)/shard_map/ppermute | solution.py:31
  6.5 5.7 %collective-permute-start.4 = (bf16[256,3072]{1,0:T(8,128)(2,1)}, bf16[256,3072]{1,0:T(8,128)(2,1)S(1)}, u32[]{:S(2)}, u32[]{:S(2)}) collective-permute-start(bf16[256,3072]{1,0:T(8,128)(2,1)} %refs_7_.1), channel_id=1, source_target_pairs={{0,1},{1,0},{2,3},{3,2},{4,5},{5,4},{6,7},{7,6},{8,9},{9,8},{10,11... | collective-permute-start | bytes 4718600 | tf_op jit(solution)/shard_map/ppermute | solution.py:31
  6.8 5.3 %collective-permute-start.1 = (bf16[16,3072]{1,0:T(8,128)(2,1)S(1)}, bf16[16,3072]{1,0:T(8,128)(2,1)S(1)}, u32[]{:S(2)}, u32[]{:S(2)}) collective-permute-start(bf16[16,3072]{1,0:T(8,128)(2,1)S(1)} %get-tuple-element.82.refs_0_), channel_id=1, source_target_pairs={{0,2},{1,3},{2,0},{3,1},{4,6},{5,7},{6,4},{7,5},{8,10},{9,11},{10,... | collective-permute-start | bytes 294920 | tf_op jit(solution)/shard_map/ppermute | solution.py:31
  8.3 4.6 %collective-permute-start.2 = (bf16[16,3072]{1,0:T(8,128)(2,1)S(1)}, bf16[16,3072]{1,0:T(8,128)(2,1)S(1)}, u32[]{:S(2)}, u32[]{:S(2)}) collective-permute-start(bf16[16,3072]{1,0:T(8,128)(2,1)S(1)} %get-tuple-element.83.refs_2_), channel_id=1, source_target_pairs={{0,4},{1,5},{2,6},{3,7},{4,0},{5,1},{6,2},{7,3},{8,12},{9,13},{10,... | collective-permute-start | bytes 294920 | tf_op jit(solution)/shard_map/ppermute | solution.py:31
  13.0 13.9 %collective-permute-start.12 = (bf16[2,16,3072]{2,1,0:T(8,128)(2,1)S(1)}, bf16[2,16,3072]{2,1,0:T(8,128)(2,1)S(1)}, u32[]{:S(2)}, u32[]{:S(2)}) collective-permute-start(bf16[2,16,3072]{2,1,0:T(8,128)(2,1)S(1)} %get-tuple-element.94), channel_id=1, source_target_pairs={{0,8},{1,9},{2,10},{3,11},{4,12},{5,13},{6,14},{7,15},{8,16},{9,17... | collective-permute-start | bytes 589832 | tf_op jit(solution)/shard_map/ppermute | solution.py:39
  14.6 6.7 %collective-permute-start.5 = (bf16[32,3072]{1,0:T(8,128)(2,1)S(1)}, bf16[32,3072]{1,0:T(8,128)(2,1)S(1)}, u32[]{:S(2)}, u32[]{:S(2)}) collective-permute-start(bf16[32,3072]{1,0:T(8,128)(2,1)S(1)} %get-tuple-element.85.refs_0_), channel_id=1, source_target_pairs={{0,4},{1,5},{2,6},{3,7},{4,0},{5,1},{6,2},{7,3},{8,12},{9,13},{10,... | collective-permute-start | bytes 589832 | tf_op jit(solution)/shard_map/ppermute | solution.py:31
  16.2 6.7 %collective-permute-start.6 = (bf16[32,3072]{1,0:T(8,128)(2,1)S(1)}, bf16[32,3072]{1,0:T(8,128)(2,1)S(1)}, u32[]{:S(2)}, u32[]{:S(2)}) collective-permute-start(bf16[32,3072]{1,0:T(8,128)(2,1)S(1)} %get-tuple-element.86.refs_2_), channel_id=1, source_target_pairs={{0,2},{1,3},{2,0},{3,1},{4,6},{5,7},{6,4},{7,5},{8,10},{9,11},{10,... | collective-permute-start | bytes 589832 | tf_op jit(solution)/shard_map/ppermute | solution.py:31
  16.8 8.4 %collective-permute-start.8 = (bf16[16,3072]{1,0:T(8,128)(2,1)S(1)}, bf16[16,3072]{1,0:T(8,128)(2,1)S(1)}, u32[]{:S(2)}, u32[]{:S(2)}) collective-permute-start(bf16[16,3072]{1,0:T(8,128)(2,1)S(1)} %get-tuple-element.88.refs_0_), channel_id=1, source_target_pairs={{0,2},{1,3},{2,0},{3,1},{4,6},{5,7},{6,4},{7,5},{8,10},{9,11},{10,... | collective-permute-start | bytes 294920 | tf_op jit(solution)/shard_map/ppermute | solution.py:31
  18.3 7.0 %collective-permute-start.9 = (bf16[16,3072]{1,0:T(8,128)(2,1)S(1)}, bf16[16,3072]{1,0:T(8,128)(2,1)S(1)}, u32[]{:S(2)}, u32[]{:S(2)}) collective-permute-start(bf16[16,3072]{1,0:T(8,128)(2,1)S(1)} %get-tuple-element.89.refs_2_), channel_id=1, source_target_pairs={{0,4},{1,5},{2,6},{3,7},{4,0},{5,1},{6,2},{7,3},{8,12},{9,13},{10,... | collective-permute-start | bytes 294920 | tf_op jit(solution)/shard_map/ppermute | solution.py:31
  22.9 20.0 %collective-permute-start.19 = (bf16[128,3072]{1,0:T(8,128)(2,1)S(1)}, bf16[128,3072]{1,0:T(8,128)(2,1)S(1)}, u32[]{:S(2)}, u32[]{:S(2)}) collective-permute-start(bf16[128,3072]{1,0:T(8,128)(2,1)S(1)} %get-tuple-element.109), channel_id=1, source_target_pairs={{0,24},{1,25},{2,26},{3,27},{4,28},{5,29},{6,30},{7,31},{8,0},{9,1... | collective-permute-start | bytes 2359304 | tf_op jit(solution)/shard_map/ppermute | solution.py:39
  25.3 11.1 %collective-permute-start.10 = (bf16[32,3072]{1,0:T(8,128)(2,1)S(1)}, bf16[32,3072]{1,0:T(8,128)(2,1)S(1)}, u32[]{:S(2)}, u32[]{:S(2)}) collective-permute-start(bf16[32,3072]{1,0:T(8,128)(2,1)S(1)} %get-tuple-element.92.refs_4_), channel_id=1, source_target_pairs={{0,4},{1,5},{2,6},{3,7},{4,0},{5,1},{6,2},{7,3},{8,12},{9,13},{10,... | collective-permute-start | bytes 589832 | tf_op jit(solution)/shard_map/ppermute | solution.py:31
  25.5 11.0 %collective-permute-start.11 = (bf16[32,3072]{1,0:T(8,128)(2,1)S(1)}, bf16[32,3072]{1,0:T(8,128)(2,1)S(1)}, u32[]{:S(2)}, u32[]{:S(2)}) collective-permute-start(bf16[32,3072]{1,0:T(8,128)(2,1)S(1)} %get-tuple-element.93.refs_6_), channel_id=1, source_target_pairs={{0,2},{1,3},{2,0},{3,1},{4,6},{5,7},{6,4},{7,5},{8,10},{9,11},{10,... | collective-permute-start | bytes 589832 | tf_op jit(solution)/shard_map/ppermute | solution.py:31
  26.9 2.6 %copy-start = (bf16[256,3072]{1,0:T(8,128)(2,1)S(1)}, bf16[256,3072]{1,0:T(8,128)(2,1)}, u32[]{:S(2)}) copy-start(bf16[256,3072]{1,0:T(8,128)(2,1)} %refs_5_.1) | copy-start | bytes 4718596
  26.9 2.6 %copy-start.1 = (bf16[256,3072]{1,0:T(8,128)(2,1)S(1)}, bf16[256,3072]{1,0:T(8,128)(2,1)}, u32[]{:S(2)}) copy-start(bf16[256,3072]{1,0:T(8,128)(2,1)} %refs_6_.1) | copy-start | bytes 4718596
  26.9 2.6 %copy-start.2 = (bf16[256,3072]{1,0:T(8,128)(2,1)S(1)}, bf16[256,3072]{1,0:T(8,128)(2,1)}, u32[]{:S(2)}) copy-start(bf16[256,3072]{1,0:T(8,128)(2,1)} %refs_7_.1) | copy-start | bytes 4718596
  26.9 5.3 %collective-permute-start.13 = (bf16[16,3072]{1,0:T(8,128)(2,1)S(1)}, bf16[16,3072]{1,0:T(8,128)(2,1)S(1)}, u32[]{:S(2)}, u32[]{:S(2)}) collective-permute-start(bf16[16,3072]{1,0:T(8,128)(2,1)S(1)} %get-tuple-element.99.refs_0_), channel_id=1, source_target_pairs={{0,2},{1,3},{2,0},{3,1},{4,6},{5,7},{6,4},{7,5},{8,10},{9,11},{10,... | collective-permute-start | bytes 294920 | tf_op jit(solution)/shard_map/ppermute | solution.py:31
  27.6 5.0 %collective-permute-start.14 = (bf16[16,3072]{1,0:T(8,128)(2,1)S(1)}, bf16[16,3072]{1,0:T(8,128)(2,1)S(1)}, u32[]{:S(2)}, u32[]{:S(2)}) collective-permute-start(bf16[16,3072]{1,0:T(8,128)(2,1)S(1)} %get-tuple-element.100.refs_2_), channel_id=1, source_target_pairs={{0,4},{1,5},{2,6},{3,7},{4,0},{5,1},{6,2},{7,3},{8,12},{9,13},{10,... | collective-permute-start | bytes 294920 | tf_op jit(solution)/shard_map/ppermute | solution.py:31
  32.7 7.7 %collective-permute-start.17 = (bf16[32,3072]{1,0:T(8,128)(2,1)S(1)}, bf16[32,3072]{1,0:T(8,128)(2,1)S(1)}, u32[]{:S(2)}, u32[]{:S(2)}) collective-permute-start(bf16[32,3072]{1,0:T(8,128)(2,1)S(1)} %get-tuple-element.107.refs_0_), channel_id=1, source_target_pairs={{0,4},{1,5},{2,6},{3,7},{4,0},{5,1},{6,2},{7,3},{8,12},{9,13},{10,... | collective-permute-start | bytes 589832 | tf_op jit(solution)/shard_map/ppermute | solution.py:31
  35.1 7.8 %collective-permute-start.18 = (bf16[32,3072]{1,0:T(8,128)(2,1)S(1)}, bf16[32,3072]{1,0:T(8,128)(2,1)S(1)}, u32[]{:S(2)}, u32[]{:S(2)}) collective-permute-start(bf16[32,3072]{1,0:T(8,128)(2,1)S(1)} %get-tuple-element.108.refs_2_), channel_id=1, source_target_pairs={{0,2},{1,3},{2,0},{3,1},{4,6},{5,7},{6,4},{7,5},{8,10},{9,11},{10,... | collective-permute-start | bytes 589832 | tf_op jit(solution)/shard_map/ppermute | solution.py:31
  39.3 12.1 %collective-permute-start.15 = (bf16[64,3072]{1,0:T(8,128)(2,1)S(1)}, bf16[64,3072]{1,0:T(8,128)(2,1)S(1)}, u32[]{:S(2)}, u32[]{:S(2)}) collective-permute-start(bf16[64,3072]{1,0:T(8,128)(2,1)S(1)} %get-tuple-element.104), channel_id=1, source_target_pairs={{0,4},{1,5},{2,6},{3,7},{4,0},{5,1},{6,2},{7,3},{8,12},{9,13},{10,... | collective-permute-start | bytes 1179656 | tf_op jit(solution)/shard_map/ppermute | solution.py:31
  39.5 12.1 %collective-permute-start.16 = (bf16[64,3072]{1,0:T(8,128)(2,1)S(1)}, bf16[64,3072]{1,0:T(8,128)(2,1)S(1)}, u32[]{:S(2)}, u32[]{:S(2)}) collective-permute-start(bf16[64,3072]{1,0:T(8,128)(2,1)S(1)} %get-tuple-element.106), channel_id=1, source_target_pairs={{0,2},{1,3},{2,0},{3,1},{4,6},{5,7},{6,4},{7,5},{8,10},{9,11},{10,... | collective-permute-start | bytes 1179656 | tf_op jit(solution)/shard_map/ppermute | solution.py:31
  45.8 13.8 %collective-permute-start.22 = (bf16[64,3072]{1,0:T(8,128)(2,1)S(1)}, bf16[64,3072]{1,0:T(8,128)(2,1)S(1)}, u32[]{:S(2)}, u32[]{:S(2)}) collective-permute-start(bf16[64,3072]{1,0:T(8,128)(2,1)S(1)} %get-tuple-element.117), channel_id=1, source_target_pairs={{0,4},{1,5},{2,6},{3,7},{4,0},{5,1},{6,2},{7,3},{8,12},{9,13},{10,... | collective-permute-start | bytes 1179656 | tf_op jit(solution)/shard_map/ppermute | solution.py:31
  45.9 14.1 %collective-permute-start.23 = (bf16[64,3072]{1,0:T(8,128)(2,1)S(1)}, bf16[64,3072]{1,0:T(8,128)(2,1)S(1)}, u32[]{:S(2)}, u32[]{:S(2)}) collective-permute-start(bf16[64,3072]{1,0:T(8,128)(2,1)S(1)} %get-tuple-element.119), channel_id=1, source_target_pairs={{0,2},{1,3},{2,0},{3,1},{4,6},{5,7},{6,4},{7,5},{8,10},{9,11},{10,... | collective-permute-start | bytes 1179656 | tf_op jit(solution)/shard_map/ppermute | solution.py:31
  51.7 11.1 %collective-permute-start.20 = (bf16[32,3072]{1,0:T(8,128)(2,1)S(1)}, bf16[32,3072]{1,0:T(8,128)(2,1)S(1)}, u32[]{:S(2)}, u32[]{:S(2)}) collective-permute-start(bf16[32,3072]{1,0:T(8,128)(2,1)S(1)} %get-tuple-element.113), channel_id=1, source_target_pairs={{0,2},{1,3},{2,0},{3,1},{4,6},{5,7},{6,4},{7,5},{8,10},{9,11},{10,... | collective-permute-start | bytes 589832 | tf_op jit(solution)/shard_map/ppermute | solution.py:31
  52.7 10.1 %collective-permute-start.21 = (bf16[32,3072]{1,0:T(8,128)(2,1)S(1)}, bf16[32,3072]{1,0:T(8,128)(2,1)S(1)}, u32[]{:S(2)}, u32[]{:S(2)}) collective-permute-start(bf16[32,3072]{1,0:T(8,128)(2,1)S(1)} %get-tuple-element.115), channel_id=1, source_target_pairs={{0,4},{1,5},{2,6},{3,7},{4,0},{5,1},{6,2},{7,3},{8,12},{9,13},{10,... | collective-permute-start | bytes 589832 | tf_op jit(solution)/shard_map/ppermute | solution.py:31
  60.1 5.7 %collective-permute-start.24 = (bf16[32,3072]{1,0:T(8,128)(2,1)S(1)}, bf16[32,3072]{1,0:T(8,128)(2,1)S(1)}, u32[]{:S(2)}, u32[]{:S(2)}) collective-permute-start(bf16[32,3072]{1,0:T(8,128)(2,1)S(1)} %get-tuple-element.135), channel_id=1, source_target_pairs={{0,2},{1,3},{2,0},{3,1},{4,6},{5,7},{6,4},{7,5},{8,10},{9,11},{10,... | collective-permute-start | bytes 589832 | tf_op jit(solution)/shard_map/ppermute | solution.py:31
  61.1 5.7 %collective-permute-start.25 = (bf16[32,3072]{1,0:T(8,128)(2,1)S(1)}, bf16[32,3072]{1,0:T(8,128)(2,1)S(1)}, u32[]{:S(2)}, u32[]{:S(2)}) collective-permute-start(bf16[32,3072]{1,0:T(8,128)(2,1)S(1)} %get-tuple-element.137), channel_id=1, source_target_pairs={{0,4},{1,5},{2,6},{3,7},{4,0},{5,1},{6,2},{7,3},{8,12},{9,13},{10,... | collective-permute-start | bytes 589832 | tf_op jit(solution)/shard_map/ppermute | solution.py:31
  62.9 7.3 %collective-permute-start.28 = (bf16[2,16,3072]{2,1,0:T(8,128)(2,1)S(1)}, bf16[2,16,3072]{2,1,0:T(8,128)(2,1)S(1)}, u32[]{:S(2)}, u32[]{:S(2)}) collective-permute-start(bf16[2,16,3072]{2,1,0:T(8,128)(2,1)S(1)} %get-tuple-element.142), channel_id=1, source_target_pairs={{0,24},{1,25},{2,26},{3,27},{4,28},{5,29},{6,30},{7,31},{8,0},{9,1... | collective-permute-start | bytes 589832 | tf_op jit(solution)/shard_map/ppermute | solution.py:39
  64.8 9.8 %collective-permute-start.27 = (bf16[3,256,3072]{2,1,0:T(8,128)(2,1)S(1)}, bf16[3,256,3072]{2,1,0:T(8,128)(2,1)S(1)}, u32[]{:S(2)}, u32[]{:S(2)}) collective-permute-start(bf16[3,256,3072]{2,1,0:T(8,128)(2,1)S(1)} %get-tuple-element.140), channel_id=1, source_target_pairs={{0,1},{1,0},{2,3},{3,2},{4,5},{5,4},{6,7},{7,6},{8,9},{9,8},{10,11... | collective-permute-start | bytes 14155784 | tf_op jit(solution)/shard_map/ppermute | solution.py:31
  66.9 11.8 %collective-permute-start.26 = (bf16[2,16,3072]{2,1,0:T(8,128)(2,1)S(1)}, bf16[2,16,3072]{2,1,0:T(8,128)(2,1)S(1)}, u32[]{:S(2)}, u32[]{:S(2)}) collective-permute-start(bf16[2,16,3072]{2,1,0:T(8,128)(2,1)S(1)} %get-tuple-element.139), channel_id=1, source_target_pairs={{0,8},{1,9},{2,10},{3,11},{4,12},{5,13},{6,14},{7,15},{8,16},{9,17... | collective-permute-start | bytes 589832 | tf_op jit(solution)/shard_map/ppermute | solution.py:39
  70.2 8.6 %collective-permute-start.29 = (bf16[2,16,3072]{2,1,0:T(8,128)(2,1)S(1)}, bf16[2,16,3072]{2,1,0:T(8,128)(2,1)S(1)}, u32[]{:S(2)}, u32[]{:S(2)}) collective-permute-start(bf16[2,16,3072]{2,1,0:T(8,128)(2,1)S(1)} %get-tuple-element.147), channel_id=1, source_target_pairs={{0,24},{1,25},{2,26},{3,27},{4,28},{5,29},{6,30},{7,31},{8,0},{9,1... | collective-permute-start | bytes 589832 | tf_op jit(solution)/shard_map/ppermute | solution.py:39

commit v7 on v6

--- a/solution.py
+++ b/solution.py
@@ -20,6 +20,7 @@
 C_TURN = 0
 C_LOAD = LONG // 5
 PANEL = 512
+WIDE = 1536
 TURN = pltpu.VMEM((8, 128), jnp.float32)
 VMEM = pl.BlockSpec(memory_space=pltpu.VMEM)
 HBM = pl.BlockSpec(memory_space=pltpu.HBM)
@@ -246,7 +247,7 @@
     works, (received, _, *grads, turn) = (refs[:5], refs[5:10]), refs[10:]
     turn[...] = jnp.zeros_like(turn)
     units = received.shape[1]
-    columns = pl.ds(pl.multiple_of(pl.program_id(0) * PANEL, PANEL), PANEL)
+    columns = pl.ds(pl.multiple_of(pl.program_id(0) * WIDE, WIDE), WIDE)
     for i, total in enumerate(slot_sums(works, slice(0, units), columns)):
         total = total + received[i, :, columns].astype(jnp.float32)
         grads[i][...] = (total * factor).astype(grads[i].dtype)
@@ -254,10 +255,10 @@
 
 def own_grads(works, received, turn, factor, dtype):
     _, units, width = received.shape
-    block = pl.BlockSpec((units, PANEL), lambda i: (0, i))
+    block = pl.BlockSpec((units, WIDE), lambda i: (0, i))
     return pl.pallas_call(
         functools.partial(own_kernel, factor),
-        grid=(width // PANEL,),
+        grid=(width // WIDE,),
         out_shape=(shape((units, width), dtype),) * 3 + (TURN,),
         in_specs=[VMEM] * 12,
         out_specs=(block,) * 3 + (VMEM,),
@@ -409,9 +410,9 @@
 
     whole, piece = held((rows, width), jnp.float32), held((rows, width))
 
-    def plane_sum(side, turn):
+    def plane_sum(side, turn, flops=0):
         out_mid, out_side, row_mid, row_side, turn = staged(
-            plane_body, "plane_sum", [whole, piece, whole, piece], *side, turn
+            plane_body, "plane_sum", [whole, piece, whole, piece], *side, turn, flops=flops
         )
         return (out_mid, swapped(out_side, along_x), row_mid, swapped(row_side, along_y)), turn
 
@@ -425,13 +426,11 @@
     middle_02, turn = plane_sum(sides[0], turn)
     sent, turn = other_grads(works, turn)
     received = swapped(sent, core)
-    middle_31, turn = plane_sum(sides[1], turn)
+    middle_31, turn = plane_sum(sides[1], turn, LONG)
     sum_0, sum_2, turn = line_sum(middle_02, turn, jnp.float32)
     passed = shifted(sum_2, -1)
     sum_1, sum_3, turn = line_sum(middle_31, turn, jnp.float32)
     three = shifted(sum_3, 1)
-    sum_1, turn = staged(relay_body, "relay", [held(own.shape)], sum_1, passed, turn, flops=LONG)
-    one = shifted(sum_1, -1)
     factor = 1.0 / math.sqrt(devices * capacity)
     if far_bits:
         *owned, turn = own_grads(works, received, turn, 1.0, jnp.float32)
@@ -441,6 +440,8 @@
         owned = [half(total * factor) for total in owned]
     else:
         *owned, turn = own_grads(works, received, turn, factor, jnp.bfloat16)
+    sum_1, turn = staged(relay_body, "relay", [held(own.shape)], sum_1, passed, turn)
+    one = shifted(sum_1, -1)
     total, turn = staged(
         near_body, "near_sum", [held(own.shape, jnp.float32)], sum_0, three, turn, flops=LONG // 10
     )

time: 79.7 us -> 77.9 us (0.977)
  waiting for transfers between devices: 23.7 us -> 22 us
  Pallas kernels: 16.6 us -> 15.6 us
  starting transfers between devices: 38.4 us -> 39.3 us
    ppermute x24, waiting for transfers between devices: 20.5 us -> 17.7 us  [swapped(): lax.ppermute(block, 'dp', [(low, low ^ mask) for low in range(count)])]
    ppermute x6, starting transfers between devices: 14.1 us -> 15.4 us  [shifted(): return lax.ppermute(block, 'dp', route)]
    pallas_call x1, Pallas kernels: 4.07 us -> 2.89 us  [own_grads(): pl.pallas_call(functools.partial(own_kernel, factor), grid=(width // WIDE...]
    ppermute x6, waiting for transfers between devices: 3.19 us -> 4.31 us  [shifted(): return lax.ppermute(block, 'dp', route)]
  transfers between devices with their start and end apart: 30 -> 30, of which waited for: 15 -> 16; matrix products, arithmetic and copies ran while one was open for 0% -> 0% of each run, Pallas kernels for 20% -> 19%
where the time goes in v7:
time: 77.9 us; the launch traced here: 77.8 us
  starting transfers between devices  39.3 us (50%)
  waiting for transfers between devices  22 us (28%)
  Pallas kernels  15.6 us (20%)
  between operations  0.78 us (1%)
    ppermute x24, starting transfers between devices, swapped(): lax.ppermute(block, 'dp', [(low, low ^ mask) for low in range(count)])  23.9 us
    ppermute x24, waiting for transfers between devices, swapped(): lax.ppermute(block, 'dp', [(low, low ^ mask) for low in range(count)])  17.7 us
    ppermute x6, starting transfers between devices, shifted(): return lax.ppermute(block, 'dp', route)  15.4 us
    pallas_call x2, Pallas kernels, expert(): pl.pallas_call(functools.partial(expert_kernel, [len(part) for part in pa...  5.98 us
    ppermute x6, waiting for transfers between devices, shifted(): return lax.ppermute(block, 'dp', route)  4.31 us
    pallas_call x15, Pallas kernels, staged(): pl.pallas_call(kernel, out_shape=(*outs, TURN), in_specs=[VMEM] * len(val...  3.92 us
    pallas_call x1, Pallas kernels, own_grads(): pl.pallas_call(functools.partial(own_kernel, factor), grid=(width // WIDE...  2.89 us
  transfers between devices with their start and end apart: 30, of which 16 were waited for; matrix products, arithmetic and copies ran while one was open for 0% of the time, Pallas kernels for 19%

profile of v7, /device:TPU:0, one launch (start us, length us, event | category | flops | bytes accessed | tf_op | source)
XLA Modules:
  0.0 77.8 jit_solution(6344492930740310458)
XLA Ops:
  0.6 0.5 collective-permute-start
  1.2 1.4 %pick.1 = (bf16[2,16,3072]{2,1,0:T(8,128)(2,1)S(1)}, f32[16,128]{1,0:T(8,128)S(1)}, f32[8,128]{1,0:T(8,128)S(1)}) custom-call(s32[1]{0:T(128)} %bitcast.place, s32[16]{0:T(128)} %token_.1, s32[32]{0:T(128)} %count.1, f32[16]{0:T(128)} %gate.1, bf16[128,3072]{1,0:T(8,128)(2,1)} %tokens.1, bf16[16,3072]{1,0:T(8,128)(2,1)} %grad.1), custom_call_target="tpu_custom_call" | custom-call | tf_op jit(solution)/shard_map/pick/pallas_call | solution.py:122
  2.6 3.7 %collective-permute-start.7 = (bf16[2,16,3072]{2,1,0:T(8,128)(2,1)S(1)}, bf16[2,16,3072]{2,1,0:T(8,128)(2,1)S(1)}, u32[]{:S(2)}, u32[]{:S(2)}) collective-permute-start(bf16[2,16,3072]{2,1,0:T(8,128)(2,1)S(1)} %get-tuple-element.80.refs_0_), channel_id=1, source_target_pairs={{0,16},{1,17},{2,18},{3,19},{4,20},{5,21},{6,22},{7,23},{8,24},{9,... | collective-permute-start | bytes 589832 | tf_op jit(solution)/shard_map/ppermute | solution.py:40
  6.2 0.2 collective-permute-start.3
  6.5 0.3 collective-permute-start.4
  6.8 1.6 %collective-permute-start.1 = (bf16[16,3072]{1,0:T(8,128)(2,1)S(1)}, bf16[16,3072]{1,0:T(8,128)(2,1)S(1)}, u32[]{:S(2)}, u32[]{:S(2)}) collective-permute-start(bf16[16,3072]{1,0:T(8,128)(2,1)S(1)} %get-tuple-element.82.refs_0_), channel_id=1, source_target_pairs={{0,2},{1,3},{2,0},{3,1},{4,6},{5,7},{6,4},{7,5},{8,10},{9,11},{10,... | collective-permute-start | bytes 294920 | tf_op jit(solution)/shard_map/ppermute | solution.py:32
  8.3 1.5 %collective-permute-start.2 = (bf16[16,3072]{1,0:T(8,128)(2,1)S(1)}, bf16[16,3072]{1,0:T(8,128)(2,1)S(1)}, u32[]{:S(2)}, u32[]{:S(2)}) collective-permute-start(bf16[16,3072]{1,0:T(8,128)(2,1)S(1)} %get-tuple-element.83.refs_2_), channel_id=1, source_target_pairs={{0,4},{1,5},{2,6},{3,7},{4,0},{5,1},{6,2},{7,3},{8,12},{9,13},{10,... | collective-permute-start | bytes 294920 | tf_op jit(solution)/shard_map/ppermute | solution.py:32
  9.9 2.2 %collective-permute-done.4.refs_5_.refs_13_.refs_10_ = bf16[256,3072]{1,0:T(8,128)(2,1)S(1)} collective-permute-done((bf16[256,3072]{1,0:T(8,128)(2,1)}, bf16[256,3072]{1,0:T(8,128)(2,1)S(1)}, u32[]{:S(2)}, u32[]{:S(2)}) %collective-permute-start.4) | collective-permute-done | bytes 1572896 | tf_op jit(solution)/shard_map/ppermute | solution.py:32
  12.1 0.8 %collective-permute-done.2.refs_3_ = bf16[16,3072]{1,0:T(8,128)(2,1)S(1)} collective-permute-done((bf16[16,3072]{1,0:T(8,128)(2,1)S(1)}, bf16[16,3072]{1,0:T(8,128)(2,1)S(1)}, u32[]{:S(2)}, u32[]{:S(2)}) %collective-permute-start.2) | collective-permute-done | bytes 98336 | tf_op jit(solution)/shard_map/ppermute | solution.py:32
  13.0 1.6 %collective-permute-start.12 = (bf16[2,16,3072]{2,1,0:T(8,128)(2,1)S(1)}, bf16[2,16,3072]{2,1,0:T(8,128)(2,1)S(1)}, u32[]{:S(2)}, u32[]{:S(2)}) collective-permute-start(bf16[2,16,3072]{2,1,0:T(8,128)(2,1)S(1)} %get-tuple-element.94), channel_id=1, source_target_pairs={{0,8},{1,9},{2,10},{3,11},{4,12},{5,13},{6,14},{7,15},{8,16},{9,17... | collective-permute-start | bytes 589832 | tf_op jit(solution)/shard_map/ppermute | solution.py:40
  14.6 1.5 %collective-permute-start.5 = (bf16[32,3072]{1,0:T(8,128)(2,1)S(1)}, bf16[32,3072]{1,0:T(8,128)(2,1)S(1)}, u32[]{:S(2)}, u32[]{:S(2)}) collective-permute-start(bf16[32,3072]{1,0:T(8,128)(2,1)S(1)} %get-tuple-element.85.refs_0_), channel_id=1, source_target_pairs={{0,4},{1,5},{2,6},{3,7},{4,0},{5,1},{6,2},{7,3},{8,12},{9,13},{10,... | collective-permute-start | bytes 589832 | tf_op jit(solution)/shard_map/ppermute | solution.py:32
  16.2 0.7 collective-permute-start.6
  16.8 1.4 %collective-permute-start.8 = (bf16[16,3072]{1,0:T(8,128)(2,1)S(1)}, bf16[16,3072]{1,0:T(8,128)(2,1)S(1)}, u32[]{:S(2)}, u32[]{:S(2)}) collective-permute-start(bf16[16,3072]{1,0:T(8,128)(2,1)S(1)} %get-tuple-element.88.refs_0_), channel_id=1, source_target_pairs={{0,2},{1,3},{2,0},{3,1},{4,6},{5,7},{6,4},{7,5},{8,10},{9,11},{10,... | collective-permute-start | bytes 294920 | tf_op jit(solution)/shard_map/ppermute | solution.py:32
  18.3 0.9 %collective-permute-start.9 = (bf16[16,3072]{1,0:T(8,128)(2,1)S(1)}, bf16[16,3072]{1,0:T(8,128)(2,1)S(1)}, u32[]{:S(2)}, u32[]{:S(2)}) collective-permute-start(bf16[16,3072]{1,0:T(8,128)(2,1)S(1)} %get-tuple-element.89.refs_2_), channel_id=1, source_target_pairs={{0,4},{1,5},{2,6},{3,7},{4,0},{5,1},{6,2},{7,3},{8,12},{9,13},{10,... | collective-permute-start | bytes 294920 | tf_op jit(solution)/shard_map/ppermute | solution.py:32
  19.2 2.2 %collective-permute-done.5.refs_1_ = bf16[32,3072]{1,0:T(8,128)(2,1)S(1)} collective-permute-done((bf16[32,3072]{1,0:T(8,128)(2,1)S(1)}, bf16[32,3072]{1,0:T(8,128)(2,1)S(1)}, u32[]{:S(2)}, u32[]{:S(2)}) %collective-permute-start.5) | collective-permute-done | bytes 196640 | tf_op jit(solution)/shard_map/ppermute | solution.py:32
  21.3 1.5 %collective-permute-done.6.refs_3_ = bf16[32,3072]{1,0:T(8,128)(2,1)S(1)} collective-permute-done((bf16[32,3072]{1,0:T(8,128)(2,1)S(1)}, bf16[32,3072]{1,0:T(8,128)(2,1)S(1)}, u32[]{:S(2)}, u32[]{:S(2)}) %collective-permute-start.6) | collective-permute-done | bytes 196640 | tf_op jit(solution)/shard_map/ppermute | solution.py:32
  22.9 2.4 %collective-permute-start.19 = (bf16[128,3072]{1,0:T(8,128)(2,1)S(1)}, bf16[128,3072]{1,0:T(8,128)(2,1)S(1)}, u32[]{:S(2)}, u32[]{:S(2)}) collective-permute-start(bf16[128,3072]{1,0:T(8,128)(2,1)S(1)} %get-tuple-element.109), channel_id=1, source_target_pairs={{0,24},{1,25},{2,26},{3,27},{4,28},{5,29},{6,30},{7,31},{8,0},{9,1... | collective-permute-start | bytes 2359304 | tf_op jit(solution)/shard_map/ppermute | solution.py:40
  25.3 0.2 collective-permute-start.10
  25.5 1.4 %collective-permute-start.11 = (bf16[32,3072]{1,0:T(8,128)(2,1)S(1)}, bf16[32,3072]{1,0:T(8,128)(2,1)S(1)}, u32[]{:S(2)}, u32[]{:S(2)}) collective-permute-start(bf16[32,3072]{1,0:T(8,128)(2,1)S(1)} %get-tuple-element.93.refs_6_), channel_id=1, source_target_pairs={{0,2},{1,3},{2,0},{3,1},{4,6},{5,7},{6,4},{7,5},{8,10},{9,11},{10,... | collective-permute-start | bytes 589832 | tf_op jit(solution)/shard_map/ppermute | solution.py:32
  26.9 0.7 collective-permute-start.13
  27.6 1.9 %collective-permute-start.14 = (bf16[16,3072]{1,0:T(8,128)(2,1)S(1)}, bf16[16,3072]{1,0:T(8,128)(2,1)S(1)}, u32[]{:S(2)}, u32[]{:S(2)}) collective-permute-start(bf16[16,3072]{1,0:T(8,128)(2,1)S(1)} %get-tuple-element.100.refs_2_), channel_id=1, source_target_pairs={{0,4},{1,5},{2,6},{3,7},{4,0},{5,1},{6,2},{7,3},{8,12},{9,13},{10,... | collective-permute-start | bytes 294920 | tf_op jit(solution)/shard_map/ppermute | solution.py:32
  29.5 2.5 %turn_panels.1 = (bf16[3,3072,256]{2,1,0:T(8,128)(2,1)S(1)}, bf16[3,3072,256]{2,1,0:T(8,128)(2,1)S(1)}, f32[8,128]{1,0:T(8,128)S(1)}) custom-call(bf16[256,3072]{1,0:T(8,128)(2,1)S(1)} %copy-done, bf16[256,3072]{1,0:T(8,128)(2,1)S(1)} %copy-done.1, bf16[256,3072]{1,0:T(8,128)(2,1)S(1)} %copy-done.2, ...), custom_call_target="tpu_custom_call" | custom-call | tf_op jit(solution)/shard_map/turn_panels/pallas_call | solution.py:276
  32.0 0.2 collective-permute-done.13.refs_1_
  32.2 0.4 collective-permute-done.14.refs_3_
  32.7 2.4 %collective-permute-start.17 = (bf16[32,3072]{1,0:T(8,128)(2,1)S(1)}, bf16[32,3072]{1,0:T(8,128)(2,1)S(1)}, u32[]{:S(2)}, u32[]{:S(2)}) collective-permute-start(bf16[32,3072]{1,0:T(8,128)(2,1)S(1)} %get-tuple-element.107.refs_0_), channel_id=1, source_target_pairs={{0,4},{1,5},{2,6},{3,7},{4,0},{5,1},{6,2},{7,3},{8,12},{9,13},{10,... | collective-permute-start | bytes 589832 | tf_op jit(solution)/shard_map/ppermute | solution.py:32
  35.1 1.3 %collective-permute-start.18 = (bf16[32,3072]{1,0:T(8,128)(2,1)S(1)}, bf16[32,3072]{1,0:T(8,128)(2,1)S(1)}, u32[]{:S(2)}, u32[]{:S(2)}) collective-permute-start(bf16[32,3072]{1,0:T(8,128)(2,1)S(1)} %get-tuple-element.108.refs_2_), channel_id=1, source_target_pairs={{0,2},{1,3},{2,0},{3,1},{4,6},{5,7},{6,4},{7,5},{8,10},{9,11},{10,... | collective-permute-start | bytes 589832 | tf_op jit(solution)/shard_map/ppermute | solution.py:32
  36.4 3.0 %expert.2 = (bf16[128,3072]{1,0:T(8,128)(2,1)S(1)}, bf16[128,3072]{1,0:T(8,128)(2,1)S(1)}, bf16[128,512]{1,0:T(8,128)(2,1)S(1)}, bf16[128,512]{1,0:T(8,128)(2,1)...) custom-call(bf16[32,3072]{1,0:T(8,128)(2,1)S(1)} %get-tuple-element., ...), custom_call_target="tpu_custom_call" | custom-call | flops 2415919104 | bytes 9437184 | tf_op jit(solution)/shard_map/expert/pallas_call | solution.py:202
  39.6 0.7 collective-permute-start.16
  40.4 2.5 %collective-permute-done.18.refs_3_ = bf16[32,3072]{1,0:T(8,128)(2,1)S(1)} collective-permute-done((bf16[32,3072]{1,0:T(8,128)(2,1)S(1)}, bf16[32,3072]{1,0:T(8,128)(2,1)S(1)}, u32[]{:S(2)}, u32[]{:S(2)}) %collective-permute-start.18) | collective-permute-done | bytes 196640 | tf_op jit(solution)/shard_map/ppermute | solution.py:32
  42.9 3.0 %expert.3 = (bf16[128,3072]{1,0:T(8,128)(2,1)S(1)}, bf16[128,3072]{1,0:T(8,128)(2,1)S(1)}, bf16[128,512]{1,0:T(8,128)(2,1)S(1)}, bf16[128,512]{1,0:T(8,128)(2,1)...) custom-call(bf16[32,3072]{1,0:T(8,128)(2,1)S(1)} %get-tuple-element., ...), custom_call_target="tpu_custom_call" | custom-call | flops 2415919104 | bytes 9437184 | tf_op jit(solution)/shard_map/expert/pallas_call | solution.py:202
  46.0 1.4 %collective-permute-start.23 = (bf16[64,3072]{1,0:T(8,128)(2,1)S(1)}, bf16[64,3072]{1,0:T(8,128)(2,1)S(1)}, u32[]{:S(2)}, u32[]{:S(2)}) collective-permute-start(bf16[64,3072]{1,0:T(8,128)(2,1)S(1)} %get-tuple-element.119), channel_id=1, source_target_pairs={{0,2},{1,3},{2,0},{3,1},{4,6},{5,7},{6,4},{7,5},{8,10},{9,11},{10,... | collective-permute-start | bytes 1179656 | tf_op jit(solution)/shard_map/ppermute | solution.py:32
  47.4 4.1 %collective-permute-done.15.refs_1_ = bf16[64,3072]{1,0:T(8,128)(2,1)S(1)} collective-permute-done((bf16[64,3072]{1,0:T(8,128)(2,1)S(1)}, bf16[64,3072]{1,0:T(8,128)(2,1)S(1)}, u32[]{:S(2)}, u32[]{:S(2)}) %collective-permute-start.15) | collective-permute-done | bytes 393248 | tf_op jit(solution)/shard_map/ppermute | solution.py:32
  51.7 1.1 %collective-permute-start.20 = (bf16[32,3072]{1,0:T(8,128)(2,1)S(1)}, bf16[32,3072]{1,0:T(8,128)(2,1)S(1)}, u32[]{:S(2)}, u32[]{:S(2)}) collective-permute-start(bf16[32,3072]{1,0:T(8,128)(2,1)S(1)} %get-tuple-element.113), channel_id=1, source_target_pairs={{0,2},{1,3},{2,0},{3,1},{4,6},{5,7},{6,4},{7,5},{8,10},{9,11},{10,... | collective-permute-start | bytes 589832 | tf_op jit(solution)/shard_map/ppermute | solution.py:32
  52.8 1.7 %collective-permute-start.21 = (bf16[32,3072]{1,0:T(8,128)(2,1)S(1)}, bf16[32,3072]{1,0:T(8,128)(2,1)S(1)}, u32[]{:S(2)}, u32[]{:S(2)}) collective-permute-start(bf16[32,3072]{1,0:T(8,128)(2,1)S(1)} %get-tuple-element.115), channel_id=1, source_target_pairs={{0,4},{1,5},{2,6},{3,7},{4,0},{5,1},{6,2},{7,3},{8,12},{9,13},{10,... | collective-permute-start | bytes 589832 | tf_op jit(solution)/shard_map/ppermute | solution.py:32
  54.4 1.4 %other_grads.1 = (bf16[3,256,3072]{2,1,0:T(8,128)(2,1)S(1)}, f32[8,128]{1,0:T(8,128)S(1)}) custom-call(bf16[128,3072]{1,0:T(8,128)(2,1)S(1)} %get-tuple-element.120.refs_0_, bf16[128,3072]{1,0:T(8,128)(2,1)S(1)} %get-tuple-element.121.refs_1_, bf16[128,512]{1,0:T(8,128)(2,1)S(1)} %get-tuple-element.122.refs_2_, ...), custom_call_target="tpu_custom_call" | custom-call | flops 2000000000 | tf_op jit(solution)/shard_map/other_grads/pallas_call | solution.py:235
  56.0 1.7 %collective-permute-done.22.refs_1_ = bf16[64,3072]{1,0:T(8,128)(2,1)S(1)} collective-permute-done((bf16[64,3072]{1,0:T(8,128)(2,1)S(1)}, bf16[64,3072]{1,0:T(8,128)(2,1)S(1)}, u32[]{:S(2)}, u32[]{:S(2)}) %collective-permute-start.22) | collective-permute-done | bytes 393248 | tf_op jit(solution)/shard_map/ppermute | solution.py:32
  57.7 0.7 collective-permute-done.23.refs_3_
  58.4 0.2 plane_sum.3
  58.6 0.8 %collective-permute-start.24 = (bf16[32,3072]{1,0:T(8,128)(2,1)S(1)}, bf16[32,3072]{1,0:T(8,128)(2,1)S(1)}, u32[]{:S(2)}, u32[]{:S(2)}) collective-permute-start(bf16[32,3072]{1,0:T(8,128)(2,1)S(1)} %get-tuple-element.135), channel_id=1, source_target_pairs={{0,2},{1,3},{2,0},{3,1},{4,6},{5,7},{6,4},{7,5},{8,10},{9,11},{10,... | collective-permute-start | bytes 589832 | tf_op jit(solution)/shard_map/ppermute | solution.py:32
  59.4 1.4 %collective-permute-start.25 = (bf16[32,3072]{1,0:T(8,128)(2,1)S(1)}, bf16[32,3072]{1,0:T(8,128)(2,1)S(1)}, u32[]{:S(2)}, u32[]{:S(2)}) collective-permute-start(bf16[32,3072]{1,0:T(8,128)(2,1)S(1)} %get-tuple-element.137), channel_id=1, source_target_pairs={{0,4},{1,5},{2,6},{3,7},{4,0},{5,1},{6,2},{7,3},{8,12},{9,13},{10,... | collective-permute-start | bytes 589832 | tf_op jit(solution)/shard_map/ppermute | solution.py:32
  60.8 0.9 %collective-permute-done.20.refs_1_ = bf16[32,3072]{1,0:T(8,128)(2,1)S(1)} collective-permute-done((bf16[32,3072]{1,0:T(8,128)(2,1)S(1)}, bf16[32,3072]{1,0:T(8,128)(2,1)S(1)}, u32[]{:S(2)}, u32[]{:S(2)}) %collective-permute-start.20) | collective-permute-done | bytes 196640 | tf_op jit(solution)/shard_map/ppermute | solution.py:32
  61.8 3.1 %collective-permute-start.27 = (bf16[2,16,3072]{2,1,0:T(8,128)(2,1)S(1)}, bf16[2,16,3072]{2,1,0:T(8,128)(2,1)S(1)}, u32[]{:S(2)}, u32[]{:S(2)}) collective-permute-start(bf16[2,16,3072]{2,1,0:T(8,128)(2,1)S(1)} %get-tuple-element.141), channel_id=1, source_target_pairs={{0,24},{1,25},{2,26},{3,27},{4,28},{5,29},{6,30},{7,31},{8,0},{9,1... | collective-permute-start | bytes 589832 | tf_op jit(solution)/shard_map/ppermute | solution.py:40
  65.2 0.4 collective-permute-start.26
  65.6 2.9 %own_grads.1 = (bf16[256,3072]{1,0:T(8,128)(2,1)}, bf16[256,3072]{1,0:T(8,128)(2,1)}, bf16[256,3072]{1,0:T(8,128)(2,1)}, f32[8,128]{1,0:T(8,128)S(1)}) custom-call(bf16[128,3072]{1,0:T(8,128)(2,1)S(1)} %get-tuple-element.120.refs_0_, bf16[128,3072]{1,0:T(8,128)(2,1)S(1)} %get-tuple-element.121.refs_1_, bf16[128,512]{1,0:T(8,128)(2,1)S(1)} %get-tuple-element.122.refs_2_, ...), custom_call_target="tpu_custom_call" | custom-call | tf_op jit(solution)/shard_map/own_grads/pallas_call | solution.py:259
  68.5 4.2 %collective-permute-start.29 = (bf16[2,16,3072]{2,1,0:T(8,128)(2,1)S(1)}, bf16[2,16,3072]{2,1,0:T(8,128)(2,1)S(1)}, u32[]{:S(2)}, u32[]{:S(2)}) collective-permute-start(bf16[2,16,3072]{2,1,0:T(8,128)(2,1)S(1)} %get-tuple-element.147), channel_id=1, source_target_pairs={{0,24},{1,25},{2,26},{3,27},{4,28},{5,29},{6,30},{7,31},{8,0},{9,1... | collective-permute-start | bytes 589832 | tf_op jit(solution)/shard_map/ppermute | solution.py:40
  72.7 2.2 %collective-permute-done.26.refs_1_ = bf16[2,16,3072]{2,1,0:T(8,128)(2,1)S(1)} collective-permute-done((bf16[2,16,3072]{2,1,0:T(8,128)(2,1)S(1)}, bf16[2,16,3072]{2,1,0:T(8,128)(2,1)S(1)}, u32[]{:S(2)}, u32[]{:S(2)}) %collective-permute-start.26) | collective-permute-done | bytes 196640 | tf_op jit(solution)/shard_map/ppermute | solution.py:40
  74.9 2.1 %collective-permute-done.29.refs_1_ = bf16[2,16,3072]{2,1,0:T(8,128)(2,1)S(1)} collective-permute-done((bf16[2,16,3072]{2,1,0:T(8,128)(2,1)S(1)}, bf16[2,16,3072]{2,1,0:T(8,128)(2,1)S(1)}, u32[]{:S(2)}, u32[]{:S(2)}) %collective-permute-start.29) | collective-permute-done | bytes 196640 | tf_op jit(solution)/shard_map/ppermute | solution.py:40
  77.0 0.7 final.1
  (38 shorter events, 1.2 us)
Async XLA Ops:
  0.6 6.1 %collective-permute-start = (bf16[256,3072]{1,0:T(8,128)(2,1)}, bf16[256,3072]{1,0:T(8,128)(2,1)S(1)}, u32[]{:S(2)}, u32[]{:S(2)}) collective-permute-start(bf16[256,3072]{1,0:T(8,128)(2,1)} %refs_5_.1), channel_id=1, source_target_pairs={{0,1},{1,0},{2,3},{3,2},{4,5},{5,4},{6,7},{7,6},{8,9},{9,8},{10,11... | collective-permute-start | bytes 4718600 | tf_op jit(solution)/shard_map/ppermute | solution.py:32
  2.6 14.2 %collective-permute-start.7 = (bf16[2,16,3072]{2,1,0:T(8,128)(2,1)S(1)}, bf16[2,16,3072]{2,1,0:T(8,128)(2,1)S(1)}, u32[]{:S(2)}, u32[]{:S(2)}) collective-permute-start(bf16[2,16,3072]{2,1,0:T(8,128)(2,1)S(1)} %get-tuple-element.80.refs_0_), channel_id=1, source_target_pairs={{0,16},{1,17},{2,18},{3,19},{4,20},{5,21},{6,22},{7,23},{8,24},{9,... | collective-permute-start | bytes 589832 | tf_op jit(solution)/shard_map/ppermute | solution.py:40
  6.2 3.6 %collective-permute-start.3 = (bf16[256,3072]{1,0:T(8,128)(2,1)}, bf16[256,3072]{1,0:T(8,128)(2,1)S(1)}, u32[]{:S(2)}, u32[]{:S(2)}) collective-permute-start(bf16[256,3072]{1,0:T(8,128)(2,1)} %refs_6_.1), channel_id=1, source_target_pairs={{0,1},{1,0},{2,3},{3,2},{4,5},{5,4},{6,7},{7,6},{8,9},{9,8},{10,11... | collective-permute-start | bytes 4718600 | tf_op jit(solution)/shard_map/ppermute | solution.py:32
  6.5 5.7 %collective-permute-start.4 = (bf16[256,3072]{1,0:T(8,128)(2,1)}, bf16[256,3072]{1,0:T(8,128)(2,1)S(1)}, u32[]{:S(2)}, u32[]{:S(2)}) collective-permute-start(bf16[256,3072]{1,0:T(8,128)(2,1)} %refs_7_.1), channel_id=1, source_target_pairs={{0,1},{1,0},{2,3},{3,2},{4,5},{5,4},{6,7},{7,6},{8,9},{9,8},{10,11... | collective-permute-start | bytes 4718600 | tf_op jit(solution)/shard_map/ppermute | solution.py:32
  6.8 5.3 %collective-permute-start.1 = (bf16[16,3072]{1,0:T(8,128)(2,1)S(1)}, bf16[16,3072]{1,0:T(8,128)(2,1)S(1)}, u32[]{:S(2)}, u32[]{:S(2)}) collective-permute-start(bf16[16,3072]{1,0:T(8,128)(2,1)S(1)} %get-tuple-element.82.refs_0_), channel_id=1, source_target_pairs={{0,2},{1,3},{2,0},{3,1},{4,6},{5,7},{6,4},{7,5},{8,10},{9,11},{10,... | collective-permute-start | bytes 294920 | tf_op jit(solution)/shard_map/ppermute | solution.py:32
  8.3 4.6 %collective-permute-start.2 = (bf16[16,3072]{1,0:T(8,128)(2,1)S(1)}, bf16[16,3072]{1,0:T(8,128)(2,1)S(1)}, u32[]{:S(2)}, u32[]{:S(2)}) collective-permute-start(bf16[16,3072]{1,0:T(8,128)(2,1)S(1)} %get-tuple-element.83.refs_2_), channel_id=1, source_target_pairs={{0,4},{1,5},{2,6},{3,7},{4,0},{5,1},{6,2},{7,3},{8,12},{9,13},{10,... | collective-permute-start | bytes 294920 | tf_op jit(solution)/shard_map/ppermute | solution.py:32
  13.0 13.9 %collective-permute-start.12 = (bf16[2,16,3072]{2,1,0:T(8,128)(2,1)S(1)}, bf16[2,16,3072]{2,1,0:T(8,128)(2,1)S(1)}, u32[]{:S(2)}, u32[]{:S(2)}) collective-permute-start(bf16[2,16,3072]{2,1,0:T(8,128)(2,1)S(1)} %get-tuple-element.94), channel_id=1, source_target_pairs={{0,8},{1,9},{2,10},{3,11},{4,12},{5,13},{6,14},{7,15},{8,16},{9,17... | collective-permute-start | bytes 589832 | tf_op jit(solution)/shard_map/ppermute | solution.py:40
  14.6 6.7 %collective-permute-start.5 = (bf16[32,3072]{1,0:T(8,128)(2,1)S(1)}, bf16[32,3072]{1,0:T(8,128)(2,1)S(1)}, u32[]{:S(2)}, u32[]{:S(2)}) collective-permute-start(bf16[32,3072]{1,0:T(8,128)(2,1)S(1)} %get-tuple-element.85.refs_0_), channel_id=1, source_target_pairs={{0,4},{1,5},{2,6},{3,7},{4,0},{5,1},{6,2},{7,3},{8,12},{9,13},{10,... | collective-permute-start | bytes 589832 | tf_op jit(solution)/shard_map/ppermute | solution.py:32
  16.2 6.7 %collective-permute-start.6 = (bf16[32,3072]{1,0:T(8,128)(2,1)S(1)}, bf16[32,3072]{1,0:T(8,128)(2,1)S(1)}, u32[]{:S(2)}, u32[]{:S(2)}) collective-permute-start(bf16[32,3072]{1,0:T(8,128)(2,1)S(1)} %get-tuple-element.86.refs_2_), channel_id=1, source_target_pairs={{0,2},{1,3},{2,0},{3,1},{4,6},{5,7},{6,4},{7,5},{8,10},{9,11},{10,... | collective-permute-start | bytes 589832 | tf_op jit(solution)/shard_map/ppermute | solution.py:32
  16.8 8.4 %collective-permute-start.8 = (bf16[16,3072]{1,0:T(8,128)(2,1)S(1)}, bf16[16,3072]{1,0:T(8,128)(2,1)S(1)}, u32[]{:S(2)}, u32[]{:S(2)}) collective-permute-start(bf16[16,3072]{1,0:T(8,128)(2,1)S(1)} %get-tuple-element.88.refs_0_), channel_id=1, source_target_pairs={{0,2},{1,3},{2,0},{3,1},{4,6},{5,7},{6,4},{7,5},{8,10},{9,11},{10,... | collective-permute-start | bytes 294920 | tf_op jit(solution)/shard_map/ppermute | solution.py:32
  18.3 7.0 %collective-permute-start.9 = (bf16[16,3072]{1,0:T(8,128)(2,1)S(1)}, bf16[16,3072]{1,0:T(8,128)(2,1)S(1)}, u32[]{:S(2)}, u32[]{:S(2)}) collective-permute-start(bf16[16,3072]{1,0:T(8,128)(2,1)S(1)} %get-tuple-element.89.refs_2_), channel_id=1, source_target_pairs={{0,4},{1,5},{2,6},{3,7},{4,0},{5,1},{6,2},{7,3},{8,12},{9,13},{10,... | collective-permute-start | bytes 294920 | tf_op jit(solution)/shard_map/ppermute | solution.py:32
  22.9 20.0 %collective-permute-start.19 = (bf16[128,3072]{1,0:T(8,128)(2,1)S(1)}, bf16[128,3072]{1,0:T(8,128)(2,1)S(1)}, u32[]{:S(2)}, u32[]{:S(2)}) collective-permute-start(bf16[128,3072]{1,0:T(8,128)(2,1)S(1)} %get-tuple-element.109), channel_id=1, source_target_pairs={{0,24},{1,25},{2,26},{3,27},{4,28},{5,29},{6,30},{7,31},{8,0},{9,1... | collective-permute-start | bytes 2359304 | tf_op jit(solution)/shard_map/ppermute | solution.py:40
  25.3 11.1 %collective-permute-start.10 = (bf16[32,3072]{1,0:T(8,128)(2,1)S(1)}, bf16[32,3072]{1,0:T(8,128)(2,1)S(1)}, u32[]{:S(2)}, u32[]{:S(2)}) collective-permute-start(bf16[32,3072]{1,0:T(8,128)(2,1)S(1)} %get-tuple-element.92.refs_4_), channel_id=1, source_target_pairs={{0,4},{1,5},{2,6},{3,7},{4,0},{5,1},{6,2},{7,3},{8,12},{9,13},{10,... | collective-permute-start | bytes 589832 | tf_op jit(solution)/shard_map/ppermute | solution.py:32
  25.5 11.0 %collective-permute-start.11 = (bf16[32,3072]{1,0:T(8,128)(2,1)S(1)}, bf16[32,3072]{1,0:T(8,128)(2,1)S(1)}, u32[]{:S(2)}, u32[]{:S(2)}) collective-permute-start(bf16[32,3072]{1,0:T(8,128)(2,1)S(1)} %get-tuple-element.93.refs_6_), channel_id=1, source_target_pairs={{0,2},{1,3},{2,0},{3,1},{4,6},{5,7},{6,4},{7,5},{8,10},{9,11},{10,... | collective-permute-start | bytes 589832 | tf_op jit(solution)/shard_map/ppermute | solution.py:32
  26.9 2.6 %copy-start = (bf16[256,3072]{1,0:T(8,128)(2,1)S(1)}, bf16[256,3072]{1,0:T(8,128)(2,1)}, u32[]{:S(2)}) copy-start(bf16[256,3072]{1,0:T(8,128)(2,1)} %refs_5_.1) | copy-start | bytes 4718596
  26.9 2.6 %copy-start.1 = (bf16[256,3072]{1,0:T(8,128)(2,1)S(1)}, bf16[256,3072]{1,0:T(8,128)(2,1)}, u32[]{:S(2)}) copy-start(bf16[256,3072]{1,0:T(8,128)(2,1)} %refs_6_.1) | copy-start | bytes 4718596
  26.9 2.6 %copy-start.2 = (bf16[256,3072]{1,0:T(8,128)(2,1)S(1)}, bf16[256,3072]{1,0:T(8,128)(2,1)}, u32[]{:S(2)}) copy-start(bf16[256,3072]{1,0:T(8,128)(2,1)} %refs_7_.1) | copy-start | bytes 4718596
  26.9 5.3 %collective-permute-start.13 = (bf16[16,3072]{1,0:T(8,128)(2,1)S(1)}, bf16[16,3072]{1,0:T(8,128)(2,1)S(1)}, u32[]{:S(2)}, u32[]{:S(2)}) collective-permute-start(bf16[16,3072]{1,0:T(8,128)(2,1)S(1)} %get-tuple-element.99.refs_0_), channel_id=1, source_target_pairs={{0,2},{1,3},{2,0},{3,1},{4,6},{5,7},{6,4},{7,5},{8,10},{9,11},{10,... | collective-permute-start | bytes 294920 | tf_op jit(solution)/shard_map/ppermute | solution.py:32
  27.6 5.0 %collective-permute-start.14 = (bf16[16,3072]{1,0:T(8,128)(2,1)S(1)}, bf16[16,3072]{1,0:T(8,128)(2,1)S(1)}, u32[]{:S(2)}, u32[]{:S(2)}) collective-permute-start(bf16[16,3072]{1,0:T(8,128)(2,1)S(1)} %get-tuple-element.100.refs_2_), channel_id=1, source_target_pairs={{0,4},{1,5},{2,6},{3,7},{4,0},{5,1},{6,2},{7,3},{8,12},{9,13},{10,... | collective-permute-start | bytes 294920 | tf_op jit(solution)/shard_map/ppermute | solution.py:32
  32.7 7.7 %collective-permute-start.17 = (bf16[32,3072]{1,0:T(8,128)(2,1)S(1)}, bf16[32,3072]{1,0:T(8,128)(2,1)S(1)}, u32[]{:S(2)}, u32[]{:S(2)}) collective-permute-start(bf16[32,3072]{1,0:T(8,128)(2,1)S(1)} %get-tuple-element.107.refs_0_), channel_id=1, source_target_pairs={{0,4},{1,5},{2,6},{3,7},{4,0},{5,1},{6,2},{7,3},{8,12},{9,13},{10,... | collective-permute-start | bytes 589832 | tf_op jit(solution)/shard_map/ppermute | solution.py:32
  35.1 7.8 %collective-permute-start.18 = (bf16[32,3072]{1,0:T(8,128)(2,1)S(1)}, bf16[32,3072]{1,0:T(8,128)(2,1)S(1)}, u32[]{:S(2)}, u32[]{:S(2)}) collective-permute-start(bf16[32,3072]{1,0:T(8,128)(2,1)S(1)} %get-tuple-element.108.refs_2_), channel_id=1, source_target_pairs={{0,2},{1,3},{2,0},{3,1},{4,6},{5,7},{6,4},{7,5},{8,10},{9,11},{10,... | collective-permute-start | bytes 589832 | tf_op jit(solution)/shard_map/ppermute | solution.py:32
  39.4 12.1 %collective-permute-start.15 = (bf16[64,3072]{1,0:T(8,128)(2,1)S(1)}, bf16[64,3072]{1,0:T(8,128)(2,1)S(1)}, u32[]{:S(2)}, u32[]{:S(2)}) collective-permute-start(bf16[64,3072]{1,0:T(8,128)(2,1)S(1)} %get-tuple-element.104), channel_id=1, source_target_pairs={{0,4},{1,5},{2,6},{3,7},{4,0},{5,1},{6,2},{7,3},{8,12},{9,13},{10,... | collective-permute-start | bytes 1179656 | tf_op jit(solution)/shard_map/ppermute | solution.py:32
  39.6 12.1 %collective-permute-start.16 = (bf16[64,3072]{1,0:T(8,128)(2,1)S(1)}, bf16[64,3072]{1,0:T(8,128)(2,1)S(1)}, u32[]{:S(2)}, u32[]{:S(2)}) collective-permute-start(bf16[64,3072]{1,0:T(8,128)(2,1)S(1)} %get-tuple-element.106), channel_id=1, source_target_pairs={{0,2},{1,3},{2,0},{3,1},{4,6},{5,7},{6,4},{7,5},{8,10},{9,11},{10,... | collective-permute-start | bytes 1179656 | tf_op jit(solution)/shard_map/ppermute | solution.py:32
  45.9 11.8 %collective-permute-start.22 = (bf16[64,3072]{1,0:T(8,128)(2,1)S(1)}, bf16[64,3072]{1,0:T(8,128)(2,1)S(1)}, u32[]{:S(2)}, u32[]{:S(2)}) collective-permute-start(bf16[64,3072]{1,0:T(8,128)(2,1)S(1)} %get-tuple-element.117), channel_id=1, source_target_pairs={{0,4},{1,5},{2,6},{3,7},{4,0},{5,1},{6,2},{7,3},{8,12},{9,13},{10,... | collective-permute-start | bytes 1179656 | tf_op jit(solution)/shard_map/ppermute | solution.py:32
  46.0 12.4 %collective-permute-start.23 = (bf16[64,3072]{1,0:T(8,128)(2,1)S(1)}, bf16[64,3072]{1,0:T(8,128)(2,1)S(1)}, u32[]{:S(2)}, u32[]{:S(2)}) collective-permute-start(bf16[64,3072]{1,0:T(8,128)(2,1)S(1)} %get-tuple-element.119), channel_id=1, source_target_pairs={{0,2},{1,3},{2,0},{3,1},{4,6},{5,7},{6,4},{7,5},{8,10},{9,11},{10,... | collective-permute-start | bytes 1179656 | tf_op jit(solution)/shard_map/ppermute | solution.py:32
  51.7 10.0 %collective-permute-start.20 = (bf16[32,3072]{1,0:T(8,128)(2,1)S(1)}, bf16[32,3072]{1,0:T(8,128)(2,1)S(1)}, u32[]{:S(2)}, u32[]{:S(2)}) collective-permute-start(bf16[32,3072]{1,0:T(8,128)(2,1)S(1)} %get-tuple-element.113), channel_id=1, source_target_pairs={{0,2},{1,3},{2,0},{3,1},{4,6},{5,7},{6,4},{7,5},{8,10},{9,11},{10,... | collective-permute-start | bytes 589832 | tf_op jit(solution)/shard_map/ppermute | solution.py:32
  52.8 8.9 %collective-permute-start.21 = (bf16[32,3072]{1,0:T(8,128)(2,1)S(1)}, bf16[32,3072]{1,0:T(8,128)(2,1)S(1)}, u32[]{:S(2)}, u32[]{:S(2)}) collective-permute-start(bf16[32,3072]{1,0:T(8,128)(2,1)S(1)} %get-tuple-element.115), channel_id=1, source_target_pairs={{0,4},{1,5},{2,6},{3,7},{4,0},{5,1},{6,2},{7,3},{8,12},{9,13},{10,... | collective-permute-start | bytes 589832 | tf_op jit(solution)/shard_map/ppermute | solution.py:32
  55.9 9.7 %collective-permute-start.28 = (bf16[3,256,3072]{2,1,0:T(8,128)(2,1)S(1)}, bf16[3,256,3072]{2,1,0:T(8,128)(2,1)S(1)}, u32[]{:S(2)}, u32[]{:S(2)}) collective-permute-start(bf16[3,256,3072]{2,1,0:T(8,128)(2,1)S(1)} %get-tuple-element.142), channel_id=1, source_target_pairs={{0,1},{1,0},{2,3},{3,2},{4,5},{5,4},{6,7},{7,6},{8,9},{9,8},{10,11... | collective-permute-start | bytes 14155784 | tf_op jit(solution)/shard_map/ppermute | solution.py:32
  58.6 6.3 %collective-permute-start.24 = (bf16[32,3072]{1,0:T(8,128)(2,1)S(1)}, bf16[32,3072]{1,0:T(8,128)(2,1)S(1)}, u32[]{:S(2)}, u32[]{:S(2)}) collective-permute-start(bf16[32,3072]{1,0:T(8,128)(2,1)S(1)} %get-tuple-element.135), channel_id=1, source_target_pairs={{0,2},{1,3},{2,0},{3,1},{4,6},{5,7},{6,4},{7,5},{8,10},{9,11},{10,... | collective-permute-start | bytes 589832 | tf_op jit(solution)/shard_map/ppermute | solution.py:32
  59.4 5.7 %collective-permute-start.25 = (bf16[32,3072]{1,0:T(8,128)(2,1)S(1)}, bf16[32,3072]{1,0:T(8,128)(2,1)S(1)}, u32[]{:S(2)}, u32[]{:S(2)}) collective-permute-start(bf16[32,3072]{1,0:T(8,128)(2,1)S(1)} %get-tuple-element.137), channel_id=1, source_target_pairs={{0,4},{1,5},{2,6},{3,7},{4,0},{5,1},{6,2},{7,3},{8,12},{9,13},{10,... | collective-permute-start | bytes 589832 | tf_op jit(solution)/shard_map/ppermute | solution.py:32
  61.8 6.7 %collective-permute-start.27 = (bf16[2,16,3072]{2,1,0:T(8,128)(2,1)S(1)}, bf16[2,16,3072]{2,1,0:T(8,128)(2,1)S(1)}, u32[]{:S(2)}, u32[]{:S(2)}) collective-permute-start(bf16[2,16,3072]{2,1,0:T(8,128)(2,1)S(1)} %get-tuple-element.141), channel_id=1, source_target_pairs={{0,24},{1,25},{2,26},{3,27},{4,28},{5,29},{6,30},{7,31},{8,0},{9,1... | collective-permute-start | bytes 589832 | tf_op jit(solution)/shard_map/ppermute | solution.py:40
  65.2 9.7 %collective-permute-start.26 = (bf16[2,16,3072]{2,1,0:T(8,128)(2,1)S(1)}, bf16[2,16,3072]{2,1,0:T(8,128)(2,1)S(1)}, u32[]{:S(2)}, u32[]{:S(2)}) collective-permute-start(bf16[2,16,3072]{2,1,0:T(8,128)(2,1)S(1)} %get-tuple-element.139), channel_id=1, source_target_pairs={{0,8},{1,9},{2,10},{3,11},{4,12},{5,13},{6,14},{7,15},{8,16},{9,17... | collective-permute-start | bytes 589832 | tf_op jit(solution)/shard_map/ppermute | solution.py:40
  68.5 8.6 %collective-permute-start.29 = (bf16[2,16,3072]{2,1,0:T(8,128)(2,1)S(1)}, bf16[2,16,3072]{2,1,0:T(8,128)(2,1)S(1)}, u32[]{:S(2)}, u32[]{:S(2)}) collective-permute-start(bf16[2,16,3072]{2,1,0:T(8,128)(2,1)S(1)} %get-tuple-element.147), channel_id=1, source_target_pairs={{0,24},{1,25},{2,26},{3,27},{4,28},{5,29},{6,30},{7,31},{8,0},{9,1... | collective-permute-start | bytes 589832 | tf_op jit(solution)/shard_map/ppermute | solution.py:40

commit v8 on v7

--- a/solution.py
+++ b/solution.py
@@ -21,6 +21,7 @@
 C_LOAD = LONG // 5
 PANEL = 512
 WIDE = 1536
+FIRST_GRADS, LAST_GRADS = (0,), (1, 2)
 TURN = pltpu.VMEM((8, 128), jnp.float32)
 VMEM = pl.BlockSpec(memory_space=pltpu.VMEM)
 HBM = pl.BlockSpec(memory_space=pltpu.HBM)
@@ -210,13 +211,12 @@
     )(*fetched(*(ref for part in parts for ref in part), *panels, turn))
 
 
-def slot_sums(works, units, columns):
-    x, e, hidden, gate_grad, up_grad = (
-        jnp.concatenate([refs[i][:, units if i > 1 else columns] for refs in works], 0)
-        for i in range(5)
-    )
-    for left, right in ((gate_grad, x), (up_grad, x), (hidden, e)):
-        yield col_product(left, right)
+def slot_sum(works, which, units, columns):
+    left, right = ((3, 0), (4, 0), (2, 1))[which]
+    return col_product(
+        jnp.concatenate([refs[left][:, units] for refs in works], 0),
+        jnp.concatenate([refs[right][:, columns] for refs in works], 0),
+    )
 
 
 def other_kernel(*refs):
@@ -225,8 +225,8 @@
     units = grads.shape[1]
     for at in range(0, grads.shape[2], PANEL):
         columns = slice(at, at + PANEL)
-        for i, total in enumerate(slot_sums(works, slice(units, 2 * units), columns)):
-            grads[i, :, columns] = half(total)
+        for i in range(3):
+            grads[i, :, columns] = half(slot_sum(works, i, slice(units, 2 * units), columns))
 
 
 def other_grads(works, turn):
@@ -243,25 +243,26 @@
     )(*fetched(*works[0], *works[1], turn))
 
 
-def own_kernel(factor, *refs):
+def own_kernel(which, factor, *refs):
     works, (received, _, *grads, turn) = (refs[:5], refs[5:10]), refs[10:]
     turn[...] = jnp.zeros_like(turn)
     units = received.shape[1]
     columns = pl.ds(pl.multiple_of(pl.program_id(0) * WIDE, WIDE), WIDE)
-    for i, total in enumerate(slot_sums(works, slice(0, units), columns)):
+    for i, grad in zip(which, grads):
+        total = slot_sum(works, i, slice(0, units), columns)
         total = total + received[i, :, columns].astype(jnp.float32)
-        grads[i][...] = (total * factor).astype(grads[i].dtype)
-
-
-def own_grads(works, received, turn, factor, dtype):
+        grad[...] = (total * factor).astype(grad.dtype)
+
+
+def own_grads(which, works, received, turn, factor, dtype):
     _, units, width = received.shape
     block = pl.BlockSpec((units, WIDE), lambda i: (0, i))
     return pl.pallas_call(
-        functools.partial(own_kernel, factor),
+        functools.partial(own_kernel, which, factor),
         grid=(width // WIDE,),
-        out_shape=(shape((units, width), dtype),) * 3 + (TURN,),
+        out_shape=(shape((units, width), dtype),) * len(which) + (TURN,),
         in_specs=[VMEM] * 12,
-        out_specs=(block,) * 3 + (VMEM,),
+        out_specs=(block,) * len(which) + (VMEM,),
         compiler_params=limit(12),
         cost_estimate=cost(0, 0),
         name="own_grads",
@@ -432,16 +433,17 @@
     sum_1, sum_3, turn = line_sum(middle_31, turn, jnp.float32)
     three = shifted(sum_3, 1)
     factor = 1.0 / math.sqrt(devices * capacity)
+    scale, dtype = (1.0, jnp.float32) if far_bits else (factor, jnp.bfloat16)
+    *owned, turn = own_grads(FIRST_GRADS, works, received, turn, scale, dtype)
+    sum_1, turn = staged(relay_body, "relay", [held(own.shape)], sum_1, passed, turn)
+    one = shifted(sum_1, -1)
+    *rest, turn = own_grads(LAST_GRADS, works, received, turn, scale, dtype)
+    owned += rest
     if far_bits:
-        *owned, turn = own_grads(works, received, turn, 1.0, jnp.float32)
         for bit in reversed(far_bits):
             cut = owned[0].shape[0] // 2
             owned = [t[:cut] + swapped(half(t[cut:]), 1 << bit) for t in owned]
         owned = [half(total * factor) for total in owned]
-    else:
-        *owned, turn = own_grads(works, received, turn, factor, jnp.bfloat16)
-    sum_1, turn = staged(relay_body, "relay", [held(own.shape)], sum_1, passed, turn)
-    one = shifted(sum_1, -1)
     total, turn = staged(
         near_body, "near_sum", [held(own.shape, jnp.float32)], sum_0, three, turn, flops=LONG // 10
     )

time: 77.9 us -> 77.5 us (level)
  waiting for transfers between devices: 22 us -> 20.3 us
  Pallas kernels: 15.6 us -> 16.7 us
    ppermute x6, waiting for transfers between devices: 4.31 us -> 2.61 us  [shifted(): return lax.ppermute(block, 'dp', route)]
    pallas_call x1 -> x2, Pallas kernels: 2.89 us -> 3.87 us  [own_grads(): pl.pallas_call(functools.partial(own_kernel, which, factor), grid=(width...]
  transfers between devices with their start and end apart: 30 -> 30, of which waited for: 16 -> 16; matrix products, arithmetic and copies ran while one was open for 0% -> 0% of each run, Pallas kernels for 19% -> 21%
where the time goes in v8:
time: 77.5 us; the launch traced here: 77.3 us
  starting transfers between devices  39.6 us (51%)
  waiting for transfers between devices  20.3 us (26%)
  Pallas kernels  16.7 us (22%)
  between operations  0.78 us (1%)
    ppermute x24, starting transfers between devices, swapped(): lax.ppermute(block, 'dp', [(low, low ^ mask) for low in range(count)])  23.9 us
    ppermute x24, waiting for transfers between devices, swapped(): lax.ppermute(block, 'dp', [(low, low ^ mask) for low in range(count)])  17.6 us
    ppermute x6, starting transfers between devices, shifted(): return lax.ppermute(block, 'dp', route)  15.7 us
    pallas_call x2, Pallas kernels, expert(): pl.pallas_call(functools.partial(expert_kernel, [len(part) for part in pa...  5.99 us
    pallas_call x15, Pallas kernels, staged(): pl.pallas_call(kernel, out_shape=(*outs, TURN), in_specs=[VMEM] * len(val...  3.97 us
    pallas_call x2, Pallas kernels, own_grads(): pl.pallas_call(functools.partial(own_kernel, which, factor), grid=(width...  3.87 us
    ppermute x6, waiting for transfers between devices, shifted(): return lax.ppermute(block, 'dp', route)  2.61 us
  transfers between devices with their start and end apart: 30, of which 16 were waited for; matrix products, arithmetic and copies ran while one was open for 0% of the time, Pallas kernels for 21%

profile of v8, /device:TPU:0, one launch (start us, length us, event | category | flops | bytes accessed | tf_op | source)
XLA Modules:
  0.0 77.3 jit_solution(15047638003750870475)
XLA Ops:
  0.6 0.5 collective-permute-start
  1.2 1.4 %pick.1 = (bf16[2,16,3072]{2,1,0:T(8,128)(2,1)S(1)}, f32[16,128]{1,0:T(8,128)S(1)}, f32[8,128]{1,0:T(8,128)S(1)}) custom-call(s32[1]{0:T(128)} %bitcast.place, s32[16]{0:T(128)} %token_.1, s32[32]{0:T(128)} %count.1, f32[16]{0:T(128)} %gate.1, bf16[128,3072]{1,0:T(8,128)(2,1)} %tokens.1, bf16[16,3072]{1,0:T(8,128)(2,1)} %grad.1), custom_call_target="tpu_custom_call" | custom-call | tf_op jit(solution)/shard_map/pick/pallas_call | solution.py:123
  2.6 3.7 %collective-permute-start.7 = (bf16[2,16,3072]{2,1,0:T(8,128)(2,1)S(1)}, bf16[2,16,3072]{2,1,0:T(8,128)(2,1)S(1)}, u32[]{:S(2)}, u32[]{:S(2)}) collective-permute-start(bf16[2,16,3072]{2,1,0:T(8,128)(2,1)S(1)} %get-tuple-element.81.refs_0_), channel_id=1, source_target_pairs={{0,16},{1,17},{2,18},{3,19},{4,20},{5,21},{6,22},{7,23},{8,24},{9,... | collective-permute-start | bytes 589832 | tf_op jit(solution)/shard_map/ppermute | solution.py:41
  6.2 0.2 collective-permute-start.3
  6.5 0.3 collective-permute-start.4
  6.8 1.6 %collective-permute-start.1 = (bf16[16,3072]{1,0:T(8,128)(2,1)S(1)}, bf16[16,3072]{1,0:T(8,128)(2,1)S(1)}, u32[]{:S(2)}, u32[]{:S(2)}) collective-permute-start(bf16[16,3072]{1,0:T(8,128)(2,1)S(1)} %get-tuple-element.83.refs_0_), channel_id=1, source_target_pairs={{0,2},{1,3},{2,0},{3,1},{4,6},{5,7},{6,4},{7,5},{8,10},{9,11},{10,... | collective-permute-start | bytes 294920 | tf_op jit(solution)/shard_map/ppermute | solution.py:33
  8.3 1.5 %collective-permute-start.2 = (bf16[16,3072]{1,0:T(8,128)(2,1)S(1)}, bf16[16,3072]{1,0:T(8,128)(2,1)S(1)}, u32[]{:S(2)}, u32[]{:S(2)}) collective-permute-start(bf16[16,3072]{1,0:T(8,128)(2,1)S(1)} %get-tuple-element.84.refs_2_), channel_id=1, source_target_pairs={{0,4},{1,5},{2,6},{3,7},{4,0},{5,1},{6,2},{7,3},{8,12},{9,13},{10,... | collective-permute-start | bytes 294920 | tf_op jit(solution)/shard_map/ppermute | solution.py:33
  9.9 2.2 %collective-permute-done.4.refs_5_.refs_13_.refs_10_ = bf16[256,3072]{1,0:T(8,128)(2,1)S(1)} collective-permute-done((bf16[256,3072]{1,0:T(8,128)(2,1)}, bf16[256,3072]{1,0:T(8,128)(2,1)S(1)}, u32[]{:S(2)}, u32[]{:S(2)}) %collective-permute-start.4) | collective-permute-done | bytes 1572896 | tf_op jit(solution)/shard_map/ppermute | solution.py:33
  12.1 0.8 %collective-permute-done.2.refs_3_ = bf16[16,3072]{1,0:T(8,128)(2,1)S(1)} collective-permute-done((bf16[16,3072]{1,0:T(8,128)(2,1)S(1)}, bf16[16,3072]{1,0:T(8,128)(2,1)S(1)}, u32[]{:S(2)}, u32[]{:S(2)}) %collective-permute-start.2) | collective-permute-done | bytes 98336 | tf_op jit(solution)/shard_map/ppermute | solution.py:33
  13.0 1.6 %collective-permute-start.12 = (bf16[2,16,3072]{2,1,0:T(8,128)(2,1)S(1)}, bf16[2,16,3072]{2,1,0:T(8,128)(2,1)S(1)}, u32[]{:S(2)}, u32[]{:S(2)}) collective-permute-start(bf16[2,16,3072]{2,1,0:T(8,128)(2,1)S(1)} %get-tuple-element.95), channel_id=1, source_target_pairs={{0,8},{1,9},{2,10},{3,11},{4,12},{5,13},{6,14},{7,15},{8,16},{9,17... | collective-permute-start | bytes 589832 | tf_op jit(solution)/shard_map/ppermute | solution.py:41
  14.6 1.5 %collective-permute-start.5 = (bf16[32,3072]{1,0:T(8,128)(2,1)S(1)}, bf16[32,3072]{1,0:T(8,128)(2,1)S(1)}, u32[]{:S(2)}, u32[]{:S(2)}) collective-permute-start(bf16[32,3072]{1,0:T(8,128)(2,1)S(1)} %get-tuple-element.86.refs_0_), channel_id=1, source_target_pairs={{0,4},{1,5},{2,6},{3,7},{4,0},{5,1},{6,2},{7,3},{8,12},{9,13},{10,... | collective-permute-start | bytes 589832 | tf_op jit(solution)/shard_map/ppermute | solution.py:33
  16.2 0.7 collective-permute-start.6
  16.8 1.4 %collective-permute-start.8 = (bf16[16,3072]{1,0:T(8,128)(2,1)S(1)}, bf16[16,3072]{1,0:T(8,128)(2,1)S(1)}, u32[]{:S(2)}, u32[]{:S(2)}) collective-permute-start(bf16[16,3072]{1,0:T(8,128)(2,1)S(1)} %get-tuple-element.89.refs_0_), channel_id=1, source_target_pairs={{0,2},{1,3},{2,0},{3,1},{4,6},{5,7},{6,4},{7,5},{8,10},{9,11},{10,... | collective-permute-start | bytes 294920 | tf_op jit(solution)/shard_map/ppermute | solution.py:33
  18.3 0.9 %collective-permute-start.9 = (bf16[16,3072]{1,0:T(8,128)(2,1)S(1)}, bf16[16,3072]{1,0:T(8,128)(2,1)S(1)}, u32[]{:S(2)}, u32[]{:S(2)}) collective-permute-start(bf16[16,3072]{1,0:T(8,128)(2,1)S(1)} %get-tuple-element.90.refs_2_), channel_id=1, source_target_pairs={{0,4},{1,5},{2,6},{3,7},{4,0},{5,1},{6,2},{7,3},{8,12},{9,13},{10,... | collective-permute-start | bytes 294920 | tf_op jit(solution)/shard_map/ppermute | solution.py:33
  19.2 2.2 %collective-permute-done.5.refs_1_ = bf16[32,3072]{1,0:T(8,128)(2,1)S(1)} collective-permute-done((bf16[32,3072]{1,0:T(8,128)(2,1)S(1)}, bf16[32,3072]{1,0:T(8,128)(2,1)S(1)}, u32[]{:S(2)}, u32[]{:S(2)}) %collective-permute-start.5) | collective-permute-done | bytes 196640 | tf_op jit(solution)/shard_map/ppermute | solution.py:33
  21.3 1.5 %collective-permute-done.6.refs_3_ = bf16[32,3072]{1,0:T(8,128)(2,1)S(1)} collective-permute-done((bf16[32,3072]{1,0:T(8,128)(2,1)S(1)}, bf16[32,3072]{1,0:T(8,128)(2,1)S(1)}, u32[]{:S(2)}, u32[]{:S(2)}) %collective-permute-start.6) | collective-permute-done | bytes 196640 | tf_op jit(solution)/shard_map/ppermute | solution.py:33
  22.9 2.4 %collective-permute-start.19 = (bf16[128,3072]{1,0:T(8,128)(2,1)S(1)}, bf16[128,3072]{1,0:T(8,128)(2,1)S(1)}, u32[]{:S(2)}, u32[]{:S(2)}) collective-permute-start(bf16[128,3072]{1,0:T(8,128)(2,1)S(1)} %get-tuple-element.110), channel_id=1, source_target_pairs={{0,24},{1,25},{2,26},{3,27},{4,28},{5,29},{6,30},{7,31},{8,0},{9,1... | collective-permute-start | bytes 2359304 | tf_op jit(solution)/shard_map/ppermute | solution.py:41
  25.3 0.2 collective-permute-start.10
  25.5 1.4 %collective-permute-start.11 = (bf16[32,3072]{1,0:T(8,128)(2,1)S(1)}, bf16[32,3072]{1,0:T(8,128)(2,1)S(1)}, u32[]{:S(2)}, u32[]{:S(2)}) collective-permute-start(bf16[32,3072]{1,0:T(8,128)(2,1)S(1)} %get-tuple-element.94.refs_6_), channel_id=1, source_target_pairs={{0,2},{1,3},{2,0},{3,1},{4,6},{5,7},{6,4},{7,5},{8,10},{9,11},{10,... | collective-permute-start | bytes 589832 | tf_op jit(solution)/shard_map/ppermute | solution.py:33
  26.9 0.7 collective-permute-start.13
  27.6 1.9 %collective-permute-start.14 = (bf16[16,3072]{1,0:T(8,128)(2,1)S(1)}, bf16[16,3072]{1,0:T(8,128)(2,1)S(1)}, u32[]{:S(2)}, u32[]{:S(2)}) collective-permute-start(bf16[16,3072]{1,0:T(8,128)(2,1)S(1)} %get-tuple-element.101.refs_2_), channel_id=1, source_target_pairs={{0,4},{1,5},{2,6},{3,7},{4,0},{5,1},{6,2},{7,3},{8,12},{9,13},{10,... | collective-permute-start | bytes 294920 | tf_op jit(solution)/shard_map/ppermute | solution.py:33
  29.5 2.5 %turn_panels.1 = (bf16[3,3072,256]{2,1,0:T(8,128)(2,1)S(1)}, bf16[3,3072,256]{2,1,0:T(8,128)(2,1)S(1)}, f32[8,128]{1,0:T(8,128)S(1)}) custom-call(bf16[256,3072]{1,0:T(8,128)(2,1)S(1)} %copy-done, bf16[256,3072]{1,0:T(8,128)(2,1)S(1)} %copy-done.1, bf16[256,3072]{1,0:T(8,128)(2,1)S(1)} %copy-done.2, ...), custom_call_target="tpu_custom_call" | custom-call | tf_op jit(solution)/shard_map/turn_panels/pallas_call | solution.py:277
  32.0 0.2 collective-permute-done.13.refs_1_
  32.2 0.4 collective-permute-done.14.refs_3_
  32.7 2.4 %collective-permute-start.17 = (bf16[32,3072]{1,0:T(8,128)(2,1)S(1)}, bf16[32,3072]{1,0:T(8,128)(2,1)S(1)}, u32[]{:S(2)}, u32[]{:S(2)}) collective-permute-start(bf16[32,3072]{1,0:T(8,128)(2,1)S(1)} %get-tuple-element.108.refs_0_), channel_id=1, source_target_pairs={{0,4},{1,5},{2,6},{3,7},{4,0},{5,1},{6,2},{7,3},{8,12},{9,13},{10,... | collective-permute-start | bytes 589832 | tf_op jit(solution)/shard_map/ppermute | solution.py:33
  35.1 1.3 %collective-permute-start.18 = (bf16[32,3072]{1,0:T(8,128)(2,1)S(1)}, bf16[32,3072]{1,0:T(8,128)(2,1)S(1)}, u32[]{:S(2)}, u32[]{:S(2)}) collective-permute-start(bf16[32,3072]{1,0:T(8,128)(2,1)S(1)} %get-tuple-element.109.refs_2_), channel_id=1, source_target_pairs={{0,2},{1,3},{2,0},{3,1},{4,6},{5,7},{6,4},{7,5},{8,10},{9,11},{10,... | collective-permute-start | bytes 589832 | tf_op jit(solution)/shard_map/ppermute | solution.py:33
  36.4 3.0 %expert.2 = (bf16[128,3072]{1,0:T(8,128)(2,1)S(1)}, bf16[128,3072]{1,0:T(8,128)(2,1)S(1)}, bf16[128,512]{1,0:T(8,128)(2,1)S(1)}, bf16[128,512]{1,0:T(8,128)(2,1)...) custom-call(bf16[32,3072]{1,0:T(8,128)(2,1)S(1)} %get-tuple-element., ...), custom_call_target="tpu_custom_call" | custom-call | flops 2415919104 | bytes 9437184 | tf_op jit(solution)/shard_map/expert/pallas_call | solution.py:203
  39.6 0.7 collective-permute-start.16
  40.4 2.5 %collective-permute-done.18.refs_3_ = bf16[32,3072]{1,0:T(8,128)(2,1)S(1)} collective-permute-done((bf16[32,3072]{1,0:T(8,128)(2,1)S(1)}, bf16[32,3072]{1,0:T(8,128)(2,1)S(1)}, u32[]{:S(2)}, u32[]{:S(2)}) %collective-permute-start.18) | collective-permute-done | bytes 196640 | tf_op jit(solution)/shard_map/ppermute | solution.py:33
  42.9 3.0 %expert.3 = (bf16[128,3072]{1,0:T(8,128)(2,1)S(1)}, bf16[128,3072]{1,0:T(8,128)(2,1)S(1)}, bf16[128,512]{1,0:T(8,128)(2,1)S(1)}, bf16[128,512]{1,0:T(8,128)(2,1)...) custom-call(bf16[32,3072]{1,0:T(8,128)(2,1)S(1)} %get-tuple-element., ...), custom_call_target="tpu_custom_call" | custom-call | flops 2415919104 | bytes 9437184 | tf_op jit(solution)/shard_map/expert/pallas_call | solution.py:203
  46.0 1.4 %collective-permute-start.23 = (bf16[64,3072]{1,0:T(8,128)(2,1)S(1)}, bf16[64,3072]{1,0:T(8,128)(2,1)S(1)}, u32[]{:S(2)}, u32[]{:S(2)}) collective-permute-start(bf16[64,3072]{1,0:T(8,128)(2,1)S(1)} %get-tuple-element.120), channel_id=1, source_target_pairs={{0,2},{1,3},{2,0},{3,1},{4,6},{5,7},{6,4},{7,5},{8,10},{9,11},{10,... | collective-permute-start | bytes 1179656 | tf_op jit(solution)/shard_map/ppermute | solution.py:33
  47.4 4.1 %collective-permute-done.15.refs_1_ = bf16[64,3072]{1,0:T(8,128)(2,1)S(1)} collective-permute-done((bf16[64,3072]{1,0:T(8,128)(2,1)S(1)}, bf16[64,3072]{1,0:T(8,128)(2,1)S(1)}, u32[]{:S(2)}, u32[]{:S(2)}) %collective-permute-start.15) | collective-permute-done | bytes 393248 | tf_op jit(solution)/shard_map/ppermute | solution.py:33
  51.8 1.1 %collective-permute-start.20 = (bf16[32,3072]{1,0:T(8,128)(2,1)S(1)}, bf16[32,3072]{1,0:T(8,128)(2,1)S(1)}, u32[]{:S(2)}, u32[]{:S(2)}) collective-permute-start(bf16[32,3072]{1,0:T(8,128)(2,1)S(1)} %get-tuple-element.114), channel_id=1, source_target_pairs={{0,2},{1,3},{2,0},{3,1},{4,6},{5,7},{6,4},{7,5},{8,10},{9,11},{10,... | collective-permute-start | bytes 589832 | tf_op jit(solution)/shard_map/ppermute | solution.py:33
  52.9 1.6 %collective-permute-start.21 = (bf16[32,3072]{1,0:T(8,128)(2,1)S(1)}, bf16[32,3072]{1,0:T(8,128)(2,1)S(1)}, u32[]{:S(2)}, u32[]{:S(2)}) collective-permute-start(bf16[32,3072]{1,0:T(8,128)(2,1)S(1)} %get-tuple-element.116), channel_id=1, source_target_pairs={{0,4},{1,5},{2,6},{3,7},{4,0},{5,1},{6,2},{7,3},{8,12},{9,13},{10,... | collective-permute-start | bytes 589832 | tf_op jit(solution)/shard_map/ppermute | solution.py:33
  54.5 1.4 %other_grads.1 = (bf16[3,256,3072]{2,1,0:T(8,128)(2,1)S(1)}, f32[8,128]{1,0:T(8,128)S(1)}) custom-call(bf16[128,3072]{1,0:T(8,128)(2,1)S(1)} %get-tuple-element.121.refs_0_, bf16[128,3072]{1,0:T(8,128)(2,1)S(1)} %get-tuple-element.122.refs_1_, bf16[128,512]{1,0:T(8,128)(2,1)S(1)} %get-tuple-element.123.refs_2_, ...), custom_call_target="tpu_custom_call" | custom-call | flops 2000000000 | tf_op jit(solution)/shard_map/other_grads/pallas_call | solution.py:235
  56.0 1.7 %collective-permute-done.22.refs_1_ = bf16[64,3072]{1,0:T(8,128)(2,1)S(1)} collective-permute-done((bf16[64,3072]{1,0:T(8,128)(2,1)S(1)}, bf16[64,3072]{1,0:T(8,128)(2,1)S(1)}, u32[]{:S(2)}, u32[]{:S(2)}) %collective-permute-start.22) | collective-permute-done | bytes 393248 | tf_op jit(solution)/shard_map/ppermute | solution.py:33
  57.7 0.8 collective-permute-done.23.refs_3_
  58.6 0.8 %collective-permute-start.24 = (bf16[32,3072]{1,0:T(8,128)(2,1)S(1)}, bf16[32,3072]{1,0:T(8,128)(2,1)S(1)}, u32[]{:S(2)}, u32[]{:S(2)}) collective-permute-start(bf16[32,3072]{1,0:T(8,128)(2,1)S(1)} %get-tuple-element.136), channel_id=1, source_target_pairs={{0,2},{1,3},{2,0},{3,1},{4,6},{5,7},{6,4},{7,5},{8,10},{9,11},{10,... | collective-permute-start | bytes 589832 | tf_op jit(solution)/shard_map/ppermute | solution.py:33
  59.4 1.4 %collective-permute-start.25 = (bf16[32,3072]{1,0:T(8,128)(2,1)S(1)}, bf16[32,3072]{1,0:T(8,128)(2,1)S(1)}, u32[]{:S(2)}, u32[]{:S(2)}) collective-permute-start(bf16[32,3072]{1,0:T(8,128)(2,1)S(1)} %get-tuple-element.138), channel_id=1, source_target_pairs={{0,4},{1,5},{2,6},{3,7},{4,0},{5,1},{6,2},{7,3},{8,12},{9,13},{10,... | collective-permute-start | bytes 589832 | tf_op jit(solution)/shard_map/ppermute | solution.py:33
  60.8 0.8 %collective-permute-done.20.refs_1_ = bf16[32,3072]{1,0:T(8,128)(2,1)S(1)} collective-permute-done((bf16[32,3072]{1,0:T(8,128)(2,1)S(1)}, bf16[32,3072]{1,0:T(8,128)(2,1)S(1)}, u32[]{:S(2)}, u32[]{:S(2)}) %collective-permute-start.20) | collective-permute-done | bytes 196640 | tf_op jit(solution)/shard_map/ppermute | solution.py:33
  61.7 3.2 %collective-permute-start.28 = (bf16[2,16,3072]{2,1,0:T(8,128)(2,1)S(1)}, bf16[2,16,3072]{2,1,0:T(8,128)(2,1)S(1)}, u32[]{:S(2)}, u32[]{:S(2)}) collective-permute-start(bf16[2,16,3072]{2,1,0:T(8,128)(2,1)S(1)} %get-tuple-element.143), channel_id=1, source_target_pairs={{0,24},{1,25},{2,26},{3,27},{4,28},{5,29},{6,30},{7,31},{8,0},{9,1... | collective-permute-start | bytes 589832 | tf_op jit(solution)/shard_map/ppermute | solution.py:41
  65.2 0.4 collective-permute-start.26
  65.6 1.7 %own_grads.2 = (bf16[256,3072]{1,0:T(8,128)(2,1)}, f32[8,128]{1,0:T(8,128)S(1)}) custom-call(bf16[128,3072]{1,0:T(8,128)(2,1)S(1)} %get-tuple-element.121.refs_0_, bf16[128,3072]{1,0:T(8,128)(2,1)S(1)} %get-tuple-element.122.refs_1_, bf16[128,512]{1,0:T(8,128)(2,1)S(1)} %get-tuple-element.123.refs_2_, bf16[128,512]{1,0:T(8,128)(2,1)S(1)} %get-tuple-element.124.refs_3_, ...), custom_call_target="tpu_custom_call" | custom-call | tf_op jit(solution)/shard_map/own_grads/pallas_call | solution.py:260
  67.3 0.9 %collective-permute-done.28.refs_1_ = bf16[2,16,3072]{2,1,0:T(8,128)(2,1)S(1)} collective-permute-done((bf16[2,16,3072]{2,1,0:T(8,128)(2,1)S(1)}, bf16[2,16,3072]{2,1,0:T(8,128)(2,1)S(1)}, u32[]{:S(2)}, u32[]{:S(2)}) %collective-permute-start.28) | collective-permute-done | bytes 196640 | tf_op jit(solution)/shard_map/ppermute | solution.py:41
  68.2 4.5 %collective-permute-start.29 = (bf16[2,16,3072]{2,1,0:T(8,128)(2,1)S(1)}, bf16[2,16,3072]{2,1,0:T(8,128)(2,1)S(1)}, u32[]{:S(2)}, u32[]{:S(2)}) collective-permute-start(bf16[2,16,3072]{2,1,0:T(8,128)(2,1)S(1)} %get-tuple-element.149), channel_id=1, source_target_pairs={{0,24},{1,25},{2,26},{3,27},{4,28},{5,29},{6,30},{7,31},{8,0},{9,1... | collective-permute-start | bytes 589832 | tf_op jit(solution)/shard_map/ppermute | solution.py:41
  72.7 2.2 %own_grads.3 = (bf16[256,3072]{1,0:T(8,128)(2,1)}, bf16[256,3072]{1,0:T(8,128)(2,1)}, f32[8,128]{1,0:T(8,128)S(1)}) custom-call(bf16[128,3072]{1,0:T(8,128)(2,1)S(1)} %get-tuple-element.121.refs_0_, bf16[128,3072]{1,0:T(8,128)(2,1)S(1)} %get-tuple-element.122.refs_1_, bf16[128,512]{1,0:T(8,128)(2,1)S(1)} %get-tuple-element.123.refs_2_, ...), custom_call_target="tpu_custom_call" | custom-call | tf_op jit(solution)/shard_map/own_grads/pallas_call | solution.py:260
  74.9 1.7 %collective-permute-done.29.refs_1_ = bf16[2,16,3072]{2,1,0:T(8,128)(2,1)S(1)} collective-permute-done((bf16[2,16,3072]{2,1,0:T(8,128)(2,1)S(1)}, bf16[2,16,3072]{2,1,0:T(8,128)(2,1)S(1)}, u32[]{:S(2)}, u32[]{:S(2)}) %collective-permute-start.29) | collective-permute-done | bytes 196640 | tf_op jit(solution)/shard_map/ppermute | solution.py:41
  76.6 0.7 final.1
  (39 shorter events, 1.4 us)
Async XLA Ops:
  0.6 6.1 %collective-permute-start = (bf16[256,3072]{1,0:T(8,128)(2,1)}, bf16[256,3072]{1,0:T(8,128)(2,1)S(1)}, u32[]{:S(2)}, u32[]{:S(2)}) collective-permute-start(bf16[256,3072]{1,0:T(8,128)(2,1)} %refs_5_.1), channel_id=1, source_target_pairs={{0,1},{1,0},{2,3},{3,2},{4,5},{5,4},{6,7},{7,6},{8,9},{9,8},{10,11... | collective-permute-start | bytes 4718600 | tf_op jit(solution)/shard_map/ppermute | solution.py:33
  2.6 14.2 %collective-permute-start.7 = (bf16[2,16,3072]{2,1,0:T(8,128)(2,1)S(1)}, bf16[2,16,3072]{2,1,0:T(8,128)(2,1)S(1)}, u32[]{:S(2)}, u32[]{:S(2)}) collective-permute-start(bf16[2,16,3072]{2,1,0:T(8,128)(2,1)S(1)} %get-tuple-element.81.refs_0_), channel_id=1, source_target_pairs={{0,16},{1,17},{2,18},{3,19},{4,20},{5,21},{6,22},{7,23},{8,24},{9,... | collective-permute-start | bytes 589832 | tf_op jit(solution)/shard_map/ppermute | solution.py:41
  6.2 3.6 %collective-permute-start.3 = (bf16[256,3072]{1,0:T(8,128)(2,1)}, bf16[256,3072]{1,0:T(8,128)(2,1)S(1)}, u32[]{:S(2)}, u32[]{:S(2)}) collective-permute-start(bf16[256,3072]{1,0:T(8,128)(2,1)} %refs_6_.1), channel_id=1, source_target_pairs={{0,1},{1,0},{2,3},{3,2},{4,5},{5,4},{6,7},{7,6},{8,9},{9,8},{10,11... | collective-permute-start | bytes 4718600 | tf_op jit(solution)/shard_map/ppermute | solution.py:33
  6.5 5.7 %collective-permute-start.4 = (bf16[256,3072]{1,0:T(8,128)(2,1)}, bf16[256,3072]{1,0:T(8,128)(2,1)S(1)}, u32[]{:S(2)}, u32[]{:S(2)}) collective-permute-start(bf16[256,3072]{1,0:T(8,128)(2,1)} %refs_7_.1), channel_id=1, source_target_pairs={{0,1},{1,0},{2,3},{3,2},{4,5},{5,4},{6,7},{7,6},{8,9},{9,8},{10,11... | collective-permute-start | bytes 4718600 | tf_op jit(solution)/shard_map/ppermute | solution.py:33
  6.8 5.3 %collective-permute-start.1 = (bf16[16,3072]{1,0:T(8,128)(2,1)S(1)}, bf16[16,3072]{1,0:T(8,128)(2,1)S(1)}, u32[]{:S(2)}, u32[]{:S(2)}) collective-permute-start(bf16[16,3072]{1,0:T(8,128)(2,1)S(1)} %get-tuple-element.83.refs_0_), channel_id=1, source_target_pairs={{0,2},{1,3},{2,0},{3,1},{4,6},{5,7},{6,4},{7,5},{8,10},{9,11},{10,... | collective-permute-start | bytes 294920 | tf_op jit(solution)/shard_map/ppermute | solution.py:33
  8.3 4.6 %collective-permute-start.2 = (bf16[16,3072]{1,0:T(8,128)(2,1)S(1)}, bf16[16,3072]{1,0:T(8,128)(2,1)S(1)}, u32[]{:S(2)}, u32[]{:S(2)}) collective-permute-start(bf16[16,3072]{1,0:T(8,128)(2,1)S(1)} %get-tuple-element.84.refs_2_), channel_id=1, source_target_pairs={{0,4},{1,5},{2,6},{3,7},{4,0},{5,1},{6,2},{7,3},{8,12},{9,13},{10,... | collective-permute-start | bytes 294920 | tf_op jit(solution)/shard_map/ppermute | solution.py:33
  13.0 13.9 %collective-permute-start.12 = (bf16[2,16,3072]{2,1,0:T(8,128)(2,1)S(1)}, bf16[2,16,3072]{2,1,0:T(8,128)(2,1)S(1)}, u32[]{:S(2)}, u32[]{:S(2)}) collective-permute-start(bf16[2,16,3072]{2,1,0:T(8,128)(2,1)S(1)} %get-tuple-element.95), channel_id=1, source_target_pairs={{0,8},{1,9},{2,10},{3,11},{4,12},{5,13},{6,14},{7,15},{8,16},{9,17... | collective-permute-start | bytes 589832 | tf_op jit(solution)/shard_map/ppermute | solution.py:41
  14.6 6.7 %collective-permute-start.5 = (bf16[32,3072]{1,0:T(8,128)(2,1)S(1)}, bf16[32,3072]{1,0:T(8,128)(2,1)S(1)}, u32[]{:S(2)}, u32[]{:S(2)}) collective-permute-start(bf16[32,3072]{1,0:T(8,128)(2,1)S(1)} %get-tuple-element.86.refs_0_), channel_id=1, source_target_pairs={{0,4},{1,5},{2,6},{3,7},{4,0},{5,1},{6,2},{7,3},{8,12},{9,13},{10,... | collective-permute-start | bytes 589832 | tf_op jit(solution)/shard_map/ppermute | solution.py:33
  16.2 6.7 %collective-permute-start.6 = (bf16[32,3072]{1,0:T(8,128)(2,1)S(1)}, bf16[32,3072]{1,0:T(8,128)(2,1)S(1)}, u32[]{:S(2)}, u32[]{:S(2)}) collective-permute-start(bf16[32,3072]{1,0:T(8,128)(2,1)S(1)} %get-tuple-element.87.refs_2_), channel_id=1, source_target_pairs={{0,2},{1,3},{2,0},{3,1},{4,6},{5,7},{6,4},{7,5},{8,10},{9,11},{10,... | collective-permute-start | bytes 589832 | tf_op jit(solution)/shard_map/ppermute | solution.py:33
  16.8 8.4 %collective-permute-start.8 = (bf16[16,3072]{1,0:T(8,128)(2,1)S(1)}, bf16[16,3072]{1,0:T(8,128)(2,1)S(1)}, u32[]{:S(2)}, u32[]{:S(2)}) collective-permute-start(bf16[16,3072]{1,0:T(8,128)(2,1)S(1)} %get-tuple-element.89.refs_0_), channel_id=1, source_target_pairs={{0,2},{1,3},{2,0},{3,1},{4,6},{5,7},{6,4},{7,5},{8,10},{9,11},{10,... | collective-permute-start | bytes 294920 | tf_op jit(solution)/shard_map/ppermute | solution.py:33
  18.3 7.0 %collective-permute-start.9 = (bf16[16,3072]{1,0:T(8,128)(2,1)S(1)}, bf16[16,3072]{1,0:T(8,128)(2,1)S(1)}, u32[]{:S(2)}, u32[]{:S(2)}) collective-permute-start(bf16[16,3072]{1,0:T(8,128)(2,1)S(1)} %get-tuple-element.90.refs_2_), channel_id=1, source_target_pairs={{0,4},{1,5},{2,6},{3,7},{4,0},{5,1},{6,2},{7,3},{8,12},{9,13},{10,... | collective-permute-start | bytes 294920 | tf_op jit(solution)/shard_map/ppermute | solution.py:33
  22.9 20.0 %collective-permute-start.19 = (bf16[128,3072]{1,0:T(8,128)(2,1)S(1)}, bf16[128,3072]{1,0:T(8,128)(2,1)S(1)}, u32[]{:S(2)}, u32[]{:S(2)}) collective-permute-start(bf16[128,3072]{1,0:T(8,128)(2,1)S(1)} %get-tuple-element.110), channel_id=1, source_target_pairs={{0,24},{1,25},{2,26},{3,27},{4,28},{5,29},{6,30},{7,31},{8,0},{9,1... | collective-permute-start | bytes 2359304 | tf_op jit(solution)/shard_map/ppermute | solution.py:41
  25.3 11.1 %collective-permute-start.10 = (bf16[32,3072]{1,0:T(8,128)(2,1)S(1)}, bf16[32,3072]{1,0:T(8,128)(2,1)S(1)}, u32[]{:S(2)}, u32[]{:S(2)}) collective-permute-start(bf16[32,3072]{1,0:T(8,128)(2,1)S(1)} %get-tuple-element.93.refs_4_), channel_id=1, source_target_pairs={{0,4},{1,5},{2,6},{3,7},{4,0},{5,1},{6,2},{7,3},{8,12},{9,13},{10,... | collective-permute-start | bytes 589832 | tf_op jit(solution)/shard_map/ppermute | solution.py:33
  25.5 11.0 %collective-permute-start.11 = (bf16[32,3072]{1,0:T(8,128)(2,1)S(1)}, bf16[32,3072]{1,0:T(8,128)(2,1)S(1)}, u32[]{:S(2)}, u32[]{:S(2)}) collective-permute-start(bf16[32,3072]{1,0:T(8,128)(2,1)S(1)} %get-tuple-element.94.refs_6_), channel_id=1, source_target_pairs={{0,2},{1,3},{2,0},{3,1},{4,6},{5,7},{6,4},{7,5},{8,10},{9,11},{10,... | collective-permute-start | bytes 589832 | tf_op jit(solution)/shard_map/ppermute | solution.py:33
  26.9 2.6 %copy-start = (bf16[256,3072]{1,0:T(8,128)(2,1)S(1)}, bf16[256,3072]{1,0:T(8,128)(2,1)}, u32[]{:S(2)}) copy-start(bf16[256,3072]{1,0:T(8,128)(2,1)} %refs_5_.1) | copy-start | bytes 4718596
  26.9 2.6 %copy-start.1 = (bf16[256,3072]{1,0:T(8,128)(2,1)S(1)}, bf16[256,3072]{1,0:T(8,128)(2,1)}, u32[]{:S(2)}) copy-start(bf16[256,3072]{1,0:T(8,128)(2,1)} %refs_6_.1) | copy-start | bytes 4718596
  26.9 2.6 %copy-start.2 = (bf16[256,3072]{1,0:T(8,128)(2,1)S(1)}, bf16[256,3072]{1,0:T(8,128)(2,1)}, u32[]{:S(2)}) copy-start(bf16[256,3072]{1,0:T(8,128)(2,1)} %refs_7_.1) | copy-start | bytes 4718596
  26.9 5.3 %collective-permute-start.13 = (bf16[16,3072]{1,0:T(8,128)(2,1)S(1)}, bf16[16,3072]{1,0:T(8,128)(2,1)S(1)}, u32[]{:S(2)}, u32[]{:S(2)}) collective-permute-start(bf16[16,3072]{1,0:T(8,128)(2,1)S(1)} %get-tuple-element.100.refs_0_), channel_id=1, source_target_pairs={{0,2},{1,3},{2,0},{3,1},{4,6},{5,7},{6,4},{7,5},{8,10},{9,11},{10,... | collective-permute-start | bytes 294920 | tf_op jit(solution)/shard_map/ppermute | solution.py:33
  27.6 5.0 %collective-permute-start.14 = (bf16[16,3072]{1,0:T(8,128)(2,1)S(1)}, bf16[16,3072]{1,0:T(8,128)(2,1)S(1)}, u32[]{:S(2)}, u32[]{:S(2)}) collective-permute-start(bf16[16,3072]{1,0:T(8,128)(2,1)S(1)} %get-tuple-element.101.refs_2_), channel_id=1, source_target_pairs={{0,4},{1,5},{2,6},{3,7},{4,0},{5,1},{6,2},{7,3},{8,12},{9,13},{10,... | collective-permute-start | bytes 294920 | tf_op jit(solution)/shard_map/ppermute | solution.py:33
  32.7 7.7 %collective-permute-start.17 = (bf16[32,3072]{1,0:T(8,128)(2,1)S(1)}, bf16[32,3072]{1,0:T(8,128)(2,1)S(1)}, u32[]{:S(2)}, u32[]{:S(2)}) collective-permute-start(bf16[32,3072]{1,0:T(8,128)(2,1)S(1)} %get-tuple-element.108.refs_0_), channel_id=1, source_target_pairs={{0,4},{1,5},{2,6},{3,7},{4,0},{5,1},{6,2},{7,3},{8,12},{9,13},{10,... | collective-permute-start | bytes 589832 | tf_op jit(solution)/shard_map/ppermute | solution.py:33
  35.1 7.8 %collective-permute-start.18 = (bf16[32,3072]{1,0:T(8,128)(2,1)S(1)}, bf16[32,3072]{1,0:T(8,128)(2,1)S(1)}, u32[]{:S(2)}, u32[]{:S(2)}) collective-permute-start(bf16[32,3072]{1,0:T(8,128)(2,1)S(1)} %get-tuple-element.109.refs_2_), channel_id=1, source_target_pairs={{0,2},{1,3},{2,0},{3,1},{4,6},{5,7},{6,4},{7,5},{8,10},{9,11},{10,... | collective-permute-start | bytes 589832 | tf_op jit(solution)/shard_map/ppermute | solution.py:33
  39.4 12.1 %collective-permute-start.15 = (bf16[64,3072]{1,0:T(8,128)(2,1)S(1)}, bf16[64,3072]{1,0:T(8,128)(2,1)S(1)}, u32[]{:S(2)}, u32[]{:S(2)}) collective-permute-start(bf16[64,3072]{1,0:T(8,128)(2,1)S(1)} %get-tuple-element.105), channel_id=1, source_target_pairs={{0,4},{1,5},{2,6},{3,7},{4,0},{5,1},{6,2},{7,3},{8,12},{9,13},{10,... | collective-permute-start | bytes 1179656 | tf_op jit(solution)/shard_map/ppermute | solution.py:33
  39.6 12.1 %collective-permute-start.16 = (bf16[64,3072]{1,0:T(8,128)(2,1)S(1)}, bf16[64,3072]{1,0:T(8,128)(2,1)S(1)}, u32[]{:S(2)}, u32[]{:S(2)}) collective-permute-start(bf16[64,3072]{1,0:T(8,128)(2,1)S(1)} %get-tuple-element.107), channel_id=1, source_target_pairs={{0,2},{1,3},{2,0},{3,1},{4,6},{5,7},{6,4},{7,5},{8,10},{9,11},{10,... | collective-permute-start | bytes 1179656 | tf_op jit(solution)/shard_map/ppermute | solution.py:33
  45.9 11.8 %collective-permute-start.22 = (bf16[64,3072]{1,0:T(8,128)(2,1)S(1)}, bf16[64,3072]{1,0:T(8,128)(2,1)S(1)}, u32[]{:S(2)}, u32[]{:S(2)}) collective-permute-start(bf16[64,3072]{1,0:T(8,128)(2,1)S(1)} %get-tuple-element.118), channel_id=1, source_target_pairs={{0,4},{1,5},{2,6},{3,7},{4,0},{5,1},{6,2},{7,3},{8,12},{9,13},{10,... | collective-permute-start | bytes 1179656 | tf_op jit(solution)/shard_map/ppermute | solution.py:33
  46.0 12.5 %collective-permute-start.23 = (bf16[64,3072]{1,0:T(8,128)(2,1)S(1)}, bf16[64,3072]{1,0:T(8,128)(2,1)S(1)}, u32[]{:S(2)}, u32[]{:S(2)}) collective-permute-start(bf16[64,3072]{1,0:T(8,128)(2,1)S(1)} %get-tuple-element.120), channel_id=1, source_target_pairs={{0,2},{1,3},{2,0},{3,1},{4,6},{5,7},{6,4},{7,5},{8,10},{9,11},{10,... | collective-permute-start | bytes 1179656 | tf_op jit(solution)/shard_map/ppermute | solution.py:33
  51.8 9.9 %collective-permute-start.20 = (bf16[32,3072]{1,0:T(8,128)(2,1)S(1)}, bf16[32,3072]{1,0:T(8,128)(2,1)S(1)}, u32[]{:S(2)}, u32[]{:S(2)}) collective-permute-start(bf16[32,3072]{1,0:T(8,128)(2,1)S(1)} %get-tuple-element.114), channel_id=1, source_target_pairs={{0,2},{1,3},{2,0},{3,1},{4,6},{5,7},{6,4},{7,5},{8,10},{9,11},{10,... | collective-permute-start | bytes 589832 | tf_op jit(solution)/shard_map/ppermute | solution.py:33
  52.9 8.7 %collective-permute-start.21 = (bf16[32,3072]{1,0:T(8,128)(2,1)S(1)}, bf16[32,3072]{1,0:T(8,128)(2,1)S(1)}, u32[]{:S(2)}, u32[]{:S(2)}) collective-permute-start(bf16[32,3072]{1,0:T(8,128)(2,1)S(1)} %get-tuple-element.116), channel_id=1, source_target_pairs={{0,4},{1,5},{2,6},{3,7},{4,0},{5,1},{6,2},{7,3},{8,12},{9,13},{10,... | collective-permute-start | bytes 589832 | tf_op jit(solution)/shard_map/ppermute | solution.py:33
  56.0 9.6 %collective-permute-start.27 = (bf16[3,256,3072]{2,1,0:T(8,128)(2,1)S(1)}, bf16[3,256,3072]{2,1,0:T(8,128)(2,1)S(1)}, u32[]{:S(2)}, u32[]{:S(2)}) collective-permute-start(bf16[3,256,3072]{2,1,0:T(8,128)(2,1)S(1)} %get-tuple-element.141), channel_id=1, source_target_pairs={{0,1},{1,0},{2,3},{3,2},{4,5},{5,4},{6,7},{7,6},{8,9},{9,8},{10,11... | collective-permute-start | bytes 14155784 | tf_op jit(solution)/shard_map/ppermute | solution.py:33
  58.6 6.3 %collective-permute-start.24 = (bf16[32,3072]{1,0:T(8,128)(2,1)S(1)}, bf16[32,3072]{1,0:T(8,128)(2,1)S(1)}, u32[]{:S(2)}, u32[]{:S(2)}) collective-permute-start(bf16[32,3072]{1,0:T(8,128)(2,1)S(1)} %get-tuple-element.136), channel_id=1, source_target_pairs={{0,2},{1,3},{2,0},{3,1},{4,6},{5,7},{6,4},{7,5},{8,10},{9,11},{10,... | collective-permute-start | bytes 589832 | tf_op jit(solution)/shard_map/ppermute | solution.py:33
  59.4 5.7 %collective-permute-start.25 = (bf16[32,3072]{1,0:T(8,128)(2,1)S(1)}, bf16[32,3072]{1,0:T(8,128)(2,1)S(1)}, u32[]{:S(2)}, u32[]{:S(2)}) collective-permute-start(bf16[32,3072]{1,0:T(8,128)(2,1)S(1)} %get-tuple-element.138), channel_id=1, source_target_pairs={{0,4},{1,5},{2,6},{3,7},{4,0},{5,1},{6,2},{7,3},{8,12},{9,13},{10,... | collective-permute-start | bytes 589832 | tf_op jit(solution)/shard_map/ppermute | solution.py:33
  61.7 6.4 %collective-permute-start.28 = (bf16[2,16,3072]{2,1,0:T(8,128)(2,1)S(1)}, bf16[2,16,3072]{2,1,0:T(8,128)(2,1)S(1)}, u32[]{:S(2)}, u32[]{:S(2)}) collective-permute-start(bf16[2,16,3072]{2,1,0:T(8,128)(2,1)S(1)} %get-tuple-element.143), channel_id=1, source_target_pairs={{0,24},{1,25},{2,26},{3,27},{4,28},{5,29},{6,30},{7,31},{8,0},{9,1... | collective-permute-start | bytes 589832 | tf_op jit(solution)/shard_map/ppermute | solution.py:41
  65.2 9.7 %collective-permute-start.26 = (bf16[2,16,3072]{2,1,0:T(8,128)(2,1)S(1)}, bf16[2,16,3072]{2,1,0:T(8,128)(2,1)S(1)}, u32[]{:S(2)}, u32[]{:S(2)}) collective-permute-start(bf16[2,16,3072]{2,1,0:T(8,128)(2,1)S(1)} %get-tuple-element.140), channel_id=1, source_target_pairs={{0,8},{1,9},{2,10},{3,11},{4,12},{5,13},{6,14},{7,15},{8,16},{9,17... | collective-permute-start | bytes 589832 | tf_op jit(solution)/shard_map/ppermute | solution.py:41
  68.2 8.4 %collective-permute-start.29 = (bf16[2,16,3072]{2,1,0:T(8,128)(2,1)S(1)}, bf16[2,16,3072]{2,1,0:T(8,128)(2,1)S(1)}, u32[]{:S(2)}, u32[]{:S(2)}) collective-permute-start(bf16[2,16,3072]{2,1,0:T(8,128)(2,1)S(1)} %get-tuple-element.149), channel_id=1, source_target_pairs={{0,24},{1,25},{2,26},{3,27},{4,28},{5,29},{6,30},{7,31},{8,0},{9,1... | collective-permute-start | bytes 589832 | tf_op jit(solution)/shard_map/ppermute | solution.py:41

commit v9 on v8

--- a/solution.py
+++ b/solution.py
@@ -100,7 +100,7 @@
     for copy in copies:
         copy.start()
     turn[...] = jnp.zeros_like(turn)
-    for copy in copies:
+    for copy in copies[:3]:
         copy.wait()
     capacity, lanes = weight.shape
     row = lax.broadcasted_iota(jnp.int32, (capacity, lanes), 0)
@@ -113,7 +113,9 @@
     weight[...] = scale
     lane = lax.broadcasted_iota(jnp.int32, (capacity, tokens.shape[0]), 1)
     chosen = jnp.where(lane == index[:, :1], 1.0, 0.0).astype(jnp.bfloat16)
+    copies[3].wait()
     rows[0] = half(product(chosen, tokens_here[...]))
+    copies[4].wait()
     rows[1] = half(scale[:, :1] * grad_here[...].astype(jnp.float32))
 
 

time: 77.5 us -> 77.5 us (level)
  no operation moved by 1% of the time
where the time goes in v9:
time: 77.5 us; the launch traced here: 77.3 us
  starting transfers between devices  39.6 us (51%)
  waiting for transfers between devices  20.2 us (26%)
  Pallas kernels  16.7 us (22%)
  between operations  0.78 us (1%)
    ppermute x24, starting transfers between devices, swapped(): lax.ppermute(block, 'dp', [(low, low ^ mask) for low in range(count)])  23.9 us
    ppermute x24, waiting for transfers between devices, swapped(): lax.ppermute(block, 'dp', [(low, low ^ mask) for low in range(count)])  17.6 us
    ppermute x6, starting transfers between devices, shifted(): return lax.ppermute(block, 'dp', route)  15.7 us
    pallas_call x2, Pallas kernels, expert(): pl.pallas_call(functools.partial(expert_kernel, [len(part) for part in pa...  5.98 us
    pallas_call x15, Pallas kernels, staged(): pl.pallas_call(kernel, out_shape=(*outs, TURN), in_specs=[VMEM] * len(val...  3.97 us
    pallas_call x2, Pallas kernels, own_grads(): pl.pallas_call(functools.partial(own_kernel, which, factor), grid=(width...  3.87 us
    ppermute x6, waiting for transfers between devices, shifted(): return lax.ppermute(block, 'dp', route)  2.55 us
  transfers between devices with their start and end apart: 30, of which 16 were waited for; matrix products, arithmetic and copies ran while one was open for 0% of the time, Pallas kernels for 21%

profile of v9, /device:TPU:0, one launch (start us, length us, event | category | flops | bytes accessed | tf_op | source)
XLA Modules:
  0.0 77.3 jit_solution(7579036832334457023)
XLA Ops:
  0.6 0.5 collective-permute-start
  1.2 1.4 %pick.1 = (bf16[2,16,3072]{2,1,0:T(8,128)(2,1)S(1)}, f32[16,128]{1,0:T(8,128)S(1)}, f32[8,128]{1,0:T(8,128)S(1)}) custom-call(s32[1]{0:T(128)} %bitcast.place, s32[16]{0:T(128)} %token_.1, s32[32]{0:T(128)} %count.1, f32[16]{0:T(128)} %gate.1, bf16[128,3072]{1,0:T(8,128)(2,1)} %tokens.1, bf16[16,3072]{1,0:T(8,128)(2,1)} %grad.1), custom_call_target="tpu_custom_call" | custom-call | tf_op jit(solution)/shard_map/pick/pallas_call | solution.py:125
  2.6 3.7 %collective-permute-start.7 = (bf16[2,16,3072]{2,1,0:T(8,128)(2,1)S(1)}, bf16[2,16,3072]{2,1,0:T(8,128)(2,1)S(1)}, u32[]{:S(2)}, u32[]{:S(2)}) collective-permute-start(bf16[2,16,3072]{2,1,0:T(8,128)(2,1)S(1)} %get-tuple-element.81.refs_0_), channel_id=1, source_target_pairs={{0,16},{1,17},{2,18},{3,19},{4,20},{5,21},{6,22},{7,23},{8,24},{9,... | collective-permute-start | bytes 589832 | tf_op jit(solution)/shard_map/ppermute | solution.py:41
  6.2 0.2 collective-permute-start.3
  6.5 0.3 collective-permute-start.4
  6.8 1.6 %collective-permute-start.1 = (bf16[16,3072]{1,0:T(8,128)(2,1)S(1)}, bf16[16,3072]{1,0:T(8,128)(2,1)S(1)}, u32[]{:S(2)}, u32[]{:S(2)}) collective-permute-start(bf16[16,3072]{1,0:T(8,128)(2,1)S(1)} %get-tuple-element.83.refs_0_), channel_id=1, source_target_pairs={{0,2},{1,3},{2,0},{3,1},{4,6},{5,7},{6,4},{7,5},{8,10},{9,11},{10,... | collective-permute-start | bytes 294920 | tf_op jit(solution)/shard_map/ppermute | solution.py:33
  8.3 1.5 %collective-permute-start.2 = (bf16[16,3072]{1,0:T(8,128)(2,1)S(1)}, bf16[16,3072]{1,0:T(8,128)(2,1)S(1)}, u32[]{:S(2)}, u32[]{:S(2)}) collective-permute-start(bf16[16,3072]{1,0:T(8,128)(2,1)S(1)} %get-tuple-element.84.refs_2_), channel_id=1, source_target_pairs={{0,4},{1,5},{2,6},{3,7},{4,0},{5,1},{6,2},{7,3},{8,12},{9,13},{10,... | collective-permute-start | bytes 294920 | tf_op jit(solution)/shard_map/ppermute | solution.py:33
  9.9 2.2 %collective-permute-done.4.refs_5_.refs_13_.refs_10_ = bf16[256,3072]{1,0:T(8,128)(2,1)S(1)} collective-permute-done((bf16[256,3072]{1,0:T(8,128)(2,1)}, bf16[256,3072]{1,0:T(8,128)(2,1)S(1)}, u32[]{:S(2)}, u32[]{:S(2)}) %collective-permute-start.4) | collective-permute-done | bytes 1572896 | tf_op jit(solution)/shard_map/ppermute | solution.py:33
  12.1 0.8 %collective-permute-done.2.refs_3_ = bf16[16,3072]{1,0:T(8,128)(2,1)S(1)} collective-permute-done((bf16[16,3072]{1,0:T(8,128)(2,1)S(1)}, bf16[16,3072]{1,0:T(8,128)(2,1)S(1)}, u32[]{:S(2)}, u32[]{:S(2)}) %collective-permute-start.2) | collective-permute-done | bytes 98336 | tf_op jit(solution)/shard_map/ppermute | solution.py:33
  13.0 1.6 %collective-permute-start.12 = (bf16[2,16,3072]{2,1,0:T(8,128)(2,1)S(1)}, bf16[2,16,3072]{2,1,0:T(8,128)(2,1)S(1)}, u32[]{:S(2)}, u32[]{:S(2)}) collective-permute-start(bf16[2,16,3072]{2,1,0:T(8,128)(2,1)S(1)} %get-tuple-element.95), channel_id=1, source_target_pairs={{0,8},{1,9},{2,10},{3,11},{4,12},{5,13},{6,14},{7,15},{8,16},{9,17... | collective-permute-start | bytes 589832 | tf_op jit(solution)/shard_map/ppermute | solution.py:41
  14.6 1.5 %collective-permute-start.5 = (bf16[32,3072]{1,0:T(8,128)(2,1)S(1)}, bf16[32,3072]{1,0:T(8,128)(2,1)S(1)}, u32[]{:S(2)}, u32[]{:S(2)}) collective-permute-start(bf16[32,3072]{1,0:T(8,128)(2,1)S(1)} %get-tuple-element.86.refs_0_), channel_id=1, source_target_pairs={{0,4},{1,5},{2,6},{3,7},{4,0},{5,1},{6,2},{7,3},{8,12},{9,13},{10,... | collective-permute-start | bytes 589832 | tf_op jit(solution)/shard_map/ppermute | solution.py:33
  16.2 0.7 collective-permute-start.6
  16.8 1.4 %collective-permute-start.8 = (bf16[16,3072]{1,0:T(8,128)(2,1)S(1)}, bf16[16,3072]{1,0:T(8,128)(2,1)S(1)}, u32[]{:S(2)}, u32[]{:S(2)}) collective-permute-start(bf16[16,3072]{1,0:T(8,128)(2,1)S(1)} %get-tuple-element.89.refs_0_), channel_id=1, source_target_pairs={{0,2},{1,3},{2,0},{3,1},{4,6},{5,7},{6,4},{7,5},{8,10},{9,11},{10,... | collective-permute-start | bytes 294920 | tf_op jit(solution)/shard_map/ppermute | solution.py:33
  18.3 0.9 %collective-permute-start.9 = (bf16[16,3072]{1,0:T(8,128)(2,1)S(1)}, bf16[16,3072]{1,0:T(8,128)(2,1)S(1)}, u32[]{:S(2)}, u32[]{:S(2)}) collective-permute-start(bf16[16,3072]{1,0:T(8,128)(2,1)S(1)} %get-tuple-element.90.refs_2_), channel_id=1, source_target_pairs={{0,4},{1,5},{2,6},{3,7},{4,0},{5,1},{6,2},{7,3},{8,12},{9,13},{10,... | collective-permute-start | bytes 294920 | tf_op jit(solution)/shard_map/ppermute | solution.py:33
  19.2 2.2 %collective-permute-done.5.refs_1_ = bf16[32,3072]{1,0:T(8,128)(2,1)S(1)} collective-permute-done((bf16[32,3072]{1,0:T(8,128)(2,1)S(1)}, bf16[32,3072]{1,0:T(8,128)(2,1)S(1)}, u32[]{:S(2)}, u32[]{:S(2)}) %collective-permute-start.5) | collective-permute-done | bytes 196640 | tf_op jit(solution)/shard_map/ppermute | solution.py:33
  21.3 1.5 %collective-permute-done.6.refs_3_ = bf16[32,3072]{1,0:T(8,128)(2,1)S(1)} collective-permute-done((bf16[32,3072]{1,0:T(8,128)(2,1)S(1)}, bf16[32,3072]{1,0:T(8,128)(2,1)S(1)}, u32[]{:S(2)}, u32[]{:S(2)}) %collective-permute-start.6) | collective-permute-done | bytes 196640 | tf_op jit(solution)/shard_map/ppermute | solution.py:33
  22.9 2.4 %collective-permute-start.19 = (bf16[128,3072]{1,0:T(8,128)(2,1)S(1)}, bf16[128,3072]{1,0:T(8,128)(2,1)S(1)}, u32[]{:S(2)}, u32[]{:S(2)}) collective-permute-start(bf16[128,3072]{1,0:T(8,128)(2,1)S(1)} %get-tuple-element.110), channel_id=1, source_target_pairs={{0,24},{1,25},{2,26},{3,27},{4,28},{5,29},{6,30},{7,31},{8,0},{9,1... | collective-permute-start | bytes 2359304 | tf_op jit(solution)/shard_map/ppermute | solution.py:41
  25.3 0.2 collective-permute-start.10
  25.5 1.4 %collective-permute-start.11 = (bf16[32,3072]{1,0:T(8,128)(2,1)S(1)}, bf16[32,3072]{1,0:T(8,128)(2,1)S(1)}, u32[]{:S(2)}, u32[]{:S(2)}) collective-permute-start(bf16[32,3072]{1,0:T(8,128)(2,1)S(1)} %get-tuple-element.94.refs_6_), channel_id=1, source_target_pairs={{0,2},{1,3},{2,0},{3,1},{4,6},{5,7},{6,4},{7,5},{8,10},{9,11},{10,... | collective-permute-start | bytes 589832 | tf_op jit(solution)/shard_map/ppermute | solution.py:33
  26.9 0.7 collective-permute-start.13
  27.6 1.9 %collective-permute-start.14 = (bf16[16,3072]{1,0:T(8,128)(2,1)S(1)}, bf16[16,3072]{1,0:T(8,128)(2,1)S(1)}, u32[]{:S(2)}, u32[]{:S(2)}) collective-permute-start(bf16[16,3072]{1,0:T(8,128)(2,1)S(1)} %get-tuple-element.101.refs_2_), channel_id=1, source_target_pairs={{0,4},{1,5},{2,6},{3,7},{4,0},{5,1},{6,2},{7,3},{8,12},{9,13},{10,... | collective-permute-start | bytes 294920 | tf_op jit(solution)/shard_map/ppermute | solution.py:33
  29.5 2.5 %turn_panels.1 = (bf16[3,3072,256]{2,1,0:T(8,128)(2,1)S(1)}, bf16[3,3072,256]{2,1,0:T(8,128)(2,1)S(1)}, f32[8,128]{1,0:T(8,128)S(1)}) custom-call(bf16[256,3072]{1,0:T(8,128)(2,1)S(1)} %copy-done, bf16[256,3072]{1,0:T(8,128)(2,1)S(1)} %copy-done.1, bf16[256,3072]{1,0:T(8,128)(2,1)S(1)} %copy-done.2, ...), custom_call_target="tpu_custom_call" | custom-call | tf_op jit(solution)/shard_map/turn_panels/pallas_call | solution.py:279
  32.0 0.2 collective-permute-done.13.refs_1_
  32.2 0.4 collective-permute-done.14.refs_3_
  32.7 2.4 %collective-permute-start.17 = (bf16[32,3072]{1,0:T(8,128)(2,1)S(1)}, bf16[32,3072]{1,0:T(8,128)(2,1)S(1)}, u32[]{:S(2)}, u32[]{:S(2)}) collective-permute-start(bf16[32,3072]{1,0:T(8,128)(2,1)S(1)} %get-tuple-element.108.refs_0_), channel_id=1, source_target_pairs={{0,4},{1,5},{2,6},{3,7},{4,0},{5,1},{6,2},{7,3},{8,12},{9,13},{10,... | collective-permute-start | bytes 589832 | tf_op jit(solution)/shard_map/ppermute | solution.py:33
  35.1 1.3 %collective-permute-start.18 = (bf16[32,3072]{1,0:T(8,128)(2,1)S(1)}, bf16[32,3072]{1,0:T(8,128)(2,1)S(1)}, u32[]{:S(2)}, u32[]{:S(2)}) collective-permute-start(bf16[32,3072]{1,0:T(8,128)(2,1)S(1)} %get-tuple-element.109.refs_2_), channel_id=1, source_target_pairs={{0,2},{1,3},{2,0},{3,1},{4,6},{5,7},{6,4},{7,5},{8,10},{9,11},{10,... | collective-permute-start | bytes 589832 | tf_op jit(solution)/shard_map/ppermute | solution.py:33
  36.4 3.0 %expert.2 = (bf16[128,3072]{1,0:T(8,128)(2,1)S(1)}, bf16[128,3072]{1,0:T(8,128)(2,1)S(1)}, bf16[128,512]{1,0:T(8,128)(2,1)S(1)}, bf16[128,512]{1,0:T(8,128)(2,1)...) custom-call(bf16[32,3072]{1,0:T(8,128)(2,1)S(1)} %get-tuple-element., ...), custom_call_target="tpu_custom_call" | custom-call | flops 2415919104 | bytes 9437184 | tf_op jit(solution)/shard_map/expert/pallas_call | solution.py:205
  39.6 0.7 collective-permute-start.16
  40.4 2.5 %collective-permute-done.18.refs_3_ = bf16[32,3072]{1,0:T(8,128)(2,1)S(1)} collective-permute-done((bf16[32,3072]{1,0:T(8,128)(2,1)S(1)}, bf16[32,3072]{1,0:T(8,128)(2,1)S(1)}, u32[]{:S(2)}, u32[]{:S(2)}) %collective-permute-start.18) | collective-permute-done | bytes 196640 | tf_op jit(solution)/shard_map/ppermute | solution.py:33
  42.9 3.0 %expert.3 = (bf16[128,3072]{1,0:T(8,128)(2,1)S(1)}, bf16[128,3072]{1,0:T(8,128)(2,1)S(1)}, bf16[128,512]{1,0:T(8,128)(2,1)S(1)}, bf16[128,512]{1,0:T(8,128)(2,1)...) custom-call(bf16[32,3072]{1,0:T(8,128)(2,1)S(1)} %get-tuple-element., ...), custom_call_target="tpu_custom_call" | custom-call | flops 2415919104 | bytes 9437184 | tf_op jit(solution)/shard_map/expert/pallas_call | solution.py:205
  46.0 1.4 %collective-permute-start.23 = (bf16[64,3072]{1,0:T(8,128)(2,1)S(1)}, bf16[64,3072]{1,0:T(8,128)(2,1)S(1)}, u32[]{:S(2)}, u32[]{:S(2)}) collective-permute-start(bf16[64,3072]{1,0:T(8,128)(2,1)S(1)} %get-tuple-element.120), channel_id=1, source_target_pairs={{0,2},{1,3},{2,0},{3,1},{4,6},{5,7},{6,4},{7,5},{8,10},{9,11},{10,... | collective-permute-start | bytes 1179656 | tf_op jit(solution)/shard_map/ppermute | solution.py:33
  47.4 4.1 %collective-permute-done.15.refs_1_ = bf16[64,3072]{1,0:T(8,128)(2,1)S(1)} collective-permute-done((bf16[64,3072]{1,0:T(8,128)(2,1)S(1)}, bf16[64,3072]{1,0:T(8,128)(2,1)S(1)}, u32[]{:S(2)}, u32[]{:S(2)}) %collective-permute-start.15) | collective-permute-done | bytes 393248 | tf_op jit(solution)/shard_map/ppermute | solution.py:33
  51.8 1.1 %collective-permute-start.20 = (bf16[32,3072]{1,0:T(8,128)(2,1)S(1)}, bf16[32,3072]{1,0:T(8,128)(2,1)S(1)}, u32[]{:S(2)}, u32[]{:S(2)}) collective-permute-start(bf16[32,3072]{1,0:T(8,128)(2,1)S(1)} %get-tuple-element.114), channel_id=1, source_target_pairs={{0,2},{1,3},{2,0},{3,1},{4,6},{5,7},{6,4},{7,5},{8,10},{9,11},{10,... | collective-permute-start | bytes 589832 | tf_op jit(solution)/shard_map/ppermute | solution.py:33
  52.9 1.6 %collective-permute-start.21 = (bf16[32,3072]{1,0:T(8,128)(2,1)S(1)}, bf16[32,3072]{1,0:T(8,128)(2,1)S(1)}, u32[]{:S(2)}, u32[]{:S(2)}) collective-permute-start(bf16[32,3072]{1,0:T(8,128)(2,1)S(1)} %get-tuple-element.116), channel_id=1, source_target_pairs={{0,4},{1,5},{2,6},{3,7},{4,0},{5,1},{6,2},{7,3},{8,12},{9,13},{10,... | collective-permute-start | bytes 589832 | tf_op jit(solution)/shard_map/ppermute | solution.py:33
  54.5 1.4 %other_grads.1 = (bf16[3,256,3072]{2,1,0:T(8,128)(2,1)S(1)}, f32[8,128]{1,0:T(8,128)S(1)}) custom-call(bf16[128,3072]{1,0:T(8,128)(2,1)S(1)} %get-tuple-element.121.refs_0_, bf16[128,3072]{1,0:T(8,128)(2,1)S(1)} %get-tuple-element.122.refs_1_, bf16[128,512]{1,0:T(8,128)(2,1)S(1)} %get-tuple-element.123.refs_2_, ...), custom_call_target="tpu_custom_call" | custom-call | flops 2000000000 | tf_op jit(solution)/shard_map/other_grads/pallas_call | solution.py:237
  56.0 1.6 %collective-permute-done.22.refs_1_ = bf16[64,3072]{1,0:T(8,128)(2,1)S(1)} collective-permute-done((bf16[64,3072]{1,0:T(8,128)(2,1)S(1)}, bf16[64,3072]{1,0:T(8,128)(2,1)S(1)}, u32[]{:S(2)}, u32[]{:S(2)}) %collective-permute-start.22) | collective-permute-done | bytes 393248 | tf_op jit(solution)/shard_map/ppermute | solution.py:33
  57.7 0.8 collective-permute-done.23.refs_3_
  58.6 0.8 %collective-permute-start.24 = (bf16[32,3072]{1,0:T(8,128)(2,1)S(1)}, bf16[32,3072]{1,0:T(8,128)(2,1)S(1)}, u32[]{:S(2)}, u32[]{:S(2)}) collective-permute-start(bf16[32,3072]{1,0:T(8,128)(2,1)S(1)} %get-tuple-element.136), channel_id=1, source_target_pairs={{0,2},{1,3},{2,0},{3,1},{4,6},{5,7},{6,4},{7,5},{8,10},{9,11},{10,... | collective-permute-start | bytes 589832 | tf_op jit(solution)/shard_map/ppermute | solution.py:33
  59.4 1.4 %collective-permute-start.25 = (bf16[32,3072]{1,0:T(8,128)(2,1)S(1)}, bf16[32,3072]{1,0:T(8,128)(2,1)S(1)}, u32[]{:S(2)}, u32[]{:S(2)}) collective-permute-start(bf16[32,3072]{1,0:T(8,128)(2,1)S(1)} %get-tuple-element.138), channel_id=1, source_target_pairs={{0,4},{1,5},{2,6},{3,7},{4,0},{5,1},{6,2},{7,3},{8,12},{9,13},{10,... | collective-permute-start | bytes 589832 | tf_op jit(solution)/shard_map/ppermute | solution.py:33
  60.8 0.8 %collective-permute-done.20.refs_1_ = bf16[32,3072]{1,0:T(8,128)(2,1)S(1)} collective-permute-done((bf16[32,3072]{1,0:T(8,128)(2,1)S(1)}, bf16[32,3072]{1,0:T(8,128)(2,1)S(1)}, u32[]{:S(2)}, u32[]{:S(2)}) %collective-permute-start.20) | collective-permute-done | bytes 196640 | tf_op jit(solution)/shard_map/ppermute | solution.py:33
  61.7 3.2 %collective-permute-start.28 = (bf16[2,16,3072]{2,1,0:T(8,128)(2,1)S(1)}, bf16[2,16,3072]{2,1,0:T(8,128)(2,1)S(1)}, u32[]{:S(2)}, u32[]{:S(2)}) collective-permute-start(bf16[2,16,3072]{2,1,0:T(8,128)(2,1)S(1)} %get-tuple-element.143), channel_id=1, source_target_pairs={{0,24},{1,25},{2,26},{3,27},{4,28},{5,29},{6,30},{7,31},{8,0},{9,1... | collective-permute-start | bytes 589832 | tf_op jit(solution)/shard_map/ppermute | solution.py:41
  65.2 0.4 collective-permute-start.26
  65.6 1.7 %own_grads.2 = (bf16[256,3072]{1,0:T(8,128)(2,1)}, f32[8,128]{1,0:T(8,128)S(1)}) custom-call(bf16[128,3072]{1,0:T(8,128)(2,1)S(1)} %get-tuple-element.121.refs_0_, bf16[128,3072]{1,0:T(8,128)(2,1)S(1)} %get-tuple-element.122.refs_1_, bf16[128,512]{1,0:T(8,128)(2,1)S(1)} %get-tuple-element.123.refs_2_, bf16[128,512]{1,0:T(8,128)(2,1)S(1)} %get-tuple-element.124.refs_3_, ...), custom_call_target="tpu_custom_call" | custom-call | tf_op jit(solution)/shard_map/own_grads/pallas_call | solution.py:262
  67.3 0.9 %collective-permute-done.28.refs_1_ = bf16[2,16,3072]{2,1,0:T(8,128)(2,1)S(1)} collective-permute-done((bf16[2,16,3072]{2,1,0:T(8,128)(2,1)S(1)}, bf16[2,16,3072]{2,1,0:T(8,128)(2,1)S(1)}, u32[]{:S(2)}, u32[]{:S(2)}) %collective-permute-start.28) | collective-permute-done | bytes 196640 | tf_op jit(solution)/shard_map/ppermute | solution.py:41
  68.2 4.5 %collective-permute-start.29 = (bf16[2,16,3072]{2,1,0:T(8,128)(2,1)S(1)}, bf16[2,16,3072]{2,1,0:T(8,128)(2,1)S(1)}, u32[]{:S(2)}, u32[]{:S(2)}) collective-permute-start(bf16[2,16,3072]{2,1,0:T(8,128)(2,1)S(1)} %get-tuple-element.149), channel_id=1, source_target_pairs={{0,24},{1,25},{2,26},{3,27},{4,28},{5,29},{6,30},{7,31},{8,0},{9,1... | collective-permute-start | bytes 589832 | tf_op jit(solution)/shard_map/ppermute | solution.py:41
  72.7 2.2 %own_grads.3 = (bf16[256,3072]{1,0:T(8,128)(2,1)}, bf16[256,3072]{1,0:T(8,128)(2,1)}, f32[8,128]{1,0:T(8,128)S(1)}) custom-call(bf16[128,3072]{1,0:T(8,128)(2,1)S(1)} %get-tuple-element.121.refs_0_, bf16[128,3072]{1,0:T(8,128)(2,1)S(1)} %get-tuple-element.122.refs_1_, bf16[128,512]{1,0:T(8,128)(2,1)S(1)} %get-tuple-element.123.refs_2_, ...), custom_call_target="tpu_custom_call" | custom-call | tf_op jit(solution)/shard_map/own_grads/pallas_call | solution.py:262
  74.9 1.6 %collective-permute-done.29.refs_1_ = bf16[2,16,3072]{2,1,0:T(8,128)(2,1)S(1)} collective-permute-done((bf16[2,16,3072]{2,1,0:T(8,128)(2,1)S(1)}, bf16[2,16,3072]{2,1,0:T(8,128)(2,1)S(1)}, u32[]{:S(2)}, u32[]{:S(2)}) %collective-permute-start.29) | collective-permute-done | bytes 196640 | tf_op jit(solution)/shard_map/ppermute | solution.py:41
  76.6 0.7 final.1
  (39 shorter events, 1.4 us)
Async XLA Ops:
  0.6 6.1 %collective-permute-start = (bf16[256,3072]{1,0:T(8,128)(2,1)}, bf16[256,3072]{1,0:T(8,128)(2,1)S(1)}, u32[]{:S(2)}, u32[]{:S(2)}) collective-permute-start(bf16[256,3072]{1,0:T(8,128)(2,1)} %refs_5_.1), channel_id=1, source_target_pairs={{0,1},{1,0},{2,3},{3,2},{4,5},{5,4},{6,7},{7,6},{8,9},{9,8},{10,11... | collective-permute-start | bytes 4718600 | tf_op jit(solution)/shard_map/ppermute | solution.py:33
  2.6 14.2 %collective-permute-start.7 = (bf16[2,16,3072]{2,1,0:T(8,128)(2,1)S(1)}, bf16[2,16,3072]{2,1,0:T(8,128)(2,1)S(1)}, u32[]{:S(2)}, u32[]{:S(2)}) collective-permute-start(bf16[2,16,3072]{2,1,0:T(8,128)(2,1)S(1)} %get-tuple-element.81.refs_0_), channel_id=1, source_target_pairs={{0,16},{1,17},{2,18},{3,19},{4,20},{5,21},{6,22},{7,23},{8,24},{9,... | collective-permute-start | bytes 589832 | tf_op jit(solution)/shard_map/ppermute | solution.py:41
  6.2 3.6 %collective-permute-start.3 = (bf16[256,3072]{1,0:T(8,128)(2,1)}, bf16[256,3072]{1,0:T(8,128)(2,1)S(1)}, u32[]{:S(2)}, u32[]{:S(2)}) collective-permute-start(bf16[256,3072]{1,0:T(8,128)(2,1)} %refs_6_.1), channel_id=1, source_target_pairs={{0,1},{1,0},{2,3},{3,2},{4,5},{5,4},{6,7},{7,6},{8,9},{9,8},{10,11... | collective-permute-start | bytes 4718600 | tf_op jit(solution)/shard_map/ppermute | solution.py:33
  6.5 5.7 %collective-permute-start.4 = (bf16[256,3072]{1,0:T(8,128)(2,1)}, bf16[256,3072]{1,0:T(8,128)(2,1)S(1)}, u32[]{:S(2)}, u32[]{:S(2)}) collective-permute-start(bf16[256,3072]{1,0:T(8,128)(2,1)} %refs_7_.1), channel_id=1, source_target_pairs={{0,1},{1,0},{2,3},{3,2},{4,5},{5,4},{6,7},{7,6},{8,9},{9,8},{10,11... | collective-permute-start | bytes 4718600 | tf_op jit(solution)/shard_map/ppermute | solution.py:33
  6.8 5.3 %collective-permute-start.1 = (bf16[16,3072]{1,0:T(8,128)(2,1)S(1)}, bf16[16,3072]{1,0:T(8,128)(2,1)S(1)}, u32[]{:S(2)}, u32[]{:S(2)}) collective-permute-start(bf16[16,3072]{1,0:T(8,128)(2,1)S(1)} %get-tuple-element.83.refs_0_), channel_id=1, source_target_pairs={{0,2},{1,3},{2,0},{3,1},{4,6},{5,7},{6,4},{7,5},{8,10},{9,11},{10,... | collective-permute-start | bytes 294920 | tf_op jit(solution)/shard_map/ppermute | solution.py:33
  8.3 4.6 %collective-permute-start.2 = (bf16[16,3072]{1,0:T(8,128)(2,1)S(1)}, bf16[16,3072]{1,0:T(8,128)(2,1)S(1)}, u32[]{:S(2)}, u32[]{:S(2)}) collective-permute-start(bf16[16,3072]{1,0:T(8,128)(2,1)S(1)} %get-tuple-element.84.refs_2_), channel_id=1, source_target_pairs={{0,4},{1,5},{2,6},{3,7},{4,0},{5,1},{6,2},{7,3},{8,12},{9,13},{10,... | collective-permute-start | bytes 294920 | tf_op jit(solution)/shard_map/ppermute | solution.py:33
  13.0 13.9 %collective-permute-start.12 = (bf16[2,16,3072]{2,1,0:T(8,128)(2,1)S(1)}, bf16[2,16,3072]{2,1,0:T(8,128)(2,1)S(1)}, u32[]{:S(2)}, u32[]{:S(2)}) collective-permute-start(bf16[2,16,3072]{2,1,0:T(8,128)(2,1)S(1)} %get-tuple-element.95), channel_id=1, source_target_pairs={{0,8},{1,9},{2,10},{3,11},{4,12},{5,13},{6,14},{7,15},{8,16},{9,17... | collective-permute-start | bytes 589832 | tf_op jit(solution)/shard_map/ppermute | solution.py:41
  14.6 6.7 %collective-permute-start.5 = (bf16[32,3072]{1,0:T(8,128)(2,1)S(1)}, bf16[32,3072]{1,0:T(8,128)(2,1)S(1)}, u32[]{:S(2)}, u32[]{:S(2)}) collective-permute-start(bf16[32,3072]{1,0:T(8,128)(2,1)S(1)} %get-tuple-element.86.refs_0_), channel_id=1, source_target_pairs={{0,4},{1,5},{2,6},{3,7},{4,0},{5,1},{6,2},{7,3},{8,12},{9,13},{10,... | collective-permute-start | bytes 589832 | tf_op jit(solution)/shard_map/ppermute | solution.py:33
  16.2 6.7 %collective-permute-start.6 = (bf16[32,3072]{1,0:T(8,128)(2,1)S(1)}, bf16[32,3072]{1,0:T(8,128)(2,1)S(1)}, u32[]{:S(2)}, u32[]{:S(2)}) collective-permute-start(bf16[32,3072]{1,0:T(8,128)(2,1)S(1)} %get-tuple-element.87.refs_2_), channel_id=1, source_target_pairs={{0,2},{1,3},{2,0},{3,1},{4,6},{5,7},{6,4},{7,5},{8,10},{9,11},{10,... | collective-permute-start | bytes 589832 | tf_op jit(solution)/shard_map/ppermute | solution.py:33
  16.8 8.4 %collective-permute-start.8 = (bf16[16,3072]{1,0:T(8,128)(2,1)S(1)}, bf16[16,3072]{1,0:T(8,128)(2,1)S(1)}, u32[]{:S(2)}, u32[]{:S(2)}) collective-permute-start(bf16[16,3072]{1,0:T(8,128)(2,1)S(1)} %get-tuple-element.89.refs_0_), channel_id=1, source_target_pairs={{0,2},{1,3},{2,0},{3,1},{4,6},{5,7},{6,4},{7,5},{8,10},{9,11},{10,... | collective-permute-start | bytes 294920 | tf_op jit(solution)/shard_map/ppermute | solution.py:33
  18.3 7.0 %collective-permute-start.9 = (bf16[16,3072]{1,0:T(8,128)(2,1)S(1)}, bf16[16,3072]{1,0:T(8,128)(2,1)S(1)}, u32[]{:S(2)}, u32[]{:S(2)}) collective-permute-start(bf16[16,3072]{1,0:T(8,128)(2,1)S(1)} %get-tuple-element.90.refs_2_), channel_id=1, source_target_pairs={{0,4},{1,5},{2,6},{3,7},{4,0},{5,1},{6,2},{7,3},{8,12},{9,13},{10,... | collective-permute-start | bytes 294920 | tf_op jit(solution)/shard_map/ppermute | solution.py:33
  22.9 20.0 %collective-permute-start.19 = (bf16[128,3072]{1,0:T(8,128)(2,1)S(1)}, bf16[128,3072]{1,0:T(8,128)(2,1)S(1)}, u32[]{:S(2)}, u32[]{:S(2)}) collective-permute-start(bf16[128,3072]{1,0:T(8,128)(2,1)S(1)} %get-tuple-element.110), channel_id=1, source_target_pairs={{0,24},{1,25},{2,26},{3,27},{4,28},{5,29},{6,30},{7,31},{8,0},{9,1... | collective-permute-start | bytes 2359304 | tf_op jit(solution)/shard_map/ppermute | solution.py:41
  25.3 11.1 %collective-permute-start.10 = (bf16[32,3072]{1,0:T(8,128)(2,1)S(1)}, bf16[32,3072]{1,0:T(8,128)(2,1)S(1)}, u32[]{:S(2)}, u32[]{:S(2)}) collective-permute-start(bf16[32,3072]{1,0:T(8,128)(2,1)S(1)} %get-tuple-element.93.refs_4_), channel_id=1, source_target_pairs={{0,4},{1,5},{2,6},{3,7},{4,0},{5,1},{6,2},{7,3},{8,12},{9,13},{10,... | collective-permute-start | bytes 589832 | tf_op jit(solution)/shard_map/ppermute | solution.py:33
  25.5 11.0 %collective-permute-start.11 = (bf16[32,3072]{1,0:T(8,128)(2,1)S(1)}, bf16[32,3072]{1,0:T(8,128)(2,1)S(1)}, u32[]{:S(2)}, u32[]{:S(2)}) collective-permute-start(bf16[32,3072]{1,0:T(8,128)(2,1)S(1)} %get-tuple-element.94.refs_6_), channel_id=1, source_target_pairs={{0,2},{1,3},{2,0},{3,1},{4,6},{5,7},{6,4},{7,5},{8,10},{9,11},{10,... | collective-permute-start | bytes 589832 | tf_op jit(solution)/shard_map/ppermute | solution.py:33
  26.9 2.6 %copy-start = (bf16[256,3072]{1,0:T(8,128)(2,1)S(1)}, bf16[256,3072]{1,0:T(8,128)(2,1)}, u32[]{:S(2)}) copy-start(bf16[256,3072]{1,0:T(8,128)(2,1)} %refs_5_.1) | copy-start | bytes 4718596
  26.9 2.6 %copy-start.1 = (bf16[256,3072]{1,0:T(8,128)(2,1)S(1)}, bf16[256,3072]{1,0:T(8,128)(2,1)}, u32[]{:S(2)}) copy-start(bf16[256,3072]{1,0:T(8,128)(2,1)} %refs_6_.1) | copy-start | bytes 4718596
  26.9 2.6 %copy-start.2 = (bf16[256,3072]{1,0:T(8,128)(2,1)S(1)}, bf16[256,3072]{1,0:T(8,128)(2,1)}, u32[]{:S(2)}) copy-start(bf16[256,3072]{1,0:T(8,128)(2,1)} %refs_7_.1) | copy-start | bytes 4718596
  26.9 5.3 %collective-permute-start.13 = (bf16[16,3072]{1,0:T(8,128)(2,1)S(1)}, bf16[16,3072]{1,0:T(8,128)(2,1)S(1)}, u32[]{:S(2)}, u32[]{:S(2)}) collective-permute-start(bf16[16,3072]{1,0:T(8,128)(2,1)S(1)} %get-tuple-element.100.refs_0_), channel_id=1, source_target_pairs={{0,2},{1,3},{2,0},{3,1},{4,6},{5,7},{6,4},{7,5},{8,10},{9,11},{10,... | collective-permute-start | bytes 294920 | tf_op jit(solution)/shard_map/ppermute | solution.py:33
  27.6 5.0 %collective-permute-start.14 = (bf16[16,3072]{1,0:T(8,128)(2,1)S(1)}, bf16[16,3072]{1,0:T(8,128)(2,1)S(1)}, u32[]{:S(2)}, u32[]{:S(2)}) collective-permute-start(bf16[16,3072]{1,0:T(8,128)(2,1)S(1)} %get-tuple-element.101.refs_2_), channel_id=1, source_target_pairs={{0,4},{1,5},{2,6},{3,7},{4,0},{5,1},{6,2},{7,3},{8,12},{9,13},{10,... | collective-permute-start | bytes 294920 | tf_op jit(solution)/shard_map/ppermute | solution.py:33
  32.7 7.7 %collective-permute-start.17 = (bf16[32,3072]{1,0:T(8,128)(2,1)S(1)}, bf16[32,3072]{1,0:T(8,128)(2,1)S(1)}, u32[]{:S(2)}, u32[]{:S(2)}) collective-permute-start(bf16[32,3072]{1,0:T(8,128)(2,1)S(1)} %get-tuple-element.108.refs_0_), channel_id=1, source_target_pairs={{0,4},{1,5},{2,6},{3,7},{4,0},{5,1},{6,2},{7,3},{8,12},{9,13},{10,... | collective-permute-start | bytes 589832 | tf_op jit(solution)/shard_map/ppermute | solution.py:33
  35.1 7.8 %collective-permute-start.18 = (bf16[32,3072]{1,0:T(8,128)(2,1)S(1)}, bf16[32,3072]{1,0:T(8,128)(2,1)S(1)}, u32[]{:S(2)}, u32[]{:S(2)}) collective-permute-start(bf16[32,3072]{1,0:T(8,128)(2,1)S(1)} %get-tuple-element.109.refs_2_), channel_id=1, source_target_pairs={{0,2},{1,3},{2,0},{3,1},{4,6},{5,7},{6,4},{7,5},{8,10},{9,11},{10,... | collective-permute-start | bytes 589832 | tf_op jit(solution)/shard_map/ppermute | solution.py:33
  39.4 12.1 %collective-permute-start.15 = (bf16[64,3072]{1,0:T(8,128)(2,1)S(1)}, bf16[64,3072]{1,0:T(8,128)(2,1)S(1)}, u32[]{:S(2)}, u32[]{:S(2)}) collective-permute-start(bf16[64,3072]{1,0:T(8,128)(2,1)S(1)} %get-tuple-element.105), channel_id=1, source_target_pairs={{0,4},{1,5},{2,6},{3,7},{4,0},{5,1},{6,2},{7,3},{8,12},{9,13},{10,... | collective-permute-start | bytes 1179656 | tf_op jit(solution)/shard_map/ppermute | solution.py:33
  39.6 12.1 %collective-permute-start.16 = (bf16[64,3072]{1,0:T(8,128)(2,1)S(1)}, bf16[64,3072]{1,0:T(8,128)(2,1)S(1)}, u32[]{:S(2)}, u32[]{:S(2)}) collective-permute-start(bf16[64,3072]{1,0:T(8,128)(2,1)S(1)} %get-tuple-element.107), channel_id=1, source_target_pairs={{0,2},{1,3},{2,0},{3,1},{4,6},{5,7},{6,4},{7,5},{8,10},{9,11},{10,... | collective-permute-start | bytes 1179656 | tf_op jit(solution)/shard_map/ppermute | solution.py:33
  45.9 11.8 %collective-permute-start.22 = (bf16[64,3072]{1,0:T(8,128)(2,1)S(1)}, bf16[64,3072]{1,0:T(8,128)(2,1)S(1)}, u32[]{:S(2)}, u32[]{:S(2)}) collective-permute-start(bf16[64,3072]{1,0:T(8,128)(2,1)S(1)} %get-tuple-element.118), channel_id=1, source_target_pairs={{0,4},{1,5},{2,6},{3,7},{4,0},{5,1},{6,2},{7,3},{8,12},{9,13},{10,... | collective-permute-start | bytes 1179656 | tf_op jit(solution)/shard_map/ppermute | solution.py:33
  46.0 12.5 %collective-permute-start.23 = (bf16[64,3072]{1,0:T(8,128)(2,1)S(1)}, bf16[64,3072]{1,0:T(8,128)(2,1)S(1)}, u32[]{:S(2)}, u32[]{:S(2)}) collective-permute-start(bf16[64,3072]{1,0:T(8,128)(2,1)S(1)} %get-tuple-element.120), channel_id=1, source_target_pairs={{0,2},{1,3},{2,0},{3,1},{4,6},{5,7},{6,4},{7,5},{8,10},{9,11},{10,... | collective-permute-start | bytes 1179656 | tf_op jit(solution)/shard_map/ppermute | solution.py:33
  51.8 9.9 %collective-permute-start.20 = (bf16[32,3072]{1,0:T(8,128)(2,1)S(1)}, bf16[32,3072]{1,0:T(8,128)(2,1)S(1)}, u32[]{:S(2)}, u32[]{:S(2)}) collective-permute-start(bf16[32,3072]{1,0:T(8,128)(2,1)S(1)} %get-tuple-element.114), channel_id=1, source_target_pairs={{0,2},{1,3},{2,0},{3,1},{4,6},{5,7},{6,4},{7,5},{8,10},{9,11},{10,... | collective-permute-start | bytes 589832 | tf_op jit(solution)/shard_map/ppermute | solution.py:33
  52.9 8.7 %collective-permute-start.21 = (bf16[32,3072]{1,0:T(8,128)(2,1)S(1)}, bf16[32,3072]{1,0:T(8,128)(2,1)S(1)}, u32[]{:S(2)}, u32[]{:S(2)}) collective-permute-start(bf16[32,3072]{1,0:T(8,128)(2,1)S(1)} %get-tuple-element.116), channel_id=1, source_target_pairs={{0,4},{1,5},{2,6},{3,7},{4,0},{5,1},{6,2},{7,3},{8,12},{9,13},{10,... | collective-permute-start | bytes 589832 | tf_op jit(solution)/shard_map/ppermute | solution.py:33
  56.0 9.6 %collective-permute-start.27 = (bf16[3,256,3072]{2,1,0:T(8,128)(2,1)S(1)}, bf16[3,256,3072]{2,1,0:T(8,128)(2,1)S(1)}, u32[]{:S(2)}, u32[]{:S(2)}) collective-permute-start(bf16[3,256,3072]{2,1,0:T(8,128)(2,1)S(1)} %get-tuple-element.141), channel_id=1, source_target_pairs={{0,1},{1,0},{2,3},{3,2},{4,5},{5,4},{6,7},{7,6},{8,9},{9,8},{10,11... | collective-permute-start | bytes 14155784 | tf_op jit(solution)/shard_map/ppermute | solution.py:33
  58.6 6.3 %collective-permute-start.24 = (bf16[32,3072]{1,0:T(8,128)(2,1)S(1)}, bf16[32,3072]{1,0:T(8,128)(2,1)S(1)}, u32[]{:S(2)}, u32[]{:S(2)}) collective-permute-start(bf16[32,3072]{1,0:T(8,128)(2,1)S(1)} %get-tuple-element.136), channel_id=1, source_target_pairs={{0,2},{1,3},{2,0},{3,1},{4,6},{5,7},{6,4},{7,5},{8,10},{9,11},{10,... | collective-permute-start | bytes 589832 | tf_op jit(solution)/shard_map/ppermute | solution.py:33
  59.4 5.7 %collective-permute-start.25 = (bf16[32,3072]{1,0:T(8,128)(2,1)S(1)}, bf16[32,3072]{1,0:T(8,128)(2,1)S(1)}, u32[]{:S(2)}, u32[]{:S(2)}) collective-permute-start(bf16[32,3072]{1,0:T(8,128)(2,1)S(1)} %get-tuple-element.138), channel_id=1, source_target_pairs={{0,4},{1,5},{2,6},{3,7},{4,0},{5,1},{6,2},{7,3},{8,12},{9,13},{10,... | collective-permute-start | bytes 589832 | tf_op jit(solution)/shard_map/ppermute | solution.py:33
  61.7 6.4 %collective-permute-start.28 = (bf16[2,16,3072]{2,1,0:T(8,128)(2,1)S(1)}, bf16[2,16,3072]{2,1,0:T(8,128)(2,1)S(1)}, u32[]{:S(2)}, u32[]{:S(2)}) collective-permute-start(bf16[2,16,3072]{2,1,0:T(8,128)(2,1)S(1)} %get-tuple-element.143), channel_id=1, source_target_pairs={{0,24},{1,25},{2,26},{3,27},{4,28},{5,29},{6,30},{7,31},{8,0},{9,1... | collective-permute-start | bytes 589832 | tf_op jit(solution)/shard_map/ppermute | solution.py:41
  65.2 9.7 %collective-permute-start.26 = (bf16[2,16,3072]{2,1,0:T(8,128)(2,1)S(1)}, bf16[2,16,3072]{2,1,0:T(8,128)(2,1)S(1)}, u32[]{:S(2)}, u32[]{:S(2)}) collective-permute-start(bf16[2,16,3072]{2,1,0:T(8,128)(2,1)S(1)} %get-tuple-element.140), channel_id=1, source_target_pairs={{0,8},{1,9},{2,10},{3,11},{4,12},{5,13},{6,14},{7,15},{8,16},{9,17... | collective-permute-start | bytes 589832 | tf_op jit(solution)/shard_map/ppermute | solution.py:41
  68.2 8.3 %collective-permute-start.29 = (bf16[2,16,3072]{2,1,0:T(8,128)(2,1)S(1)}, bf16[2,16,3072]{2,1,0:T(8,128)(2,1)S(1)}, u32[]{:S(2)}, u32[]{:S(2)}) collective-permute-start(bf16[2,16,3072]{2,1,0:T(8,128)(2,1)S(1)} %get-tuple-element.149), channel_id=1, source_target_pairs={{0,24},{1,25},{2,26},{3,27},{4,28},{5,29},{6,30},{7,31},{8,0},{9,1... | collective-permute-start | bytes 589832 | tf_op jit(solution)/shard_map/ppermute | solution.py:41

commit v10 on v9

--- a/solution.py
+++ b/solution.py
@@ -21,7 +21,7 @@
 C_LOAD = LONG // 5
 PANEL = 512
 WIDE = 1536
-FIRST_GRADS, LAST_GRADS = (0,), (1, 2)
+FIRST_GRADS, LAST_GRADS = (0, 1), (2,)
 TURN = pltpu.VMEM((8, 128), jnp.float32)
 VMEM = pl.BlockSpec(memory_space=pltpu.VMEM)
 HBM = pl.BlockSpec(memory_space=pltpu.HBM)

time: 77.5 us -> 77.6 us (level)
  transfers between devices with their start and end apart: 30 -> 30, of which waited for: 16 -> 17; matrix products, arithmetic and copies ran while one was open for 0% -> 0% of each run, Pallas kernels for 21% -> 21%
where the time goes in v10:
time: 77.6 us; the launch traced here: 77.5 us
  starting transfers between devices  39.6 us (51%)
  waiting for transfers between devices  20.3 us (26%)
  Pallas kernels  16.7 us (22%)
  between operations  0.78 us (1%)
    ppermute x24, starting transfers between devices, swapped(): lax.ppermute(block, 'dp', [(low, low ^ mask) for low in range(count)])  23.9 us
    ppermute x24, waiting for transfers between devices, swapped(): lax.ppermute(block, 'dp', [(low, low ^ mask) for low in range(count)])  17.6 us
    ppermute x6, starting transfers between devices, shifted(): return lax.ppermute(block, 'dp', route)  15.7 us
    pallas_call x2, Pallas kernels, expert(): pl.pallas_call(functools.partial(expert_kernel, [len(part) for part in pa...  5.98 us
    pallas_call x15, Pallas kernels, staged(): pl.pallas_call(kernel, out_shape=(*outs, TURN), in_specs=[VMEM] * len(val...  3.97 us
    pallas_call x2, Pallas kernels, own_grads(): pl.pallas_call(functools.partial(own_kernel, which, factor), grid=(width...  3.88 us
    ppermute x6, waiting for transfers between devices, shifted(): return lax.ppermute(block, 'dp', route)  2.7 us
  transfers between devices with their start and end apart: 30, of which 17 were waited for; matrix products, arithmetic and copies ran while one was open for 0% of the time, Pallas kernels for 21%

profile of v10, /device:TPU:0, one launch (start us, length us, event | category | flops | bytes accessed | tf_op | source)
XLA Modules:
  0.0 77.5 jit_solution(4282920715914921529)
XLA Ops:
  0.6 0.5 collective-permute-start
  1.2 1.4 %pick.1 = (bf16[2,16,3072]{2,1,0:T(8,128)(2,1)S(1)}, f32[16,128]{1,0:T(8,128)S(1)}, f32[8,128]{1,0:T(8,128)S(1)}) custom-call(s32[1]{0:T(128)} %bitcast.place, s32[16]{0:T(128)} %token_.1, s32[32]{0:T(128)} %count.1, f32[16]{0:T(128)} %gate.1, bf16[128,3072]{1,0:T(8,128)(2,1)} %tokens.1, bf16[16,3072]{1,0:T(8,128)(2,1)} %grad.1), custom_call_target="tpu_custom_call" | custom-call | tf_op jit(solution)/shard_map/pick/pallas_call | solution.py:125
  2.6 3.7 %collective-permute-start.7 = (bf16[2,16,3072]{2,1,0:T(8,128)(2,1)S(1)}, bf16[2,16,3072]{2,1,0:T(8,128)(2,1)S(1)}, u32[]{:S(2)}, u32[]{:S(2)}) collective-permute-start(bf16[2,16,3072]{2,1,0:T(8,128)(2,1)S(1)} %get-tuple-element.81.refs_0_), channel_id=1, source_target_pairs={{0,16},{1,17},{2,18},{3,19},{4,20},{5,21},{6,22},{7,23},{8,24},{9,... | collective-permute-start | bytes 589832 | tf_op jit(solution)/shard_map/ppermute | solution.py:41
  6.2 0.2 collective-permute-start.3
  6.5 0.3 collective-permute-start.4
  6.8 1.6 %collective-permute-start.1 = (bf16[16,3072]{1,0:T(8,128)(2,1)S(1)}, bf16[16,3072]{1,0:T(8,128)(2,1)S(1)}, u32[]{:S(2)}, u32[]{:S(2)}) collective-permute-start(bf16[16,3072]{1,0:T(8,128)(2,1)S(1)} %get-tuple-element.83.refs_0_), channel_id=1, source_target_pairs={{0,2},{1,3},{2,0},{3,1},{4,6},{5,7},{6,4},{7,5},{8,10},{9,11},{10,... | collective-permute-start | bytes 294920 | tf_op jit(solution)/shard_map/ppermute | solution.py:33
  8.3 1.5 %collective-permute-start.2 = (bf16[16,3072]{1,0:T(8,128)(2,1)S(1)}, bf16[16,3072]{1,0:T(8,128)(2,1)S(1)}, u32[]{:S(2)}, u32[]{:S(2)}) collective-permute-start(bf16[16,3072]{1,0:T(8,128)(2,1)S(1)} %get-tuple-element.84.refs_2_), channel_id=1, source_target_pairs={{0,4},{1,5},{2,6},{3,7},{4,0},{5,1},{6,2},{7,3},{8,12},{9,13},{10,... | collective-permute-start | bytes 294920 | tf_op jit(solution)/shard_map/ppermute | solution.py:33
  9.9 2.2 %collective-permute-done.4.refs_5_.refs_13_.refs_10_ = bf16[256,3072]{1,0:T(8,128)(2,1)S(1)} collective-permute-done((bf16[256,3072]{1,0:T(8,128)(2,1)}, bf16[256,3072]{1,0:T(8,128)(2,1)S(1)}, u32[]{:S(2)}, u32[]{:S(2)}) %collective-permute-start.4) | collective-permute-done | bytes 1572896 | tf_op jit(solution)/shard_map/ppermute | solution.py:33
  12.1 0.8 %collective-permute-done.2.refs_3_ = bf16[16,3072]{1,0:T(8,128)(2,1)S(1)} collective-permute-done((bf16[16,3072]{1,0:T(8,128)(2,1)S(1)}, bf16[16,3072]{1,0:T(8,128)(2,1)S(1)}, u32[]{:S(2)}, u32[]{:S(2)}) %collective-permute-start.2) | collective-permute-done | bytes 98336 | tf_op jit(solution)/shard_map/ppermute | solution.py:33
  13.0 1.6 %collective-permute-start.12 = (bf16[2,16,3072]{2,1,0:T(8,128)(2,1)S(1)}, bf16[2,16,3072]{2,1,0:T(8,128)(2,1)S(1)}, u32[]{:S(2)}, u32[]{:S(2)}) collective-permute-start(bf16[2,16,3072]{2,1,0:T(8,128)(2,1)S(1)} %get-tuple-element.95), channel_id=1, source_target_pairs={{0,8},{1,9},{2,10},{3,11},{4,12},{5,13},{6,14},{7,15},{8,16},{9,17... | collective-permute-start | bytes 589832 | tf_op jit(solution)/shard_map/ppermute | solution.py:41
  14.6 1.5 %collective-permute-start.5 = (bf16[32,3072]{1,0:T(8,128)(2,1)S(1)}, bf16[32,3072]{1,0:T(8,128)(2,1)S(1)}, u32[]{:S(2)}, u32[]{:S(2)}) collective-permute-start(bf16[32,3072]{1,0:T(8,128)(2,1)S(1)} %get-tuple-element.86.refs_0_), channel_id=1, source_target_pairs={{0,4},{1,5},{2,6},{3,7},{4,0},{5,1},{6,2},{7,3},{8,12},{9,13},{10,... | collective-permute-start | bytes 589832 | tf_op jit(solution)/shard_map/ppermute | solution.py:33
  16.2 0.7 collective-permute-start.6
  16.8 1.4 %collective-permute-start.8 = (bf16[16,3072]{1,0:T(8,128)(2,1)S(1)}, bf16[16,3072]{1,0:T(8,128)(2,1)S(1)}, u32[]{:S(2)}, u32[]{:S(2)}) collective-permute-start(bf16[16,3072]{1,0:T(8,128)(2,1)S(1)} %get-tuple-element.89.refs_0_), channel_id=1, source_target_pairs={{0,2},{1,3},{2,0},{3,1},{4,6},{5,7},{6,4},{7,5},{8,10},{9,11},{10,... | collective-permute-start | bytes 294920 | tf_op jit(solution)/shard_map/ppermute | solution.py:33
  18.3 0.9 %collective-permute-start.9 = (bf16[16,3072]{1,0:T(8,128)(2,1)S(1)}, bf16[16,3072]{1,0:T(8,128)(2,1)S(1)}, u32[]{:S(2)}, u32[]{:S(2)}) collective-permute-start(bf16[16,3072]{1,0:T(8,128)(2,1)S(1)} %get-tuple-element.90.refs_2_), channel_id=1, source_target_pairs={{0,4},{1,5},{2,6},{3,7},{4,0},{5,1},{6,2},{7,3},{8,12},{9,13},{10,... | collective-permute-start | bytes 294920 | tf_op jit(solution)/shard_map/ppermute | solution.py:33
  19.2 2.2 %collective-permute-done.5.refs_1_ = bf16[32,3072]{1,0:T(8,128)(2,1)S(1)} collective-permute-done((bf16[32,3072]{1,0:T(8,128)(2,1)S(1)}, bf16[32,3072]{1,0:T(8,128)(2,1)S(1)}, u32[]{:S(2)}, u32[]{:S(2)}) %collective-permute-start.5) | collective-permute-done | bytes 196640 | tf_op jit(solution)/shard_map/ppermute | solution.py:33
  21.3 1.5 %collective-permute-done.6.refs_3_ = bf16[32,3072]{1,0:T(8,128)(2,1)S(1)} collective-permute-done((bf16[32,3072]{1,0:T(8,128)(2,1)S(1)}, bf16[32,3072]{1,0:T(8,128)(2,1)S(1)}, u32[]{:S(2)}, u32[]{:S(2)}) %collective-permute-start.6) | collective-permute-done | bytes 196640 | tf_op jit(solution)/shard_map/ppermute | solution.py:33
  22.9 2.4 %collective-permute-start.19 = (bf16[128,3072]{1,0:T(8,128)(2,1)S(1)}, bf16[128,3072]{1,0:T(8,128)(2,1)S(1)}, u32[]{:S(2)}, u32[]{:S(2)}) collective-permute-start(bf16[128,3072]{1,0:T(8,128)(2,1)S(1)} %get-tuple-element.110), channel_id=1, source_target_pairs={{0,24},{1,25},{2,26},{3,27},{4,28},{5,29},{6,30},{7,31},{8,0},{9,1... | collective-permute-start | bytes 2359304 | tf_op jit(solution)/shard_map/ppermute | solution.py:41
  25.5 1.4 %collective-permute-start.11 = (bf16[32,3072]{1,0:T(8,128)(2,1)S(1)}, bf16[32,3072]{1,0:T(8,128)(2,1)S(1)}, u32[]{:S(2)}, u32[]{:S(2)}) collective-permute-start(bf16[32,3072]{1,0:T(8,128)(2,1)S(1)} %get-tuple-element.94.refs_6_), channel_id=1, source_target_pairs={{0,2},{1,3},{2,0},{3,1},{4,6},{5,7},{6,4},{7,5},{8,10},{9,11},{10,... | collective-permute-start | bytes 589832 | tf_op jit(solution)/shard_map/ppermute | solution.py:33
  26.9 0.7 collective-permute-start.13
  27.6 1.9 %collective-permute-start.14 = (bf16[16,3072]{1,0:T(8,128)(2,1)S(1)}, bf16[16,3072]{1,0:T(8,128)(2,1)S(1)}, u32[]{:S(2)}, u32[]{:S(2)}) collective-permute-start(bf16[16,3072]{1,0:T(8,128)(2,1)S(1)} %get-tuple-element.101.refs_2_), channel_id=1, source_target_pairs={{0,4},{1,5},{2,6},{3,7},{4,0},{5,1},{6,2},{7,3},{8,12},{9,13},{10,... | collective-permute-start | bytes 294920 | tf_op jit(solution)/shard_map/ppermute | solution.py:33
  29.5 2.5 %turn_panels.1 = (bf16[3,3072,256]{2,1,0:T(8,128)(2,1)S(1)}, bf16[3,3072,256]{2,1,0:T(8,128)(2,1)S(1)}, f32[8,128]{1,0:T(8,128)S(1)}) custom-call(bf16[256,3072]{1,0:T(8,128)(2,1)S(1)} %copy-done, bf16[256,3072]{1,0:T(8,128)(2,1)S(1)} %copy-done.1, bf16[256,3072]{1,0:T(8,128)(2,1)S(1)} %copy-done.2, ...), custom_call_target="tpu_custom_call" | custom-call | tf_op jit(solution)/shard_map/turn_panels/pallas_call | solution.py:279
  32.0 0.2 collective-permute-done.13.refs_1_
  32.2 0.4 collective-permute-done.14.refs_3_
  32.7 2.4 %collective-permute-start.17 = (bf16[32,3072]{1,0:T(8,128)(2,1)S(1)}, bf16[32,3072]{1,0:T(8,128)(2,1)S(1)}, u32[]{:S(2)}, u32[]{:S(2)}) collective-permute-start(bf16[32,3072]{1,0:T(8,128)(2,1)S(1)} %get-tuple-element.108.refs_0_), channel_id=1, source_target_pairs={{0,4},{1,5},{2,6},{3,7},{4,0},{5,1},{6,2},{7,3},{8,12},{9,13},{10,... | collective-permute-start | bytes 589832 | tf_op jit(solution)/shard_map/ppermute | solution.py:33
  35.1 1.3 %collective-permute-start.18 = (bf16[32,3072]{1,0:T(8,128)(2,1)S(1)}, bf16[32,3072]{1,0:T(8,128)(2,1)S(1)}, u32[]{:S(2)}, u32[]{:S(2)}) collective-permute-start(bf16[32,3072]{1,0:T(8,128)(2,1)S(1)} %get-tuple-element.109.refs_2_), channel_id=1, source_target_pairs={{0,2},{1,3},{2,0},{3,1},{4,6},{5,7},{6,4},{7,5},{8,10},{9,11},{10,... | collective-permute-start | bytes 589832 | tf_op jit(solution)/shard_map/ppermute | solution.py:33
  36.4 3.0 %expert.2 = (bf16[128,3072]{1,0:T(8,128)(2,1)S(1)}, bf16[128,3072]{1,0:T(8,128)(2,1)S(1)}, bf16[128,512]{1,0:T(8,128)(2,1)S(1)}, bf16[128,512]{1,0:T(8,128)(2,1)...) custom-call(bf16[32,3072]{1,0:T(8,128)(2,1)S(1)} %get-tuple-element., ...), custom_call_target="tpu_custom_call" | custom-call | flops 2415919104 | bytes 9437184 | tf_op jit(solution)/shard_map/expert/pallas_call | solution.py:205
  39.6 0.7 collective-permute-start.16
  40.4 2.5 %collective-permute-done.18.refs_3_ = bf16[32,3072]{1,0:T(8,128)(2,1)S(1)} collective-permute-done((bf16[32,3072]{1,0:T(8,128)(2,1)S(1)}, bf16[32,3072]{1,0:T(8,128)(2,1)S(1)}, u32[]{:S(2)}, u32[]{:S(2)}) %collective-permute-start.18) | collective-permute-done | bytes 196640 | tf_op jit(solution)/shard_map/ppermute | solution.py:33
  42.9 3.0 %expert.3 = (bf16[128,3072]{1,0:T(8,128)(2,1)S(1)}, bf16[128,3072]{1,0:T(8,128)(2,1)S(1)}, bf16[128,512]{1,0:T(8,128)(2,1)S(1)}, bf16[128,512]{1,0:T(8,128)(2,1)...) custom-call(bf16[32,3072]{1,0:T(8,128)(2,1)S(1)} %get-tuple-element., ...), custom_call_target="tpu_custom_call" | custom-call | flops 2415919104 | bytes 9437184 | tf_op jit(solution)/shard_map/expert/pallas_call | solution.py:205
  46.0 1.4 %collective-permute-start.23 = (bf16[64,3072]{1,0:T(8,128)(2,1)S(1)}, bf16[64,3072]{1,0:T(8,128)(2,1)S(1)}, u32[]{:S(2)}, u32[]{:S(2)}) collective-permute-start(bf16[64,3072]{1,0:T(8,128)(2,1)S(1)} %get-tuple-element.120), channel_id=1, source_target_pairs={{0,2},{1,3},{2,0},{3,1},{4,6},{5,7},{6,4},{7,5},{8,10},{9,11},{10,... | collective-permute-start | bytes 1179656 | tf_op jit(solution)/shard_map/ppermute | solution.py:33
  47.4 4.1 %collective-permute-done.15.refs_1_ = bf16[64,3072]{1,0:T(8,128)(2,1)S(1)} collective-permute-done((bf16[64,3072]{1,0:T(8,128)(2,1)S(1)}, bf16[64,3072]{1,0:T(8,128)(2,1)S(1)}, u32[]{:S(2)}, u32[]{:S(2)}) %collective-permute-start.15) | collective-permute-done | bytes 393248 | tf_op jit(solution)/shard_map/ppermute | solution.py:33
  51.8 1.1 %collective-permute-start.20 = (bf16[32,3072]{1,0:T(8,128)(2,1)S(1)}, bf16[32,3072]{1,0:T(8,128)(2,1)S(1)}, u32[]{:S(2)}, u32[]{:S(2)}) collective-permute-start(bf16[32,3072]{1,0:T(8,128)(2,1)S(1)} %get-tuple-element.114), channel_id=1, source_target_pairs={{0,2},{1,3},{2,0},{3,1},{4,6},{5,7},{6,4},{7,5},{8,10},{9,11},{10,... | collective-permute-start | bytes 589832 | tf_op jit(solution)/shard_map/ppermute | solution.py:33
  52.9 1.6 %collective-permute-start.21 = (bf16[32,3072]{1,0:T(8,128)(2,1)S(1)}, bf16[32,3072]{1,0:T(8,128)(2,1)S(1)}, u32[]{:S(2)}, u32[]{:S(2)}) collective-permute-start(bf16[32,3072]{1,0:T(8,128)(2,1)S(1)} %get-tuple-element.116), channel_id=1, source_target_pairs={{0,4},{1,5},{2,6},{3,7},{4,0},{5,1},{6,2},{7,3},{8,12},{9,13},{10,... | collective-permute-start | bytes 589832 | tf_op jit(solution)/shard_map/ppermute | solution.py:33
  54.5 1.4 %other_grads.1 = (bf16[3,256,3072]{2,1,0:T(8,128)(2,1)S(1)}, f32[8,128]{1,0:T(8,128)S(1)}) custom-call(bf16[128,3072]{1,0:T(8,128)(2,1)S(1)} %get-tuple-element.121.refs_0_, bf16[128,3072]{1,0:T(8,128)(2,1)S(1)} %get-tuple-element.122.refs_1_, bf16[128,512]{1,0:T(8,128)(2,1)S(1)} %get-tuple-element.123.refs_2_, ...), custom_call_target="tpu_custom_call" | custom-call | flops 2000000000 | tf_op jit(solution)/shard_map/other_grads/pallas_call | solution.py:237
  56.0 1.6 %collective-permute-done.22.refs_1_ = bf16[64,3072]{1,0:T(8,128)(2,1)S(1)} collective-permute-done((bf16[64,3072]{1,0:T(8,128)(2,1)S(1)}, bf16[64,3072]{1,0:T(8,128)(2,1)S(1)}, u32[]{:S(2)}, u32[]{:S(2)}) %collective-permute-start.22) | collective-permute-done | bytes 393248 | tf_op jit(solution)/shard_map/ppermute | solution.py:33
  57.7 0.8 collective-permute-done.23.refs_3_
  58.6 0.8 %collective-permute-start.24 = (bf16[32,3072]{1,0:T(8,128)(2,1)S(1)}, bf16[32,3072]{1,0:T(8,128)(2,1)S(1)}, u32[]{:S(2)}, u32[]{:S(2)}) collective-permute-start(bf16[32,3072]{1,0:T(8,128)(2,1)S(1)} %get-tuple-element.136), channel_id=1, source_target_pairs={{0,2},{1,3},{2,0},{3,1},{4,6},{5,7},{6,4},{7,5},{8,10},{9,11},{10,... | collective-permute-start | bytes 589832 | tf_op jit(solution)/shard_map/ppermute | solution.py:33
  59.4 1.4 %collective-permute-start.25 = (bf16[32,3072]{1,0:T(8,128)(2,1)S(1)}, bf16[32,3072]{1,0:T(8,128)(2,1)S(1)}, u32[]{:S(2)}, u32[]{:S(2)}) collective-permute-start(bf16[32,3072]{1,0:T(8,128)(2,1)S(1)} %get-tuple-element.138), channel_id=1, source_target_pairs={{0,4},{1,5},{2,6},{3,7},{4,0},{5,1},{6,2},{7,3},{8,12},{9,13},{10,... | collective-permute-start | bytes 589832 | tf_op jit(solution)/shard_map/ppermute | solution.py:33
  60.8 0.8 %collective-permute-done.20.refs_1_ = bf16[32,3072]{1,0:T(8,128)(2,1)S(1)} collective-permute-done((bf16[32,3072]{1,0:T(8,128)(2,1)S(1)}, bf16[32,3072]{1,0:T(8,128)(2,1)S(1)}, u32[]{:S(2)}, u32[]{:S(2)}) %collective-permute-start.20) | collective-permute-done | bytes 196640 | tf_op jit(solution)/shard_map/ppermute | solution.py:33
  61.7 3.2 %collective-permute-start.28 = (bf16[2,16,3072]{2,1,0:T(8,128)(2,1)S(1)}, bf16[2,16,3072]{2,1,0:T(8,128)(2,1)S(1)}, u32[]{:S(2)}, u32[]{:S(2)}) collective-permute-start(bf16[2,16,3072]{2,1,0:T(8,128)(2,1)S(1)} %get-tuple-element.143), channel_id=1, source_target_pairs={{0,24},{1,25},{2,26},{3,27},{4,28},{5,29},{6,30},{7,31},{8,0},{9,1... | collective-permute-start | bytes 589832 | tf_op jit(solution)/shard_map/ppermute | solution.py:41
  65.2 0.4 collective-permute-start.26
  65.6 2.2 %own_grads.2 = (bf16[256,3072]{1,0:T(8,128)(2,1)}, bf16[256,3072]{1,0:T(8,128)(2,1)}, f32[8,128]{1,0:T(8,128)S(1)}) custom-call(bf16[128,3072]{1,0:T(8,128)(2,1)S(1)} %get-tuple-element.121.refs_0_, bf16[128,3072]{1,0:T(8,128)(2,1)S(1)} %get-tuple-element.122.refs_1_, bf16[128,512]{1,0:T(8,128)(2,1)S(1)} %get-tuple-element.123.refs_2_, ...), custom_call_target="tpu_custom_call" | custom-call | tf_op jit(solution)/shard_map/own_grads/pallas_call | solution.py:262
  67.8 0.4 collective-permute-done.28.refs_1_
  68.2 4.5 %collective-permute-start.29 = (bf16[2,16,3072]{2,1,0:T(8,128)(2,1)S(1)}, bf16[2,16,3072]{2,1,0:T(8,128)(2,1)S(1)}, u32[]{:S(2)}, u32[]{:S(2)}) collective-permute-start(bf16[2,16,3072]{2,1,0:T(8,128)(2,1)S(1)} %get-tuple-element.149), channel_id=1, source_target_pairs={{0,24},{1,25},{2,26},{3,27},{4,28},{5,29},{6,30},{7,31},{8,0},{9,1... | collective-permute-start | bytes 589832 | tf_op jit(solution)/shard_map/ppermute | solution.py:41
  72.7 1.7 %own_grads.3 = (bf16[256,3072]{1,0:T(8,128)(2,1)}, f32[8,128]{1,0:T(8,128)S(1)}) custom-call(bf16[128,3072]{1,0:T(8,128)(2,1)S(1)} %get-tuple-element.121.refs_0_, bf16[128,3072]{1,0:T(8,128)(2,1)S(1)} %get-tuple-element.122.refs_1_, bf16[128,512]{1,0:T(8,128)(2,1)S(1)} %get-tuple-element.123.refs_2_, bf16[128,512]{1,0:T(8,128)(2,1)S(1)} %get-tuple-element.124.refs_3_, ...), custom_call_target="tpu_custom_call" | custom-call | tf_op jit(solution)/shard_map/own_grads/pallas_call | solution.py:262
  74.4 0.5 collective-permute-done.26.refs_1_
  74.9 1.8 %collective-permute-done.29.refs_1_ = bf16[2,16,3072]{2,1,0:T(8,128)(2,1)S(1)} collective-permute-done((bf16[2,16,3072]{2,1,0:T(8,128)(2,1)S(1)}, bf16[2,16,3072]{2,1,0:T(8,128)(2,1)S(1)}, u32[]{:S(2)}, u32[]{:S(2)}) %collective-permute-start.29) | collective-permute-done | bytes 196640 | tf_op jit(solution)/shard_map/ppermute | solution.py:41
  76.7 0.7 final.1
  (39 shorter events, 1.6 us)
Async XLA Ops:
  0.6 6.1 %collective-permute-start = (bf16[256,3072]{1,0:T(8,128)(2,1)}, bf16[256,3072]{1,0:T(8,128)(2,1)S(1)}, u32[]{:S(2)}, u32[]{:S(2)}) collective-permute-start(bf16[256,3072]{1,0:T(8,128)(2,1)} %refs_5_.1), channel_id=1, source_target_pairs={{0,1},{1,0},{2,3},{3,2},{4,5},{5,4},{6,7},{7,6},{8,9},{9,8},{10,11... | collective-permute-start | bytes 4718600 | tf_op jit(solution)/shard_map/ppermute | solution.py:33
  2.6 14.2 %collective-permute-start.7 = (bf16[2,16,3072]{2,1,0:T(8,128)(2,1)S(1)}, bf16[2,16,3072]{2,1,0:T(8,128)(2,1)S(1)}, u32[]{:S(2)}, u32[]{:S(2)}) collective-permute-start(bf16[2,16,3072]{2,1,0:T(8,128)(2,1)S(1)} %get-tuple-element.81.refs_0_), channel_id=1, source_target_pairs={{0,16},{1,17},{2,18},{3,19},{4,20},{5,21},{6,22},{7,23},{8,24},{9,... | collective-permute-start | bytes 589832 | tf_op jit(solution)/shard_map/ppermute | solution.py:41
  6.2 3.6 %collective-permute-start.3 = (bf16[256,3072]{1,0:T(8,128)(2,1)}, bf16[256,3072]{1,0:T(8,128)(2,1)S(1)}, u32[]{:S(2)}, u32[]{:S(2)}) collective-permute-start(bf16[256,3072]{1,0:T(8,128)(2,1)} %refs_6_.1), channel_id=1, source_target_pairs={{0,1},{1,0},{2,3},{3,2},{4,5},{5,4},{6,7},{7,6},{8,9},{9,8},{10,11... | collective-permute-start | bytes 4718600 | tf_op jit(solution)/shard_map/ppermute | solution.py:33
  6.5 5.7 %collective-permute-start.4 = (bf16[256,3072]{1,0:T(8,128)(2,1)}, bf16[256,3072]{1,0:T(8,128)(2,1)S(1)}, u32[]{:S(2)}, u32[]{:S(2)}) collective-permute-start(bf16[256,3072]{1,0:T(8,128)(2,1)} %refs_7_.1), channel_id=1, source_target_pairs={{0,1},{1,0},{2,3},{3,2},{4,5},{5,4},{6,7},{7,6},{8,9},{9,8},{10,11... | collective-permute-start | bytes 4718600 | tf_op jit(solution)/shard_map/ppermute | solution.py:33
  6.8 5.3 %collective-permute-start.1 = (bf16[16,3072]{1,0:T(8,128)(2,1)S(1)}, bf16[16,3072]{1,0:T(8,128)(2,1)S(1)}, u32[]{:S(2)}, u32[]{:S(2)}) collective-permute-start(bf16[16,3072]{1,0:T(8,128)(2,1)S(1)} %get-tuple-element.83.refs_0_), channel_id=1, source_target_pairs={{0,2},{1,3},{2,0},{3,1},{4,6},{5,7},{6,4},{7,5},{8,10},{9,11},{10,... | collective-permute-start | bytes 294920 | tf_op jit(solution)/shard_map/ppermute | solution.py:33
  8.3 4.6 %collective-permute-start.2 = (bf16[16,3072]{1,0:T(8,128)(2,1)S(1)}, bf16[16,3072]{1,0:T(8,128)(2,1)S(1)}, u32[]{:S(2)}, u32[]{:S(2)}) collective-permute-start(bf16[16,3072]{1,0:T(8,128)(2,1)S(1)} %get-tuple-element.84.refs_2_), channel_id=1, source_target_pairs={{0,4},{1,5},{2,6},{3,7},{4,0},{5,1},{6,2},{7,3},{8,12},{9,13},{10,... | collective-permute-start | bytes 294920 | tf_op jit(solution)/shard_map/ppermute | solution.py:33
  13.0 13.9 %collective-permute-start.12 = (bf16[2,16,3072]{2,1,0:T(8,128)(2,1)S(1)}, bf16[2,16,3072]{2,1,0:T(8,128)(2,1)S(1)}, u32[]{:S(2)}, u32[]{:S(2)}) collective-permute-start(bf16[2,16,3072]{2,1,0:T(8,128)(2,1)S(1)} %get-tuple-element.95), channel_id=1, source_target_pairs={{0,8},{1,9},{2,10},{3,11},{4,12},{5,13},{6,14},{7,15},{8,16},{9,17... | collective-permute-start | bytes 589832 | tf_op jit(solution)/shard_map/ppermute | solution.py:41
  14.6 6.7 %collective-permute-start.5 = (bf16[32,3072]{1,0:T(8,128)(2,1)S(1)}, bf16[32,3072]{1,0:T(8,128)(2,1)S(1)}, u32[]{:S(2)}, u32[]{:S(2)}) collective-permute-start(bf16[32,3072]{1,0:T(8,128)(2,1)S(1)} %get-tuple-element.86.refs_0_), channel_id=1, source_target_pairs={{0,4},{1,5},{2,6},{3,7},{4,0},{5,1},{6,2},{7,3},{8,12},{9,13},{10,... | collective-permute-start | bytes 589832 | tf_op jit(solution)/shard_map/ppermute | solution.py:33
  16.2 6.7 %collective-permute-start.6 = (bf16[32,3072]{1,0:T(8,128)(2,1)S(1)}, bf16[32,3072]{1,0:T(8,128)(2,1)S(1)}, u32[]{:S(2)}, u32[]{:S(2)}) collective-permute-start(bf16[32,3072]{1,0:T(8,128)(2,1)S(1)} %get-tuple-element.87.refs_2_), channel_id=1, source_target_pairs={{0,2},{1,3},{2,0},{3,1},{4,6},{5,7},{6,4},{7,5},{8,10},{9,11},{10,... | collective-permute-start | bytes 589832 | tf_op jit(solution)/shard_map/ppermute | solution.py:33
  16.8 8.4 %collective-permute-start.8 = (bf16[16,3072]{1,0:T(8,128)(2,1)S(1)}, bf16[16,3072]{1,0:T(8,128)(2,1)S(1)}, u32[]{:S(2)}, u32[]{:S(2)}) collective-permute-start(bf16[16,3072]{1,0:T(8,128)(2,1)S(1)} %get-tuple-element.89.refs_0_), channel_id=1, source_target_pairs={{0,2},{1,3},{2,0},{3,1},{4,6},{5,7},{6,4},{7,5},{8,10},{9,11},{10,... | collective-permute-start | bytes 294920 | tf_op jit(solution)/shard_map/ppermute | solution.py:33
  18.3 7.0 %collective-permute-start.9 = (bf16[16,3072]{1,0:T(8,128)(2,1)S(1)}, bf16[16,3072]{1,0:T(8,128)(2,1)S(1)}, u32[]{:S(2)}, u32[]{:S(2)}) collective-permute-start(bf16[16,3072]{1,0:T(8,128)(2,1)S(1)} %get-tuple-element.90.refs_2_), channel_id=1, source_target_pairs={{0,4},{1,5},{2,6},{3,7},{4,0},{5,1},{6,2},{7,3},{8,12},{9,13},{10,... | collective-permute-start | bytes 294920 | tf_op jit(solution)/shard_map/ppermute | solution.py:33
  22.9 20.0 %collective-permute-start.19 = (bf16[128,3072]{1,0:T(8,128)(2,1)S(1)}, bf16[128,3072]{1,0:T(8,128)(2,1)S(1)}, u32[]{:S(2)}, u32[]{:S(2)}) collective-permute-start(bf16[128,3072]{1,0:T(8,128)(2,1)S(1)} %get-tuple-element.110), channel_id=1, source_target_pairs={{0,24},{1,25},{2,26},{3,27},{4,28},{5,29},{6,30},{7,31},{8,0},{9,1... | collective-permute-start | bytes 2359304 | tf_op jit(solution)/shard_map/ppermute | solution.py:41
  25.3 11.1 %collective-permute-start.10 = (bf16[32,3072]{1,0:T(8,128)(2,1)S(1)}, bf16[32,3072]{1,0:T(8,128)(2,1)S(1)}, u32[]{:S(2)}, u32[]{:S(2)}) collective-permute-start(bf16[32,3072]{1,0:T(8,128)(2,1)S(1)} %get-tuple-element.93.refs_4_), channel_id=1, source_target_pairs={{0,4},{1,5},{2,6},{3,7},{4,0},{5,1},{6,2},{7,3},{8,12},{9,13},{10,... | collective-permute-start | bytes 589832 | tf_op jit(solution)/shard_map/ppermute | solution.py:33
  25.5 11.0 %collective-permute-start.11 = (bf16[32,3072]{1,0:T(8,128)(2,1)S(1)}, bf16[32,3072]{1,0:T(8,128)(2,1)S(1)}, u32[]{:S(2)}, u32[]{:S(2)}) collective-permute-start(bf16[32,3072]{1,0:T(8,128)(2,1)S(1)} %get-tuple-element.94.refs_6_), channel_id=1, source_target_pairs={{0,2},{1,3},{2,0},{3,1},{4,6},{5,7},{6,4},{7,5},{8,10},{9,11},{10,... | collective-permute-start | bytes 589832 | tf_op jit(solution)/shard_map/ppermute | solution.py:33
  26.9 2.6 %copy-start = (bf16[256,3072]{1,0:T(8,128)(2,1)S(1)}, bf16[256,3072]{1,0:T(8,128)(2,1)}, u32[]{:S(2)}) copy-start(bf16[256,3072]{1,0:T(8,128)(2,1)} %refs_5_.1) | copy-start | bytes 4718596
  26.9 2.6 %copy-start.1 = (bf16[256,3072]{1,0:T(8,128)(2,1)S(1)}, bf16[256,3072]{1,0:T(8,128)(2,1)}, u32[]{:S(2)}) copy-start(bf16[256,3072]{1,0:T(8,128)(2,1)} %refs_6_.1) | copy-start | bytes 4718596
  26.9 2.6 %copy-start.2 = (bf16[256,3072]{1,0:T(8,128)(2,1)S(1)}, bf16[256,3072]{1,0:T(8,128)(2,1)}, u32[]{:S(2)}) copy-start(bf16[256,3072]{1,0:T(8,128)(2,1)} %refs_7_.1) | copy-start | bytes 4718596
  26.9 5.3 %collective-permute-start.13 = (bf16[16,3072]{1,0:T(8,128)(2,1)S(1)}, bf16[16,3072]{1,0:T(8,128)(2,1)S(1)}, u32[]{:S(2)}, u32[]{:S(2)}) collective-permute-start(bf16[16,3072]{1,0:T(8,128)(2,1)S(1)} %get-tuple-element.100.refs_0_), channel_id=1, source_target_pairs={{0,2},{1,3},{2,0},{3,1},{4,6},{5,7},{6,4},{7,5},{8,10},{9,11},{10,... | collective-permute-start | bytes 294920 | tf_op jit(solution)/shard_map/ppermute | solution.py:33
  27.6 5.0 %collective-permute-start.14 = (bf16[16,3072]{1,0:T(8,128)(2,1)S(1)}, bf16[16,3072]{1,0:T(8,128)(2,1)S(1)}, u32[]{:S(2)}, u32[]{:S(2)}) collective-permute-start(bf16[16,3072]{1,0:T(8,128)(2,1)S(1)} %get-tuple-element.101.refs_2_), channel_id=1, source_target_pairs={{0,4},{1,5},{2,6},{3,7},{4,0},{5,1},{6,2},{7,3},{8,12},{9,13},{10,... | collective-permute-start | bytes 294920 | tf_op jit(solution)/shard_map/ppermute | solution.py:33
  32.7 7.7 %collective-permute-start.17 = (bf16[32,3072]{1,0:T(8,128)(2,1)S(1)}, bf16[32,3072]{1,0:T(8,128)(2,1)S(1)}, u32[]{:S(2)}, u32[]{:S(2)}) collective-permute-start(bf16[32,3072]{1,0:T(8,128)(2,1)S(1)} %get-tuple-element.108.refs_0_), channel_id=1, source_target_pairs={{0,4},{1,5},{2,6},{3,7},{4,0},{5,1},{6,2},{7,3},{8,12},{9,13},{10,... | collective-permute-start | bytes 589832 | tf_op jit(solution)/shard_map/ppermute | solution.py:33
  35.1 7.8 %collective-permute-start.18 = (bf16[32,3072]{1,0:T(8,128)(2,1)S(1)}, bf16[32,3072]{1,0:T(8,128)(2,1)S(1)}, u32[]{:S(2)}, u32[]{:S(2)}) collective-permute-start(bf16[32,3072]{1,0:T(8,128)(2,1)S(1)} %get-tuple-element.109.refs_2_), channel_id=1, source_target_pairs={{0,2},{1,3},{2,0},{3,1},{4,6},{5,7},{6,4},{7,5},{8,10},{9,11},{10,... | collective-permute-start | bytes 589832 | tf_op jit(solution)/shard_map/ppermute | solution.py:33
  39.4 12.1 %collective-permute-start.15 = (bf16[64,3072]{1,0:T(8,128)(2,1)S(1)}, bf16[64,3072]{1,0:T(8,128)(2,1)S(1)}, u32[]{:S(2)}, u32[]{:S(2)}) collective-permute-start(bf16[64,3072]{1,0:T(8,128)(2,1)S(1)} %get-tuple-element.105), channel_id=1, source_target_pairs={{0,4},{1,5},{2,6},{3,7},{4,0},{5,1},{6,2},{7,3},{8,12},{9,13},{10,... | collective-permute-start | bytes 1179656 | tf_op jit(solution)/shard_map/ppermute | solution.py:33
  39.6 12.1 %collective-permute-start.16 = (bf16[64,3072]{1,0:T(8,128)(2,1)S(1)}, bf16[64,3072]{1,0:T(8,128)(2,1)S(1)}, u32[]{:S(2)}, u32[]{:S(2)}) collective-permute-start(bf16[64,3072]{1,0:T(8,128)(2,1)S(1)} %get-tuple-element.107), channel_id=1, source_target_pairs={{0,2},{1,3},{2,0},{3,1},{4,6},{5,7},{6,4},{7,5},{8,10},{9,11},{10,... | collective-permute-start | bytes 1179656 | tf_op jit(solution)/shard_map/ppermute | solution.py:33
  45.9 11.8 %collective-permute-start.22 = (bf16[64,3072]{1,0:T(8,128)(2,1)S(1)}, bf16[64,3072]{1,0:T(8,128)(2,1)S(1)}, u32[]{:S(2)}, u32[]{:S(2)}) collective-permute-start(bf16[64,3072]{1,0:T(8,128)(2,1)S(1)} %get-tuple-element.118), channel_id=1, source_target_pairs={{0,4},{1,5},{2,6},{3,7},{4,0},{5,1},{6,2},{7,3},{8,12},{9,13},{10,... | collective-permute-start | bytes 1179656 | tf_op jit(solution)/shard_map/ppermute | solution.py:33
  46.0 12.5 %collective-permute-start.23 = (bf16[64,3072]{1,0:T(8,128)(2,1)S(1)}, bf16[64,3072]{1,0:T(8,128)(2,1)S(1)}, u32[]{:S(2)}, u32[]{:S(2)}) collective-permute-start(bf16[64,3072]{1,0:T(8,128)(2,1)S(1)} %get-tuple-element.120), channel_id=1, source_target_pairs={{0,2},{1,3},{2,0},{3,1},{4,6},{5,7},{6,4},{7,5},{8,10},{9,11},{10,... | collective-permute-start | bytes 1179656 | tf_op jit(solution)/shard_map/ppermute | solution.py:33
  51.8 9.9 %collective-permute-start.20 = (bf16[32,3072]{1,0:T(8,128)(2,1)S(1)}, bf16[32,3072]{1,0:T(8,128)(2,1)S(1)}, u32[]{:S(2)}, u32[]{:S(2)}) collective-permute-start(bf16[32,3072]{1,0:T(8,128)(2,1)S(1)} %get-tuple-element.114), channel_id=1, source_target_pairs={{0,2},{1,3},{2,0},{3,1},{4,6},{5,7},{6,4},{7,5},{8,10},{9,11},{10,... | collective-permute-start | bytes 589832 | tf_op jit(solution)/shard_map/ppermute | solution.py:33
  52.9 8.7 %collective-permute-start.21 = (bf16[32,3072]{1,0:T(8,128)(2,1)S(1)}, bf16[32,3072]{1,0:T(8,128)(2,1)S(1)}, u32[]{:S(2)}, u32[]{:S(2)}) collective-permute-start(bf16[32,3072]{1,0:T(8,128)(2,1)S(1)} %get-tuple-element.116), channel_id=1, source_target_pairs={{0,4},{1,5},{2,6},{3,7},{4,0},{5,1},{6,2},{7,3},{8,12},{9,13},{10,... | collective-permute-start | bytes 589832 | tf_op jit(solution)/shard_map/ppermute | solution.py:33
  56.0 9.6 %collective-permute-start.27 = (bf16[3,256,3072]{2,1,0:T(8,128)(2,1)S(1)}, bf16[3,256,3072]{2,1,0:T(8,128)(2,1)S(1)}, u32[]{:S(2)}, u32[]{:S(2)}) collective-permute-start(bf16[3,256,3072]{2,1,0:T(8,128)(2,1)S(1)} %get-tuple-element.141), channel_id=1, source_target_pairs={{0,1},{1,0},{2,3},{3,2},{4,5},{5,4},{6,7},{7,6},{8,9},{9,8},{10,11... | collective-permute-start | bytes 14155784 | tf_op jit(solution)/shard_map/ppermute | solution.py:33
  58.6 6.3 %collective-permute-start.24 = (bf16[32,3072]{1,0:T(8,128)(2,1)S(1)}, bf16[32,3072]{1,0:T(8,128)(2,1)S(1)}, u32[]{:S(2)}, u32[]{:S(2)}) collective-permute-start(bf16[32,3072]{1,0:T(8,128)(2,1)S(1)} %get-tuple-element.136), channel_id=1, source_target_pairs={{0,2},{1,3},{2,0},{3,1},{4,6},{5,7},{6,4},{7,5},{8,10},{9,11},{10,... | collective-permute-start | bytes 589832 | tf_op jit(solution)/shard_map/ppermute | solution.py:33
  59.4 5.7 %collective-permute-start.25 = (bf16[32,3072]{1,0:T(8,128)(2,1)S(1)}, bf16[32,3072]{1,0:T(8,128)(2,1)S(1)}, u32[]{:S(2)}, u32[]{:S(2)}) collective-permute-start(bf16[32,3072]{1,0:T(8,128)(2,1)S(1)} %get-tuple-element.138), channel_id=1, source_target_pairs={{0,4},{1,5},{2,6},{3,7},{4,0},{5,1},{6,2},{7,3},{8,12},{9,13},{10,... | collective-permute-start | bytes 589832 | tf_op jit(solution)/shard_map/ppermute | solution.py:33
  61.7 6.4 %collective-permute-start.28 = (bf16[2,16,3072]{2,1,0:T(8,128)(2,1)S(1)}, bf16[2,16,3072]{2,1,0:T(8,128)(2,1)S(1)}, u32[]{:S(2)}, u32[]{:S(2)}) collective-permute-start(bf16[2,16,3072]{2,1,0:T(8,128)(2,1)S(1)} %get-tuple-element.143), channel_id=1, source_target_pairs={{0,24},{1,25},{2,26},{3,27},{4,28},{5,29},{6,30},{7,31},{8,0},{9,1... | collective-permute-start | bytes 589832 | tf_op jit(solution)/shard_map/ppermute | solution.py:41
  65.2 9.7 %collective-permute-start.26 = (bf16[2,16,3072]{2,1,0:T(8,128)(2,1)S(1)}, bf16[2,16,3072]{2,1,0:T(8,128)(2,1)S(1)}, u32[]{:S(2)}, u32[]{:S(2)}) collective-permute-start(bf16[2,16,3072]{2,1,0:T(8,128)(2,1)S(1)} %get-tuple-element.140), channel_id=1, source_target_pairs={{0,8},{1,9},{2,10},{3,11},{4,12},{5,13},{6,14},{7,15},{8,16},{9,17... | collective-permute-start | bytes 589832 | tf_op jit(solution)/shard_map/ppermute | solution.py:41
  68.2 8.5 %collective-permute-start.29 = (bf16[2,16,3072]{2,1,0:T(8,128)(2,1)S(1)}, bf16[2,16,3072]{2,1,0:T(8,128)(2,1)S(1)}, u32[]{:S(2)}, u32[]{:S(2)}) collective-permute-start(bf16[2,16,3072]{2,1,0:T(8,128)(2,1)S(1)} %get-tuple-element.149), channel_id=1, source_target_pairs={{0,24},{1,25},{2,26},{3,27},{4,28},{5,29},{6,30},{7,31},{8,0},{9,1... | collective-permute-start | bytes 589832 | tf_op jit(solution)/shard_map/ppermute | solution.py:41
